TPU v7x, 32 devices: a whole 2x2x4 slice. The times are simulated.
32 devices in a mesh: ctx: 4 (over z), fsdp: 8 (over y, x, core).
Axes of the slice: x: 2, y: 2, z: 4, core: 2. Of those that a mesh axis runs over, the one named last changes fastest.
Arguments:
- tokens: bfloat16 [8, 512, 1536], P('fsdp', 'ctx'), may hold values from -6 to 6
- positions: int32 [8, 512], P('fsdp', 'ctx'), may hold values from 0 to 511, as said below
- norm1_gain: bfloat16 [1536], P(('ctx', 'fsdp')), may hold values from 0.5 to 1.5
- q_weight: bfloat16 [1536, 1536], P(('ctx', 'fsdp')), may hold values from -0.15625 to 0.15625
- q_bias: bfloat16 [1536], P(('ctx', 'fsdp')), may hold values from -3 to 3
- key_projection: bfloat16 [1536, 256], P(('ctx', 'fsdp')), may hold values from -0.15625 to 0.15625
- key_bias_vector: bfloat16 [256], P(('ctx', 'fsdp')), may hold values from -3 to 3
- value_projection: bfloat16 [1536, 256], P(('ctx', 'fsdp')), may hold values from -0.15625 to 0.15625
- value_bias_vector: bfloat16 [256], P(('ctx', 'fsdp')), may hold values from -0.59765625 to 0.59765625
- o_weight: bfloat16 [1536, 1536], P(('ctx', 'fsdp')), may hold values from -0.625 to 0.625
- norm2_gain: bfloat16 [1536], P(('ctx', 'fsdp')), may hold values from 0.5 to 1.5
- gate_weight: bfloat16 [1536, 8960], P(('ctx', 'fsdp')), may hold values from -0.15625 to 0.15625
- up_weight: bfloat16 [1536, 8960], P(('ctx', 'fsdp')), may hold values from -0.15625 to 0.15625
- down_weight: bfloat16 [8960, 1536], P(None, ('ctx', 'fsdp')), may hold values from -0.0625 to 0.0625
- cotangent: bfloat16 [8, 512, 1536], P('fsdp', 'ctx'), may hold values from -6 to 6
Outputs:
- layer_out: float32 [8, 512, 1536], P('fsdp', 'ctx')
- grad_tokens: float32 [8, 512, 1536], P('fsdp', 'ctx')
- grad_norm1_gain: float32 [1536], P(('ctx', 'fsdp'))
- grad_q_weight: float32 [1536, 1536], P('fsdp', 'ctx')
- grad_q_bias: float32 [1536], P(('ctx', 'fsdp'))
- grad_k_weight: float32 [1536, 256], P('fsdp', 'ctx')
- grad_k_bias: float32 [256], P(('ctx', 'fsdp'))
- grad_v_weight: float32 [1536, 256], P('fsdp', 'ctx')
- grad_v_bias: float32 [256], P(('ctx', 'fsdp'))
- grad_o_weight: float32 [1536, 1536], P('fsdp', 'ctx')
- grad_norm2_gain: float32 [1536], P(('ctx', 'fsdp'))
- grad_gate_weight: float32 [1536, 8960], P('fsdp', 'ctx')
- grad_up_weight: float32 [1536, 8960], P('fsdp', 'ctx')
- grad_down_weight: float32 [8960, 1536], P('ctx', 'fsdp')
Inputs may be any that keep to these rules, and one draw needn't show every extreme that they name: `positions`: each row of 512 tokens is split into one to four documents at points drawn at random; a token's position counts from 0 at the first token of its document, so documents never cross rows; in every draw one row is a single document.
All inputs are finite; a program needn't handle non-finite values.
Results may differ from a plain program's by a relative error of at most 0.03.
Values may be sent and summed in bfloat16 or wider, within the bound.
No kernel may reach another device: no remote copies, remote signals or barrier semaphores. Data moves between devices by JAX's collectives and lax.ppermute only.
A program may use at most 256 MiB of HBM per device.

v0:
```python
import jax
import jax.numpy as jnp
from jax import lax
from jax.sharding import PartitionSpec as P

QUERY_HEADS = 12
KEY_VALUE_HEADS = 2
HEAD_SIZE = 128


EPSILON = 1e-06


def rms_scale(matrix):
    return lax.rsqrt(jnp.mean(matrix * matrix, axis=-1, keepdims=True) + EPSILON)


def angle_tables(positions):
    step_index = jnp.arange(HEAD_SIZE // 2, dtype=jnp.float32) * 2.0
    frequency = 10000.0 ** (-step_index / HEAD_SIZE)
    angles = positions.astype(jnp.float32)[:, None] * frequency[None, :]
    return (jnp.cos(angles)[:, None, :], jnp.sin(angles)[:, None, :])


def rotate(matrix, cosine, sine_term):
    row_count = matrix.shape[0]
    per_head = matrix.reshape(row_count, -1, HEAD_SIZE)
    half_size = HEAD_SIZE // 2
    first_half = per_head[..., :half_size]
    second_half = per_head[..., half_size:]
    turned = jnp.concatenate(
        [
            first_half * cosine - second_half * sine_term,
            second_half * cosine + first_half * sine_term,
        ],
        axis=-1,
    )
    return turned.reshape(row_count, -1)


def rotate_back(matrix, cosine, sine_term):
    row_count = matrix.shape[0]
    per_head = matrix.reshape(row_count, -1, HEAD_SIZE)
    half_size = HEAD_SIZE // 2
    first_half = per_head[..., :half_size]
    second_half = per_head[..., half_size:]
    turned = jnp.concatenate(
        [
            first_half * cosine + second_half * sine_term,
            second_half * cosine - first_half * sine_term,
        ],
        axis=-1,
    )
    return turned.reshape(row_count, -1)


def across(left_side, right_side):
    return lax.dot_general(
        left_side, right_side, (((0,), (0,)), ((), ())), preferred_element_type=jnp.float32
    )


def compared_keys(left_side, right_side):
    return lax.dot_general(
        left_side, right_side, (((1,), (1,)), ((), ())), preferred_element_type=jnp.float32
    )


def per_device(
    tokens,
    positions,
    norm1_gain,
    q_weight,
    q_bias,
    key_projection,
    key_bias_vector,
    value_projection,
    value_bias_vector,
    o_weight,
    norm2_gain,
    gate_weight,
    up_weight,
    down_weight,
    cotangent,
):
    heads_per_group = QUERY_HEADS // KEY_VALUE_HEADS
    key_value_width = KEY_VALUE_HEADS * HEAD_SIZE
    score_scale = HEAD_SIZE ** (-0.5)
    gathered = (
        lax.all_gather(norm1_gain, ("ctx", "fsdp"), axis=0, tiled=True),
        lax.all_gather(q_weight, ("ctx", "fsdp"), axis=0, tiled=True),
        lax.all_gather(q_bias, ("ctx", "fsdp"), axis=0, tiled=True),
        lax.all_gather(key_projection, ("ctx", "fsdp"), axis=0, tiled=True),
        lax.all_gather(key_bias_vector, ("ctx", "fsdp"), axis=0, tiled=True),
        lax.all_gather(value_projection, ("ctx", "fsdp"), axis=0, tiled=True),
        lax.all_gather(value_bias_vector, ("ctx", "fsdp"), axis=0, tiled=True),
        lax.all_gather(o_weight, ("ctx", "fsdp"), axis=0, tiled=True),
        lax.all_gather(norm2_gain, ("ctx", "fsdp"), axis=0, tiled=True),
        lax.all_gather(gate_weight, ("ctx", "fsdp"), axis=0, tiled=True),
        lax.all_gather(up_weight, ("ctx", "fsdp"), axis=0, tiled=True),
        lax.all_gather(down_weight, ("ctx", "fsdp"), axis=1, tiled=True),
    )
    (
        gain_one,
        weight_q,
        bias_q,
        weight_k,
        bias_k,
        weight_v,
        bias_v,
        output_projection,
        gain_two,
        weight_gate,
        weight_up,
        weight_down,
    ) = gathered
    stream = tokens[0].astype(jnp.float32)
    local_pos = positions[0]
    token_count = stream.shape[0]
    scale_one = rms_scale(stream)
    unit_one = stream * scale_one
    normed_one = (unit_one * gain_one.astype(jnp.float32)).astype(jnp.bfloat16)
    cosine, sine_term = angle_tables(local_pos)
    q_linear = jnp.dot(normed_one, weight_q, preferred_element_type=jnp.float32) + bias_q.astype(
        jnp.float32
    )
    k_linear = jnp.dot(normed_one, weight_k, preferred_element_type=jnp.float32) + bias_k.astype(
        jnp.float32
    )
    v_linear = jnp.dot(normed_one, weight_v, preferred_element_type=jnp.float32) + bias_v.astype(
        jnp.float32
    )
    query_rows = (
        rotate(q_linear, cosine, sine_term)
        .astype(jnp.bfloat16)
        .reshape(token_count, KEY_VALUE_HEADS, heads_per_group, HEAD_SIZE)
    )
    local_pairs = jnp.concatenate([rotate(k_linear, cosine, sine_term), v_linear], axis=1).astype(
        jnp.bfloat16
    )
    group_pairs = lax.all_gather(local_pairs, "ctx", axis=0, tiled=True)
    group_len = group_pairs.shape[0]
    block_length = min(512, group_len)
    block_count = group_len // block_length
    block_pairs = group_pairs.reshape(block_count, block_length, 2 * key_value_width)
    block_numbers = jnp.arange(block_count)
    query_index = lax.axis_index("ctx") * token_count + jnp.arange(token_count)
    doc_start = query_index - local_pos
    last_query = query_index[-1]
    first_start = jnp.min(doc_start)

    def block_scores(key_tile_block, block_base):
        key_portion = key_tile_block[:, :key_value_width].reshape(
            block_length, KEY_VALUE_HEADS, HEAD_SIZE
        )
        value_portion = key_tile_block[:, key_value_width:].reshape(
            block_length, KEY_VALUE_HEADS, HEAD_SIZE
        )
        scores = (
            jnp.einsum(
                "qkgd,rkd->kgqr", query_rows, key_portion, preferred_element_type=jnp.float32
            )
            * score_scale
        )
        key_index = block_base + jnp.arange(block_length)
        allowed = (key_index[None, :] >= doc_start[:, None]) & (
            key_index[None, :] <= query_index[:, None]
        )
        masked = jnp.where(allowed, scores, -1e30)
        return (masked, allowed, key_portion, value_portion)

    def needed_for(block_base):
        return (block_base <= last_query) & (block_base + block_length > first_start)

    def stats_step(running, scan_item):
        key_tile_block, number = scan_item
        block_base = number * block_length

        def refresh(running):
            row_top, row_total = running
            masked, allowed, key_portion, value_portion = block_scores(key_tile_block, block_base)
            new_top = jnp.maximum(row_top, jnp.max(masked, axis=-1))
            fresh = jnp.sum(jnp.where(allowed, jnp.exp(masked - new_top[..., None]), 0.0), axis=-1)
            return (new_top, row_total * jnp.exp(row_top - new_top) + fresh)

        return (
            lax.cond(needed_for(block_base), refresh, lambda kept_state: kept_state, running),
            None,
        )

    start_state = (
        jnp.full((KEY_VALUE_HEADS, heads_per_group, token_count), -1e30, jnp.float32),
        jnp.zeros((KEY_VALUE_HEADS, heads_per_group, token_count), jnp.float32),
    )
    (row_top, row_total), ignored = lax.scan(stats_step, start_state, (block_pairs, block_numbers))
    log_total = row_top + jnp.log(row_total)

    def mixing_update(carried, scan_item):
        key_tile_block, number = scan_item
        block_base = number * block_length

        def accumulate(carried):
            attended, remainder = carried
            masked, allowed, key_portion, value_portion = block_scores(key_tile_block, block_base)
            softmax_full = jnp.exp(masked - log_total[..., None])
            softmax_part = softmax_full.astype(jnp.bfloat16)
            leftover = (softmax_full - softmax_part.astype(jnp.float32)).astype(jnp.bfloat16)
            attended = attended + jnp.einsum(
                "kgqr,rkd->qkgd", softmax_part, value_portion, preferred_element_type=jnp.float32
            )
            remainder = remainder + jnp.einsum(
                "kgqr,rkd->qkgd", leftover, value_portion, preferred_element_type=jnp.float32
            )
            return (attended, remainder)

        return (
            lax.cond(needed_for(block_base), accumulate, lambda kept_state: kept_state, carried),
            None,
        )

    empty_mix = jnp.zeros((token_count, KEY_VALUE_HEADS, heads_per_group, HEAD_SIZE), jnp.float32)
    (attended, remainder), ignored = lax.scan(
        mixing_update, (empty_mix, empty_mix), (block_pairs, block_numbers)
    )
    mixed_low = attended.reshape(token_count, QUERY_HEADS * HEAD_SIZE).astype(jnp.bfloat16)
    hidden_one = stream + jnp.dot(mixed_low, output_projection, preferred_element_type=jnp.float32)
    scale_two = rms_scale(hidden_one)
    unit_two = hidden_one * scale_two
    normed_two = (unit_two * gain_two.astype(jnp.float32)).astype(jnp.bfloat16)
    gate_pre = jnp.dot(normed_two, weight_gate, preferred_element_type=jnp.float32)
    up_pre = jnp.dot(normed_two, weight_up, preferred_element_type=jnp.float32)
    sigmoid_gate = jax.nn.sigmoid(gate_pre)
    activated = (gate_pre * sigmoid_gate * up_pre).astype(jnp.bfloat16)
    layer_out = hidden_one + jnp.dot(activated, weight_down, preferred_element_type=jnp.float32)
    gain_two, weight_gate, weight_up, weight_down = (
        lax.all_gather(norm2_gain, ("ctx", "fsdp"), axis=0, tiled=True),
        lax.all_gather(gate_weight, ("ctx", "fsdp"), axis=0, tiled=True),
        lax.all_gather(up_weight, ("ctx", "fsdp"), axis=0, tiled=True),
        lax.all_gather(down_weight, ("ctx", "fsdp"), axis=1, tiled=True),
    )
    out_low = cotangent[0]
    out_grad = out_low.astype(jnp.float32)
    grad_act = compared_keys(out_low, weight_down)
    grad_gate_low = (
        grad_act * up_pre * sigmoid_gate * (1.0 + gate_pre * (1.0 - sigmoid_gate))
    ).astype(jnp.bfloat16)
    grad_up_low = (grad_act * gate_pre * sigmoid_gate).astype(jnp.bfloat16)
    grad_normed_two = compared_keys(grad_gate_low, weight_gate) + compared_keys(
        grad_up_low, weight_up
    )
    grad_gain_two = jnp.sum(grad_normed_two * unit_two, axis=0)
    weighted_two = grad_normed_two * gain_two.astype(jnp.float32)
    grad_hidden = out_grad + scale_two * (
        weighted_two - unit_two * jnp.mean(weighted_two * unit_two, axis=-1, keepdims=True)
    )
    gain_one, weight_q, weight_k, weight_v, output_projection = (
        lax.all_gather(norm1_gain, ("ctx", "fsdp"), axis=0, tiled=True),
        lax.all_gather(q_weight, ("ctx", "fsdp"), axis=0, tiled=True),
        lax.all_gather(key_projection, ("ctx", "fsdp"), axis=0, tiled=True),
        lax.all_gather(value_projection, ("ctx", "fsdp"), axis=0, tiled=True),
        lax.all_gather(o_weight, ("ctx", "fsdp"), axis=0, tiled=True),
    )
    attention_reduced = grad_hidden.astype(jnp.bfloat16)
    grad_mixed = (
        compared_keys(attention_reduced, output_projection)
        .astype(jnp.bfloat16)
        .reshape(token_count, KEY_VALUE_HEADS, heads_per_group, HEAD_SIZE)
    )
    exact_mix = attended + remainder
    row_delta = jnp.transpose(
        jnp.sum(grad_mixed.astype(jnp.float32) * exact_mix, axis=-1), (1, 2, 0)
    )

    def grad_step(grad_query, scan_item):
        key_tile_block, number = scan_item
        block_base = number * block_length

        def compute(grad_query):
            masked, allowed, key_portion, value_portion = block_scores(key_tile_block, block_base)
            softmax_part = jnp.exp(masked - log_total[..., None])
            grad_probs = jnp.einsum(
                "qkgd,rkd->kgqr", grad_mixed, value_portion, preferred_element_type=jnp.float32
            )
            grad_scores = (softmax_part * (grad_probs - row_delta[..., None])).astype(jnp.bfloat16)
            grad_query = grad_query + jnp.einsum(
                "kgqr,rkd->qkgd", grad_scores, key_portion, preferred_element_type=jnp.float32
            )
            grad_key = (
                jnp.einsum(
                    "kgqr,qkgd->rkd", grad_scores, query_rows, preferred_element_type=jnp.float32
                )
                * score_scale
            )
            grad_value = jnp.einsum(
                "kgqr,qkgd->rkd",
                softmax_part.astype(jnp.bfloat16),
                grad_mixed,
                preferred_element_type=jnp.float32,
            )
            pieces = jnp.concatenate(
                [
                    grad_key.reshape(block_length, key_value_width),
                    grad_value.reshape(block_length, key_value_width),
                ],
                axis=1,
            )
            return (grad_query, pieces)

        def skip_block(grad_query):
            return (grad_query, jnp.zeros((block_length, 2 * key_value_width), jnp.float32))

        return lax.cond(needed_for(block_base), compute, skip_block, grad_query)

    grad_query, pair_terms = lax.scan(
        grad_step,
        jnp.zeros((token_count, KEY_VALUE_HEADS, heads_per_group, HEAD_SIZE), jnp.float32),
        (block_pairs, block_numbers),
    )
    pair_grads = lax.psum_scatter(
        pair_terms.reshape(group_len, 2 * key_value_width), "ctx", scatter_dimension=0, tiled=True
    )
    grad_q_low = rotate_back(
        grad_query.reshape(token_count, QUERY_HEADS * HEAD_SIZE) * score_scale, cosine, sine_term
    ).astype(jnp.bfloat16)
    grad_k_low = rotate_back(pair_grads[:, :key_value_width], cosine, sine_term).astype(
        jnp.bfloat16
    )
    grad_v_low = pair_grads[:, key_value_width:].astype(jnp.bfloat16)
    grad_normed_one = (
        compared_keys(grad_q_low, weight_q)
        + compared_keys(grad_k_low, weight_k)
        + compared_keys(grad_v_low, weight_v)
    )
    grad_gain_one = jnp.sum(grad_normed_one * unit_one, axis=0)
    weighted_one = grad_normed_one * gain_one.astype(jnp.float32)
    grad_stream = grad_hidden + scale_one * (
        weighted_one - unit_one * jnp.mean(weighted_one * unit_one, axis=-1, keepdims=True)
    )
    row_normed_one, row_mixed, row_normed_two, row_out = (
        lax.all_gather(normed_one, "ctx", axis=0, tiled=True),
        lax.all_gather(mixed_low, "ctx", axis=0, tiled=True),
        lax.all_gather(normed_two, "ctx", axis=0, tiled=True),
        lax.all_gather(out_low, "ctx", axis=0, tiled=True),
    )
    share_q, share_k, share_v, share_o, share_gate, share_up, share_act = (
        lax.all_to_all(grad_q_low, "ctx", split_axis=1, concat_axis=0, tiled=True),
        lax.all_to_all(grad_k_low, "ctx", split_axis=1, concat_axis=0, tiled=True),
        lax.all_to_all(grad_v_low, "ctx", split_axis=1, concat_axis=0, tiled=True),
        lax.all_to_all(attention_reduced, "ctx", split_axis=1, concat_axis=0, tiled=True),
        lax.all_to_all(grad_gate_low, "ctx", split_axis=1, concat_axis=0, tiled=True),
        lax.all_to_all(grad_up_low, "ctx", split_axis=1, concat_axis=0, tiled=True),
        lax.all_to_all(activated, "ctx", split_axis=1, concat_axis=0, tiled=True),
    )
    term_q = across(row_normed_one, share_q)
    term_k = across(row_normed_one, share_k)
    term_v = across(row_normed_one, share_v)
    term_o = across(row_mixed, share_o)
    term_gate = across(row_normed_two, share_gate)
    term_up = across(row_normed_two, share_up)
    term_down = across(row_out, share_act)
    term_bias_q = jnp.sum(share_q.astype(jnp.float32), axis=0)
    term_bias_k = jnp.sum(share_k.astype(jnp.float32), axis=0)
    term_bias_v = jnp.sum(share_v.astype(jnp.float32), axis=0)
    summed = (
        lax.psum_scatter(
            term_q.astype(jnp.bfloat16), "fsdp", scatter_dimension=0, tiled=True
        ).astype(jnp.float32),
        lax.psum_scatter(
            term_bias_q.astype(jnp.bfloat16), "fsdp", scatter_dimension=0, tiled=True
        ).astype(jnp.float32),
        lax.psum_scatter(
            term_k.astype(jnp.bfloat16), "fsdp", scatter_dimension=0, tiled=True
        ).astype(jnp.float32),
        lax.psum_scatter(
            term_bias_k.astype(jnp.bfloat16), "fsdp", scatter_dimension=0, tiled=True
        ).astype(jnp.float32),
        lax.psum_scatter(
            term_v.astype(jnp.bfloat16), "fsdp", scatter_dimension=0, tiled=True
        ).astype(jnp.float32),
        lax.psum_scatter(
            term_bias_v.astype(jnp.bfloat16), "fsdp", scatter_dimension=0, tiled=True
        ).astype(jnp.float32),
        lax.psum_scatter(
            term_o.astype(jnp.bfloat16), "fsdp", scatter_dimension=0, tiled=True
        ).astype(jnp.float32),
        lax.psum_scatter(
            term_gate.astype(jnp.bfloat16), "fsdp", scatter_dimension=0, tiled=True
        ).astype(jnp.float32),
        lax.psum_scatter(
            term_up.astype(jnp.bfloat16), "fsdp", scatter_dimension=0, tiled=True
        ).astype(jnp.float32),
        lax.psum_scatter(
            term_down.astype(jnp.bfloat16), "fsdp", scatter_dimension=0, tiled=True
        ).astype(jnp.float32),
    )
    (
        grad_wq,
        grad_bq,
        grad_wk,
        grad_bk,
        grad_wv,
        grad_bv,
        grad_wo,
        grad_gate_part,
        grad_up_part,
        grad_down_part,
    ) = summed
    gain_grad_one, gain_grad_two = (
        lax.psum_scatter(grad_gain_one, ("ctx", "fsdp"), scatter_dimension=0, tiled=True),
        lax.psum_scatter(grad_gain_two, ("ctx", "fsdp"), scatter_dimension=0, tiled=True),
    )
    return (
        layer_out[None],
        grad_stream[None],
        gain_grad_one,
        grad_wq,
        grad_bq,
        grad_wk,
        grad_bk,
        grad_wv,
        grad_bv,
        grad_wo,
        gain_grad_two,
        grad_gate_part,
        grad_up_part,
        jnp.transpose(grad_down_part),
    )


def solution(mesh):
    in_specs = (
        P("fsdp", "ctx", None),
        P("fsdp", "ctx"),
        P(("ctx", "fsdp")),
        P(("ctx", "fsdp"), None),
        P(("ctx", "fsdp")),
        P(("ctx", "fsdp"), None),
        P(("ctx", "fsdp")),
        P(("ctx", "fsdp"), None),
        P(("ctx", "fsdp")),
        P(("ctx", "fsdp"), None),
        P(("ctx", "fsdp")),
        P(("ctx", "fsdp"), None),
        P(("ctx", "fsdp"), None),
        P(None, ("ctx", "fsdp")),
        P("fsdp", "ctx", None),
    )
    out_specs = (
        P("fsdp", "ctx", None),
        P("fsdp", "ctx", None),
        P(("ctx", "fsdp")),
        P("fsdp", "ctx"),
        P(("ctx", "fsdp")),
        P("fsdp", "ctx"),
        P(("ctx", "fsdp")),
        P("fsdp", "ctx"),
        P(("ctx", "fsdp")),
        P("fsdp", "ctx"),
        P(("ctx", "fsdp")),
        P("fsdp", "ctx"),
        P("fsdp", "ctx"),
        P("ctx", "fsdp"),
    )
    return jax.shard_map(
        per_device, mesh=mesh, in_specs=in_specs, out_specs=out_specs, check_vma=False
    )
```

profile of v0, /device:TPU:0, one launch (start us, length us, event | category | flops | bytes accessed | tf_op | source)
XLA Modules:
  0.0 1292.9 jit_solution(16499004965898563316)
XLA Ops:
  14.9 42.6 %all-reduce.11 = (bf16[1536]{0:T(1024)(128)(2,1)S(1)}, bf16[256]{0:T(256)(128)(2,1)S(1)}, bf16[256]{0:T(256)(128)(2,1)S(1)}, bf16[1536]{0:T(1024)(128)(2,1)S(1)}, bf16[1536]{0:T(1024)(128)(2,1)S(1)}) all-reduce(bf16[1536]{0:T(1024)(128)(2,1)S(1)} %dynamic-update-slice, ...), channel_id=1, replica_groups=mesh['ctx'=4,'fsdp'=8] {'ctx','fsdp'}, use_global_device_ids=true, to_apply=%add | all-reduce | flops 5120 | bytes 20480
  61.8 43.4 %all_gather.63 = bf16[1536,256]{1,0:T(8,128)(2,1)S(1)} all-gather(bf16[48,256]{1,0:T(8,128)(2,1)S(1)} %copy-done.25), channel_id=1, replica_groups=mesh['ctx'=4,'fsdp'=8] {'ctx','fsdp'}, dimensions={0}, use_global_device_ids=true | all-gather | bytes 811008 | tf_op jit(solution)/shard_map/all_gather | solution.py:95
  105.2 41.1 %all_gather.61 = bf16[1536,256]{1,0:T(8,128)(2,1)S(1)} all-gather(bf16[48,256]{1,0:T(8,128)(2,1)S(1)} %copy-done.26), channel_id=1, replica_groups=mesh['ctx'=4,'fsdp'=8] {'ctx','fsdp'}, dimensions={0}, use_global_device_ids=true | all-gather | bytes 811008 | tf_op jit(solution)/shard_map/all_gather | solution.py:93
  149.2 17.0 %all_gather.65 = bf16[512,512]{1,0:T(8,128)(2,1)S(1)} all-gather(bf16[128,512]{1,0:T(8,128)(2,1)S(1)} %pad_maximum_fusion.2), channel_id=1, replica_groups=mesh['ctx'=4,'fsdp'=8] {'ctx'}, dimensions={0}, use_global_device_ids=true | all-gather | bytes 655360 | tf_op jit(solution)/shard_map/all_gather | solution.py:141
  167.4 4.0 convolution_add_fusion.3
  173.1 1.8 conditional.3
  175.6 5.9 conditional.4
  176.6 1.7 fusion.17
  178.3 2.7 fusion.20
  184.6 3.6 multiply_reduce_fusion.3
  188.2 2.3 copy.110
  190.7 125.4 %all-gather.15.cloned.1.call-done = bf16[1536,8960]{1,0:T(8,128)(2,1)} async-done(((bf16[48,8960]{1,0:T(8,128)(2,1)}), bf16[1536,8960]{1,0:T(8,128)(2,1)}) %all-gather.15.cloned.1.call-update) | async-done | bytes 27525136 | tf_op jit(solution)/shard_map/all_gather | solution.py:99
  316.1 14.9 %fusion.68 = f32[128,8960]{1,0:T(8,128)} fusion(bf16[128,1536]{1,0:T(8,128)(2,1)S(1)} %multiply_convert_fusion.3, bf16[1536,8960]{1,0:T(8,128)(2,1)} %all-gather.15.cloned.1.call-done), kind=kOutput, calls=%fused_computation.137 | convolution fusion | flops 3523215360 | bytes 32505856 | tf_op jit(solution)/shard_map/dot_general | solution.py:230
  331.0 152.0 %all-gather.17.cloned.1.call-done = bf16[1536,8960]{1,0:T(8,128)(2,1)} async-done(((bf16[48,8960]{1,0:T(8,128)(2,1)}), bf16[1536,8960]{1,0:T(8,128)(2,1)}) %all-gather.17.cloned.1.call-update) | async-done | bytes 27525136 | tf_op jit(solution)/shard_map/all_gather | solution.py:100
  483.0 14.8 %fusion.69 = f32[128,8960]{1,0:T(8,128)} fusion(bf16[128,1536]{1,0:T(8,128)(2,1)S(1)} %multiply_convert_fusion.3, bf16[1536,8960]{1,0:T(8,128)(2,1)} %all-gather.17.cloned.1.call-done), kind=kOutput, calls=%fused_computation.138 | convolution fusion | flops 3523215360 | bytes 32505856 | tf_op jit(solution)/shard_map/dot_general | solution.py:231
  497.8 152.1 %all-gather.19.cloned.1.call-done = bf16[8960,1536]{0,1:T(8,128)(2,1)} async-done(((bf16[8960,48]{0,1:T(8,128)(2,1)}), bf16[8960,1536]{0,1:T(8,128)(2,1)}) %all-gather.19.cloned.1.call-update) | async-done | bytes 27525136 | tf_op jit(solution)/shard_map/all_gather | solution.py:101
  649.9 17.9 %multiply_convert_fusion = (bf16[128,8960]{1,0:T(8,128)(2,1)}, bf16[128,8960]{1,0:T(8,128)(2,1)}, bf16[128,8960]{1,0:T(8,128)(2,1)}) fusion(f32[128,8960]{1,0:T(8,128)} %fusion.68, f32[128,8960]{1,0:T(8,128)} %fusion.69, bf16[8960,1536]{0,1:T(8,128)(2,1)} %all-gather.19.cloned.1.call-done, bf16[1,128,1536]{2,1,0:T(8,128)(2,1)} %param.35), kind=kOutput, calls=%fused_computation.53 | convolution fusion | flops 3541565440 | bytes 43974656 | tf_op jit(solution)/shard_map/dot_general | solution.py:64
  667.8 15.3 %fusion.70 = f32[128,1536]{1,0:T(8,128)} fusion(bf16[128,8960]{1,0:T(8,128)(2,1)} %get-tuple-element.370, bf16[1536,8960]{1,0:T(8,128)(2,1)} %all-gather.15.cloned.1.call-done), kind=kOutput, calls=%fused_computation.139 | convolution fusion | flops 3523215360 | bytes 30605312 | tf_op jit(solution)/shard_map/dot_general | solution.py:64
  683.2 16.1 %multiply_reduce_fusion = (f32[1536]{0:T(1024)}, f32[128]{0:T(128)S(1)}, f32[128,1536]{1,0:T(8,128)}) fusion(f32[128,1536]{1,0:T(8,128)S(1)} %get-tuple-element.383, f32[128]{0:T(128)S(1)} %add_rsqrt_fusion, f32[1536]{0:T(1024)S(1)} %convert_element_type.199, f32[128,1536]{1,0:T(8,128)} %fusion.70, bf16[128,8960]{1,0:T(8,128)(2,1)} %get-tuple-element.369, ...), kind=kOutput, calls=%fused_computation.89 | convolution fusion | flops 3524590080 | bytes 32191488 | tf_op jit(solution)/shard_map/dot_general | solution.py:64
  701.5 4.7 convolution_convert_fusion.5
  707.4 2.1 multiply_reduce_fusion.1
  709.5 9.1 conditional.5
  713.2 1.8 fusion.27
  723.0 3.5 all-to-all-start
  727.3 22.3 %all-to-all-done = bf16[128,4,384]{0,2,1:T(8,128)(2,1)S(1)} async-done(((bf16[128,4,384]{0,2,1:T(8,128)(2,1)}), bf16[128,4,384]{0,2,1:T(8,128)(2,1)S(1)}, u32[]{:S(2)}, u32[]{:S(2)}) %all-to-all-start) | async-done | bytes 393248 | tf_op jit(solution)/shard_map/all_to_all | solution.py:346
  749.6 4.1 all-to-all-start.3
  754.8 3.6 convolution_convert_fusion.4
  760.1 12.0 all-to-all-done.3
  772.0 3.3 all-to-all-start.1
  776.9 4.5 all-to-all-done.1
  781.4 5.3 all-to-all-start.2
  786.7 2.5 copy.121
  789.2 3.7 all-to-all-done.2
  792.9 3.6 all-to-all-start.6
  796.6 3.5 convolution_convert_fusion.3
  800.1 2.5 convolution_convert_fusion.7
  802.6 1.8 copy.157
  804.5 2.5 convolution_convert_fusion.6
  807.1 1.9 copy.159
  809.0 64.5 %all-to-all-done.6 = bf16[128,4,2240]{0,2,1:T(8,128)(2,1)S(1)} async-done(((bf16[128,4,2240]{0,2,1:T(8,128)(2,1)}), bf16[128,4,2240]{0,2,1:T(8,128)(2,1)S(1)}, u32[]{:S(2)}, u32[]{:S(2)}) %all-to-all-start.6) | async-done | bytes 2293792 | tf_op jit(solution)/shard_map/all_to_all | solution.py:352
  873.4 2.8 copy.122
  876.2 8.7 fusion.39
  884.9 10.3 copy.161
  896.8 2.5 copy.117
  899.3 59.1 %all_to_all.127 = bf16[128,4,2240]{0,2,1:T(8,128)(2,1)S(1)} all-to-all(bf16[128,4,2240]{0,2,1:T(8,128)(2,1)} %bitcast.241), channel_id=1, replica_groups=mesh['ctx'=4,'fsdp'=8] {'ctx'}, dimensions={1} | all-to-all | bytes 4587520 | tf_op jit(solution)/shard_map/all_to_all | solution.py:350
  958.4 2.8 copy.118
  961.2 8.9 convolution_convert_fusion.2
  971.8 2.5 copy.119
  974.2 56.2 %all_to_all.128 = bf16[128,4,2240]{0,2,1:T(8,128)(2,1)S(1)} all-to-all(bf16[128,4,2240]{0,2,1:T(8,128)(2,1)} %bitcast.243), channel_id=1, replica_groups=mesh['ctx'=4,'fsdp'=8] {'ctx'}, dimensions={1} | all-to-all | bytes 4587520 | tf_op jit(solution)/shard_map/all_to_all | solution.py:351
  1030.5 2.8 copy.120
  1033.3 8.9 convolution_convert_fusion.1
  1044.9 5.1 fusion.71
  1050.0 14.9 %fusion.40 = f32[1,128,1536]{2,1,0:T(8,128)} fusion(f32[128,1536]{1,0:T(8,128)S(1)} %get-tuple-element.383, bf16[128,8960]{1,0:T(8,128)(2,1)S(1)} %copy-done.2, bf16[8960,1536]{0,1:T(8,128)(2,1)} %all-gather.19.cloned.1.call-done), kind=kOutput, calls=%fused_computation.65 | convolution fusion | flops 3523411968 | bytes 31391744 | tf_op jit(solution)/shard_map/dot_general | solution.py:234
  1066.3 1.8 convolution_add_fusion.1
  1068.1 2.2 fusion.53
  1070.3 39.3 %all-reduce.10 = (f32[1536]{0:T(1024)S(1)}, f32[1536]{0:T(1024)S(1)}) all-reduce(f32[1536]{0:T(1024)S(1)} %get-tuple-element.349, f32[1536]{0:T(1024)S(1)} %copy-done.24), channel_id=4, replica_groups=mesh['ctx'=4,'fsdp'=8] {'ctx','fsdp'}, use_global_device_ids=true, to_apply=%region_16.17.clone | all-reduce | flops 3072 | bytes 24576
  1110.8 2.4 fusion.52
  1114.4 13.0 %all-reduce.12 = (bf16[384]{0:T(512)(128)(2,1)S(1)}, bf16[64]{0:T(256)(128)(2,1)S(1)}, bf16[64]{0:T(256)(128)(2,1)S(1)}) all-reduce(bf16[384]{0:T(512)(128)(2,1)S(1)} %reduce_sum.114, bf16[64]{0:T(256)(128)(2,1)S(1)} %reduce_sum.115, bf16[64]{0:T(256)(128)(2,1)S(1)} %reduce_sum.116), channel_id=6, replica_groups=mesh['ctx'=4,'fsdp'=8] {'fsdp'}, use_global_device_ids=true, to_apply=%region_19.20.clone | all-reduce | flops 512 | bytes 2048
  1134.9 10.5 reduce-scatter.29.cloned.1.call-done
  1147.4 1.9 copy.123
  1149.3 65.0 %reduce-scatter.21.cloned.1.call-done = bf16[192,2240]{1,0:T(8,128)(2,1)} async-done(((bf16[1536,2240]{1,0:T(8,128)(2,1)}), bf16[192,2240]{1,0:T(8,128)(2,1)}) %reduce-scatter.21.cloned.1.call-update) | async-done | bytes 860176 | tf_op jit(solution)/shard_map/reduce_scatter | solution.py:386
  1214.4 2.5 convert_element_type.226
  1216.8 66.8 %reduce-scatter.23.cloned.1.call-done = bf16[192,2240]{1,0:T(8,128)(2,1)} async-done(((bf16[1536,2240]{1,0:T(8,128)(2,1)}), bf16[192,2240]{1,0:T(8,128)(2,1)}) %reduce-scatter.23.cloned.1.call-update) | async-done | bytes 860176 | tf_op jit(solution)/shard_map/reduce_scatter | solution.py:389
  1283.7 2.5 convert_element_type.228
  (217 shorter events, 60.2 us)
Async XLA Ops:
  7.2 50.3 %copy-start.4 = (bf16[1,128,1536]{2,1,0:T(8,128)(2,1)S(1)}, bf16[1,128,1536]{2,1,0:T(8,128)(2,1)}, u32[]{:S(2)}) copy-start(bf16[1,128,1536]{2,1,0:T(8,128)(2,1)} %param.21) | copy-start | bytes 1179652
  7.2 51.5 %copy-start.39 = (s32[1,128]{1,0:T(1,128)S(1)}, s32[1,128]{1,0:T(1,128)}, u32[]{:S(2)}) copy-start(s32[1,128]{1,0:T(1,128)} %param.22) | copy-start | bytes 1540
  7.2 54.6 %copy-start.25 = (bf16[48,256]{1,0:T(8,128)(2,1)S(1)}, bf16[48,256]{1,0:T(8,128)(2,1)}, u32[]{:S(2)}) copy-start(bf16[48,256]{1,0:T(8,128)(2,1)} %param.28) | copy-start | bytes 73732
  7.2 98.0 %copy-start.26 = (bf16[48,256]{1,0:T(8,128)(2,1)S(1)}, bf16[48,256]{1,0:T(8,128)(2,1)}, u32[]{:S(2)}) copy-start(bf16[48,256]{1,0:T(8,128)(2,1)} %param.26) | copy-start | bytes 73732
  7.2 160.2 %all-gather.11.cloned.1.call-start = ((), (), s32[]{:S(2)}) async-start(), calls=%async_computation.15 | async-start | bytes 4866048 | tf_op jit(solution)/shard_map/all_gather | solution.py:91
  8.0 175.9 %all-gather.13.cloned.1.call-start = ((), (), s32[]{:S(2)}) async-start(), calls=%async_computation.16 | async-start | bytes 4866048 | tf_op jit(solution)/shard_map/all_gather | solution.py:97
  8.7 307.4 %all-gather.15.cloned.1.call-start = ((), (), s32[]{:S(2)}) async-start(), calls=%async_computation.17 | async-start | bytes 28385280 | tf_op jit(solution)/shard_map/all_gather | solution.py:99
  9.4 473.6 %all-gather.17.cloned.1.call-start = ((), (), s32[]{:S(2)}) async-start(), calls=%async_computation.18 | async-start | bytes 28385280 | tf_op jit(solution)/shard_map/all_gather | solution.py:100
  10.0 639.9 %all-gather.19.cloned.1.call-start = ((), (), s32[]{:S(2)}) async-start(), calls=%async_computation.19 | async-start | bytes 28385280 | tf_op jit(solution)/shard_map/all_gather | solution.py:101
  10.6 744.2 %all-gather.21.cloned.1.call-start = ((), (), s32[]{:S(2)}) async-start(), calls=%async_computation.21 | async-start | bytes 1966080 | tf_op jit(solution)/shard_map/all_gather | solution.py:340
  57.7 1.0 copy-start.35
  58.6 90.3 %copy-start.5 = (bf16[128,1536]{1,0:T(8,128)(2,1)S(1)}, bf16[128,1536]{1,0:T(8,128)(2,1)}, u32[]{:S(2)}) copy-start(bf16[128,1536]{1,0:T(8,128)(2,1)} %fusion.47) | copy-start | bytes 1179652
  58.6 699.8 %reduce-scatter.15.cloned.1.call-start = ((), (), s32[]{:S(2)}) async-start(), calls=%async_computation.20 | async-start | bytes 1310720 | tf_op jit(solution)/shard_map/reduce_scatter | solution.py:319
  58.7 89.7 %copy-start.32 = (s32[128]{0:T(128)}, s32[128]{0:T(128)S(1)}, u32[]{:S(2)}) copy-start(s32[128]{0:T(128)S(1)} %iota_add_fusion) | copy-start | bytes 1540
  105.2 66.2 %copy-start.8 = (bf16[1536,256]{1,0:T(8,128)(2,1)}, bf16[1536,256]{1,0:T(8,128)(2,1)S(1)}, u32[]{:S(2)}) copy-start(bf16[1536,256]{1,0:T(8,128)(2,1)S(1)} %all_gather.63) | copy-start | bytes 2359300
  146.3 0.9 copy-start.6
  171.4 1.6 copy-start.22
  171.4 1.6 copy-start.23
  171.4 1.6 copy-start.30
  171.5 1.6 copy-start.33
  181.5 0.9 copy-start.19
  183.8 0.9 copy-start.7
  183.8 4.4 copy-start.13
  188.2 511.1 %copy-start.28 = (f32[128]{0:T(128)}, f32[128]{0:T(128)S(1)}, u32[]{:S(2)}) copy-start(f32[128]{0:T(128)S(1)} %add_rsqrt_fusion) | copy-start | bytes 1540
  190.7 292.4 %copy-start.11 = (bf16[128,1536]{1,0:T(8,128)(2,1)}, bf16[128,1536]{1,0:T(8,128)(2,1)S(1)}, u32[]{:S(2)}) copy-start(bf16[128,1536]{1,0:T(8,128)(2,1)S(1)} %multiply_convert_fusion.3) | copy-start | bytes 1179652
  683.2 16.2 %copy-start.15 = (bf16[1,128,1536]{2,1,0:T(8,128)(2,1)S(1)}, bf16[1,128,1536]{2,1,0:T(8,128)(2,1)}, u32[]{:S(2)}) copy-start(bf16[1,128,1536]{2,1,0:T(8,128)(2,1)} %param.35) | copy-start | bytes 1179652
  699.3 6.9 copy-start.37
  700.7 0.8 copy-start.17
  709.5 0.7 copy-start.20
  711.3 1.8 copy-start.31
  711.3 1.8 copy-start.34
  711.3 1.8 copy-start.21
  711.3 1.8 copy-start.27
  718.7 1.0 copy-start.12
  719.7 76.9 %all-gather.23.cloned.1.call-start = ((), (), s32[]{:S(2)}) async-start(), calls=%async_computation.23 | async-start | bytes 1966080 | tf_op jit(solution)/shard_map/all_gather | solution.py:341
  720.4 155.8 %all-gather.27.cloned.1.call-start = ((), (), s32[]{:S(2)}) async-start(), calls=%async_computation.28 | async-start | bytes 1966080 | tf_op jit(solution)/shard_map/all_gather | solution.py:343
  721.2 5.3 copy-start.18
  721.2 240.0 %all-gather.25.cloned.1.call-start = ((), (), s32[]{:S(2)}) async-start(), calls=%async_computation.25 | async-start | bytes 1966080 | tf_op jit(solution)/shard_map/all_gather | solution.py:342
  723.0 26.6 %all-to-all-start = ((bf16[128,4,384]{0,2,1:T(8,128)(2,1)}), bf16[128,4,384]{0,2,1:T(8,128)(2,1)S(1)}, u32[]{:S(2)}, u32[]{:S(2)}) async-start(bf16[128,4,384]{0,2,1:T(8,128)(2,1)} %bitcast.44), calls=%async_computation.1 | async-start | bytes 786432 | tf_op jit(solution)/shard_map/all_to_all | solution.py:346
  749.6 5.1 copy-start.14
  749.6 22.4 %all-to-all-start.3 = ((bf16[128,4,384]{2,0,1:T(8,128)(2,1)}), bf16[128,4,384]{2,0,1:T(8,128)(2,1)}, u32[]{:S(2)}, u32[]{:S(2)}) async-start(bf16[128,4,384]{2,0,1:T(8,128)(2,1)} %bitcast.235), calls=%async_computation.5 | async-start | bytes 786432 | tf_op jit(solution)/shard_map/all_to_all | solution.py:349
  753.7 374.8 %reduce-scatter.17.cloned.1.call-start = ((), (), s32[]{:S(2)}) async-start(), calls=%async_computation.22 | async-start | bytes 1327104 | tf_op jit(solution)/shard_map/reduce_scatter | solution.py:365
  754.8 32.0 %copy-start.1 = (bf16[128,8960]{1,0:T(8,128)(2,1)S(1)}, bf16[128,8960]{1,0:T(8,128)(2,1)}, u32[]{:S(2)}) copy-start(bf16[128,8960]{1,0:T(8,128)(2,1)} %get-tuple-element.371) | copy-start | bytes 6881284
  772.0 9.4 all-to-all-start.1
  781.4 11.5 all-to-all-start.2
  792.9 80.5 %all-to-all-start.6 = ((bf16[128,4,2240]{0,2,1:T(8,128)(2,1)}), bf16[128,4,2240]{0,2,1:T(8,128)(2,1)S(1)}, u32[]{:S(2)}, u32[]{:S(2)}) async-start(bf16[128,4,2240]{0,2,1:T(8,128)(2,1)} %bitcast.239), calls=%async_computation.11 | async-start | bytes 4587520 | tf_op jit(solution)/shard_map/all_to_all | solution.py:352
  796.5 333.7 %reduce-scatter.19.cloned.1.call-start = ((), (), s32[]{:S(2)}) async-start(), calls=%async_computation.24 | async-start | bytes 1327104 | tf_op jit(solution)/shard_map/reduce_scatter | solution.py:383
  800.1 331.8 %reduce-scatter.25.cloned.1.call-start = ((), (), s32[]{:S(2)}) async-start(), calls=%async_computation.29 | async-start | bytes 442368
  804.5 328.9 %reduce-scatter.27.cloned.1.call-start = ((), (), s32[]{:S(2)}) async-start(), calls=%async_computation.30 | async-start | bytes 442368
  808.9 336.5 %reduce-scatter.29.cloned.1.call-start = ((), (), s32[]{:S(2)}) async-start(), calls=%async_computation.31 | async-start | bytes 7962624
  895.1 1.7 copy-start
  895.1 319.2 %reduce-scatter.21.cloned.1.call-start = ((), (), s32[]{:S(2)}) async-start(), calls=%async_computation.26 | async-start | bytes 7962624 | tf_op jit(solution)/shard_map/reduce_scatter | solution.py:386
  970.1 1.7 copy-start.3
  970.1 313.6 %reduce-scatter.23.cloned.1.call-start = ((), (), s32[]{:S(2)}) async-start(), calls=%async_computation.27 | async-start | bytes 7962624 | tf_op jit(solution)/shard_map/reduce_scatter | solution.py:389
  1042.2 7.8 copy-start.2
  1064.9 3.1 copy-start.9
  1064.9 5.4 copy-start.24
  1064.9 45.9 %copy-start.10 = (f32[128,1536]{1,0:T(8,128)S(1)}, f32[128,1536]{1,0:T(8,128)}, u32[]{:S(2)}) copy-start(f32[128,1536]{1,0:T(8,128)} %get-tuple-element.384) | copy-start | bytes 2359300
  1064.9 45.9 %copy-start.16 = (bf16[1,128,1536]{2,1,0:T(8,128)(2,1)S(1)}, bf16[1,128,1536]{2,1,0:T(8,128)(2,1)}, u32[]{:S(2)}) copy-start(bf16[1,128,1536]{2,1,0:T(8,128)(2,1)} %param.35) | copy-start | bytes 1179652
  1064.9 45.9 %copy-start.29 = (f32[128]{0:T(128)S(1)}, f32[128]{0:T(128)}, u32[]{:S(2)}) copy-start(f32[128]{0:T(128)} %copy-done.28) | copy-start | bytes 1540
  1064.9 45.9 %copy-start.36 = (f32[128]{0:T(128)S(1)}, f32[128]{0:T(128)}, u32[]{:S(2)}) copy-start(f32[128]{0:T(128)} %copy-done.35) | copy-start | bytes 1540
  1065.0 45.9 %copy-start.38 = (f32[128]{0:T(128)S(1)}, f32[128]{0:T(128)}, u32[]{:S(2)}) copy-start(f32[128]{0:T(128)} %copy-done.37) | copy-start | bytes 1540
Sparse Core Ops, SparseCore 0:
  11.0 68.1 all-gather.10
  82.0 65.1 all-gather.12
  150.2 165.8 all-gather.14
  318.9 164.0 all-gather.16
  485.8 164.0 all-gather.18
  651.9 35.2 all-gather.20
  719.8 31.7 reduce-scatter.14
  753.2 42.7 all-gather.22
  797.6 67.0 all-gather.26
  866.2 46.9 all-gather.24
  917.3 43.4 reduce-scatter.16
  964.5 36.7 reduce-scatter.18
  1004.6 33.8 reduce-scatter.24
  1041.7 33.8 reduce-scatter.26
  1079.4 66.0 reduce-scatter.28
  1148.8 65.4 reduce-scatter.20
  1218.1 65.4 reduce-scatter.22
where the time goes:
time: 1300 us; the launch traced here: 1290 us
  waiting for transfers between devices  684 us (53%)
  blocking collectives  312 us (24%)
  matrix products  167 us (13%)
  local copies, waits for them, and re-layouts  65.8 us (5%)
  other arithmetic  25.3 us (2%)
  starting transfers between devices  20.5 us (2%)
  between operations  17.4 us (1%)
    all_gather x1, waiting for transfers between devices, per_device(): lax.all_gather(down_weight, ('ctx', 'fsdp'), axis=1, tiled=True)  152 us
    all_gather x1, waiting for transfers between devices, per_device(): lax.all_gather(up_weight, ('ctx', 'fsdp'), axis=0, tiled=True)  152 us
    all_gather x1, waiting for transfers between devices, per_device(): lax.all_gather(gate_weight, ('ctx', 'fsdp'), axis=0, tiled=True)  125 us
    unnamed x3, blocking collectives  95 us
    reduce_scatter x1, waiting for transfers between devices, per_device(): lax.psum_scatter(term_up.astype(jnp.bfloat16), 'fsdp', scatter_dimension=...  66.8 us
    reduce_scatter x1, waiting for transfers between devices, per_device(): lax.psum_scatter(term_gate.astype(jnp.bfloat16), 'fsdp', scatter_dimensio...  65 us
    all_to_all x1, waiting for transfers between devices, per_device(): lax.all_to_all(activated, 'ctx', split_axis=1, concat_axis=0, tiled=True)  64.5 us
    dot_general x7, matrix products, compared_keys(): lax.dot_general(left_side, right_side, (((1,), (1,)), ((), ())), preferre...  63.2 us
  transfers between devices with their start and end apart: 22, of which 11 were waited for; matrix products, arithmetic and copies ran while one was open for 19% of the time, Pallas kernels for 0%

commit v1 on v0

v1 whole, which is shorter than its diff:
```python
import jax
import jax.numpy as jnp
from jax import lax
from jax.sharding import PartitionSpec as P

QUERY_HEADS = 12
KEY_VALUE_HEADS = 2
HEAD_SIZE = 128
GROUP = QUERY_HEADS // KEY_VALUE_HEADS
KV_WIDTH = KEY_VALUE_HEADS * HEAD_SIZE
EPSILON = 1e-06
BOTH = ("ctx", "fsdp")
F32 = jnp.float32
BF16 = jnp.bfloat16


def dot(a, b, dims):
    return lax.dot_general(a, b, ((dims[:1], dims[1:]), ((), ())), preferred_element_type=F32)


def nn(a, b):
    return dot(a, b, (1, 0))


def nt(a, b):
    return dot(a, b, (1, 1))


def tn(a, b):
    return dot(a, b, (0, 0))


def rms_scale(matrix):
    return lax.rsqrt(jnp.mean(matrix * matrix, axis=-1, keepdims=True) + EPSILON)


def angle_tables(positions):
    step_index = jnp.arange(HEAD_SIZE // 2, dtype=F32) * 2.0
    frequency = 10000.0 ** (-step_index / HEAD_SIZE)
    angles = positions.astype(F32)[:, None] * frequency[None, :]
    return jnp.cos(angles)[:, None, :], jnp.sin(angles)[:, None, :]


def rotate(matrix, cosine, sine):
    rows = matrix.shape[0]
    heads = matrix.reshape(rows, -1, HEAD_SIZE)
    a, b = heads[..., : HEAD_SIZE // 2], heads[..., HEAD_SIZE // 2 :]
    turned = jnp.concatenate([a * cosine - b * sine, b * cosine + a * sine], axis=-1)
    return turned.reshape(rows, -1)


def pick(stacked, index):
    return lax.dynamic_index_in_dim(stacked, index, 0, keepdims=False)


class Links:
    def __init__(self, ctx_size, fsdp_size):
        self.ctx_size, self.fsdp_size = ctx_size, fsdp_size
        self.planes = [m for m in (2, 4, 8, 16, 32, 64) if m < fsdp_size]

    def send(self, x, target):
        pairs = []
        for c in range(self.ctx_size):
            for f in range(self.fsdp_size):
                to = target(c, f)
                if to is not None:
                    pairs.append((c * self.fsdp_size + f, to[0] * self.fsdp_size + to[1]))
        return lax.ppermute(x, BOTH, pairs)

    def core(self, x):
        return self.send(x, lambda c, f: (c, f ^ 1))

    def plane(self, x, mask):
        return self.send(x, lambda c, f: (c, f ^ mask))

    def turn(self, x, step):
        return self.send(x, lambda c, f: ((c + step) % self.ctx_size, f))

    def shift(self, x, step):
        return self.send(
            x, lambda c, f: (c + step, f) if 0 <= c + step < self.ctx_size else None
        )


def plane_gather(links, shard):
    first, second, *rest = links.planes
    half = shard.shape[0] // 2
    a = links.plane(shard, first)
    b = links.plane(shard, second)
    low = links.plane(b[:half], first)
    high = links.plane(a[half:], second)
    pieces = {0: shard, first: a, second: b, first | second: jnp.concatenate([low, high])}
    for mask in rest:
        pieces.update({had | mask: links.plane(piece, mask) for had, piece in pieces.items()})
    return pieces


def ff_weight(links, ctx, chip, core, shard):
    ctx_size = links.ctx_size
    rows, hidden = shard.shape
    block = hidden // (2 * ctx_size)
    parts = jnp.transpose(shard.reshape(rows, ctx_size, 2, block), (2, 1, 0, 3))
    mine, other = pick(parts, core), pick(parts, 1 - core)
    got = links.core(other)
    even = core == 0
    pairs = jnp.stack([jnp.where(even, mine, got), jnp.where(even, got, mine)], axis=1)
    by_source = jnp.zeros_like(pairs)
    by_source = lax.dynamic_update_index_in_dim(by_source, pick(pairs, ctx), ctx, 0)
    for step in range(1, ctx_size):
        piece = links.turn(pick(pairs, (ctx + step) % ctx_size), step)
        by_source = lax.dynamic_update_index_in_dim(by_source, piece, (ctx - step) % ctx_size, 0)
    pieces = plane_gather(links, by_source)
    whole = jnp.zeros((ctx_size, links.fsdp_size // 2, 2, rows, block), shard.dtype)
    for mask, piece in pieces.items():
        whole = lax.dynamic_update_index_in_dim(whole, piece, chip ^ (mask // 2), 1)
    return whole.reshape(-1, block)


def spread_tokens(links, x):
    row = jnp.concatenate([x] + [links.turn(x, step) for step in range(1, links.ctx_size)])
    return jnp.concatenate([row, links.core(row)])


def collect_tokens(links, partial):
    rows = partial.shape[0] // 2
    got = links.core(partial[rows:].astype(BF16))
    count = rows // links.ctx_size
    row = (partial[:rows].astype(F32) + got.astype(F32)).reshape(links.ctx_size, count, -1)
    total = row[0]
    for step in range(1, links.ctx_size):
        total = total + links.turn(row[step].astype(BF16), -step).astype(F32)
    return total


def per_device(
    tokens,
    positions,
    norm1_gain,
    q_weight,
    q_bias,
    key_projection,
    key_bias_vector,
    value_projection,
    value_bias_vector,
    o_weight,
    norm2_gain,
    gate_weight,
    up_weight,
    down_weight,
    cotangent,
    *,
    links,
):
    ctx_size, fsdp_size = links.ctx_size, links.fsdp_size
    ctx, row_index = lax.axis_index("ctx"), lax.axis_index("fsdp")
    chip, core = row_index // 2, row_index % 2
    count, width = tokens.shape[1:]
    scale = HEAD_SIZE ** (-0.5)
    even = core == 0

    shard_rows = q_weight.shape[0]

    def column(x):
        return jnp.pad(x, (0, shard_rows - x.shape[0]))[:, None]

    kv_bias_rows = key_bias_vector.shape[0]
    extra = jnp.concatenate(
        [
            column(x)
            for x in (norm1_gain, q_bias, norm2_gain, key_bias_vector, value_bias_vector)
        ],
        axis=1,
    )
    extra = jnp.pad(extra, ((0, 0), (0, 128 - extra.shape[1])))
    packed = jnp.concatenate([q_weight, key_projection, value_projection, extra], axis=1)
    packed = lax.all_gather(packed, BOTH, axis=0, tiled=True)
    weight_o = lax.all_gather(o_weight, BOTH, axis=0, tiled=True)

    weight_gate = ff_weight(links, ctx, chip, core, gate_weight)
    weight_up = ff_weight(links, ctx, chip, core, up_weight)
    weight_down = ff_weight(links, ctx, chip, core, jnp.transpose(down_weight))

    qkv_width = width + 2 * KV_WIDTH
    weight_qkv = packed[:, :qkv_width]
    small = jnp.transpose(packed[:, qkv_width:])[:5].astype(F32)
    gain_one, bias_q, gain_two = small[0:1], small[1:2], small[2:3]

    def bias_of(row):
        return row.reshape(-1, shard_rows)[:, :kv_bias_rows].reshape(1, -1)

    bias_k, bias_v = bias_of(small[3]), bias_of(small[4])
    out_low = cotangent[0]
    group_out = spread_tokens(links, out_low)

    stream = tokens[0].astype(F32)
    scale_one = rms_scale(stream)
    unit_one = stream * scale_one
    normed_one = (unit_one * gain_one).astype(BF16)
    cosine, sine = angle_tables(positions[0])
    linear = nn(normed_one, weight_qkv)
    query = rotate(linear[:, :width] + bias_q, cosine, sine).astype(BF16)
    key = rotate(linear[:, width : width + KV_WIDTH] + bias_k, cosine, sine).astype(BF16)
    value = (linear[:, width + KV_WIDTH :] + bias_v).astype(BF16)
    pairs = jnp.concatenate([key, value], axis=1)
    row_pairs = jnp.concatenate(
        [pairs] + [links.shift(pairs, step) for step in range(1, ctx_size)]
    )
    keys = row_pairs[:, :KV_WIDTH].reshape(-1, KEY_VALUE_HEADS, HEAD_SIZE)
    values = row_pairs[:, KV_WIDTH:].reshape(-1, KEY_VALUE_HEADS, HEAD_SIZE)
    local_index = jnp.arange(count)
    key_index = jnp.concatenate(
        [(ctx - step) * count + local_index for step in range(ctx_size)]
    )
    query_index = ctx * count + local_index
    doc_start = query_index - positions[0]
    allowed = (key_index[None, :] >= doc_start[:, None]) & (
        key_index[None, :] <= query_index[:, None]
    )
    query_heads = query.reshape(count, KEY_VALUE_HEADS, GROUP, HEAD_SIZE)
    scores = jnp.einsum("qkgd,rkd->kgqr", query_heads, keys, preferred_element_type=F32) * scale
    scores = jnp.where(allowed, scores, -1e30)
    top = jnp.max(scores, axis=-1, keepdims=True)
    weights = jnp.where(allowed, jnp.exp(scores - top), 0.0)
    probs = weights / jnp.sum(weights, axis=-1, keepdims=True)
    probs_low = probs.astype(BF16)
    mixed = jnp.einsum("kgqr,rkd->qkgd", probs_low, values, preferred_element_type=F32)
    mixed_low = mixed.reshape(count, -1).astype(BF16)
    hidden_one = stream + nn(mixed_low, weight_o)

    scale_two = rms_scale(hidden_one)
    unit_two = hidden_one * scale_two
    normed_two = (unit_two * gain_two).astype(BF16)
    group_normed = spread_tokens(links, normed_two)
    gate_pre = nn(group_normed, weight_gate)
    up_pre = nn(group_normed, weight_up)
    grad_act = nn(group_out, weight_down)
    sigmoid_gate = jax.nn.sigmoid(gate_pre)
    activated = (gate_pre * sigmoid_gate * up_pre).astype(BF16)
    grad_gate_low = (
        grad_act * up_pre * sigmoid_gate * (1.0 + gate_pre * (1.0 - sigmoid_gate))
    ).astype(BF16)
    grad_up_low = (grad_act * gate_pre * sigmoid_gate).astype(BF16)
    grad_normed_two = collect_tokens(
        links, nt(grad_gate_low, weight_gate) + nt(grad_up_low, weight_up)
    )
    layer_out = hidden_one + collect_tokens(links, nt(activated, weight_down))

    planes = [
        [c * fsdp_size + 2 * p + k for p in range(fsdp_size // 2)]
        for c in range(ctx_size)
        for k in range(2)
    ]

    def ff_grad(left, right):
        term = tn(left, right).astype(BF16)
        part = lax.psum_scatter(
            term, BOTH, scatter_dimension=0, tiled=True, axis_index_groups=planes
        )
        part = part.reshape(2, -1, part.shape[1])
        mine, got = pick(part, core), links.core(pick(part, 1 - core))
        return jnp.concatenate(
            [jnp.where(even, mine, got), jnp.where(even, got, mine)], axis=1
        ).astype(F32)

    grad_gate = ff_grad(group_normed, grad_gate_low)
    grad_up = ff_grad(group_normed, grad_up_low)
    grad_down = jnp.transpose(ff_grad(group_out, activated))

    grad_gain_two = jnp.sum(grad_normed_two * unit_two, axis=0)
    weighted_two = grad_normed_two * gain_two
    grad_hidden = out_low.astype(F32) + scale_two * (
        weighted_two - unit_two * jnp.mean(weighted_two * unit_two, axis=-1, keepdims=True)
    )

    grad_hidden_low = grad_hidden.astype(BF16)
    grad_mixed = nt(grad_hidden_low, weight_o).astype(BF16)
    grad_mixed = grad_mixed.reshape(count, KEY_VALUE_HEADS, GROUP, HEAD_SIZE)
    grad_probs = jnp.einsum("qkgd,rkd->kgqr", grad_mixed, values, preferred_element_type=F32)
    delta = jnp.sum(probs * grad_probs, axis=-1, keepdims=True)
    grad_scores = (probs * (grad_probs - delta)).astype(BF16)
    grad_query = jnp.einsum("kgqr,rkd->qkgd", grad_scores, keys, preferred_element_type=F32)
    grad_key = (
        jnp.einsum("kgqr,qkgd->rkd", grad_scores, query_heads, preferred_element_type=F32) * scale
    )
    grad_value = jnp.einsum("kgqr,qkgd->rkd", probs_low, grad_mixed, preferred_element_type=F32)
    pair_terms = jnp.concatenate(
        [grad_key.reshape(-1, KV_WIDTH), grad_value.reshape(-1, KV_WIDTH)], axis=1
    ).reshape(ctx_size, count, -1)
    pair_grads = pair_terms[0]
    for step in range(1, ctx_size):
        pair_grads = pair_grads + links.shift(pair_terms[step].astype(BF16), -step).astype(F32)
    grad_q_low = rotate(grad_query.reshape(count, -1) * scale, cosine, -sine).astype(BF16)
    grad_k_low = rotate(pair_grads[:, :KV_WIDTH], cosine, -sine).astype(BF16)
    grad_v_low = pair_grads[:, KV_WIDTH:].astype(BF16)
    grad_qkv = jnp.concatenate([grad_q_low, grad_k_low, grad_v_low], axis=1)
    grad_normed_one = nt(grad_qkv, weight_qkv)
    grad_gain_one = jnp.sum(grad_normed_one * unit_one, axis=0)
    weighted_one = grad_normed_one * gain_one
    grad_stream = grad_hidden + scale_one * (
        weighted_one - unit_one * jnp.mean(weighted_one * unit_one, axis=-1, keepdims=True)
    )

    def columns_over_ctx(arrays):
        parts = jnp.concatenate([x.reshape(count, ctx_size, -1) for x in arrays], axis=2)
        parts = jnp.transpose(parts, (1, 0, 2))
        whole = jnp.zeros_like(parts)
        whole = lax.dynamic_update_index_in_dim(whole, pick(parts, ctx), ctx, 0)
        for step in range(1, ctx_size):
            piece = links.turn(pick(parts, (ctx + step) % ctx_size), step)
            whole = lax.dynamic_update_index_in_dim(whole, piece, (ctx - step) % ctx_size, 0)
        return whole.reshape(ctx_size * count, -1)

    def attention_grad(rows, arrays):
        left = lax.all_gather(rows, "ctx", axis=0, tiled=True)
        term = tn(left, columns_over_ctx(arrays)).astype(BF16)
        return lax.psum_scatter(term, "fsdp", scatter_dimension=0, tiled=True).astype(F32)

    grad_o = attention_grad(mixed_low, [grad_hidden_low])
    grad_packed = attention_grad(normed_one, [grad_q_low, grad_k_low, grad_v_low])
    q_columns, kv_columns = width // ctx_size, KV_WIDTH // ctx_size

    sums = jnp.concatenate(
        [grad_gain_one, grad_gain_two, jnp.sum(grad_qkv.astype(F32), axis=0)]
    )
    sums = lax.psum(sums, BOTH)
    device = ctx * fsdp_size + row_index

    def own(start, size):
        part = size // (ctx_size * fsdp_size)
        return lax.dynamic_slice_in_dim(sums, start + device * part, part)

    return (
        layer_out[None],
        grad_stream[None],
        own(0, width),
        grad_packed[:, :q_columns],
        own(2 * width, width),
        grad_packed[:, q_columns : q_columns + kv_columns],
        own(3 * width, KV_WIDTH),
        grad_packed[:, q_columns + kv_columns :],
        own(3 * width + KV_WIDTH, KV_WIDTH),
        grad_o,
        own(width, width),
        grad_gate,
        grad_up,
        grad_down,
    )


def solution(mesh):
    links = Links(mesh.shape["ctx"], mesh.shape["fsdp"])
    vector, matrix, stream = P(BOTH), P(BOTH, None), P("fsdp", "ctx", None)
    grid = P("fsdp", "ctx")
    in_specs = (
        stream,
        grid,
        vector,
        matrix,
        vector,
        matrix,
        vector,
        matrix,
        vector,
        matrix,
        vector,
        matrix,
        matrix,
        P(None, BOTH),
        stream,
    )
    out_specs = (
        stream,
        stream,
        vector,
        grid,
        vector,
        grid,
        vector,
        grid,
        vector,
        grid,
        vector,
        grid,
        grid,
        P("ctx", "fsdp"),
    )

    def run(*arrays):
        return per_device(*arrays, links=links)

    return jax.shard_map(run, mesh=mesh, in_specs=in_specs, out_specs=out_specs, check_vma=False)
```

time: 1300 us -> 729 us (0.56)
  waiting for transfers between devices: 684 us -> 301 us
  blocking collectives: 312 us -> 49.2 us
  starting transfers between devices: 20.5 us -> 114 us
  matrix products: 167 us -> 104 us
  local copies, waits for them, and re-layouts: 65.8 us -> 94.5 us
  other arithmetic: 25.3 us -> 39 us
    all_gather x9 -> x4, waiting for transfers between devices: 430 us -> 0.05 us  [the longest x2 0.02 us: attention_grad(): left = lax.all_gather(rows, 'ctx', axis=0, tiled=True)]
    ppermute x0 -> x55, waiting for transfers between devices: none -> 221 us  [send(): return lax.ppermute(x, BOTH, pairs)]
    all_to_all x2 -> x0, blocking collectives: 115 us -> none  [the longest x1 59.1 us: per_device(): lax.all_to_all(grad_gate_low, 'ctx', split_axis=1, concat_axis=0, tiled=T...]
    ppermute x0 -> x55, starting transfers between devices: none -> 113 us  [send(): return lax.ppermute(x, BOTH, pairs)]
    all_to_all x5 -> x0, waiting for transfers between devices: 107 us -> none  [the longest x1 64.5 us: per_device(): lax.all_to_all(activated, 'ctx', split_axis=1, concat_axis=0, tiled=True)]
    all_gather x3 -> x0, blocking collectives: 101 us -> none  [the longest x1 43.4 us: per_device(): lax.all_gather(value_projection, ('ctx', 'fsdp'), axis=0, tiled=True)]
    unnamed x3 -> x0, blocking collectives: 95 us -> none
    dot_general x30 -> x20, matrix products: 167 us -> 101 us  [the longest x15 94.6 us: dot(): lax.dot_general(a, b, ((dims[:1], dims[1:]), ((), ())), preferred_element...]
  transfers between devices with their start and end apart: 22 -> 64, of which waited for: 11 -> 28; matrix products, arithmetic and copies ran while one was open for 19% -> 27% of each run, Pallas kernels for 0% -> 0%
where the time goes in v1:
time: 729 us; the launch traced here: 718 us
  waiting for transfers between devices  301 us (41%)
  starting transfers between devices  114 us (16%)
  matrix products  104 us (14%)
  local copies, waits for them, and re-layouts  94.5 us (13%)
  blocking collectives  49.2 us (7%)
  other arithmetic  39 us (5%)
  between operations  15.8 us (2%)
    ppermute x55, waiting for transfers between devices, send(): return lax.ppermute(x, BOTH, pairs)  221 us
    ppermute x55, starting transfers between devices, send(): return lax.ppermute(x, BOTH, pairs)  113 us
    dot_general x15, matrix products, dot(): lax.dot_general(a, b, ((dims[:1], dims[1:]), ((), ())), preferred_element...  94.6 us
    reduce_scatter x3, waiting for transfers between devices, ff_grad(): lax.psum_scatter(term, BOTH, scatter_dimension=0, tiled=True, axis_index_...  79.9 us
    psum x1, blocking collectives, per_device(): sums = lax.psum(sums, BOTH)  49.2 us
    unnamed x97, local copies, waits for them, and re-layouts  29.6 us
  transfers between devices with their start and end apart: 64, of which 28 were waited for; matrix products, arithmetic and copies ran while one was open for 27% of the time, Pallas kernels for 0%

profile of v1, /device:TPU:0, one launch (start us, length us, event | category | flops | bytes accessed | tf_op | source)
XLA Modules:
  0.0 718.1 jit_solution(18305880899014755388)
XLA Ops:
  10.4 3.1 collective-permute-start.35
  17.5 3.5 reshape.287
  21.0 3.5 reshape.291
  24.5 4.6 dynamic-slice_bitcast_fusion.2
  29.9 3.5 reshape.289
  41.0 4.6 collective-permute-done.36
  53.4 9.4 %collective-permute-start.8 = (bf16[2,48,1120]{2,1,0:T(8,128)(2,1)S(1)}, bf16[2,48,1120]{2,1,0:T(8,128)(2,1)S(1)}, u32[]{:S(2)}, u32[]{:S(2)}) collective-permute-start(bf16[2,48,1120]{2,1,0:T(8,128)(2,1)S(1)} %get-tuple-element.143), channel_id=1, source_target_pairs={{0,8},{1,9},{2,10},{3,11},{4,12},{5,13},{6,14},{7,15},{8,16},{9,17... | collective-permute-start | bytes 645128 | tf_op jit(solution)/shard_map/ppermute | solution.py:68
  67.4 7.2 %collective-permute-done.8 = bf16[2,48,1120]{2,1,0:T(8,128)(2,1)S(1)} collective-permute-done((bf16[2,48,1120]{2,1,0:T(8,128)(2,1)S(1)}, bf16[2,48,1120]{2,1,0:T(8,128)(2,1)S(1)}, u32[]{:S(2)}, u32[]{:S(2)}) %collective-permute-start.8) | collective-permute-done | bytes 215072 | tf_op jit(solution)/shard_map/ppermute | solution.py:68
  75.5 10.9 %collective-permute-done.9 = bf16[2,48,1120]{2,1,0:T(8,128)(2,1)S(1)} collective-permute-done((bf16[2,48,1120]{2,1,0:T(8,128)(2,1)S(1)}, bf16[2,48,1120]{2,1,0:T(8,128)(2,1)S(1)}, u32[]{:S(2)}, u32[]{:S(2)}) %collective-permute-start.9) | collective-permute-done | bytes 215072 | tf_op jit(solution)/shard_map/ppermute | solution.py:68
  86.4 6.0 collective-permute-start.18
  92.4 17.9 %collective-permute-start.24 = (bf16[2,48,1120]{2,1,0:T(8,128)(2,1)S(1)}, bf16[2,48,1120]{2,1,0:T(8,128)(2,1)S(1)}, u32[]{:S(2)}, u32[]{:S(2)}) collective-permute-start(bf16[2,48,1120]{2,1,0:T(8,128)(2,1)S(1)} %get-tuple-element.138), channel_id=1, source_target_pairs={{0,8},{1,9},{2,10},{3,11},{4,12},{5,13},{6,14},{7,15},{8,16},{9,17... | collective-permute-start | bytes 645128 | tf_op jit(solution)/shard_map/ppermute | solution.py:68
  113.4 3.7 collective-permute-start.25
  117.1 15.3 %collective-permute-done.17 = bf16[2,48,1120]{2,1,0:T(8,128)(2,1)S(1)} collective-permute-done((bf16[2,48,1120]{2,1,0:T(8,128)(2,1)S(1)}, bf16[2,48,1120]{2,1,0:T(8,128)(2,1)S(1)}, u32[]{:S(2)}, u32[]{:S(2)}) %collective-permute-start.17) | collective-permute-done | bytes 215072 | tf_op jit(solution)/shard_map/ppermute | solution.py:68
  149.2 13.0 %collective-permute-done.12 = bf16[4,2,48,1120]{3,2,1,0:T(8,128)(2,1)S(1)} collective-permute-done((bf16[4,2,48,1120]{3,2,1,0:T(8,128)(2,1)S(1)}, bf16[4,2,48,1120]{3,2,1,0:T(8,128)(2,1)S(1)}, u32[]{:S(2)}, u32[]{:S(2)}) %collective-permute-start.12) | collective-permute-done | bytes 860192 | tf_op jit(solution)/shard_map/ppermute | solution.py:68
  164.4 18.9 %collective-permute-done.20 = bf16[4,2,48,1120]{3,2,1,0:T(8,128)(2,1)S(1)} collective-permute-done((bf16[4,2,48,1120]{3,2,1,0:T(8,128)(2,1)S(1)}, bf16[4,2,48,1120]{3,2,1,0:T(8,128)(2,1)S(1)}, u32[]{:S(2)}, u32[]{:S(2)}) %collective-permute-start.20) | collective-permute-done | bytes 860192 | tf_op jit(solution)/shard_map/ppermute | solution.py:68
  189.5 18.6 %collective-permute-done.27 = bf16[4,2,48,1120]{3,2,1,0:T(8,128)(2,1)S(1)} collective-permute-done((bf16[4,2,48,1120]{3,2,1,0:T(8,128)(2,1)S(1)}, bf16[4,2,48,1120]{3,2,1,0:T(8,128)(2,1)S(1)}, u32[]{:S(2)}, u32[]{:S(2)}) %collective-permute-start.27) | collective-permute-done | bytes 860192 | tf_op jit(solution)/shard_map/ppermute | solution.py:68
  214.8 2.7 collective-permute-done.13
  221.2 5.8 collective-permute-done.21
  232.8 3.9 fusion.3
  237.7 6.7 collective-permute-start
  253.6 3.0 fusion.95
  259.0 3.4 multiply_reduce_fusion.2
  262.6 3.5 collective-permute-start.3
  266.0 3.3 collective-permute-start.4
  274.5 4.4 collective-permute-done.3
  278.9 14.4 %collective-permute-done.4 = bf16[128,1536]{1,0:T(8,128)(2,1)S(1)} collective-permute-done((bf16[128,1536]{1,0:T(8,128)(2,1)S(1)}, bf16[128,1536]{1,0:T(8,128)(2,1)S(1)}, u32[]{:S(2)}, u32[]{:S(2)}) %collective-permute-start.4) | collective-permute-done | bytes 393248 | tf_op jit(solution)/shard_map/ppermute | solution.py:68
  293.5 6.0 fusion.98
  299.7 8.6 %fusion.96 = f32[1024,1120]{0,1:T(8,128)} fusion(bf16[1024,1536]{1,0:T(8,128)(2,1)S(1)} %constant_dynamic-update-slice_fusion, bf16[1536,1120]{1,0:T(8,128)(2,1)} %bitcast.61), kind=kOutput, calls=%fused_computation.282 | convolution fusion | flops 3523215360 | bytes 11173888 | tf_op jit(solution)/shard_map/dot_general | solution.py:18
  308.3 10.1 %multiply_convert_fusion.1 = (bf16[1024,1120]{0,1:T(8,128)(2,1)S(1)}, bf16[1024,1120]{0,1:T(8,128)(2,1)}, bf16[1024,1120]{0,1:T(8,128)(2,1)S(1)}) fusion(f32[1024,1120]{0,1:T(8,128)S(1)} %fusion.98, f32[1024,1120]{0,1:T(8,128)} %fusion.96, bf16[1024,1536]{1,0:T(8,128)(2,1)S(1)} %constant_dynamic-update-slice_fusion, bf16[1536,1120]{1,0:T(8,128)(2,1)} %bitcast.38), kind=kOutput, calls=%fused_computation.9 | convolution fusion | flops 3541565440 | bytes 22642688 | tf_op jit(solution)/shard_map/dot_general | solution.py:18
  318.4 8.0 %fusion.99 = f32[1024,1536]{1,0:T(8,128)S(1)} fusion(bf16[1024,1120]{0,1:T(8,128)(2,1)S(1)} %get-tuple-element.116, bf16[1536,1120]{1,0:T(8,128)(2,1)} %bitcast.61), kind=kOutput, calls=%fused_computation.285 | convolution fusion | flops 3523215360 | bytes 12025856 | tf_op jit(solution)/shard_map/dot_general | solution.py:18
  326.4 6.4 convolution_add_fusion
  332.8 2.6 copy-done.3
  337.3 3.2 collective-permute-done.39
  340.4 4.1 fusion.86
  344.6 6.9 collective-permute-start.40
  351.5 3.5 collective-permute-start.41
  355.3 19.7 %collective-permute-done.40 = bf16[128,1536]{1,0:T(8,128)(2,1)S(1)} collective-permute-done((bf16[128,1536]{1,0:T(8,128)(2,1)S(1)}, bf16[128,1536]{1,0:T(8,128)(2,1)S(1)}, u32[]{:S(2)}, u32[]{:S(2)}) %collective-permute-start.40) | collective-permute-done | bytes 393248 | tf_op jit(solution)/shard_map/ppermute | solution.py:68
  375.0 39.1 %collective-permute-done.41 = bf16[128,1536]{1,0:T(8,128)(2,1)S(1)} collective-permute-done((bf16[128,1536]{1,0:T(8,128)(2,1)S(1)}, bf16[128,1536]{1,0:T(8,128)(2,1)S(1)}, u32[]{:S(2)}, u32[]{:S(2)}) %collective-permute-start.41) | collective-permute-done | bytes 393248 | tf_op jit(solution)/shard_map/ppermute | solution.py:68
  417.2 4.0 convolution_convert_fusion.5
  421.4 2.7 fusion.5
  426.5 3.5 collective-permute-start.51
  439.1 2.7 collective-permute-done.50
  443.1 3.5 convolution_convert_fusion.4
  446.7 3.2 collective-permute-done.43
  449.8 20.3 %collective-permute-done.44 = bf16[128,512]{0,1:T(8,128)(2,1)} collective-permute-done((bf16[128,512]{0,1:T(8,128)(2,1)}, bf16[128,512]{0,1:T(8,128)(2,1)}, u32[]{:S(2)}, u32[]{:S(2)}) %collective-permute-start.44) | collective-permute-done | bytes 131104 | tf_op jit(solution)/shard_map/ppermute | solution.py:68
  473.9 3.8 collective-permute-start.48
  477.8 3.2 collective-permute-done.46
  482.0 3.2 collective-permute-done.47
  486.1 3.6 convolution_convert_fusion.3
  489.8 8.1 %convolution_convert_fusion = bf16[1536,1120]{0,1:T(8,128)(2,1)} fusion(bf16[1024,1120]{0,1:T(8,128)(2,1)} %get-tuple-element.115, bf16[1024,1536]{1,0:T(8,128)(2,1)} %copy-done.27), kind=kOutput, calls=%fused_computation.1 | convolution fusion | flops 3524935680 | bytes 8880128 | tf_op jit(solution)/shard_map/dot_general | solution.py:18
  497.9 5.7 copy.341
  503.9 8.1 %convolution_convert_fusion.1 = bf16[1536,1120]{0,1:T(8,128)(2,1)} fusion(bf16[1024,1120]{0,1:T(8,128)(2,1)} %copy-done.39, bf16[1024,1536]{1,0:T(8,128)(2,1)} %copy-done.28), kind=kOutput, calls=%fused_computation.2 | convolution fusion | flops 3524935680 | bytes 8880128 | tf_op jit(solution)/shard_map/dot_general | solution.py:18
  512.0 5.7 copy.339
  517.7 8.2 %convolution_convert_fusion.2 = bf16[1536,1120]{0,1:T(8,128)(2,1)} fusion(bf16[1024,1120]{0,1:T(8,128)(2,1)} %copy-done.38, bf16[1024,1536]{1,0:T(8,128)(2,1)} %copy-done.28), kind=kOutput, calls=%fused_computation.3 | convolution fusion | flops 3524935680 | bytes 8880128 | tf_op jit(solution)/shard_map/dot_general | solution.py:18
  526.0 5.7 copy.337
  531.7 7.3 %fusion.97 = f32[1024,1536]{1,0:T(8,128)S(1)} fusion(bf16[1024,1120]{0,1:T(8,128)(2,1)} %get-tuple-element.115, bf16[1536,1120]{1,0:T(8,128)(2,1)} %bitcast.84), kind=kOutput, calls=%fused_computation.283 | convolution fusion | flops 3523215360 | bytes 12025856 | tf_op jit(solution)/shard_map/dot_general | solution.py:18
  539.0 2.7 copy-done.2
  543.0 3.7 collective-permute-done.31
  546.8 4.7 fusion.87
  556.5 5.7 fusion.27
  562.2 49.2 %psum.7 = f32[5120]{0:T(1024)S(1)} all-reduce(f32[5120]{0:T(1024)S(1)} %pad_maximum_fusion.10), channel_id=1, replica_groups=mesh['ctx'=4,'fsdp'=8] {'ctx','fsdp'}, use_global_device_ids=true, to_apply=%region_10.11 | all-reduce | flops 5120 | bytes 40960 | tf_op jit(solution)/shard_map/psum | solution.py:325
  613.3 3.1 fusion.26
  623.2 30.5 %reduce-scatter.18.cloned.1.call-done = bf16[384,1120]{1,0:T(8,128)(2,1)} async-done(((bf16[1536,1120]{1,0:T(8,128)(2,1)}), bf16[384,1120]{1,0:T(8,128)(2,1)}) %reduce-scatter.18.cloned.1.call-update) | async-done | bytes 860176 | tf_op jit(solution)/shard_map/reduce_scatter | solution.py:256
  654.9 49.4 %reduce-scatter.16.cloned.1.call-done = bf16[384,1120]{1,0:T(8,128)(2,1)} async-done(((bf16[1536,1120]{1,0:T(8,128)(2,1)}), bf16[384,1120]{1,0:T(8,128)(2,1)}) %reduce-scatter.16.cloned.1.call-update) | async-done | bytes 860176 | tf_op jit(solution)/shard_map/reduce_scatter | solution.py:256
  (339 shorter events, 138.2 us)
Async XLA Ops:
  7.2 222.0 %all-gather.5.cloned.1.call-start = ((), (), s32[]{:S(2)}) async-start(), calls=%async_computation.5 | async-start | bytes 6893568 | tf_op jit(solution)/shard_map/all_gather | solution.py:176
  10.4 248.6 %all-gather.7.cloned.1.call-start = ((), (), s32[]{:S(2)}) async-start(), calls=%async_computation.6 | async-start | bytes 4866048 | tf_op jit(solution)/shard_map/all_gather | solution.py:177
  10.4 30.5 %collective-permute-start.35 = (bf16[128,1536]{1,0:T(8,128)(2,1)}, bf16[128,1536]{1,0:T(8,128)(2,1)}, u32[]{:S(2)}, u32[]{:S(2)}) collective-permute-start(bf16[128,1536]{1,0:T(8,128)(2,1)} %bitcast.338), channel_id=1, source_target_pairs={{0,8},{1,9},{2,10},{3,11},{4,12},{5,13},{6,14},{7,15},{8,16},{9,17... | collective-permute-start | bytes 1179656 | tf_op jit(solution)/shard_map/ppermute | solution.py:68
  13.5 32.1 %collective-permute-start.36 = (bf16[128,1536]{1,0:T(8,128)(2,1)}, bf16[128,1536]{1,0:T(8,128)(2,1)}, u32[]{:S(2)}, u32[]{:S(2)}) collective-permute-start(bf16[128,1536]{1,0:T(8,128)(2,1)} %bitcast.339), channel_id=1, source_target_pairs={{0,16},{1,17},{2,18},{3,19},{4,20},{5,21},{6,22},{7,23},{8,24},{9,... | collective-permute-start | bytes 1179656 | tf_op jit(solution)/shard_map/ppermute | solution.py:68
  16.1 29.9 %collective-permute-start.37 = (bf16[128,1536]{1,0:T(8,128)(2,1)}, bf16[128,1536]{1,0:T(8,128)(2,1)}, u32[]{:S(2)}, u32[]{:S(2)}) collective-permute-start(bf16[128,1536]{1,0:T(8,128)(2,1)} %bitcast.340), channel_id=1, source_target_pairs={{0,24},{1,25},{2,26},{3,27},{4,28},{5,29},{6,30},{7,31},{8,0},{9,1... | collective-permute-start | bytes 1179656 | tf_op jit(solution)/shard_map/ppermute | solution.py:68
  29.9 21.7 %collective-permute-start.7 = (bf16[4,48,1120]{2,1,0:T(8,128)(2,1)}, bf16[4,48,1120]{2,1,0:T(8,128)(2,1)}, u32[]{:S(2)}, u32[]{:S(2)}) collective-permute-start(bf16[4,48,1120]{2,1,0:T(8,128)(2,1)} %bitcast.332), channel_id=1, source_target_pairs={{0,1},{1,0},{2,3},{3,2},{4,5},{5,4},{6,7},{7,6},{8,9},{9,8},{10,11... | collective-permute-start | bytes 1290248 | tf_op jit(solution)/shard_map/ppermute | solution.py:68
  36.1 28.4 %collective-permute-start.15 = (bf16[4,48,1120]{2,1,0:T(8,128)(2,1)}, bf16[4,48,1120]{2,1,0:T(8,128)(2,1)S(1)}, u32[]{:S(2)}, u32[]{:S(2)}) collective-permute-start(bf16[4,48,1120]{2,1,0:T(8,128)(2,1)} %bitcast.330), channel_id=1, source_target_pairs={{0,1},{1,0},{2,3},{3,2},{4,5},{5,4},{6,7},{7,6},{8,9},{9,8},{10,11... | collective-permute-start | bytes 1290248 | tf_op jit(solution)/shard_map/ppermute | solution.py:68
  36.6 406.5 %all-gather.11.cloned.1.call-start = ((), (), s32[]{:S(2)}) async-start(), calls=%async_computation.9 | async-start | bytes 1966080 | tf_op jit(solution)/shard_map/all_gather | solution.py:314
  40.9 24.9 %collective-permute-start.23 = (bf16[4,48,1120]{2,1,0:T(8,128)(2,1)}, bf16[4,48,1120]{2,1,0:T(8,128)(2,1)S(1)}, u32[]{:S(2)}, u32[]{:S(2)}) collective-permute-start(bf16[4,48,1120]{2,1,0:T(8,128)(2,1)} %bitcast.370), channel_id=1, source_target_pairs={{0,1},{1,0},{2,3},{3,2},{4,5},{5,4},{6,7},{7,6},{8,9},{9,8},{10,11... | collective-permute-start | bytes 1290248 | tf_op jit(solution)/shard_map/ppermute | solution.py:68
  48.5 224.4 %collective-permute-start.38 = (bf16[512,1536]{1,0:T(8,128)(2,1)}, bf16[512,1536]{1,0:T(8,128)(2,1)}, u32[]{:S(2)}, u32[]{:S(2)}) collective-permute-start(bf16[512,1536]{1,0:T(8,128)(2,1)} %pad_maximum_fusion.1), channel_id=1, source_target_pairs={{0,1},{1,0},{2,3},{3,2},{4,5},{5,4},{6,7},{7,6},{8,9},{9,8},{10,11... | collective-permute-start | bytes 4718600 | tf_op jit(solution)/shard_map/ppermute | solution.py:68
  53.4 21.2 %collective-permute-start.8 = (bf16[2,48,1120]{2,1,0:T(8,128)(2,1)S(1)}, bf16[2,48,1120]{2,1,0:T(8,128)(2,1)S(1)}, u32[]{:S(2)}, u32[]{:S(2)}) collective-permute-start(bf16[2,48,1120]{2,1,0:T(8,128)(2,1)S(1)} %get-tuple-element.143), channel_id=1, source_target_pairs={{0,8},{1,9},{2,10},{3,11},{4,12},{5,13},{6,14},{7,15},{8,16},{9,17... | collective-permute-start | bytes 645128 | tf_op jit(solution)/shard_map/ppermute | solution.py:68
  62.8 23.6 %collective-permute-start.9 = (bf16[2,48,1120]{2,1,0:T(8,128)(2,1)S(1)}, bf16[2,48,1120]{2,1,0:T(8,128)(2,1)S(1)}, u32[]{:S(2)}, u32[]{:S(2)}) collective-permute-start(bf16[2,48,1120]{2,1,0:T(8,128)(2,1)S(1)} %get-tuple-element.144), channel_id=1, source_target_pairs={{0,16},{1,17},{2,18},{3,19},{4,20},{5,21},{6,22},{7,23},{8,24},{9,... | collective-permute-start | bytes 645128 | tf_op jit(solution)/shard_map/ppermute | solution.py:68
  64.5 27.9 %collective-permute-start.10 = (bf16[2,48,1120]{2,1,0:T(8,128)(2,1)S(1)}, bf16[2,48,1120]{2,1,0:T(8,128)(2,1)S(1)}, u32[]{:S(2)}, u32[]{:S(2)}) collective-permute-start(bf16[2,48,1120]{2,1,0:T(8,128)(2,1)S(1)} %get-tuple-element.142), channel_id=1, source_target_pairs={{0,24},{1,25},{2,26},{3,27},{4,28},{5,29},{6,30},{7,31},{8,0},{9,1... | collective-permute-start | bytes 645128 | tf_op jit(solution)/shard_map/ppermute | solution.py:68
  65.8 47.6 %collective-permute-start.16 = (bf16[2,48,1120]{2,1,0:T(8,128)(2,1)S(1)}, bf16[2,48,1120]{2,1,0:T(8,128)(2,1)S(1)}, u32[]{:S(2)}, u32[]{:S(2)}) collective-permute-start(bf16[2,48,1120]{2,1,0:T(8,128)(2,1)S(1)} %get-tuple-element.148), channel_id=1, source_target_pairs={{0,8},{1,9},{2,10},{3,11},{4,12},{5,13},{6,14},{7,15},{8,16},{9,17... | collective-permute-start | bytes 645128 | tf_op jit(solution)/shard_map/ppermute | solution.py:68
  74.6 57.7 %collective-permute-start.17 = (bf16[2,48,1120]{2,1,0:T(8,128)(2,1)S(1)}, bf16[2,48,1120]{2,1,0:T(8,128)(2,1)S(1)}, u32[]{:S(2)}, u32[]{:S(2)}) collective-permute-start(bf16[2,48,1120]{2,1,0:T(8,128)(2,1)S(1)} %get-tuple-element.149), channel_id=1, source_target_pairs={{0,16},{1,17},{2,18},{3,19},{4,20},{5,21},{6,22},{7,23},{8,24},{9,... | collective-permute-start | bytes 645128 | tf_op jit(solution)/shard_map/ppermute | solution.py:68
  86.4 47.5 %collective-permute-start.18 = (bf16[2,48,1120]{2,1,0:T(8,128)(2,1)S(1)}, bf16[2,48,1120]{2,1,0:T(8,128)(2,1)S(1)}, u32[]{:S(2)}, u32[]{:S(2)}) collective-permute-start(bf16[2,48,1120]{2,1,0:T(8,128)(2,1)S(1)} %get-tuple-element.147), channel_id=1, source_target_pairs={{0,24},{1,25},{2,26},{3,27},{4,28},{5,29},{6,30},{7,31},{8,0},{9,1... | collective-permute-start | bytes 645128 | tf_op jit(solution)/shard_map/ppermute | solution.py:68
  92.4 46.2 %collective-permute-start.24 = (bf16[2,48,1120]{2,1,0:T(8,128)(2,1)S(1)}, bf16[2,48,1120]{2,1,0:T(8,128)(2,1)S(1)}, u32[]{:S(2)}, u32[]{:S(2)}) collective-permute-start(bf16[2,48,1120]{2,1,0:T(8,128)(2,1)S(1)} %get-tuple-element.138), channel_id=1, source_target_pairs={{0,8},{1,9},{2,10},{3,11},{4,12},{5,13},{6,14},{7,15},{8,16},{9,17... | collective-permute-start | bytes 645128 | tf_op jit(solution)/shard_map/ppermute | solution.py:68
  113.4 28.9 %collective-permute-start.25 = (bf16[2,48,1120]{2,1,0:T(8,128)(2,1)S(1)}, bf16[2,48,1120]{2,1,0:T(8,128)(2,1)S(1)}, u32[]{:S(2)}, u32[]{:S(2)}) collective-permute-start(bf16[2,48,1120]{2,1,0:T(8,128)(2,1)S(1)} %get-tuple-element.139), channel_id=1, source_target_pairs={{0,16},{1,17},{2,18},{3,19},{4,20},{5,21},{6,22},{7,23},{8,24},{9,... | collective-permute-start | bytes 645128 | tf_op jit(solution)/shard_map/ppermute | solution.py:68
  132.3 12.2 %collective-permute-start.26 = (bf16[2,48,1120]{2,1,0:T(8,128)(2,1)S(1)}, bf16[2,48,1120]{2,1,0:T(8,128)(2,1)S(1)}, u32[]{:S(2)}, u32[]{:S(2)}) collective-permute-start(bf16[2,48,1120]{2,1,0:T(8,128)(2,1)S(1)} %get-tuple-element.137), channel_id=1, source_target_pairs={{0,24},{1,25},{2,26},{3,27},{4,28},{5,29},{6,30},{7,31},{8,0},{9,1... | collective-permute-start | bytes 645128 | tf_op jit(solution)/shard_map/ppermute | solution.py:68
  133.8 28.8 %collective-permute-start.11 = (bf16[4,2,48,1120]{3,2,1,0:T(8,128)(2,1)S(1)}, bf16[4,2,48,1120]{3,2,1,0:T(8,128)(2,1)S(1)}, u32[]{:S(2)}, u32[]{:S(2)}) collective-permute-start(bf16[4,2,48,1120]{3,2,1,0:T(8,128)(2,1)S(1)} %bitcast_dynamic-update-slice_fusion.15), channel_id=1, source_target_pairs={{0,2},{1,3},{2,0},{3,1},{4,6},{5,7},{6,4},{7,5},{8,10},{9,11},{10,... | collective-permute-start | bytes 2580488 | tf_op jit(solution)/shard_map/ppermute | solution.py:68
  138.6 23.6 %collective-permute-start.12 = (bf16[4,2,48,1120]{3,2,1,0:T(8,128)(2,1)S(1)}, bf16[4,2,48,1120]{3,2,1,0:T(8,128)(2,1)S(1)}, u32[]{:S(2)}, u32[]{:S(2)}) collective-permute-start(bf16[4,2,48,1120]{3,2,1,0:T(8,128)(2,1)S(1)} %bitcast_dynamic-update-slice_fusion.15), channel_id=1, source_target_pairs={{0,4},{1,5},{2,6},{3,7},{4,0},{5,1},{6,2},{7,3},{8,12},{9,13},{10,... | collective-permute-start | bytes 2580488 | tf_op jit(solution)/shard_map/ppermute | solution.py:68
  142.3 41.4 %collective-permute-start.19 = (bf16[4,2,48,1120]{3,2,1,0:T(8,128)(2,1)S(1)}, bf16[4,2,48,1120]{3,2,1,0:T(8,128)(2,1)S(1)}, u32[]{:S(2)}, u32[]{:S(2)}) collective-permute-start(bf16[4,2,48,1120]{3,2,1,0:T(8,128)(2,1)S(1)} %bitcast_dynamic-update-slice_fusion.12), channel_id=1, source_target_pairs={{0,2},{1,3},{2,0},{3,1},{4,6},{5,7},{6,4},{7,5},{8,10},{9,11},{10,... | collective-permute-start | bytes 2580488 | tf_op jit(solution)/shard_map/ppermute | solution.py:68
  144.5 38.8 %collective-permute-start.20 = (bf16[4,2,48,1120]{3,2,1,0:T(8,128)(2,1)S(1)}, bf16[4,2,48,1120]{3,2,1,0:T(8,128)(2,1)S(1)}, u32[]{:S(2)}, u32[]{:S(2)}) collective-permute-start(bf16[4,2,48,1120]{3,2,1,0:T(8,128)(2,1)S(1)} %bitcast_dynamic-update-slice_fusion.12), channel_id=1, source_target_pairs={{0,4},{1,5},{2,6},{3,7},{4,0},{5,1},{6,2},{7,3},{8,12},{9,13},{10,... | collective-permute-start | bytes 2580488 | tf_op jit(solution)/shard_map/ppermute | solution.py:68
  162.2 45.8 %collective-permute-start.27 = (bf16[4,2,48,1120]{3,2,1,0:T(8,128)(2,1)S(1)}, bf16[4,2,48,1120]{3,2,1,0:T(8,128)(2,1)S(1)}, u32[]{:S(2)}, u32[]{:S(2)}) collective-permute-start(bf16[4,2,48,1120]{3,2,1,0:T(8,128)(2,1)S(1)} %bitcast_dynamic-update-slice_fusion.9), channel_id=1, source_target_pairs={{0,2},{1,3},{2,0},{3,1},{4,6},{5,7},{6,4},{7,5},{8,10},{9,11},{10,... | collective-permute-start | bytes 2580488 | tf_op jit(solution)/shard_map/ppermute | solution.py:68
  162.7 48.0 %collective-permute-start.28 = (bf16[4,2,48,1120]{3,2,1,0:T(8,128)(2,1)S(1)}, bf16[4,2,48,1120]{3,2,1,0:T(8,128)(2,1)S(1)}, u32[]{:S(2)}, u32[]{:S(2)}) collective-permute-start(bf16[4,2,48,1120]{3,2,1,0:T(8,128)(2,1)S(1)} %bitcast_dynamic-update-slice_fusion.9), channel_id=1, source_target_pairs={{0,4},{1,5},{2,6},{3,7},{4,0},{5,1},{6,2},{7,3},{8,12},{9,13},{10,... | collective-permute-start | bytes 2580488 | tf_op jit(solution)/shard_map/ppermute | solution.py:68
  183.3 34.2 %collective-permute-start.13 = (bf16[2,2,48,1120]{3,2,1,0:T(8,128)(2,1)S(1)}, bf16[2,2,48,1120]{3,2,1,0:T(8,128)(2,1)S(1)}, u32[]{:S(2)}, u32[]{:S(2)}) collective-permute-start(bf16[2,2,48,1120]{3,2,1,0:T(8,128)(2,1)S(1)} %slice.243), channel_id=1, source_target_pairs={{0,2},{1,3},{2,0},{3,1},{4,6},{5,7},{6,4},{7,5},{8,10},{9,11},{10,... | collective-permute-start | bytes 1290248 | tf_op jit(solution)/shard_map/ppermute | solution.py:68
  183.7 36.4 %collective-permute-start.14 = (bf16[2,2,48,1120]{3,2,1,0:T(8,128)(2,1)S(1)}, bf16[2,2,48,1120]{3,2,1,0:T(8,128)(2,1)S(1)}, u32[]{:S(2)}, u32[]{:S(2)}) collective-permute-start(bf16[2,2,48,1120]{3,2,1,0:T(8,128)(2,1)S(1)} %slice.244), channel_id=1, source_target_pairs={{0,4},{1,5},{2,6},{3,7},{4,0},{5,1},{6,2},{7,3},{8,12},{9,13},{10,... | collective-permute-start | bytes 1290248 | tf_op jit(solution)/shard_map/ppermute | solution.py:68
  208.0 19.0 %collective-permute-start.21 = (bf16[2,2,48,1120]{3,2,1,0:T(8,128)(2,1)S(1)}, bf16[2,2,48,1120]{3,2,1,0:T(8,128)(2,1)S(1)}, u32[]{:S(2)}, u32[]{:S(2)}) collective-permute-start(bf16[2,2,48,1120]{3,2,1,0:T(8,128)(2,1)S(1)} %slice.245), channel_id=1, source_target_pairs={{0,2},{1,3},{2,0},{3,1},{4,6},{5,7},{6,4},{7,5},{8,10},{9,11},{10,... | collective-permute-start | bytes 1290248 | tf_op jit(solution)/shard_map/ppermute | solution.py:68
  210.7 17.5 %collective-permute-start.22 = (bf16[2,2,48,1120]{3,2,1,0:T(8,128)(2,1)S(1)}, bf16[2,2,48,1120]{3,2,1,0:T(8,128)(2,1)S(1)}, u32[]{:S(2)}, u32[]{:S(2)}) collective-permute-start(bf16[2,2,48,1120]{3,2,1,0:T(8,128)(2,1)S(1)} %slice.246), channel_id=1, source_target_pairs={{0,4},{1,5},{2,6},{3,7},{4,0},{5,1},{6,2},{7,3},{8,12},{9,13},{10,... | collective-permute-start | bytes 1290248 | tf_op jit(solution)/shard_map/ppermute | solution.py:68
  217.5 51.8 %collective-permute-start.29 = (bf16[2,2,48,1120]{3,2,1,0:T(8,128)(2,1)}, bf16[2,2,48,1120]{3,2,1,0:T(8,128)(2,1)}, u32[]{:S(2)}, u32[]{:S(2)}) collective-permute-start(bf16[2,2,48,1120]{3,2,1,0:T(8,128)(2,1)} %slice.247), channel_id=1, source_target_pairs={{0,2},{1,3},{2,0},{3,1},{4,6},{5,7},{6,4},{7,5},{8,10},{9,11},{10,... | collective-permute-start | bytes 1290248 | tf_op jit(solution)/shard_map/ppermute | solution.py:68
  237.7 11.7 %collective-permute-start = (bf16[128,512]{1,0:T(8,128)(2,1)}, bf16[128,512]{1,0:T(8,128)(2,1)}, u32[]{:S(2)}, u32[]{:S(2)}) collective-permute-start(bf16[128,512]{1,0:T(8,128)(2,1)} %pad_maximum_fusion.8), channel_id=1, source_target_pairs={{0,8},{1,9},{2,10},{3,11},{4,12},{5,13},{6,14},{7,15},{8,16},{9,17... | collective-permute-start | bytes 393224 | tf_op jit(solution)/shard_map/ppermute | solution.py:68
  244.4 6.6 collective-permute-start.1
  246.5 5.7 collective-permute-start.2
  249.4 21.5 %collective-permute-start.30 = (bf16[2,2,48,1120]{3,2,1,0:T(8,128)(2,1)}, bf16[2,2,48,1120]{3,2,1,0:T(8,128)(2,1)S(1)}, u32[]{:S(2)}, u32[]{:S(2)}) collective-permute-start(bf16[2,2,48,1120]{3,2,1,0:T(8,128)(2,1)} %slice.248), channel_id=1, source_target_pairs={{0,4},{1,5},{2,6},{3,7},{4,0},{5,1},{6,2},{7,3},{8,12},{9,13},{10,... | collective-permute-start | bytes 1290248 | tf_op jit(solution)/shard_map/ppermute | solution.py:68
  262.6 16.3 %collective-permute-start.3 = (bf16[128,1536]{1,0:T(8,128)(2,1)S(1)}, bf16[128,1536]{1,0:T(8,128)(2,1)S(1)}, u32[]{:S(2)}, u32[]{:S(2)}) collective-permute-start(bf16[128,1536]{1,0:T(8,128)(2,1)S(1)} %get-tuple-element.113), channel_id=1, source_target_pairs={{0,8},{1,9},{2,10},{3,11},{4,12},{5,13},{6,14},{7,15},{8,16},{9,17... | collective-permute-start | bytes 1179656 | tf_op jit(solution)/shard_map/ppermute | solution.py:68
  266.0 27.2 %collective-permute-start.4 = (bf16[128,1536]{1,0:T(8,128)(2,1)S(1)}, bf16[128,1536]{1,0:T(8,128)(2,1)S(1)}, u32[]{:S(2)}, u32[]{:S(2)}) collective-permute-start(bf16[128,1536]{1,0:T(8,128)(2,1)S(1)} %get-tuple-element.113), channel_id=1, source_target_pairs={{0,16},{1,17},{2,18},{3,19},{4,20},{5,21},{6,22},{7,23},{8,24},{9,... | collective-permute-start | bytes 1179656 | tf_op jit(solution)/shard_map/ppermute | solution.py:68
  269.3 23.9 %collective-permute-start.5 = (bf16[128,1536]{1,0:T(8,128)(2,1)S(1)}, bf16[128,1536]{1,0:T(8,128)(2,1)S(1)}, u32[]{:S(2)}, u32[]{:S(2)}) collective-permute-start(bf16[128,1536]{1,0:T(8,128)(2,1)S(1)} %get-tuple-element.113), channel_id=1, source_target_pairs={{0,24},{1,25},{2,26},{3,27},{4,28},{5,29},{6,30},{7,31},{8,0},{9,1... | collective-permute-start | bytes 1179656 | tf_op jit(solution)/shard_map/ppermute | solution.py:68
  293.4 6.2 collective-permute-start.6
  336.7 3.7 collective-permute-start.39
  337.2 148.9 %all-gather.9.cloned.1.call-start = ((), (), s32[]{:S(2)}) async-start(), calls=%async_computation.7 | async-start | bytes 1966080 | tf_op jit(solution)/shard_map/all_gather | solution.py:314
  344.6 30.4 %collective-permute-start.40 = (bf16[128,1536]{1,0:T(8,128)(2,1)S(1)}, bf16[128,1536]{1,0:T(8,128)(2,1)S(1)}, u32[]{:S(2)}, u32[]{:S(2)}) collective-permute-start(bf16[128,1536]{1,0:T(8,128)(2,1)S(1)} %get-tuple-element.117), channel_id=1, source_target_pairs={{0,24},{1,25},{2,26},{3,27},{4,28},{5,29},{6,30},{7,31},{8,0},{9,1... | collective-permute-start | bytes 1179656 | tf_op jit(solution)/shard_map/ppermute | solution.py:68
  351.5 62.6 %collective-permute-start.41 = (bf16[128,1536]{1,0:T(8,128)(2,1)S(1)}, bf16[128,1536]{1,0:T(8,128)(2,1)S(1)}, u32[]{:S(2)}, u32[]{:S(2)}) collective-permute-start(bf16[128,1536]{1,0:T(8,128)(2,1)S(1)} %get-tuple-element.119), channel_id=1, source_target_pairs={{0,16},{1,17},{2,18},{3,19},{4,20},{5,21},{6,22},{7,23},{8,24},{9,... | collective-permute-start | bytes 1179656 | tf_op jit(solution)/shard_map/ppermute | solution.py:68
  355.0 59.1 %collective-permute-start.42 = (bf16[128,1536]{1,0:T(8,128)(2,1)S(1)}, bf16[128,1536]{1,0:T(8,128)(2,1)}, u32[]{:S(2)}, u32[]{:S(2)}) collective-permute-start(bf16[128,1536]{1,0:T(8,128)(2,1)S(1)} %get-tuple-element.118), channel_id=1, source_target_pairs={{0,8},{1,9},{2,10},{3,11},{4,12},{5,13},{6,14},{7,15},{8,16},{9,17... | collective-permute-start | bytes 1179656 | tf_op jit(solution)/shard_map/ppermute | solution.py:68
  355.1 261.4 %reduce-scatter.14.cloned.1.call-start = ((), (), s32[]{:S(2)}) async-start(), calls=%async_computation.10 | async-start | bytes 1327104 | tf_op jit(solution)/shard_map/reduce_scatter | solution.py:316
  426.0 11.2 %collective-permute-start.49 = (bf16[128,384]{1,0:T(8,128)(2,1)S(1)}, bf16[128,384]{1,0:T(8,128)(2,1)S(1)}, u32[]{:S(2)}, u32[]{:S(2)}) collective-permute-start(bf16[128,384]{1,0:T(8,128)(2,1)S(1)} %bitcast.378), channel_id=1, source_target_pairs={{0,8},{1,9},{2,10},{3,11},{4,12},{5,13},{6,14},{7,15},{8,16},{9,17... | collective-permute-start | bytes 294920 | tf_op jit(solution)/shard_map/ppermute | solution.py:68
  426.1 15.8 %collective-permute-start.50 = (bf16[128,384]{1,0:T(8,128)(2,1)S(1)}, bf16[128,384]{1,0:T(8,128)(2,1)S(1)}, u32[]{:S(2)}, u32[]{:S(2)}) collective-permute-start(bf16[128,384]{1,0:T(8,128)(2,1)S(1)} %bitcast.377), channel_id=1, source_target_pairs={{0,16},{1,17},{2,18},{3,19},{4,20},{5,21},{6,22},{7,23},{8,24},{9,... | collective-permute-start | bytes 294920 | tf_op jit(solution)/shard_map/ppermute | solution.py:68
  426.5 16.0 %collective-permute-start.51 = (bf16[128,384]{1,0:T(8,128)(2,1)S(1)}, bf16[128,384]{1,0:T(8,128)(2,1)S(1)}, u32[]{:S(2)}, u32[]{:S(2)}) collective-permute-start(bf16[128,384]{1,0:T(8,128)(2,1)S(1)} %bitcast.376), channel_id=1, source_target_pairs={{0,24},{1,25},{2,26},{3,27},{4,28},{5,29},{6,30},{7,31},{8,0},{9,1... | collective-permute-start | bytes 294920 | tf_op jit(solution)/shard_map/ppermute | solution.py:68
  432.6 17.3 %collective-permute-start.43 = (bf16[128,512]{0,1:T(8,128)(2,1)}, bf16[128,512]{0,1:T(8,128)(2,1)}, u32[]{:S(2)}, u32[]{:S(2)}) collective-permute-start(bf16[128,512]{0,1:T(8,128)(2,1)} %get-tuple-element.162), channel_id=1, source_target_pairs={{8,0},{9,1},{10,2},{11,3},{12,4},{13,5},{14,6},{15,7},{16,8},{17,9... | collective-permute-start | bytes 393224 | tf_op jit(solution)/shard_map/ppermute | solution.py:68
  433.8 36.3 %collective-permute-start.44 = (bf16[128,512]{0,1:T(8,128)(2,1)}, bf16[128,512]{0,1:T(8,128)(2,1)}, u32[]{:S(2)}, u32[]{:S(2)}) collective-permute-start(bf16[128,512]{0,1:T(8,128)(2,1)} %get-tuple-element.164), channel_id=1, source_target_pairs={{16,0},{17,1},{18,2},{19,3},{20,4},{21,5},{22,6},{23,7},{24,8},{25... | collective-permute-start | bytes 393224 | tf_op jit(solution)/shard_map/ppermute | solution.py:68
  437.2 33.0 %collective-permute-start.45 = (bf16[128,512]{0,1:T(8,128)(2,1)S(1)}, bf16[128,512]{0,1:T(8,128)(2,1)}, u32[]{:S(2)}, u32[]{:S(2)}) collective-permute-start(bf16[128,512]{0,1:T(8,128)(2,1)S(1)} %get-tuple-element.163), channel_id=1, source_target_pairs={{24,0},{25,1},{26,2},{27,3},{28,4},{29,5},{30,6},{31,7}} | collective-permute-start | bytes 393224 | tf_op jit(solution)/shard_map/ppermute | solution.py:68
  446.6 171.4 %reduce-scatter.12.cloned.1.call-start = ((), (), s32[]{:S(2)}) async-start(), calls=%async_computation.8 | async-start | bytes 1769472 | tf_op jit(solution)/shard_map/reduce_scatter | solution.py:316
  472.4 8.7 %collective-permute-start.46 = (bf16[128,512]{1,0:T(8,128)(2,1)}, bf16[128,512]{1,0:T(8,128)(2,1)}, u32[]{:S(2)}, u32[]{:S(2)}) collective-permute-start(bf16[128,512]{1,0:T(8,128)(2,1)} %bitcast.111), channel_id=1, source_target_pairs={{0,8},{1,9},{2,10},{3,11},{4,12},{5,13},{6,14},{7,15},{8,16},{9,17... | collective-permute-start | bytes 393224 | tf_op jit(solution)/shard_map/ppermute | solution.py:68
  473.2 12.0 %collective-permute-start.47 = (bf16[128,512]{1,0:T(8,128)(2,1)}, bf16[128,512]{1,0:T(8,128)(2,1)}, u32[]{:S(2)}, u32[]{:S(2)}) collective-permute-start(bf16[128,512]{1,0:T(8,128)(2,1)} %bitcast.113), channel_id=1, source_target_pairs={{0,16},{1,17},{2,18},{3,19},{4,20},{5,21},{6,22},{7,23},{8,24},{9,... | collective-permute-start | bytes 393224 | tf_op jit(solution)/shard_map/ppermute | solution.py:68
  473.9 12.1 %collective-permute-start.48 = (bf16[128,512]{1,0:T(8,128)(2,1)}, bf16[128,512]{1,0:T(8,128)(2,1)S(1)}, u32[]{:S(2)}, u32[]{:S(2)}) collective-permute-start(bf16[128,512]{1,0:T(8,128)(2,1)} %bitcast.115), channel_id=1, source_target_pairs={{0,24},{1,25},{2,26},{3,27},{4,28},{5,29},{6,30},{7,31},{8,0},{9,1... | collective-permute-start | bytes 393224 | tf_op jit(solution)/shard_map/ppermute | solution.py:68
  489.7 132.4 %reduce-scatter.20.cloned.1.call-start = ((), (), s32[]{:S(2)}) async-start(), calls=%async_computation.13 | async-start | bytes 4423680 | tf_op jit(solution)/shard_map/reduce_scatter | solution.py:256
  503.6 150.1 %reduce-scatter.18.cloned.1.call-start = ((), (), s32[]{:S(2)}) async-start(), calls=%async_computation.12 | async-start | bytes 4423680 | tf_op jit(solution)/shard_map/reduce_scatter | solution.py:256
  517.7 186.7 %reduce-scatter.16.cloned.1.call-start = ((), (), s32[]{:S(2)}) async-start(), calls=%async_computation.11 | async-start | bytes 4423680 | tf_op jit(solution)/shard_map/reduce_scatter | solution.py:256
  543.0 3.8 collective-permute-start.31
  552.5 60.8 %collective-permute-start.32 = (bf16[128,1536]{1,0:T(8,128)(2,1)}, bf16[128,1536]{1,0:T(8,128)(2,1)}, u32[]{:S(2)}, u32[]{:S(2)}) collective-permute-start(bf16[128,1536]{1,0:T(8,128)(2,1)} %get-tuple-element.120), channel_id=1, source_target_pairs={{0,24},{1,25},{2,26},{3,27},{4,28},{5,29},{6,30},{7,31},{8,0},{9,1... | collective-permute-start | bytes 1179656 | tf_op jit(solution)/shard_map/ppermute | solution.py:68
  555.0 58.3 %collective-permute-start.33 = (bf16[128,1536]{1,0:T(8,128)(2,1)}, bf16[128,1536]{1,0:T(8,128)(2,1)}, u32[]{:S(2)}, u32[]{:S(2)}) collective-permute-start(bf16[128,1536]{1,0:T(8,128)(2,1)} %get-tuple-element.122), channel_id=1, source_target_pairs={{0,16},{1,17},{2,18},{3,19},{4,20},{5,21},{6,22},{7,23},{8,24},{9,... | collective-permute-start | bytes 1179656 | tf_op jit(solution)/shard_map/ppermute | solution.py:68
  556.0 57.3 %collective-permute-start.34 = (bf16[128,1536]{1,0:T(8,128)(2,1)}, bf16[128,1536]{1,0:T(8,128)(2,1)}, u32[]{:S(2)}, u32[]{:S(2)}) collective-permute-start(bf16[128,1536]{1,0:T(8,128)(2,1)} %get-tuple-element.121), channel_id=1, source_target_pairs={{0,8},{1,9},{2,10},{3,11},{4,12},{5,13},{6,14},{7,15},{8,16},{9,17... | collective-permute-start | bytes 1179656 | tf_op jit(solution)/shard_map/ppermute | solution.py:68
  623.1 82.3 %collective-permute-start.54 = (bf16[192,1120]{1,0:T(8,128)(2,1)S(1)}, bf16[192,1120]{1,0:T(8,128)(2,1)S(1)}, u32[]{:S(2)}, u32[]{:S(2)}) collective-permute-start(bf16[192,1120]{1,0:T(8,128)(2,1)S(1)} %dynamic-slice_bitcast_fusion.3), channel_id=1, source_target_pairs={{0,1},{1,0},{2,3},{3,2},{4,5},{5,4},{6,7},{7,6},{8,9},{9,8},{10,11... | collective-permute-start | bytes 1290248 | tf_op jit(solution)/shard_map/ppermute | solution.py:68
  654.8 51.8 %collective-permute-start.53 = (bf16[192,1120]{1,0:T(8,128)(2,1)S(1)}, bf16[192,1120]{1,0:T(8,128)(2,1)S(1)}, u32[]{:S(2)}, u32[]{:S(2)}) collective-permute-start(bf16[192,1120]{1,0:T(8,128)(2,1)S(1)} %dynamic-slice_bitcast_fusion.4), channel_id=1, source_target_pairs={{0,1},{1,0},{2,3},{3,2},{4,5},{5,4},{6,7},{7,6},{8,9},{9,8},{10,11... | collective-permute-start | bytes 1290248 | tf_op jit(solution)/shard_map/ppermute | solution.py:68
  705.4 4.2 collective-permute-start.52
  (40 other events, 896.2 us)
Sparse Core Ops, SparseCore 0:
  11.5 123.5 all-gather.4
  138.0 73.3 all-gather.6
  337.3 76.9 all-gather.10
  415.7 54.7 all-gather.8
  474.2 34.9 reduce-scatter.13
  513.2 38.4 reduce-scatter.11
  555.1 47.8 reduce-scatter.19
  606.4 47.2 reduce-scatter.17
  657.1 47.2 reduce-scatter.15

commit v2 on v1

--- a/solution.py
+++ b/solution.py
@@ -1,6 +1,8 @@
 import jax
 import jax.numpy as jnp
 from jax import lax
+from jax.experimental import pallas as pl
+from jax.experimental.pallas import tpu as pltpu
 from jax.sharding import PartitionSpec as P
 
 QUERY_HEADS = 12
@@ -9,6 +11,7 @@
 GROUP = QUERY_HEADS // KEY_VALUE_HEADS
 KV_WIDTH = KEY_VALUE_HEADS * HEAD_SIZE
 EPSILON = 1e-06
+BACK_COST = 8 * 10**9
 BOTH = ("ctx", "fsdp")
 F32 = jnp.float32
 BF16 = jnp.bfloat16
@@ -56,6 +59,7 @@
 class Links:
     def __init__(self, ctx_size, fsdp_size):
         self.ctx_size, self.fsdp_size = ctx_size, fsdp_size
+        self.label = "move"
         self.planes = [m for m in (2, 4, 8, 16, 32, 64) if m < fsdp_size]
 
     def send(self, x, target):
@@ -65,7 +69,8 @@
                 to = target(c, f)
                 if to is not None:
                     pairs.append((c * self.fsdp_size + f, to[0] * self.fsdp_size + to[1]))
-        return lax.ppermute(x, BOTH, pairs)
+        with jax.named_scope(self.label):
+            return lax.ppermute(x, BOTH, pairs)
 
     def core(self, x):
         return self.send(x, lambda c, f: (c, f ^ 1))
@@ -132,7 +137,7 @@
     return total
 
 
-def per_device(
+def per_device_any_mesh(
     tokens,
     positions,
     norm1_gain,
@@ -347,6 +352,725 @@
     )
 
 
+def after(x, *others):
+    return lax.optimization_barrier((x, *others))[0]
+
+
+def phase(*groups):
+    flat = lax.optimization_barrier(tuple(x for group in groups for x in group))
+    out = []
+    for group in groups:
+        out.append(list(flat[: len(group)]))
+        flat = flat[len(group) :]
+    return out
+
+
+def plane_start(links, shard):
+    return links.plane(shard, 2), links.plane(shard, 4)
+
+
+def plane_end(links, shard, a, b):
+    half = shard.shape[0] // 2
+    return shard, a, b, links.plane(b[:half], 2), links.plane(a[half:], 4)
+
+
+def laid_out(entries, shard, a, b, low, high):
+    half = len(entries) // 2
+    return [
+        (entries, 0, shard),
+        (entries, 1, a),
+        (entries, 2, b),
+        (entries[:half], 3, low),
+        (entries[half:], 3, high),
+    ]
+
+
+def ff_kernel(layout, sizes, place, normed, out_grad, *refs):
+    ctx_size, chips, rows = sizes
+    pieces, refs = refs[: len(layout)], refs[len(layout) :]
+    act_ref, gate_ref, up_ref, down_ref, y_ref, weights, semaphores = refs
+
+    @pl.when(pl.program_id(0) == 0)
+    def _():
+        ctx, chip = place[0], place[1]
+        for which in range(3):
+            for (entries, mask, _), piece in zip(layout, pieces):
+                for i, (step, core) in enumerate(entries):
+                    source = lax.rem(ctx - step + ctx_size, ctx_size)
+                    start = ((source * chips + (chip ^ mask)) * 2 + core) * rows
+                    pltpu.make_async_copy(
+                        piece.at[i, which],
+                        weights.at[which, pl.ds(pl.multiple_of(start, rows), rows)],
+                        semaphores.at[which],
+                    ).start()
+
+    def arrived(which):
+        @pl.when(pl.program_id(0) == 0)
+        def _():
+            pltpu.make_async_copy(
+                weights.at[which], weights.at[which], semaphores.at[which]
+            ).wait()
+
+    x, gy = normed[...], out_grad[...]
+    arrived(0)
+    gate = nn(x, weights[0])
+    arrived(1)
+    up = nn(x, weights[1])
+    arrived(2)
+    grad = nn(gy, weights[2])
+    sigmoid = 1.0 / (1.0 + jnp.exp(-gate))
+    silu = gate * sigmoid
+    act = (silu * up).astype(BF16)
+    grad_gate = (grad * up * sigmoid * (1.0 + gate * (1.0 - sigmoid))).astype(BF16)
+    grad_up = (grad * silu).astype(BF16)
+    act_ref[...] = act
+    gate_ref[...] = grad_gate
+    up_ref[...] = grad_up
+    down_ref[...] = (nt(grad_gate, weights[0]) + nt(grad_up, weights[1])).astype(BF16)
+    y_ref[...] = nt(act, weights[2]).astype(BF16)
+
+
+def feed_forward(links, layout, place, normed, out_grad):
+    tokens, width = normed.shape
+    rows, block = layout[0][2].shape[2:]
+    tile = 256
+    wide = pl.BlockSpec((tile, width), lambda i, place: (i, 0))
+    narrow = pl.BlockSpec((tile, block), lambda i, place: (i, 0))
+    small = jax.ShapeDtypeStruct((tokens, block), BF16)
+    large = jax.ShapeDtypeStruct((tokens, width), BF16)
+    sizes = (links.ctx_size, links.fsdp_size // 2, rows)
+
+    def body(*refs):
+        ff_kernel(layout, sizes, *refs)
+
+    return pl.pallas_call(
+        body,
+        grid_spec=pltpu.PrefetchScalarGridSpec(
+            num_scalar_prefetch=1,
+            grid=(tokens // tile,),
+            in_specs=[wide, wide] + [pl.BlockSpec(memory_space=pl.ANY)] * len(layout),
+            out_specs=[narrow, narrow, narrow, wide, wide],
+            scratch_shapes=[
+                pltpu.VMEM((3, width, block), BF16),
+                pltpu.SemaphoreType.DMA((3,)),
+            ],
+        ),
+        out_shape=[small, small, small, large, large],
+        compiler_params=pltpu.CompilerParams(vmem_limit_bytes=56 * 2**20),
+        cost_estimate=pl.CostEstimate(flops=0, bytes_accessed=0, transcendentals=0),
+    )(place, normed, out_grad, *[piece for _, _, piece in layout])
+
+
+def grad_kernel(place, *refs):
+    lefts, rights, outs = refs[:4], refs[4:10], refs[10:]
+    keep_low, send_low, keep_high, send_high = outs
+    j = pl.program_id(0)
+    for which in range(3):
+        left_a, left_b = lefts[:2] if which < 2 else lefts[2:]
+        right_a, right_b = rights[2 * which : 2 * which + 2]
+        out = tn(left_a[...], right_a[...]) + tn(left_b[...], right_b[...])
+        half = out.shape[0] // 2
+        low, high = out[:half].astype(BF16), out[half:].astype(BF16)
+
+        @pl.when(j < 2)
+        def _():
+            keep_low[0, which] = low
+
+        @pl.when(j >= 2)
+        def _():
+            send_low[0, which] = low
+
+        @pl.when(j % 2 == 0)
+        def _():
+            keep_high[0, which] = high
+
+        @pl.when(j % 2 == 1)
+        def _():
+            send_high[0, which] = high
+
+
+def ff_grad_terms(place, lefts, rights):
+    tokens, width = lefts[0].shape
+    block = rights[0].shape[1]
+    part = width // 4
+    left = pl.BlockSpec((tokens, part), lambda j, place: (0, place[1] ^ j))
+    right = pl.BlockSpec((tokens, block), lambda j, place: (0, 0))
+
+    def out(index):
+        return pl.BlockSpec((1, 3, part // 2, block), lambda j, place: (index(j), 0, 0, 0))
+
+    return pl.pallas_call(
+        grad_kernel,
+        grid_spec=pltpu.PrefetchScalarGridSpec(
+            num_scalar_prefetch=1,
+            grid=(4,),
+            in_specs=[left] * 4 + [right] * 6,
+            out_specs=[
+                out(lambda j: jnp.minimum(j, 1)),
+                out(lambda j: jnp.maximum(j - 2, 0)),
+                out(lambda j: j // 2),
+                out(lambda j: j // 2),
+            ],
+        ),
+        out_shape=[jax.ShapeDtypeStruct((2, 3, part // 2, block), BF16)] * 4,
+        compiler_params=pltpu.CompilerParams(vmem_limit_bytes=56 * 2**20),
+        cost_estimate=pl.CostEstimate(flops=0, bytes_accessed=0, transcendentals=0),
+    )(place, *lefts, *rights)
+
+
+def added(a, b):
+    return (a.astype(F32) + b.astype(F32)).astype(BF16)
+
+
+def reduce_start(links, terms):
+    return links.plane(terms[1], 4), links.plane(terms[3], 2)
+
+
+def reduce_next(links, terms, first):
+    keep_low, _, keep_high, _ = terms
+    return (
+        links.plane(added(keep_low[1], first[0][1]), 2),
+        links.plane(added(keep_high[1], first[1][1]), 4),
+    )
+
+
+def reduce_end(terms, first, second):
+    return [
+        keep[0].astype(F32) + one[0].astype(F32) + two.astype(F32)
+        for keep, one, two in zip(terms[::2], first, second)
+    ]
+
+
+def split_kernel(place, gate, up, down, mine, other):
+    block = mine.shape[3]
+
+    def write(core):
+        for which, ref in enumerate((gate, up, down)):
+            for target in range(mine.shape[0]):
+                start = (2 * target + core) * block
+                mine[target, which] = ref[:, start : start + block]
+                start = (2 * target + 1 - core) * block
+                other[target, which] = ref[:, start : start + block]
+
+    @pl.when(place[2] == 0)
+    def _():
+        write(0)
+
+    @pl.when(place[2] != 0)
+    def _():
+        write(1)
+
+
+def split_hidden(links, place, shards):
+    rows, hidden = shards[0].shape
+    whole = pl.BlockSpec((rows, hidden), lambda i, place: (0, 0))
+    shape = (links.ctx_size, 3, rows, hidden // (2 * links.ctx_size))
+    out = pl.BlockSpec(shape, lambda i, place: (0, 0, 0, 0))
+    return pl.pallas_call(
+        split_kernel,
+        grid_spec=pltpu.PrefetchScalarGridSpec(
+            num_scalar_prefetch=1, grid=(1,), in_specs=[whole] * 3, out_specs=[out] * 2
+        ),
+        out_shape=[jax.ShapeDtypeStruct(shape, BF16)] * 2,
+        compiler_params=pltpu.CompilerParams(vmem_limit_bytes=32 * 2**20),
+    )(place, *shards)
+
+
+class Rows:
+    def __init__(self, ctx_size, chips, pieces, layout):
+        self.pieces, self.layout = pieces, layout
+        self.sizes = (ctx_size, chips)
+        self.rows, self.columns = pieces[0].shape[-2:]
+        self.shape = (2 * ctx_size * chips * self.rows, self.columns)
+
+    def start(self, place, refs, weight, semaphore):
+        chips = self.sizes[1]
+        for piece, index, source, mask, turned in self.layout:
+            start = ((source * chips + (place[1] ^ mask)) * 2 + (place[2] ^ turned)) * self.rows
+            pltpu.make_async_copy(
+                refs[piece].at[index],
+                weight.at[pl.ds(pl.multiple_of(start, self.rows), self.rows)],
+                semaphore,
+            ).start()
+
+
+def by_ctx(links, ctx, got):
+    ctx_size, shard = links.ctx_size, got[0]
+    whole = jnp.zeros((ctx_size, *shard.shape), shard.dtype)
+    for step, piece in enumerate(got):
+        whole = lax.dynamic_update_index_in_dim(whole, piece, (ctx - step) % ctx_size, 0)
+    return whole
+
+
+def rows_of_plane(links, mine, a, b, low, high):
+    ctx_size = links.ctx_size
+    half = ctx_size // 2
+    early = links.core(jnp.stack([mine, a, b]))
+    late = links.core(jnp.concatenate([low, high]))
+    pieces = [mine, a, b, low, high, early, late]
+    layout = []
+    for c in range(ctx_size):
+        layout += [(mask, (c,), c, mask, 0) for mask in range(3)]
+        layout.append((3, (c,), c, 3, 0) if c < half else (4, (c - half,), c, 3, 0))
+        layout += [(5, (mask, c), c, mask, 1) for mask in range(3)]
+        layout.append((6, (c,), c, 3, 1))
+    return Rows(ctx_size, links.fsdp_size // 2, pieces, layout)
+
+
+def wait_all(weight, semaphore):
+    pltpu.make_async_copy(weight, weight, semaphore).wait()
+
+
+def call(body, place, arrays, weight, out_shapes, cost):
+    any_spec = pl.BlockSpec(memory_space=pl.ANY)
+    vmem = pl.BlockSpec(memory_space=pltpu.VMEM)
+    count, pieces = len(arrays), len(weight.pieces)
+
+    def kernel(place, *refs):
+        ins, parts, outs = refs[:count], refs[count : count + pieces], refs[count + pieces : -2]
+        scratch, semaphore = refs[-2:]
+        weight.start(place, parts, scratch, semaphore)
+        body(place, ins, outs, scratch, lambda: wait_all(scratch, semaphore))
+
+    return pl.pallas_call(
+        kernel,
+        in_specs=[pl.BlockSpec(memory_space=pltpu.SMEM)] + [vmem] * count + [any_spec] * pieces,
+        out_specs=[vmem] * len(out_shapes),
+        out_shape=[jax.ShapeDtypeStruct(shape, dtype) for shape, dtype in out_shapes],
+        scratch_shapes=[pltpu.VMEM(weight.shape, BF16), pltpu.SemaphoreType.DMA],
+        compiler_params=pltpu.CompilerParams(vmem_limit_bytes=56 * 2**20),
+        cost_estimate=pl.CostEstimate(flops=cost, bytes_accessed=0, transcendentals=0),
+    )(place, *arrays, *weight.pieces)
+
+
+def turn_halves(x, cosine, sine):
+    return x * cosine + pltpu.roll(x, HEAD_SIZE // 2, 1) * sine
+
+
+def turned_heads(x, cosine, sine):
+    heads = [x[:, i : i + HEAD_SIZE] for i in range(0, x.shape[1], HEAD_SIZE)]
+    return jnp.concatenate([turn_halves(x, cosine, sine) for x in heads], axis=1)
+
+
+def qkv_body(shard_rows, place, ins, outs, weight, wait):
+    tokens, cosine, sine = ins
+    normed_ref, query_ref, pairs_ref, small_ref = outs
+    width = tokens.shape[1]
+    qkv_width = width + 2 * KV_WIDTH
+    x = tokens[...].astype(F32)
+    unit = x * rms_scale(x)
+    wait()
+    small = jnp.transpose(weight[:, qkv_width:].astype(F32))[:8]
+    bias_rows = KV_WIDTH * shard_rows // width
+    row = lax.broadcasted_iota(jnp.int32, (width, KV_WIDTH), 0)
+    at = lax.broadcasted_iota(jnp.int32, (width, KV_WIDTH), 1)
+    chosen = row == (at // bias_rows) * shard_rows + at % bias_rows
+    kv_bias = nn(small.astype(BF16), chosen.astype(BF16))
+    normed = (unit * small[0:1]).astype(BF16)
+    normed_ref[...] = normed
+    small_ref[...] = small
+    linear = nn(normed, weight[:, :qkv_width])
+    query = linear[:, :width] + small[1:2]
+    key = linear[:, width : width + KV_WIDTH] + kv_bias[3:4]
+    query_ref[...] = turned_heads(query, cosine[...], sine[...]).astype(BF16)
+    pairs_ref[:, :KV_WIDTH] = turned_heads(key, cosine[...], sine[...]).astype(BF16)
+    pairs_ref[:, KV_WIDTH:] = (linear[:, width + KV_WIDTH :] + kv_bias[4:5]).astype(BF16)
+
+
+def allowed_keys(ctx, positions, blocks):
+    count = positions.shape[0]
+    shape = (count, blocks * count)
+    column = lax.broadcasted_iota(jnp.int32, shape, 1)
+    query = ctx * count + lax.broadcasted_iota(jnp.int32, shape, 0)
+    key = (ctx - column // count) * count + column % count
+    return (key >= query - positions) & (key <= query)
+
+
+def heads_of(x, group):
+    first = group * GROUP
+    return jnp.concatenate(
+        [x[:, i * HEAD_SIZE : (i + 1) * HEAD_SIZE] for i in range(first, first + GROUP)], axis=0
+    )
+
+
+def softmax_of(query, keys, allowed):
+    scores = nt(query, keys) * HEAD_SIZE ** (-0.5)
+    scores = jnp.where(allowed, scores, -1e30)
+    weights = jnp.exp(scores - jnp.max(scores, axis=-1, keepdims=True))
+    weights = jnp.where(allowed, weights, 0.0)
+    return weights / jnp.sum(weights, axis=-1, keepdims=True)
+
+
+def group_pairs(blocks, group):
+    def columns(start):
+        return jnp.concatenate([b[:, start : start + HEAD_SIZE] for b in blocks], axis=0)
+
+    return columns(group * HEAD_SIZE), columns(KV_WIDTH + group * HEAD_SIZE)
+
+
+def mix_body(place, ins, outs, weight, wait):
+    tokens, small, positions, query, *blocks = ins
+    mixed_ref, hidden_ref, normed_ref = outs
+    count = tokens.shape[0]
+    allowed = allowed_keys(place[0], positions[...], len(blocks))
+    allowed = jnp.concatenate([allowed.astype(F32)] * GROUP, axis=0) > 0
+    for group in range(KEY_VALUE_HEADS):
+        keys, values = group_pairs(blocks, group)
+        probs = softmax_of(heads_of(query, group), keys, allowed)
+        mixed = nn(probs.astype(BF16), values).astype(BF16)
+        for h in range(GROUP):
+            start = (group * GROUP + h) * HEAD_SIZE
+            mixed_ref[:, start : start + HEAD_SIZE] = mixed[h * count : (h + 1) * count]
+    wait()
+    hidden = tokens[...].astype(F32) + nn(mixed_ref[...], weight[...])
+    hidden_ref[...] = hidden
+    normed_ref[...] = (hidden * rms_scale(hidden) * small[2:3]).astype(BF16)
+
+
+def norm_back(unit, scale, grad, gain):
+    weighted = grad * gain
+    return scale * (weighted - unit * jnp.mean(weighted * unit, axis=-1, keepdims=True))
+
+
+def mix_back_body(steps, place, ins, outs, weight, wait):
+    terms, ins = ins[:steps], ins[steps:]
+    hidden_ref, small, out_grad, positions, query, cosine, sine, *blocks = ins
+    grad_hidden_ref, low_ref, grad_query_ref, gain_ref, *pair_refs = outs
+    count = hidden_ref.shape[0]
+    hidden = hidden_ref[...]
+    scale = rms_scale(hidden)
+    unit = hidden * scale
+    grad = terms[0][...].astype(F32)
+    for term in terms[1:]:
+        grad = grad + term[...].astype(F32)
+    gain_ref[...] = jnp.sum(grad * unit, axis=0, keepdims=True)
+    grad_hidden = out_grad[...].astype(F32) + norm_back(unit, scale, grad, small[2:3])
+    grad_hidden_ref[...] = grad_hidden
+    low = grad_hidden.astype(BF16)
+    low_ref[...] = low
+    wait()
+    grad_mixed = nt(low, weight[...]).astype(BF16)
+    allowed = allowed_keys(place[0], positions[...], len(blocks))
+    allowed = jnp.concatenate([allowed.astype(F32)] * GROUP, axis=0) > 0
+    score_scale = HEAD_SIZE ** (-0.5)
+    for group in range(KEY_VALUE_HEADS):
+        keys, values = group_pairs(blocks, group)
+        queries, grads = heads_of(query, group), heads_of(grad_mixed, group)
+        probs = softmax_of(queries, keys, allowed)
+        grad_probs = nt(grads, values)
+        delta = jnp.sum(probs * grad_probs, axis=-1, keepdims=True)
+        grad_scores = (probs * (grad_probs - delta)).astype(BF16)
+        grad_query = nn(grad_scores, keys) * score_scale
+        for h in range(GROUP):
+            start = (group * GROUP + h) * HEAD_SIZE
+            grad_query_ref[:, start : start + HEAD_SIZE] = turn_halves(
+                grad_query[h * count : (h + 1) * count], cosine[...], -sine[...]
+            ).astype(BF16)
+        grad_key = (tn(grad_scores, queries) * score_scale).astype(BF16)
+        grad_value = tn(probs.astype(BF16), grads).astype(BF16)
+        start = group * HEAD_SIZE
+        for block, ref in enumerate(pair_refs):
+            rows = slice(block * count, (block + 1) * count)
+            ref[:, start : start + HEAD_SIZE] = grad_key[rows]
+            ref[:, KV_WIDTH + start : KV_WIDTH + start + HEAD_SIZE] = grad_value[rows]
+
+
+def qkv_back_body(steps, place, ins, outs, weight, wait):
+    terms, ins = ins[:steps], ins[steps:]
+    tokens, small, cosine, sine, grad_query, grad_hidden, grad_hidden_low, gain_two = ins
+    stream_ref, share_ref = outs
+    count, width = tokens.shape
+    pairs = terms[0][...].astype(F32)
+    for term in terms[1:]:
+        pairs = pairs + term[...].astype(F32)
+    grad_key = turned_heads(pairs[:, :KV_WIDTH], cosine[...], -sine[...]).astype(BF16)
+    grad_value = pairs[:, KV_WIDTH:].astype(BF16)
+    wait()
+    kv_end = width + KV_WIDTH
+    grad = (
+        nt(grad_query[...], weight[:, :width])
+        + nt(grad_key, weight[:, width:kv_end])
+        + nt(grad_value, weight[:, kv_end : kv_end + KV_WIDTH])
+    )
+    x = tokens[...].astype(F32)
+    scale = rms_scale(x)
+    unit = x * scale
+    stream_ref[...] = grad_hidden[...] + norm_back(unit, scale, grad, small[0:1])
+    gains = jnp.concatenate([jnp.sum(grad * unit, axis=0, keepdims=True), gain_two[...]], axis=0)
+    gains = jnp.concatenate([gains, jnp.zeros((14, width), F32)], axis=0).astype(BF16)
+    targets = share_ref.shape[0]
+    q_columns, kv_columns = width // targets, KV_WIDTH // targets
+    for target in range(targets):
+        q, kv = target * q_columns, target * kv_columns
+        share_ref[target, :count, :q_columns] = grad_query[:, q : q + q_columns]
+        kv_end = q_columns + 2 * kv_columns
+        share_ref[target, :count, q_columns:kv_end] = jnp.concatenate(
+            [grad_key[:, kv : kv + kv_columns], grad_value[:, kv : kv + kv_columns]], axis=1
+        )
+        share_ref[target, :count, kv_end:] = grad_hidden_low[:, q : q + q_columns]
+        share_ref[target, count:, :q_columns] = gains[:, q : q + q_columns]
+        share_ref[target, count:, q_columns:] = jnp.zeros(
+            (16, share_ref.shape[2] - q_columns), BF16
+        )
+
+
+def per_device_plane_of_four(
+    tokens,
+    positions,
+    norm1_gain,
+    q_weight,
+    q_bias,
+    key_projection,
+    key_bias_vector,
+    value_projection,
+    value_bias_vector,
+    o_weight,
+    norm2_gain,
+    gate_weight,
+    up_weight,
+    down_weight,
+    cotangent,
+    *,
+    links,
+):
+    ctx_size, fsdp_size = links.ctx_size, links.fsdp_size
+    ctx, row_index = lax.axis_index("ctx"), lax.axis_index("fsdp")
+    chip, core = row_index // 2, row_index % 2
+    place = jnp.stack([ctx, chip, core])
+    count, width = tokens.shape[1:]
+    shard_rows = q_weight.shape[0]
+    even = core == 0
+    steps = range(1, ctx_size)
+
+    def column(x):
+        return jnp.pad(x, (0, shard_rows - x.shape[0]))[:, None]
+
+    extra = jnp.concatenate(
+        [
+            column(x)
+            for x in (norm1_gain, q_bias, norm2_gain, key_bias_vector, value_bias_vector)
+        ],
+        axis=1,
+    )
+    extra = jnp.pad(extra, ((0, 0), (0, 128 - extra.shape[1])))
+    packed = jnp.concatenate([q_weight, key_projection, value_projection, extra], axis=1)
+    links.label = "qkv_ctx"
+    qkv_got = [packed] + [links.turn(packed, step) for step in steps]
+    links.label = "o_ctx"
+    o_got = [o_weight] + [links.turn(o_weight, step) for step in steps]
+
+    mine, other = split_hidden(
+        links, place, (gate_weight, up_weight, jnp.transpose(down_weight))
+    )
+    links.label = "ff_core"
+    qkv_got, o_got, (mine, got) = phase(qkv_got, o_got, (mine, links.core(other)))
+
+    def for_ctx(step):
+        target = (ctx + step) % ctx_size
+        a, b = pick(mine, target), pick(got, target)
+        return jnp.stack([jnp.where(even, a, b), jnp.where(even, b, a)])
+
+    qkv_mine = by_ctx(links, ctx, qkv_got)
+    o_mine = by_ctx(links, ctx, o_got)
+    own_piece = for_ctx(0)
+    links.label = "qkv_plane1"
+    qkv_stage = plane_start(links, qkv_mine)
+    links.label = "ff_own1"
+    own_stage = plane_start(links, own_piece)
+    links.label = "ff_ctx_a"
+    moved = {step: links.turn(for_ctx(step), step) for step in (1, ctx_size - 1)}
+    far = {step: for_ctx(step) for step in range(2, ctx_size - 1)}
+    qkv_stage, own_stage, near, far_list, (o_mine,) = phase(
+        qkv_stage, own_stage, moved.values(), far.values(), (o_mine,)
+    )
+    moved = dict(zip(moved, near))
+    links.label = "ff_ctx_b"
+    for step, piece in zip(far, far_list):
+        moved[step] = links.turn(piece, step)
+    links.label = "qkv_plane2"
+    qkv_parts = plane_end(links, qkv_mine, *qkv_stage)
+    links.label = "ff_own2"
+    own_parts = plane_end(links, own_piece, *own_stage)
+    links.label = "o_plane1"
+    o_stage = plane_start(links, o_mine)
+    moved_list, qkv_late, own_late, o_stage = phase(
+        [moved[step] for step in steps], qkv_parts[3:], own_parts[3:], o_stage
+    )
+    own_parts = (*own_parts[:3], *own_late)
+    links.label = "qkv_core"
+    weight_qkv = rows_of_plane(links, *qkv_parts[:3], *qkv_late)
+    links.label = "o_plane2"
+    o_parts = plane_end(links, o_mine, *o_stage)
+    links.label = "o_core"
+    weight_o = rows_of_plane(links, *o_parts)
+    links.label = "ff_plane1"
+    moved_piece = jnp.concatenate(moved_list)
+    moved_stage = plane_start(links, moved_piece)
+
+    low_tokens, out_low = tokens[0], cotangent[0]
+    cosine, sine = (x[:, 0] for x in angle_tables(positions[0]))
+    cosine = jnp.concatenate([cosine, cosine], axis=1)
+    sine = jnp.concatenate([-sine, sine], axis=1)
+    place_column = positions[0][:, None]
+    wide, narrow = (count, width), (count, 2 * KV_WIDTH)
+
+    def qkv(*refs):
+        qkv_body(shard_rows, *refs)
+
+    normed_one, query, pairs, small = call(
+        qkv,
+        place,
+        (low_tokens, cosine, sine),
+        weight_qkv,
+        [(wide, BF16), (wide, BF16), (narrow, BF16), ((8, width), F32)],
+        0,
+    )
+    links.label = "kv"
+    blocks = [pairs] + [links.shift(pairs, step) for step in steps]
+    mixed_low, hidden_one, normed_two = call(
+        mix_body,
+        place,
+        (low_tokens, small, place_column, query, *blocks),
+        weight_o,
+        [(wide, BF16), (wide, F32), (wide, BF16)],
+        0,
+    )
+
+    out_row = lax.all_gather(after(out_low, *moved_list), "ctx", axis=0, tiled=True)
+    normed_row = lax.all_gather(normed_two, "ctx", axis=0, tiled=True)
+    links.label = "gy_core"
+    out_other = links.core(out_row)
+    links.label = "ff_plane2"
+    moved_parts = plane_end(links, moved_piece, *moved_stage)
+    layout = [
+        *laid_out([(0, 0), (0, 1)], *own_parts),
+        *laid_out([(step, core) for step in steps for core in range(2)], *moved_parts),
+    ]
+    links.label = "n2_core"
+    normed_other = links.core(after(normed_row, *moved_parts[3:]))
+    act_a, gate_a, up_a, down_a, y_a = feed_forward(links, layout, place, normed_row, out_row)
+    act_b, gate_b, up_b, down_b, y_b = feed_forward(links, layout, place, normed_other, out_other)
+    links.label = "gn2_core"
+    down_got = links.core(down_b)
+    grad_normed_two = lax.psum_scatter(
+        added(down_a, down_got), "ctx", scatter_dimension=0, tiled=True
+    )
+
+    ff_terms = ff_grad_terms(
+        place,
+        (after(normed_row, down_got), normed_other, out_row, out_other),
+        (gate_a, gate_b, up_a, up_b, act_a, act_b),
+    )
+    links.label = "ff_sum1"
+    ff_first = reduce_start(links, ff_terms)
+    grad_normed_two = after(grad_normed_two, ff_terms[0])
+
+    def mix_back(*refs):
+        mix_back_body(1, *refs)
+
+    grad_hidden, grad_hidden_low, grad_query, gain_two, *pair_terms = call(
+        mix_back,
+        place,
+        (grad_normed_two, hidden_one, small, out_low, place_column, query, cosine, sine, *blocks),
+        weight_o,
+        [(wide, F32), (wide, BF16), (wide, BF16), ((1, width), F32)] + [(narrow, BF16)] * ctx_size,
+        BACK_COST,
+    )
+    links.label = "y_core"
+    both_rows = lax.all_gather(
+        after(jnp.concatenate([normed_one, mixed_low], axis=1), grad_normed_two),
+        "ctx",
+        axis=0,
+        tiled=True,
+    )
+    y_both = after(added(y_a, links.core(y_b)), both_rows)
+    y_sum = lax.psum_scatter(y_both, "ctx", scatter_dimension=0, tiled=True)
+    layer_out = hidden_one + y_sum.astype(F32)
+    links.label = "gkv"
+    pair_terms = [pair_terms[0]] + [links.shift(pair_terms[step], -step) for step in steps]
+    def columns_over_ctx(parts):
+        whole = jnp.zeros_like(parts)
+        whole = lax.dynamic_update_index_in_dim(whole, pick(parts, ctx), ctx, 0)
+        for step in steps:
+            piece = links.turn(pick(parts, (ctx + step) % ctx_size), step)
+            whole = lax.dynamic_update_index_in_dim(whole, piece, (ctx - step) % ctx_size, 0)
+        return whole
+
+    def qkv_back(*refs):
+        qkv_back_body(ctx_size, *refs)
+
+    columns = (width + 2 * KV_WIDTH) // ctx_size
+    grad_stream, parts = call(
+        qkv_back,
+        place,
+        (*pair_terms, low_tokens, small, cosine, sine, grad_query, grad_hidden, grad_hidden_low, gain_two),
+        weight_qkv,
+        [(wide, F32), ((ctx_size, count + 16, columns + width // ctx_size), BF16)],
+        0,
+    )
+
+
+    links.label = "gqkv_ctx"
+    share = after(columns_over_ctx(parts), *ff_first)
+    links.label = "ff_sum2"
+    ff_second = reduce_next(links, ff_terms, ff_first)
+    gain_sums = jnp.sum(share[:, count:].astype(F32), axis=0)[:2]
+    share = share[:, :count].reshape(ctx_size * count, -1)
+    share_o, share = share[:, columns:], share[:, :columns]
+    bias_sums = jnp.sum(share.astype(F32), axis=0)
+    q_columns, kv_columns = width // ctx_size, KV_WIDTH // ctx_size
+    bounds = (0, q_columns, q_columns + kv_columns, columns)
+    sums = [gain_sums[0, :q_columns], gain_sums[1, :q_columns]]
+    sums += [bias_sums[i:j] for i, j in zip(bounds, bounds[1:])]
+    sums = jnp.concatenate([x.reshape(fsdp_size, -1) for x in sums], axis=1)
+    sums = jnp.pad(sums, ((0, 0), (0, columns - sums.shape[1])))
+    sums = jnp.pad(sums[:, None], ((0, 0), (0, 15), (0, 0)))
+    term = tn(both_rows[:, :width], share).reshape(fsdp_size, -1, columns)
+    term = jnp.concatenate([term, sums], axis=1).astype(BF16)
+    term_o = tn(both_rows[:, width:], share_o).astype(BF16).reshape(fsdp_size, -1, q_columns)
+    term_o = jnp.pad(term_o, ((0, 0), (0, 16), (0, 0)))
+    term = jnp.concatenate([term, term_o], axis=2)
+    term = jnp.transpose(term.reshape(fsdp_size // 2, 2, *term.shape[1:]), (1, 0, 2, 3))
+    links.label = "term_core"
+    term = added(pick(term, core), links.core(pick(term, 1 - core)))
+    links.label = "term_plane"
+    total = pick(term, chip).astype(F32)
+    for mask in range(1, fsdp_size // 2):
+        total = total + links.plane(pick(term, chip ^ mask), 2 * mask).astype(F32)
+    grad_packed, grad_o, sums = total[:-16, :columns], total[:-16, columns:], total[-16]
+    vectors = []
+    start = 0
+    for size in (width, width, width, KV_WIDTH, KV_WIDTH):
+        part = size // (ctx_size * fsdp_size)
+        vectors.append(sums[start : start + part])
+        start += part
+
+    links.label = "final_core"
+    links.label = "final_core"
+    low, high = reduce_end(ff_terms, ff_first, ff_second)
+    mine = jnp.where(even, low, high)
+    got = links.core(jnp.where(even, high, low).astype(BF16)).astype(F32)
+    ff_grads = jnp.concatenate([jnp.where(even, mine, got), jnp.where(even, got, mine)], axis=2)
+    grad_gate, grad_up, grad_down = ff_grads[0], ff_grads[1], jnp.transpose(ff_grads[2])
+
+    return (
+        layer_out[None],
+        grad_stream[None],
+        vectors[0],
+        grad_packed[:, :q_columns],
+        vectors[2],
+        grad_packed[:, q_columns : q_columns + kv_columns],
+        vectors[3],
+        grad_packed[:, q_columns + kv_columns :],
+        vectors[4],
+        grad_o,
+        vectors[1],
+        grad_gate,
+        grad_up,
+        grad_down,
+    )
+
+
 def solution(mesh):
     links = Links(mesh.shape["ctx"], mesh.shape["fsdp"])
     vector, matrix, stream = P(BOTH), P(BOTH, None), P("fsdp", "ctx", None)
@@ -386,6 +1110,8 @@
     )
 
     def run(*arrays):
-        return per_device(*arrays, links=links)
+        plane_of_four = mesh.shape["fsdp"] == 8 and arrays[3].shape[0] % 16 == 0
+        form = per_device_plane_of_four if plane_of_four else per_device_any_mesh
+        return form(*arrays, links=links)
 
     return jax.shard_map(run, mesh=mesh, in_specs=in_specs, out_specs=out_specs, check_vma=False)

time: 729 us -> 476 us (0.65)
  matrix products: 104 us -> 3.66 us
  Pallas kernels: 0 us -> 93.6 us
  waiting for transfers between devices: 301 us -> 230 us
  local copies, waits for them, and re-layouts: 94.5 us -> 27.2 us
  starting transfers between devices: 114 us -> 61.7 us
  blocking collectives: 49.2 us -> 0 us
    pallas_call x0 -> x8, Pallas kernels: none -> 93.6 us  [the longest x2 37.5 us: feed_forward(): pl.pallas_call(body, grid_spec=pltpu.PrefetchScalarGridSpec(num_scalar_pr...]
    dot_general x15 -> x2, matrix products: 94.6 us -> 3.66 us  [dot(): lax.dot_general(a, b, ((dims[:1], dims[1:]), ((), ())), preferred_element...]
    reduce_scatter x5 -> x2, waiting for transfers between devices: 79.9 us -> 11.5 us  [the longest x1 5.92 us: per_device_plane_of_four(): y_sum = lax.psum_scatter(y_both, 'ctx', scatter_dimension=0, tiled=True)]
    ppermute x55 -> x52, starting transfers between devices: 113 us -> 61.1 us  [send(): return lax.ppermute(x, BOTH, pairs)]
    psum x1 -> x0, blocking collectives: 49.2 us -> none  [per_device(): sums = lax.psum(sums, BOTH)]
    unnamed x97 -> x105, local copies, waits for them, and re-layouts: 29.6 us -> 11.1 us
    convert_element_type x9 -> x6, other arithmetic: 5.5 us -> 18 us  [the longest x5 13 us: added(): return (a.astype(F32) + b.astype(F32)).astype(BF16)]
    another operation x15 -> x2, local copies, waits for them, and re-layouts: 11.8 us -> 0.17 us  [per_device_plane_of_four(): sums = jnp.concatenate([x.reshape(fsdp_size, -1) for x in sums], axis=1)]
  transfers between devices with their start and end apart: 64 -> 57, of which waited for: 28 -> 31; matrix products, arithmetic and copies ran while one was open for 27% -> 12% of each run, Pallas kernels for 0% -> 16%
where the time goes in v2:
time: 476 us; the launch traced here: 467 us
  waiting for transfers between devices  230 us (48%)
  Pallas kernels  93.6 us (20%)
  starting transfers between devices  61.7 us (13%)
  other arithmetic  35.9 us (8%)
  local copies, waits for them, and re-layouts  27.2 us (6%)
  between operations  15.2 us (3%)
    ppermute x52, waiting for transfers between devices, send(): return lax.ppermute(x, BOTH, pairs)  216 us
    ppermute x52, starting transfers between devices, send(): return lax.ppermute(x, BOTH, pairs)  61.1 us
    pallas_call x2, Pallas kernels, feed_forward(): pl.pallas_call(body, grid_spec=pltpu.PrefetchScalarGridSpec(num_scalar_pr...  37.5 us
    pallas_call x4, Pallas kernels, call(): pl.pallas_call(kernel, in_specs=[pl.BlockSpec(memory_space=pltpu.SMEM)] +...  30.4 us
    pallas_call x1, Pallas kernels, ff_grad_terms(): pl.pallas_call(grad_kernel, grid_spec=pltpu.PrefetchScalarGridSpec(num_sc...  24.5 us
    convert_element_type x5, other arithmetic, added(): return (a.astype(F32) + b.astype(F32)).astype(BF16)  13 us
    unnamed x105, local copies, waits for them, and re-layouts  11.1 us
  transfers between devices with their start and end apart: 57, of which 31 were waited for; matrix products, arithmetic and copies ran while one was open for 12% of the time, Pallas kernels for 16%

profile of v2, /device:TPU:0, one launch (start us, length us, event | category | flops | bytes accessed | tf_op | source)
XLA Modules:
  0.0 467.4 jit_solution(16305060530860746118)
XLA Ops:
  12.6 2.6 collective-permute-start.3
  15.2 2.6 collective-permute-start.4
  18.2 1.8 collective-permute-start.1
  20.0 2.4 collective-permute-done.3
  22.4 2.1 collective-permute-start.2
  24.5 13.0 %collective-permute-done.4 = bf16[48,1536]{1,0:T(8,128)(2,1)} collective-permute-done((bf16[48,1536]{1,0:T(8,128)(2,1)}, bf16[48,1536]{1,0:T(8,128)(2,1)}, u32[]{:S(2)}, u32[]{:S(2)}) %collective-permute-start.4) | collective-permute-done | bytes 147488 | tf_op jit(solution)/shard_map/o_ctx/ppermute | solution.py:73
  37.4 7.6 %collective-permute-done.5 = bf16[48,1536]{1,0:T(8,128)(2,1)} collective-permute-done((bf16[48,1536]{1,0:T(8,128)(2,1)}, bf16[48,1536]{1,0:T(8,128)(2,1)}, u32[]{:S(2)}, u32[]{:S(2)}) %collective-permute-start.5) | collective-permute-done | bytes 147488 | tf_op jit(solution)/shard_map/o_ctx/ppermute | solution.py:73
  45.2 1.6 collective-permute-start.7
  46.8 1.5 collective-permute-start.8
  48.3 1.5 broadcast_select_fusion.1
  51.2 5.1 %collective-permute-start.11 = (bf16[2,3,48,1120]{3,2,1,0:T(8,128)(2,1)S(1)}, bf16[2,3,48,1120]{3,2,1,0:T(8,128)(2,1)S(1)}, u32[]{:S(2)}, u32[]{:S(2)}) collective-permute-start(bf16[2,3,48,1120]{3,2,1,0:T(8,128)(2,1)S(1)} %pad_maximum_fusion.6), channel_id=1, source_target_pairs={{0,8},{1,9},{2,10},{3,11},{4,12},{5,13},{6,14},{7,15},{8,16},{9,17... | collective-permute-start | bytes 1935368 | tf_op jit(solution)/shard_map/ff_ctx_a/ppermute | solution.py:73
  59.2 20.8 %collective-permute-done.9.refs_4_ = bf16[2,3,48,1120]{3,2,1,0:T(8,128)(2,1)S(1)} collective-permute-done((bf16[2,3,48,1120]{3,2,1,0:T(8,128)(2,1)S(1)}, bf16[2,3,48,1120]{3,2,1,0:T(8,128)(2,1)S(1)}, u32[]{:S(2)}, u32[]{:S(2)}) %collective-permute-start.9) | collective-permute-done | bytes 645152 | tf_op jit(solution)/shard_map/ff_own1/ppermute | solution.py:73
  80.0 5.6 %collective-permute-start.12 = (bf16[2,3,48,1120]{3,2,1,0:T(8,128)(2,1)S(1)}, bf16[2,3,48,1120]{3,2,1,0:T(8,128)(2,1)S(1)}, u32[]{:S(2)}, u32[]{:S(2)}) collective-permute-start(bf16[2,3,48,1120]{3,2,1,0:T(8,128)(2,1)S(1)} %pad_maximum_fusion.7), channel_id=1, source_target_pairs={{0,24},{1,25},{2,26},{3,27},{4,28},{5,29},{6,30},{7,31},{8,0},{9,1... | collective-permute-start | bytes 1935368 | tf_op jit(solution)/shard_map/ff_ctx_a/ppermute | solution.py:73
  86.7 12.6 %collective-permute-done.12 = bf16[2,3,48,1120]{3,2,1,0:T(8,128)(2,1)S(1)} collective-permute-done((bf16[2,3,48,1120]{3,2,1,0:T(8,128)(2,1)S(1)}, bf16[2,3,48,1120]{3,2,1,0:T(8,128)(2,1)S(1)}, u32[]{:S(2)}, u32[]{:S(2)}) %collective-permute-start.12) | collective-permute-done | bytes 645152 | tf_op jit(solution)/shard_map/ff_ctx_a/ppermute | solution.py:73
  99.4 1.6 collective-permute-start.16
  101.0 1.6 collective-permute-start.17
  104.4 5.8 %collective-permute-done.16.refs_6_ = bf16[1,3,48,1120]{3,2,1,0:T(8,128)(2,1)S(1)} collective-permute-done((bf16[1,3,48,1120]{3,2,1,0:T(8,128)(2,1)S(1)}, bf16[1,3,48,1120]{3,2,1,0:T(8,128)(2,1)S(1)}, u32[]{:S(2)}, u32[]{:S(2)}) %collective-permute-start.16) | collective-permute-done | bytes 322592 | tf_op jit(solution)/shard_map/ff_own2/ppermute | solution.py:73
  110.2 1.5 collective-permute-start.14
  111.9 1.5 collective-permute-start.15
  113.4 1.8 pad_maximum_fusion
  115.2 14.1 %collective-permute-done.14.refs_6_.refs_15_ = bf16[2,48,2176]{2,1,0:T(8,128)(2,1)S(1)} collective-permute-done((bf16[2,48,2176]{2,1,0:T(8,128)(2,1)S(1)}, bf16[2,48,2176]{2,1,0:T(8,128)(2,1)S(1)}, u32[]{:S(2)}, u32[]{:S(2)}) %collective-permute-start.14) | collective-permute-done | bytes 417824 | tf_op jit(solution)/shard_map/qkv_plane2/ppermute | solution.py:73
  130.7 2.0 collective-permute-done.13
  135.7 2.0 constant_dynamic-update-slice_fusion.1
  137.7 5.0 %collective-permute-done.25.refs_11_.refs_15_ = bf16[2,48,1536]{2,1,0:T(8,128)(2,1)S(1)} collective-permute-done((bf16[2,48,1536]{2,1,0:T(8,128)(2,1)S(1)}, bf16[2,48,1536]{2,1,0:T(8,128)(2,1)S(1)}, u32[]{:S(2)}, u32[]{:S(2)}) %collective-permute-start.25) | collective-permute-done | bytes 294944 | tf_op jit(solution)/shard_map/o_plane2/ppermute | solution.py:73
  144.6 1.5 collective-permute-start.29
  147.2 6.1 %shard_map.255 = (bf16[128,1536]{1,0:T(8,128)(2,1)}, bf16[128,1536]{1,0:T(8,128)(2,1)}, bf16[128,512]{1,0:T(8,128)(2,1)}, f32[8,1536]{1,0:T(8,128)}) custom-call(s32[3]{0:T(128)} %copy-done.3, bf16[128,1536]{1,0:T(8,128)(2,1)} %bitcast.125, f32[128,128]{1,0:T(8,128)} %get-tuple-element.226.refs_1_.refs_6_, f32[128,128]{1,0:T(8,128)} %get-tuple-element.227.refs_2_.refs_7_, ...), custom_call_target="tpu_custom_call" | custom-call | tf_op jit(solution)/shard_map/pallas_call | solution.py:635
  153.3 3.0 collective-permute-start.22
  156.3 3.9 collective-permute-start.23
  163.2 5.6 %collective-permute-done.23.refs_6_.refs_10_ = bf16[128,512]{1,0:T(8,128)(2,1)S(1)} collective-permute-done((bf16[128,512]{1,0:T(8,128)(2,1)}, bf16[128,512]{1,0:T(8,128)(2,1)S(1)}, u32[]{:S(2)}, u32[]{:S(2)}) %collective-permute-start.23) | collective-permute-done | bytes 131104 | tf_op jit(solution)/shard_map/kv/ppermute | solution.py:73
  168.8 3.6 collective-permute-done.24.refs_7_.refs_11_
  173.1 5.7 %shard_map.256 = (bf16[128,1536]{1,0:T(8,128)(2,1)}, f32[128,1536]{1,0:T(8,128)}, bf16[128,1536]{1,0:T(8,128)(2,1)}) custom-call(s32[3]{0:T(128)} %copy-done.3, bf16[128,1536]{1,0:T(8,128)(2,1)} %bitcast.126, f32[8,1536]{1,0:T(8,128)} %get-tuple-element.103.refs_1_.refs_2_.refs_5_, s32[128,1]{1,0:T(8,128)} %copy.49.refs_2_.refs_4_, ...), custom_call_target="tpu_custom_call" | custom-call | tf_op jit(solution)/shard_map/pallas_call | solution.py:635
  179.1 10.9 %collective-permute-done.30.refs_10_ = bf16[6,3,48,1120]{3,2,1,0:T(8,128)(2,1)S(1)} collective-permute-done((bf16[6,3,48,1120]{3,2,1,0:T(8,128)(2,1)}, bf16[6,3,48,1120]{3,2,1,0:T(8,128)(2,1)S(1)}, u32[]{:S(2)}, u32[]{:S(2)}) %collective-permute-start.30) | collective-permute-done | bytes 1935392 | tf_op jit(solution)/shard_map/ff_plane1/ppermute | solution.py:73
  192.6 2.2 slice.211
  195.4 19.7 %collective-permute-done.31.refs_11_ = bf16[3,3,48,1120]{3,2,1,0:T(8,128)(2,1)S(1)} collective-permute-done((bf16[3,3,48,1120]{3,2,1,0:T(8,128)(2,1)}, bf16[3,3,48,1120]{3,2,1,0:T(8,128)(2,1)S(1)}, u32[]{:S(2)}, u32[]{:S(2)}) %collective-permute-start.31) | collective-permute-done | bytes 967712 | tf_op jit(solution)/shard_map/ff_plane2/ppermute | solution.py:73
  215.1 3.6 collective-permute-done.32.refs_12_
  218.7 2.3 all-gather.4.cloned.1.call-done.refs_1_.refs_0_
  221.0 3.6 collective-permute-done.33.refs_1_
  225.7 18.7 %shard_map.258 = (bf16[512,1120]{1,0:T(8,128)(2,1)}, bf16[512,1120]{1,0:T(8,128)(2,1)}, bf16[512,1120]{1,0:T(8,128)(2,1)}, bf16[512,1536]{1,0:T(8,128)(2,1)}, bf16[512,1536]{1,0:T(8,128)(2,1)}) custom-call(s32[3]{0:T(128)} %copy-done.3, bf16[512,1536]{1,0:T(8,128)(2,1)} %copy-done.8, bf16[512,1536]{1,0:T(8,128)(2,1)} %collective-permute-done.34.refs_2_.refs_3_, ...), custom_call_target="tpu_custom_call" | custom-call | tf_op jit(solution)/shard_map/pallas_call | solution.py:446
  244.7 18.8 %shard_map.257 = (bf16[512,1120]{1,0:T(8,128)(2,1)}, bf16[512,1120]{1,0:T(8,128)(2,1)}, bf16[512,1120]{1,0:T(8,128)(2,1)}, bf16[512,1536]{1,0:T(8,128)(2,1)}, bf16[512,1536]{1,0:T(8,128)(2,1)}) custom-call(s32[3]{0:T(128)} %copy-done.3, bf16[512,1536]{1,0:T(8,128)(2,1)} %all-gather.4.cloned.1.call-done.refs_1_.refs_0_, ...), custom_call_target="tpu_custom_call" | custom-call | tf_op jit(solution)/shard_map/pallas_call | solution.py:446
  263.5 2.9 add_convert_fusion
  266.7 24.5 %shard_map.259 = (bf16[2,3,192,1120]{3,2,1,0:T(8,128)(2,1)}, bf16[2,3,192,1120]{3,2,1,0:T(8,128)(2,1)}, bf16[2,3,192,1120]{3,2,1,0:T(8,128)(2,1)}, bf16[2,3,192,1120]{3,2,1,0:T(8,128)(2,1)}) custom-call(s32[3]{0:T(128)} %copy-done.3, bf16[512,1536]{1,0:T(8,128)(2,1)} %all-gather.4.cloned.1.call-done.refs_1_.refs_0_, bf16[512,1536]{1,0:T(8,128)(2,1)} %copy-done.8, ...), custom_call_target="tpu_custom_call" | custom-call | tf_op jit(solution)/shard_map/pallas_call | solution.py:502
  291.2 1.5 collective-permute-start.43
  295.2 5.6 %reduce-scatter.3.cloned.1.call-done.refs_0_ = bf16[128,1536]{1,0:T(8,128)(2,1)} async-done(((bf16[512,1536]{1,0:T(8,128)(2,1)}), bf16[128,1536]{1,0:T(8,128)(2,1)}) %reduce-scatter.3.cloned.1.call-update) | async-done | bytes 393232 | tf_op jit(solution)/shard_map/reduce_scatter | solution.py:955
  301.0 10.2 %shard_map.260 = (f32[128,1536]{1,0:T(8,128)}, bf16[128,1536]{1,0:T(8,128)(2,1)}, bf16[128,1536]{1,0:T(8,128)(2,1)}, f32[1,1536]{1,0:T(1,128)}, bf16[128,512]{1,...) custom-call(s32[3]{0:T(128)} %copy-done.3, ...), custom_call_target="tpu_custom_call" | custom-call | flops 8000000000 | tf_op jit(solution)/shard_map/pallas_call | solution.py:635
  313.8 37.6 %collective-permute-done.43 = bf16[2,3,192,1120]{3,2,1,0:T(8,128)(2,1)} collective-permute-done((bf16[2,3,192,1120]{3,2,1,0:T(8,128)(2,1)}, bf16[2,3,192,1120]{3,2,1,0:T(8,128)(2,1)}, u32[]{:S(2)}, u32[]{:S(2)}) %collective-permute-start.43) | collective-permute-done | bytes 2580512 | tf_op jit(solution)/shard_map/ff_sum1/ppermute | solution.py:73
  352.7 2.7 fusion.15
  356.9 7.1 %collective-permute-done.39.refs_3_ = bf16[128,512]{1,0:T(8,128)(2,1)S(1)} collective-permute-done((bf16[128,512]{1,0:T(8,128)(2,1)}, bf16[128,512]{1,0:T(8,128)(2,1)S(1)}, u32[]{:S(2)}, u32[]{:S(2)}) %collective-permute-start.39) | collective-permute-done | bytes 131104 | tf_op jit(solution)/shard_map/gkv/ppermute | solution.py:73
  364.6 8.4 %shard_map.261 = (f32[128,1536]{1,0:T(8,128)}, bf16[4,144,896]{2,1,0:T(8,128)(2,1)}) custom-call(s32[3]{0:T(128)} %copy-done.3, bf16[128,512]{1,0:T(8,128)(2,1)} %get-tuple-element.134.refs_0_, bf16[128,512]{1,0:T(8,128)(2,1)} %copy-done.35, bf16[128,512]{1,0:T(8,128)(2,1)} %copy-done.36, bf16[128,512]{1,0:T(8,128)(2,1)} %copy-done.37, ...), custom_call_target="tpu_custom_call" | custom-call | tf_op jit(solution)/shard_map/pallas_call | solution.py:635
  373.1 1.6 dynamic-slice_bitcast_fusion.4
  375.3 2.7 fusion.16
  379.4 6.4 %collective-permute-done.40 = bf16[144,896]{1,0:T(8,128)(2,1)S(1)} collective-permute-done((bf16[144,896]{1,0:T(8,128)(2,1)S(1)}, bf16[144,896]{1,0:T(8,128)(2,1)S(1)}, u32[]{:S(2)}, u32[]{:S(2)}) %collective-permute-start.40) | collective-permute-done | bytes 258080 | tf_op jit(solution)/shard_map/gqkv_ctx/ppermute | solution.py:73
  386.1 8.6 %collective-permute-done.41 = bf16[144,896]{1,0:T(8,128)(2,1)S(1)} collective-permute-done((bf16[144,896]{1,0:T(8,128)(2,1)S(1)}, bf16[144,896]{1,0:T(8,128)(2,1)S(1)}, u32[]{:S(2)}, u32[]{:S(2)}) %collective-permute-start.41) | collective-permute-done | bytes 258080 | tf_op jit(solution)/shard_map/gqkv_ctx/ppermute | solution.py:73
  398.5 9.5 %collective-permute-done.50 = bf16[3,192,1120]{2,1,0:T(8,128)(2,1)} collective-permute-done((bf16[3,192,1120]{2,1,0:T(8,128)(2,1)}, bf16[3,192,1120]{2,1,0:T(8,128)(2,1)}, u32[]{:S(2)}, u32[]{:S(2)}) %collective-permute-start.50) | collective-permute-done | bytes 1290272 | tf_op jit(solution)/shard_map/ff_sum2/ppermute | solution.py:73
  408.0 5.0 %select_convert_fusion = bf16[3,192,1120]{2,1,0:T(8,128)(2,1)} fusion(bf16[3,192,1120]{2,1,0:T(8,128)(2,1)} %collective-permute-done.49, bf16[3,192,1120]{2,1,0:T(8,128)(2,1)} %collective-permute-done.50, pred[]{:T(512)S(6)} %eq.23, bf16[2,3,192,1120]{3,2,1,0:T(8,128)(2,1)} %collective-permute-done.44, bf16[2,3,192,1120]{3,2,1,0:T(8,128)(2,1)} %collective-permute-done.43, ...), kind=kLoop, calls=%fused_computation.23 | loop fusion | flops 7741440 | bytes 9031681 | tf_op jit(solution)/shard_map/convert_element_type | solution.py:1052
  413.0 2.6 convolution_convert_fusion.1
  419.0 2.9 add_convert_fusion.1
  422.0 4.9 %convert_select_fusion = (f32[3,192,1120]{2,1,0:T(8,128)S(1)}, f32[3,192,1120]{2,1,0:T(8,128)S(1)}) fusion(bf16[3,192,1120]{2,1,0:T(8,128)(2,1)} %collective-permute-done.51, pred[]{:T(512)S(6)} %eq.23, bf16[3,192,1120]{2,1,0:T(8,128)(2,1)} %collective-permute-done.50, bf16[2,3,192,1120]{3,2,1,0:T(8,128)(2,1)} %collective-permute-done.44, ...), kind=kLoop, calls=%fused_computation.11 | loop fusion | flops 9031680 | bytes 14192641 | tf_op jit(solution)/shard_map/jit(_where)/select_n | solution.py:1053
  426.9 1.7 fusion.6
  428.8 2.4 collective-permute-start.48
  432.3 3.2 fusion.11
  435.5 5.7 %collective-permute-done.48 = bf16[208,896]{1,0:T(8,128)(2,1)S(1)} collective-permute-done((bf16[208,896]{1,0:T(8,128)(2,1)S(1)}, bf16[208,896]{1,0:T(8,128)(2,1)S(1)}, u32[]{:S(2)}, u32[]{:S(2)}) %collective-permute-start.48) | collective-permute-done | bytes 372768 | tf_op jit(solution)/shard_map/term_plane/ppermute | solution.py:73
  441.3 7.5 %collective-permute-done.47 = bf16[208,896]{1,0:T(8,128)(2,1)S(1)} collective-permute-done((bf16[208,896]{1,0:T(8,128)(2,1)S(1)}, bf16[208,896]{1,0:T(8,128)(2,1)S(1)}, u32[]{:S(2)}, u32[]{:S(2)}) %collective-permute-start.47) | collective-permute-done | bytes 372768 | tf_op jit(solution)/shard_map/term_plane/ppermute | solution.py:73
  452.5 5.9 %reduce-scatter.5.cloned.1.call-done = bf16[128,1536]{1,0:T(8,128)(2,1)} async-done(((bf16[512,1536]{1,0:T(8,128)(2,1)}), bf16[128,1536]{1,0:T(8,128)(2,1)}) %reduce-scatter.5.cloned.1.call-update) | async-done | bytes 393232 | tf_op jit(solution)/shard_map/reduce_scatter | solution.py:987
  458.5 2.0 add_bitcast_fusion
  (243 shorter events, 52.1 us)
Async XLA Ops:
  7.3 188.1 %all-gather.6.cloned.1.call-start = ((), (), s32[]{:S(2)}) async-start(), calls=%async_computation.3 | async-start | bytes 1966080 | tf_op jit(solution)/shard_map/all_gather | solution.py:939
  7.4 37.7 %copy-start.3 = (s32[3]{0:T(128)}, s32[3]{0:T(128)S(1)}, u32[]{:S(2)}) copy-start(s32[3]{0:T(128)S(1)} %pad_add_fusion.place.refs_0_) | copy-start | bytes 40
  12.1 32.9 %collective-permute-start.6 = (bf16[4,3,48,1120]{3,2,1,0:T(8,128)(2,1)S(1)}, bf16[4,3,48,1120]{3,2,1,0:T(8,128)(2,1)}, u32[]{:S(2)}, u32[]{:S(2)}) collective-permute-start(bf16[4,3,48,1120]{3,2,1,0:T(8,128)(2,1)S(1)} %get-tuple-element.82), channel_id=1, source_target_pairs={{0,1},{1,0},{2,3},{3,2},{4,5},{5,4},{6,7},{7,6},{8,9},{9,8},{10,11... | collective-permute-start | bytes 3870728 | tf_op jit(solution)/shard_map/ff_core/ppermute | solution.py:73
  12.6 9.8 %collective-permute-start.3 = (bf16[48,1536]{1,0:T(8,128)(2,1)}, bf16[48,1536]{1,0:T(8,128)(2,1)}, u32[]{:S(2)}, u32[]{:S(2)}) collective-permute-start(bf16[48,1536]{1,0:T(8,128)(2,1)} %param.24), channel_id=1, source_target_pairs={{0,8},{1,9},{2,10},{3,11},{4,12},{5,13},{6,14},{7,15},{8,16},{9,17... | collective-permute-start | bytes 442376 | tf_op jit(solution)/shard_map/o_ctx/ppermute | solution.py:73
  15.2 22.2 %collective-permute-start.4 = (bf16[48,1536]{1,0:T(8,128)(2,1)}, bf16[48,1536]{1,0:T(8,128)(2,1)}, u32[]{:S(2)}, u32[]{:S(2)}) collective-permute-start(bf16[48,1536]{1,0:T(8,128)(2,1)} %param.24), channel_id=1, source_target_pairs={{0,16},{1,17},{2,18},{3,19},{4,20},{5,21},{6,22},{7,23},{8,24},{9,... | collective-permute-start | bytes 442376 | tf_op jit(solution)/shard_map/o_ctx/ppermute | solution.py:73
  18.1 26.9 %collective-permute-start = (bf16[48,2176]{1,0:T(8,128)(2,1)S(1)}, bf16[48,2176]{1,0:T(8,128)(2,1)S(1)}, u32[]{:S(2)}, u32[]{:S(2)}) collective-permute-start(bf16[48,2176]{1,0:T(8,128)(2,1)S(1)} %fusion.22), channel_id=1, source_target_pairs={{0,8},{1,9},{2,10},{3,11},{4,12},{5,13},{6,14},{7,15},{8,16},{9,17... | collective-permute-start | bytes 626696 | tf_op jit(solution)/shard_map/qkv_ctx/ppermute | solution.py:73
  18.2 26.8 %collective-permute-start.1 = (bf16[48,2176]{1,0:T(8,128)(2,1)S(1)}, bf16[48,2176]{1,0:T(8,128)(2,1)S(1)}, u32[]{:S(2)}, u32[]{:S(2)}) collective-permute-start(bf16[48,2176]{1,0:T(8,128)(2,1)S(1)} %fusion.22), channel_id=1, source_target_pairs={{0,16},{1,17},{2,18},{3,19},{4,20},{5,21},{6,22},{7,23},{8,24},{9,... | collective-permute-start | bytes 626696 | tf_op jit(solution)/shard_map/qkv_ctx/ppermute | solution.py:73
  22.4 22.6 %collective-permute-start.2 = (bf16[48,2176]{1,0:T(8,128)(2,1)S(1)}, bf16[48,2176]{1,0:T(8,128)(2,1)S(1)}, u32[]{:S(2)}, u32[]{:S(2)}) collective-permute-start(bf16[48,2176]{1,0:T(8,128)(2,1)S(1)} %fusion.22), channel_id=1, source_target_pairs={{0,24},{1,25},{2,26},{3,27},{4,28},{5,29},{6,30},{7,31},{8,0},{9,1... | collective-permute-start | bytes 626696 | tf_op jit(solution)/shard_map/qkv_ctx/ppermute | solution.py:73
  37.4 7.6 %collective-permute-start.5 = (bf16[48,1536]{1,0:T(8,128)(2,1)}, bf16[48,1536]{1,0:T(8,128)(2,1)}, u32[]{:S(2)}, u32[]{:S(2)}) collective-permute-start(bf16[48,1536]{1,0:T(8,128)(2,1)} %param.24), channel_id=1, source_target_pairs={{0,24},{1,25},{2,26},{3,27},{4,28},{5,29},{6,30},{7,31},{8,0},{9,1... | collective-permute-start | bytes 442376 | tf_op jit(solution)/shard_map/o_ctx/ppermute | solution.py:73
  45.2 68.2 %copy-start.4 = (bf16[4,48,2176]{2,1,0:T(8,128)(2,1)}, bf16[4,48,2176]{2,1,0:T(8,128)(2,1)S(1)}, u32[]{:S(2)}) copy-start(bf16[4,48,2176]{2,1,0:T(8,128)(2,1)S(1)} %bitcast_dynamic-update-slice_fusion.3.refs_3_.refs_12_) | copy-start | bytes 2506756
  45.2 54.1 %collective-permute-start.7 = (bf16[4,48,2176]{2,1,0:T(8,128)(2,1)S(1)}, bf16[4,48,2176]{2,1,0:T(8,128)(2,1)S(1)}, u32[]{:S(2)}, u32[]{:S(2)}) collective-permute-start(bf16[4,48,2176]{2,1,0:T(8,128)(2,1)S(1)} %bitcast_dynamic-update-slice_fusion.3.refs_3_.refs_12_), channel_id=1, source_target_pairs={{0,2},{1,3},{2,0},{3,1},{4,6},{5,7},{6,4},{7,5},{8,10},{9,11},{10,... | collective-permute-start | bytes 2506760 | tf_op jit(solution)/shard_map/qkv_plane1/ppermute | solution.py:73
  46.8 52.6 %collective-permute-start.8 = (bf16[4,48,2176]{2,1,0:T(8,128)(2,1)S(1)}, bf16[4,48,2176]{2,1,0:T(8,128)(2,1)S(1)}, u32[]{:S(2)}, u32[]{:S(2)}) collective-permute-start(bf16[4,48,2176]{2,1,0:T(8,128)(2,1)S(1)} %bitcast_dynamic-update-slice_fusion.3.refs_3_.refs_12_), channel_id=1, source_target_pairs={{0,4},{1,5},{2,6},{3,7},{4,0},{5,1},{6,2},{7,3},{8,12},{9,13},{10,... | collective-permute-start | bytes 2506760 | tf_op jit(solution)/shard_map/qkv_plane1/ppermute | solution.py:73
  50.0 30.1 %collective-permute-start.9 = (bf16[2,3,48,1120]{3,2,1,0:T(8,128)(2,1)S(1)}, bf16[2,3,48,1120]{3,2,1,0:T(8,128)(2,1)S(1)}, u32[]{:S(2)}, u32[]{:S(2)}) collective-permute-start(bf16[2,3,48,1120]{3,2,1,0:T(8,128)(2,1)S(1)} %pad_maximum_fusion.5.refs_3_), channel_id=1, source_target_pairs={{0,2},{1,3},{2,0},{3,1},{4,6},{5,7},{6,4},{7,5},{8,10},{9,11},{10,... | collective-permute-start | bytes 1935368 | tf_op jit(solution)/shard_map/ff_own1/ppermute | solution.py:73
  50.6 36.1 %collective-permute-start.10 = (bf16[2,3,48,1120]{3,2,1,0:T(8,128)(2,1)S(1)}, bf16[2,3,48,1120]{3,2,1,0:T(8,128)(2,1)S(1)}, u32[]{:S(2)}, u32[]{:S(2)}) collective-permute-start(bf16[2,3,48,1120]{3,2,1,0:T(8,128)(2,1)S(1)} %pad_maximum_fusion.5.refs_3_), channel_id=1, source_target_pairs={{0,4},{1,5},{2,6},{3,7},{4,0},{5,1},{6,2},{7,3},{8,12},{9,13},{10,... | collective-permute-start | bytes 1935368 | tf_op jit(solution)/shard_map/ff_own1/ppermute | solution.py:73
  51.2 35.5 %collective-permute-start.11 = (bf16[2,3,48,1120]{3,2,1,0:T(8,128)(2,1)S(1)}, bf16[2,3,48,1120]{3,2,1,0:T(8,128)(2,1)S(1)}, u32[]{:S(2)}, u32[]{:S(2)}) collective-permute-start(bf16[2,3,48,1120]{3,2,1,0:T(8,128)(2,1)S(1)} %pad_maximum_fusion.6), channel_id=1, source_target_pairs={{0,8},{1,9},{2,10},{3,11},{4,12},{5,13},{6,14},{7,15},{8,16},{9,17... | collective-permute-start | bytes 1935368 | tf_op jit(solution)/shard_map/ff_ctx_a/ppermute | solution.py:73
  80.0 19.3 %collective-permute-start.12 = (bf16[2,3,48,1120]{3,2,1,0:T(8,128)(2,1)S(1)}, bf16[2,3,48,1120]{3,2,1,0:T(8,128)(2,1)S(1)}, u32[]{:S(2)}, u32[]{:S(2)}) collective-permute-start(bf16[2,3,48,1120]{3,2,1,0:T(8,128)(2,1)S(1)} %pad_maximum_fusion.7), channel_id=1, source_target_pairs={{0,24},{1,25},{2,26},{3,27},{4,28},{5,29},{6,30},{7,31},{8,0},{9,1... | collective-permute-start | bytes 1935368 | tf_op jit(solution)/shard_map/ff_ctx_a/ppermute | solution.py:73
  86.7 46.1 %copy-start.12 = (bf16[4,48,1536]{2,1,0:T(8,128)(2,1)}, bf16[4,48,1536]{2,1,0:T(8,128)(2,1)S(1)}, u32[]{:S(2)}) copy-start(bf16[4,48,1536]{2,1,0:T(8,128)(2,1)S(1)} %bitcast_dynamic-update-slice_fusion.7.refs_8_.refs_12_) | copy-start | bytes 1769476
  99.4 10.8 %collective-permute-start.16 = (bf16[1,3,48,1120]{3,2,1,0:T(8,128)(2,1)S(1)}, bf16[1,3,48,1120]{3,2,1,0:T(8,128)(2,1)S(1)}, u32[]{:S(2)}, u32[]{:S(2)}) collective-permute-start(bf16[1,3,48,1120]{3,2,1,0:T(8,128)(2,1)S(1)} %slice.168), channel_id=1, source_target_pairs={{0,2},{1,3},{2,0},{3,1},{4,6},{5,7},{6,4},{7,5},{8,10},{9,11},{10,... | collective-permute-start | bytes 967688 | tf_op jit(solution)/shard_map/ff_own2/ppermute | solution.py:73
  101.0 10.9 %collective-permute-start.17 = (bf16[1,3,48,1120]{3,2,1,0:T(8,128)(2,1)S(1)}, bf16[1,3,48,1120]{3,2,1,0:T(8,128)(2,1)}, u32[]{:S(2)}, u32[]{:S(2)}) collective-permute-start(bf16[1,3,48,1120]{3,2,1,0:T(8,128)(2,1)S(1)} %slice.169), channel_id=1, source_target_pairs={{0,4},{1,5},{2,6},{3,7},{4,0},{5,1},{6,2},{7,3},{8,12},{9,13},{10,... | collective-permute-start | bytes 967688 | tf_op jit(solution)/shard_map/ff_own2/ppermute | solution.py:73
  102.6 30.0 %collective-permute-start.13 = (bf16[2,3,48,1120]{3,2,1,0:T(8,128)(2,1)S(1)}, bf16[2,3,48,1120]{3,2,1,0:T(8,128)(2,1)}, u32[]{:S(2)}, u32[]{:S(2)}) collective-permute-start(bf16[2,3,48,1120]{3,2,1,0:T(8,128)(2,1)S(1)} %pad_maximum_fusion.8), channel_id=1, source_target_pairs={{0,16},{1,17},{2,18},{3,19},{4,20},{5,21},{6,22},{7,23},{8,24},{9,... | collective-permute-start | bytes 1935368 | tf_op jit(solution)/shard_map/ff_ctx_b/ppermute | solution.py:73
  103.3 27.3 %collective-permute-start.18 = (bf16[4,48,1536]{2,1,0:T(8,128)(2,1)S(1)}, bf16[4,48,1536]{2,1,0:T(8,128)(2,1)S(1)}, u32[]{:S(2)}, u32[]{:S(2)}) collective-permute-start(bf16[4,48,1536]{2,1,0:T(8,128)(2,1)S(1)} %bitcast_dynamic-update-slice_fusion.7.refs_8_.refs_12_), channel_id=1, source_target_pairs={{0,2},{1,3},{2,0},{3,1},{4,6},{5,7},{6,4},{7,5},{8,10},{9,11},{10,... | collective-permute-start | bytes 1769480 | tf_op jit(solution)/shard_map/o_plane1/ppermute | solution.py:73
  103.8 26.8 %collective-permute-start.19 = (bf16[4,48,1536]{2,1,0:T(8,128)(2,1)S(1)}, bf16[4,48,1536]{2,1,0:T(8,128)(2,1)S(1)}, u32[]{:S(2)}, u32[]{:S(2)}) collective-permute-start(bf16[4,48,1536]{2,1,0:T(8,128)(2,1)S(1)} %bitcast_dynamic-update-slice_fusion.7.refs_8_.refs_12_), channel_id=1, source_target_pairs={{0,4},{1,5},{2,6},{3,7},{4,0},{5,1},{6,2},{7,3},{8,12},{9,13},{10,... | collective-permute-start | bytes 1769480 | tf_op jit(solution)/shard_map/o_plane1/ppermute | solution.py:73
  110.2 19.1 %collective-permute-start.14 = (bf16[2,48,2176]{2,1,0:T(8,128)(2,1)S(1)}, bf16[2,48,2176]{2,1,0:T(8,128)(2,1)S(1)}, u32[]{:S(2)}, u32[]{:S(2)}) collective-permute-start(bf16[2,48,2176]{2,1,0:T(8,128)(2,1)S(1)} %slice.166), channel_id=1, source_target_pairs={{0,2},{1,3},{2,0},{3,1},{4,6},{5,7},{6,4},{7,5},{8,10},{9,11},{10,... | collective-permute-start | bytes 1253384 | tf_op jit(solution)/shard_map/qkv_plane2/ppermute | solution.py:73
  111.9 18.7 %collective-permute-start.15 = (bf16[2,48,2176]{2,1,0:T(8,128)(2,1)S(1)}, bf16[2,48,2176]{2,1,0:T(8,128)(2,1)S(1)}, u32[]{:S(2)}, u32[]{:S(2)}) collective-permute-start(bf16[2,48,2176]{2,1,0:T(8,128)(2,1)S(1)} %slice.167), channel_id=1, source_target_pairs={{0,4},{1,5},{2,6},{3,7},{4,0},{5,1},{6,2},{7,3},{8,12},{9,13},{10,... | collective-permute-start | bytes 1253384 | tf_op jit(solution)/shard_map/qkv_plane2/ppermute | solution.py:73
  129.3 17.8 %collective-permute-start.20 = (bf16[3,4,48,2176]{3,2,1,0:T(8,128)(2,1)}, bf16[3,4,48,2176]{3,2,1,0:T(8,128)(2,1)}, u32[]{:S(2)}, u32[]{:S(2)}) collective-permute-start(bf16[3,4,48,2176]{3,2,1,0:T(8,128)(2,1)} %pad_maximum_fusion), channel_id=1, source_target_pairs={{0,1},{1,0},{2,3},{3,2},{4,5},{5,4},{6,7},{7,6},{8,9},{9,8},{10,11... | collective-permute-start | bytes 7520264 | tf_op jit(solution)/shard_map/qkv_core/ppermute | solution.py:73
  132.6 88.3 %all-gather.4.cloned.1.call-start = ((), (), s32[]{:S(2)}) async-start(), calls=%async_computation.2 | async-start | bytes 1966080 | tf_op jit(solution)/shard_map/all_gather | solution.py:940
  133.0 27.2 %collective-permute-start.27 = (bf16[3,4,48,1536]{3,2,1,0:T(8,128)(2,1)S(1)}, bf16[3,4,48,1536]{3,2,1,0:T(8,128)(2,1)}, u32[]{:S(2)}, u32[]{:S(2)}) collective-permute-start(bf16[3,4,48,1536]{3,2,1,0:T(8,128)(2,1)S(1)} %pad_maximum_fusion.2), channel_id=1, source_target_pairs={{0,1},{1,0},{2,3},{3,2},{4,5},{5,4},{6,7},{7,6},{8,9},{9,8},{10,11... | collective-permute-start | bytes 5308424 | tf_op jit(solution)/shard_map/o_core/ppermute | solution.py:73
  133.2 11.3 %collective-permute-start.21 = (bf16[4,48,2176]{2,1,0:T(8,128)(2,1)S(1)}, bf16[4,48,2176]{2,1,0:T(8,128)(2,1)S(1)}, u32[]{:S(2)}, u32[]{:S(2)}) collective-permute-start(bf16[4,48,2176]{2,1,0:T(8,128)(2,1)S(1)} %pad_maximum_fusion.3), channel_id=1, source_target_pairs={{0,1},{1,0},{2,3},{3,2},{4,5},{5,4},{6,7},{7,6},{8,9},{9,8},{10,11... | collective-permute-start | bytes 2506760 | tf_op jit(solution)/shard_map/qkv_core/ppermute | solution.py:73
  133.8 9.0 %collective-permute-start.25 = (bf16[2,48,1536]{2,1,0:T(8,128)(2,1)S(1)}, bf16[2,48,1536]{2,1,0:T(8,128)(2,1)S(1)}, u32[]{:S(2)}, u32[]{:S(2)}) collective-permute-start(bf16[2,48,1536]{2,1,0:T(8,128)(2,1)S(1)} %slice.170), channel_id=1, source_target_pairs={{0,2},{1,3},{2,0},{3,1},{4,6},{5,7},{6,4},{7,5},{8,10},{9,11},{10,... | collective-permute-start | bytes 884744 | tf_op jit(solution)/shard_map/o_plane2/ppermute | solution.py:73
  134.3 8.7 %collective-permute-start.26 = (bf16[2,48,1536]{2,1,0:T(8,128)(2,1)S(1)}, bf16[2,48,1536]{2,1,0:T(8,128)(2,1)S(1)}, u32[]{:S(2)}, u32[]{:S(2)}) collective-permute-start(bf16[2,48,1536]{2,1,0:T(8,128)(2,1)S(1)} %slice.171), channel_id=1, source_target_pairs={{0,4},{1,5},{2,6},{3,7},{4,0},{5,1},{6,2},{7,3},{8,12},{9,13},{10,... | collective-permute-start | bytes 884744 | tf_op jit(solution)/shard_map/o_plane2/ppermute | solution.py:73
  143.1 13.2 %collective-permute-start.28 = (bf16[4,48,1536]{2,1,0:T(8,128)(2,1)S(1)}, bf16[4,48,1536]{2,1,0:T(8,128)(2,1)S(1)}, u32[]{:S(2)}, u32[]{:S(2)}) collective-permute-start(bf16[4,48,1536]{2,1,0:T(8,128)(2,1)S(1)} %pad_maximum_fusion.9), channel_id=1, source_target_pairs={{0,1},{1,0},{2,3},{3,2},{4,5},{5,4},{6,7},{7,6},{8,9},{9,8},{10,11... | collective-permute-start | bytes 1769480 | tf_op jit(solution)/shard_map/o_core/ppermute | solution.py:73
  144.1 46.0 %collective-permute-start.30 = (bf16[6,3,48,1120]{3,2,1,0:T(8,128)(2,1)}, bf16[6,3,48,1120]{3,2,1,0:T(8,128)(2,1)S(1)}, u32[]{:S(2)}, u32[]{:S(2)}) collective-permute-start(bf16[6,3,48,1120]{3,2,1,0:T(8,128)(2,1)} %constant_dynamic-update-slice_fusion.refs_8_), channel_id=1, source_target_pairs={{0,4},{1,5},{2,6},{3,7},{4,0},{5,1},{6,2},{7,3},{8,12},{9,13},{10,... | collective-permute-start | bytes 5806088 | tf_op jit(solution)/shard_map/ff_plane1/ppermute | solution.py:73
  144.6 48.1 %collective-permute-start.29 = (bf16[6,3,48,1120]{3,2,1,0:T(8,128)(2,1)}, bf16[6,3,48,1120]{3,2,1,0:T(8,128)(2,1)}, u32[]{:S(2)}, u32[]{:S(2)}) collective-permute-start(bf16[6,3,48,1120]{3,2,1,0:T(8,128)(2,1)} %constant_dynamic-update-slice_fusion.refs_8_), channel_id=1, source_target_pairs={{0,2},{1,3},{2,0},{3,1},{4,6},{5,7},{6,4},{7,5},{8,10},{9,11},{10,... | collective-permute-start | bytes 5806088 | tf_op jit(solution)/shard_map/ff_plane1/ppermute | solution.py:73
  153.3 10.0 %collective-permute-start.22 = (bf16[128,512]{1,0:T(8,128)(2,1)}, bf16[128,512]{1,0:T(8,128)(2,1)S(1)}, u32[]{:S(2)}, u32[]{:S(2)}) collective-permute-start(bf16[128,512]{1,0:T(8,128)(2,1)} %get-tuple-element.105.refs_4_.refs_8_), channel_id=1, source_target_pairs={{0,8},{1,9},{2,10},{3,11},{4,12},{5,13},{6,14},{7,15},{8,16},{9,17... | collective-permute-start | bytes 393224 | tf_op jit(solution)/shard_map/kv/ppermute | solution.py:73
  156.3 12.5 %collective-permute-start.23 = (bf16[128,512]{1,0:T(8,128)(2,1)}, bf16[128,512]{1,0:T(8,128)(2,1)S(1)}, u32[]{:S(2)}, u32[]{:S(2)}) collective-permute-start(bf16[128,512]{1,0:T(8,128)(2,1)} %get-tuple-element.105.refs_4_.refs_8_), channel_id=1, source_target_pairs={{0,16},{1,17},{2,18},{3,19},{4,20},{5,21},{6,22},{7,23},{8,24},{9,... | collective-permute-start | bytes 393224 | tf_op jit(solution)/shard_map/kv/ppermute | solution.py:73
  160.3 12.2 %collective-permute-start.24 = (bf16[128,512]{1,0:T(8,128)(2,1)}, bf16[128,512]{1,0:T(8,128)(2,1)S(1)}, u32[]{:S(2)}, u32[]{:S(2)}) collective-permute-start(bf16[128,512]{1,0:T(8,128)(2,1)} %get-tuple-element.105.refs_4_.refs_8_), channel_id=1, source_target_pairs={{0,24},{1,25},{2,26},{3,27},{4,28},{5,29},{6,30},{7,31}} | collective-permute-start | bytes 393224 | tf_op jit(solution)/shard_map/kv/ppermute | solution.py:73
  178.9 121.9 %reduce-scatter.3.cloned.1.call-start = ((), (), s32[]{:S(2)}) async-start(), calls=%async_computation.4 | async-start | bytes 1966080 | tf_op jit(solution)/shard_map/reduce_scatter | solution.py:955
  190.0 34.6 %copy-start.5 = (bf16[6,3,48,1120]{3,2,1,0:T(8,128)(2,1)}, bf16[6,3,48,1120]{3,2,1,0:T(8,128)(2,1)S(1)}, u32[]{:S(2)}) copy-start(bf16[6,3,48,1120]{3,2,1,0:T(8,128)(2,1)S(1)} %collective-permute-done.30.refs_10_) | copy-start | bytes 5806084
  191.1 23.9 %collective-permute-start.31 = (bf16[3,3,48,1120]{3,2,1,0:T(8,128)(2,1)}, bf16[3,3,48,1120]{3,2,1,0:T(8,128)(2,1)S(1)}, u32[]{:S(2)}, u32[]{:S(2)}) collective-permute-start(bf16[3,3,48,1120]{3,2,1,0:T(8,128)(2,1)} %slice.210), channel_id=1, source_target_pairs={{0,2},{1,3},{2,0},{3,1},{4,6},{5,7},{6,4},{7,5},{8,10},{9,11},{10,... | collective-permute-start | bytes 2903048 | tf_op jit(solution)/shard_map/ff_plane2/ppermute | solution.py:73
  194.9 23.8 %collective-permute-start.32 = (bf16[3,3,48,1120]{3,2,1,0:T(8,128)(2,1)}, bf16[3,3,48,1120]{3,2,1,0:T(8,128)(2,1)}, u32[]{:S(2)}, u32[]{:S(2)}) collective-permute-start(bf16[3,3,48,1120]{3,2,1,0:T(8,128)(2,1)} %slice.211), channel_id=1, source_target_pairs={{0,4},{1,5},{2,6},{3,7},{4,0},{5,1},{6,2},{7,3},{8,12},{9,13},{10,... | collective-permute-start | bytes 2903048 | tf_op jit(solution)/shard_map/ff_plane2/ppermute | solution.py:73
  195.4 25.6 %collective-permute-start.34 = (bf16[512,1536]{1,0:T(8,128)(2,1)}, bf16[512,1536]{1,0:T(8,128)(2,1)}, u32[]{:S(2)}, u32[]{:S(2)}) collective-permute-start(bf16[512,1536]{1,0:T(8,128)(2,1)} %all-gather.6.cloned.1.call-done.refs_2_), channel_id=1, source_target_pairs={{0,1},{1,0},{2,3},{3,2},{4,5},{5,4},{6,7},{7,6},{8,9},{9,8},{10,11... | collective-permute-start | bytes 4718600 | tf_op jit(solution)/shard_map/gy_core/ppermute | solution.py:73
  221.0 3.6 collective-permute-start.33
  244.5 19.0 %collective-permute-start.36 = (bf16[512,1536]{1,0:T(8,128)(2,1)}, bf16[512,1536]{1,0:T(8,128)(2,1)S(1)}, u32[]{:S(2)}, u32[]{:S(2)}) collective-permute-start(bf16[512,1536]{1,0:T(8,128)(2,1)} %get-tuple-element.122), channel_id=1, source_target_pairs={{0,1},{1,0},{2,3},{3,2},{4,5},{5,4},{6,7},{7,6},{8,9},{9,8},{10,11... | collective-permute-start | bytes 4718600 | tf_op jit(solution)/shard_map/gn2_core/ppermute | solution.py:73
  266.4 146.6 %all-gather.8.cloned.1.call-start = ((), (), s32[]{:S(2)}) async-start(), calls=%async_computation.5 | async-start | bytes 3932160 | tf_op jit(solution)/shard_map/all_gather | solution.py:980
  266.7 27.5 %copy-start.32 = (bf16[128,1536]{1,0:T(8,128)(2,1)S(1)}, bf16[128,1536]{1,0:T(8,128)(2,1)}, u32[]{:S(2)}) copy-start(bf16[128,1536]{1,0:T(8,128)(2,1)} %get-tuple-element.119) | copy-start | bytes 1179652
  266.7 27.5 %copy-start.33 = (bf16[128,1536]{1,0:T(8,128)(2,1)S(1)}, bf16[128,1536]{1,0:T(8,128)(2,1)}, u32[]{:S(2)}) copy-start(bf16[128,1536]{1,0:T(8,128)(2,1)} %get-tuple-element.120) | copy-start | bytes 1179652
  291.2 60.2 %collective-permute-start.43 = (bf16[2,3,192,1120]{3,2,1,0:T(8,128)(2,1)}, bf16[2,3,192,1120]{3,2,1,0:T(8,128)(2,1)}, u32[]{:S(2)}, u32[]{:S(2)}) collective-permute-start(bf16[2,3,192,1120]{3,2,1,0:T(8,128)(2,1)} %get-tuple-element.144), channel_id=1, source_target_pairs={{0,4},{1,5},{2,6},{3,7},{4,0},{5,1},{6,2},{7,3},{8,12},{9,13},{10,... | collective-permute-start | bytes 7741448 | tf_op jit(solution)/shard_map/ff_sum1/ppermute | solution.py:73
  292.7 82.3 %collective-permute-start.44 = (bf16[2,3,192,1120]{3,2,1,0:T(8,128)(2,1)}, bf16[2,3,192,1120]{3,2,1,0:T(8,128)(2,1)}, u32[]{:S(2)}, u32[]{:S(2)}) collective-permute-start(bf16[2,3,192,1120]{3,2,1,0:T(8,128)(2,1)} %get-tuple-element.145), channel_id=1, source_target_pairs={{0,2},{1,3},{2,0},{3,1},{4,6},{5,7},{6,4},{7,5},{8,10},{9,11},{10,... | collective-permute-start | bytes 7741448 | tf_op jit(solution)/shard_map/ff_sum1/ppermute | solution.py:73
  300.8 157.6 %reduce-scatter.5.cloned.1.call-start = ((), (), s32[]{:S(2)}) async-start(), calls=%async_computation.6 | async-start | bytes 1966080 | tf_op jit(solution)/shard_map/reduce_scatter | solution.py:987
  300.9 117.9 %collective-permute-start.35 = (bf16[512,1536]{1,0:T(8,128)(2,1)}, bf16[512,1536]{1,0:T(8,128)(2,1)}, u32[]{:S(2)}, u32[]{:S(2)}) collective-permute-start(bf16[512,1536]{1,0:T(8,128)(2,1)} %get-tuple-element.118), channel_id=1, source_target_pairs={{0,1},{1,0},{2,3},{3,2},{4,5},{5,4},{6,7},{7,6},{8,9},{9,8},{10,11... | collective-permute-start | bytes 4718600 | tf_op jit(solution)/shard_map/y_core/ppermute | solution.py:73
  301.0 51.7 %copy-start.9 = (bf16[2,3,192,1120]{3,2,1,0:T(8,128)(2,1)S(1)}, bf16[2,3,192,1120]{3,2,1,0:T(8,128)(2,1)}, u32[]{:S(2)}) copy-start(bf16[2,3,192,1120]{3,2,1,0:T(8,128)(2,1)} %get-tuple-element.130) | copy-start | bytes 7741444
  311.2 44.2 %collective-permute-start.37 = (bf16[128,512]{1,0:T(8,128)(2,1)}, bf16[128,512]{1,0:T(8,128)(2,1)S(1)}, u32[]{:S(2)}, u32[]{:S(2)}) collective-permute-start(bf16[128,512]{1,0:T(8,128)(2,1)} %get-tuple-element.135), channel_id=1, source_target_pairs={{8,0},{9,1},{10,2},{11,3},{12,4},{13,5},{14,6},{15,7},{16,8},{17,9... | collective-permute-start | bytes 393224 | tf_op jit(solution)/shard_map/gkv/ppermute | solution.py:73
  312.5 44.4 %collective-permute-start.38 = (bf16[128,512]{1,0:T(8,128)(2,1)}, bf16[128,512]{1,0:T(8,128)(2,1)S(1)}, u32[]{:S(2)}, u32[]{:S(2)}) collective-permute-start(bf16[128,512]{1,0:T(8,128)(2,1)} %get-tuple-element.136), channel_id=1, source_target_pairs={{16,0},{17,1},{18,2},{19,3},{20,4},{21,5},{22,6},{23,7},{24,8},{25... | collective-permute-start | bytes 393224 | tf_op jit(solution)/shard_map/gkv/ppermute | solution.py:73
  351.4 12.6 %collective-permute-start.39 = (bf16[128,512]{1,0:T(8,128)(2,1)}, bf16[128,512]{1,0:T(8,128)(2,1)S(1)}, u32[]{:S(2)}, u32[]{:S(2)}) collective-permute-start(bf16[128,512]{1,0:T(8,128)(2,1)} %get-tuple-element.137), channel_id=1, source_target_pairs={{24,0},{25,1},{26,2},{27,3},{28,4},{29,5},{30,6},{31,7}} | collective-permute-start | bytes 393224 | tf_op jit(solution)/shard_map/gkv/ppermute | solution.py:73
  355.4 43.1 %collective-permute-start.49 = (bf16[3,192,1120]{2,1,0:T(8,128)(2,1)}, bf16[3,192,1120]{2,1,0:T(8,128)(2,1)}, u32[]{:S(2)}, u32[]{:S(2)}) collective-permute-start(bf16[3,192,1120]{2,1,0:T(8,128)(2,1)} %fusion.15), channel_id=1, source_target_pairs={{0,2},{1,3},{2,0},{3,1},{4,6},{5,7},{6,4},{7,5},{8,10},{9,11},{10,... | collective-permute-start | bytes 3870728 | tf_op jit(solution)/shard_map/ff_sum2/ppermute | solution.py:73
  374.7 11.1 %collective-permute-start.40 = (bf16[144,896]{1,0:T(8,128)(2,1)S(1)}, bf16[144,896]{1,0:T(8,128)(2,1)S(1)}, u32[]{:S(2)}, u32[]{:S(2)}) collective-permute-start(bf16[144,896]{1,0:T(8,128)(2,1)S(1)} %get-tuple-element.210), channel_id=1, source_target_pairs={{0,8},{1,9},{2,10},{3,11},{4,12},{5,13},{6,14},{7,15},{8,16},{9,17... | collective-permute-start | bytes 774152 | tf_op jit(solution)/shard_map/gqkv_ctx/ppermute | solution.py:73
  374.8 19.9 %collective-permute-start.41 = (bf16[144,896]{1,0:T(8,128)(2,1)S(1)}, bf16[144,896]{1,0:T(8,128)(2,1)S(1)}, u32[]{:S(2)}, u32[]{:S(2)}) collective-permute-start(bf16[144,896]{1,0:T(8,128)(2,1)S(1)} %get-tuple-element.209), channel_id=1, source_target_pairs={{0,16},{1,17},{2,18},{3,19},{4,20},{5,21},{6,22},{7,23},{8,24},{9,... | collective-permute-start | bytes 774152 | tf_op jit(solution)/shard_map/gqkv_ctx/ppermute | solution.py:73
  378.0 30.1 %collective-permute-start.50 = (bf16[3,192,1120]{2,1,0:T(8,128)(2,1)}, bf16[3,192,1120]{2,1,0:T(8,128)(2,1)}, u32[]{:S(2)}, u32[]{:S(2)}) collective-permute-start(bf16[3,192,1120]{2,1,0:T(8,128)(2,1)} %fusion.16), channel_id=1, source_target_pairs={{0,4},{1,5},{2,6},{3,7},{4,0},{5,1},{6,2},{7,3},{8,12},{9,13},{10,... | collective-permute-start | bytes 3870728 | tf_op jit(solution)/shard_map/ff_sum2/ppermute | solution.py:73
  385.8 9.8 %collective-permute-start.42 = (bf16[144,896]{1,0:T(8,128)(2,1)S(1)}, bf16[144,896]{1,0:T(8,128)(2,1)S(1)}, u32[]{:S(2)}, u32[]{:S(2)}) collective-permute-start(bf16[144,896]{1,0:T(8,128)(2,1)S(1)} %get-tuple-element.208), channel_id=1, source_target_pairs={{0,24},{1,25},{2,26},{3,27},{4,28},{5,29},{6,30},{7,31},{8,0},{9,1... | collective-permute-start | bytes 774152 | tf_op jit(solution)/shard_map/gqkv_ctx/ppermute | solution.py:73
  413.0 9.0 %collective-permute-start.51 = (bf16[3,192,1120]{2,1,0:T(8,128)(2,1)}, bf16[3,192,1120]{2,1,0:T(8,128)(2,1)}, u32[]{:S(2)}, u32[]{:S(2)}) collective-permute-start(bf16[3,192,1120]{2,1,0:T(8,128)(2,1)} %select_convert_fusion), channel_id=1, source_target_pairs={{0,1},{1,0},{2,3},{3,2},{4,5},{5,4},{6,7},{7,6},{8,9},{9,8},{10,11... | collective-permute-start | bytes 3870728 | tf_op jit(solution)/shard_map/final_core/ppermute | solution.py:73
  418.4 8.5 %collective-permute-start.45 = (bf16[4,208,896]{2,1,0:T(8,128)(2,1)}, bf16[4,208,896]{2,1,0:T(8,128)(2,1)}, u32[]{:S(2)}, u32[]{:S(2)}) collective-permute-start(bf16[4,208,896]{2,1,0:T(8,128)(2,1)} %dynamic-slice_bitcast_fusion), channel_id=1, source_target_pairs={{0,1},{1,0},{2,3},{3,2},{4,5},{5,4},{6,7},{7,6},{8,9},{9,8},{10,11... | collective-permute-start | bytes 4472840 | tf_op jit(solution)/shard_map/term_core/ppermute | solution.py:73
  428.8 12.5 %collective-permute-start.48 = (bf16[208,896]{1,0:T(8,128)(2,1)S(1)}, bf16[208,896]{1,0:T(8,128)(2,1)S(1)}, u32[]{:S(2)}, u32[]{:S(2)}) collective-permute-start(bf16[208,896]{1,0:T(8,128)(2,1)S(1)} %get-tuple-element.206), channel_id=1, source_target_pairs={{0,6},{1,7},{2,4},{3,5},{4,2},{5,3},{6,0},{7,1},{8,14},{9,15},{10,... | collective-permute-start | bytes 1118216 | tf_op jit(solution)/shard_map/term_plane/ppermute | solution.py:73
  431.2 17.5 %collective-permute-start.47 = (bf16[208,896]{1,0:T(8,128)(2,1)S(1)}, bf16[208,896]{1,0:T(8,128)(2,1)S(1)}, u32[]{:S(2)}, u32[]{:S(2)}) collective-permute-start(bf16[208,896]{1,0:T(8,128)(2,1)S(1)} %get-tuple-element.207), channel_id=1, source_target_pairs={{0,4},{1,5},{2,6},{3,7},{4,0},{5,1},{6,2},{7,3},{8,12},{9,13},{10,... | collective-permute-start | bytes 1118216 | tf_op jit(solution)/shard_map/term_plane/ppermute | solution.py:73
  431.8 17.0 %collective-permute-start.46 = (bf16[208,896]{1,0:T(8,128)(2,1)S(1)}, bf16[208,896]{1,0:T(8,128)(2,1)S(1)}, u32[]{:S(2)}, u32[]{:S(2)}) collective-permute-start(bf16[208,896]{1,0:T(8,128)(2,1)S(1)} %get-tuple-element.205), channel_id=1, source_target_pairs={{0,2},{1,3},{2,0},{3,1},{4,6},{5,7},{6,4},{7,5},{8,10},{9,11},{10,... | collective-permute-start | bytes 1118216 | tf_op jit(solution)/shard_map/term_plane/ppermute | solution.py:73
  (43 other events, 359.2 us)
Sparse Core Ops, SparseCore 0:
  132.8 38.4 all-gather.5
  179.0 41.9 all-gather.3
  266.6 34.1 reduce-scatter.2
  302.2 73.4 all-gather.7
  422.1 36.2 reduce-scatter.4

commit v3 on v2

--- a/solution.py
+++ b/solution.py
@@ -374,17 +374,6 @@
     return shard, a, b, links.plane(b[:half], 2), links.plane(a[half:], 4)
 
 
-def laid_out(entries, shard, a, b, low, high):
-    half = len(entries) // 2
-    return [
-        (entries, 0, shard),
-        (entries, 1, a),
-        (entries, 2, b),
-        (entries[:half], 3, low),
-        (entries[half:], 3, high),
-    ]
-
-
 def ff_kernel(layout, sizes, place, normed, out_grad, *refs):
     ctx_size, chips, rows = sizes
     pieces, refs = refs[: len(layout)], refs[len(layout) :]
@@ -462,60 +451,46 @@
 
 
 def grad_kernel(place, *refs):
-    lefts, rights, outs = refs[:4], refs[4:10], refs[10:]
-    keep_low, send_low, keep_high, send_high = outs
-    j = pl.program_id(0)
+    lefts, rights, outs = refs[:8], refs[8:14], refs[14:]
+    low, high = outs[: len(outs) // 2], outs[len(outs) // 2 :]
     for which in range(3):
-        left_a, left_b = lefts[:2] if which < 2 else lefts[2:]
-        right_a, right_b = rights[2 * which : 2 * which + 2]
-        out = tn(left_a[...], right_a[...]) + tn(left_b[...], right_b[...])
-        half = out.shape[0] // 2
-        low, high = out[:half].astype(BF16), out[half:].astype(BF16)
-
-        @pl.when(j < 2)
-        def _():
-            keep_low[0, which] = low
-
-        @pl.when(j >= 2)
-        def _():
-            send_low[0, which] = low
-
-        @pl.when(j % 2 == 0)
-        def _():
-            keep_high[0, which] = high
-
-        @pl.when(j % 2 == 1)
-        def _():
-            send_high[0, which] = high
-
-
-def ff_grad_terms(place, lefts, rights):
+        first = 4 * (which // 2)
+        for parts, (left_a, left_b), core in (
+            (low, lefts[first : first + 2], 0),
+            (high, lefts[first + 2 : first + 4], 1),
+        ):
+            out, at = (parts[0], which) if len(parts) == 1 else (parts[which > 0], max(which - 1, 0))
+            half = left_a.shape[1] // 2
+            rows = slice(core * half, (core + 1) * half)
+            right_a, right_b = rights[2 * which : 2 * which + 2]
+            term = tn(left_a[:, rows], right_a[...]) + tn(left_b[:, rows], right_b[...])
+            out[0, at] = term.astype(BF16)
+
+
+def ff_grad_terms(place, lefts, rights, low_at, high_at, parts):
     tokens, width = lefts[0].shape
     block = rights[0].shape[1]
     part = width // 4
-    left = pl.BlockSpec((tokens, part), lambda j, place: (0, place[1] ^ j))
+
+    def left(at):
+        return pl.BlockSpec((tokens, part), lambda j, place: (0, place[1] ^ at(j)))
+
     right = pl.BlockSpec((tokens, block), lambda j, place: (0, 0))
-
-    def out(index):
-        return pl.BlockSpec((1, 3, part // 2, block), lambda j, place: (index(j), 0, 0, 0))
-
+    outs = [pl.BlockSpec((1, n, part // 2, block), lambda j, place: (j, 0, 0, 0)) for n in parts]
+    low, high = left(low_at), left(high_at)
+    x_a, x_b, y_a, y_b = lefts
     return pl.pallas_call(
         grad_kernel,
         grid_spec=pltpu.PrefetchScalarGridSpec(
             num_scalar_prefetch=1,
-            grid=(4,),
-            in_specs=[left] * 4 + [right] * 6,
-            out_specs=[
-                out(lambda j: jnp.minimum(j, 1)),
-                out(lambda j: jnp.maximum(j - 2, 0)),
-                out(lambda j: j // 2),
-                out(lambda j: j // 2),
-            ],
+            grid=(2,),
+            in_specs=[low, low, high, high] * 2 + [right] * 6,
+            out_specs=outs * 2,
         ),
-        out_shape=[jax.ShapeDtypeStruct((2, 3, part // 2, block), BF16)] * 4,
+        out_shape=[jax.ShapeDtypeStruct((2, n, part // 2, block), BF16) for n in parts] * 2,
         compiler_params=pltpu.CompilerParams(vmem_limit_bytes=56 * 2**20),
         cost_estimate=pl.CostEstimate(flops=0, bytes_accessed=0, transcendentals=0),
-    )(place, *lefts, *rights)
+    )(place, x_a, x_b, x_a, x_b, y_a, y_b, y_a, y_b, *rights)
 
 
 def added(a, b):
@@ -523,22 +498,103 @@
 
 
 def reduce_start(links, terms):
-    return links.plane(terms[1], 4), links.plane(terms[3], 2)
+    return [links.plane(x, mask) for x, mask in zip(terms, (4, 4, 2, 2))]
+
+
+def add_pairs_kernel(*refs):
+    for i, out in enumerate(refs[6:]):
+        keep, one, rest = refs[3 * i : 3 * i + 3]
+        out[:1] = (keep[0, :1].astype(F32) + one[0].astype(F32)).astype(BF16)
+        out[1:] = (keep[0, 1:].astype(F32) + rest[0].astype(F32)).astype(BF16)
+
+
+def first_specs(index):
+    def spec(x):
+        return pl.BlockSpec((1, *x.shape[1:]), lambda i, *place: (index, 0, 0, 0))
+
+    return spec
 
 
 def reduce_next(links, terms, first):
-    keep_low, _, keep_high, _ = terms
-    return (
-        links.plane(added(keep_low[1], first[0][1]), 2),
-        links.plane(added(keep_high[1], first[1][1]), 4),
-    )
-
-
-def reduce_end(terms, first, second):
-    return [
-        keep[0].astype(F32) + one[0].astype(F32) + two.astype(F32)
-        for keep, one, two in zip(terms[::2], first, second)
-    ]
+    shape = terms[0].shape
+    arrays = (terms[0], first[0], first[1], terms[1], first[2], first[3])
+    spec = first_specs(1)
+    whole = pl.BlockSpec(shape[1:], lambda i: (0, 0, 0))
+    low, high = pl.pallas_call(
+        add_pairs_kernel,
+        grid=(1,),
+        in_specs=[spec(x) for x in arrays],
+        out_specs=[whole] * 2,
+        out_shape=[jax.ShapeDtypeStruct(shape[1:], BF16)] * 2,
+        compiler_params=pltpu.CompilerParams(vmem_limit_bytes=56 * 2**20),
+        cost_estimate=pl.CostEstimate(flops=0, bytes_accessed=0, transcendentals=0),
+    )(*arrays)
+    return links.plane(low, 2), links.plane(high, 4)
+
+
+def reduce_end_kernel(place, *refs):
+    low, high, (mine, send) = refs[:4], refs[4:8], refs[8:]
+
+    def write(ref, parts):
+        keep, one, rest, last = parts
+        total = keep[0, :1].astype(F32) + one[0].astype(F32) + last[:1].astype(F32)
+        ref[:1] = total.astype(ref.dtype)
+        total = keep[0, 1:].astype(F32) + rest[0].astype(F32) + last[1:].astype(F32)
+        ref[1:] = total.astype(ref.dtype)
+
+    @pl.when(place[2] == 0)
+    def _():
+        write(mine, low)
+        write(send, high)
+
+    @pl.when(place[2] != 0)
+    def _():
+        write(mine, high)
+        write(send, low)
+
+
+def reduce_end(place, terms, first, second):
+    shape = terms[0].shape[1:]
+    spec = first_specs(0)
+    whole = pl.BlockSpec(shape, lambda i, place: (0, 0, 0))
+    low = (terms[0], first[0], first[1])
+    high = (terms[1], first[2], first[3])
+    return pl.pallas_call(
+        reduce_end_kernel,
+        grid_spec=pltpu.PrefetchScalarGridSpec(
+            num_scalar_prefetch=1,
+            grid=(1,),
+            in_specs=[*map(spec, low), whole, *map(spec, high), whole],
+            out_specs=[whole] * 2,
+        ),
+        out_shape=[jax.ShapeDtypeStruct(shape, F32), jax.ShapeDtypeStruct(shape, BF16)],
+        compiler_params=pltpu.CompilerParams(vmem_limit_bytes=56 * 2**20),
+        cost_estimate=pl.CostEstimate(flops=12 * 10**9, bytes_accessed=0, transcendentals=0),
+    )(place, *low, second[0], *high, second[1])
+
+
+def join_cores_kernel(place, mine, got, gate, up, down):
+    block = mine.shape[2]
+
+    def write(even, odd):
+        for which, ref in enumerate((gate, up)):
+            ref[...] = jnp.concatenate([even(which), odd(which)], axis=1)
+        down[:block] = jnp.transpose(even(2))
+        down[block:] = jnp.transpose(odd(2))
+
+    def own(which):
+        return mine[which]
+
+    def others(which):
+        return got[which].astype(F32)
+
+    @pl.when(place[2] == 0)
+    def _():
+        write(own, others)
+
+    @pl.when(place[2] != 0)
+    def _():
+        write(others, own)
 
 
 def split_kernel(place, gate, up, down, mine, other):
@@ -577,67 +633,56 @@
 
 
 class Rows:
-    def __init__(self, ctx_size, chips, pieces, layout):
-        self.pieces, self.layout = pieces, layout
-        self.sizes = (ctx_size, chips)
-        self.rows, self.columns = pieces[0].shape[-2:]
-        self.shape = (2 * ctx_size * chips * self.rows, self.columns)
+    def __init__(self, sizes, pieces, layout, first, columns):
+        self.sizes, self.pieces, self.layout = sizes, pieces, layout
+        self.first, self.columns = first, columns
+        self.rows = pieces[0].shape[-2]
+        self.shape = (2 * sizes[0] * sizes[1] * self.rows, columns)
 
     def start(self, place, refs, weight, semaphore):
-        chips = self.sizes[1]
-        for piece, index, source, mask, turned in self.layout:
+        ctx_size, chips = self.sizes
+        for piece, index, step, mask, turned in self.layout:
+            source = lax.rem(place[0] - step + ctx_size, ctx_size)
             start = ((source * chips + (place[1] ^ mask)) * 2 + (place[2] ^ turned)) * self.rows
             pltpu.make_async_copy(
-                refs[piece].at[index],
+                refs[piece].at[(*index, slice(None), pl.ds(self.first, self.columns))],
                 weight.at[pl.ds(pl.multiple_of(start, self.rows), self.rows)],
                 semaphore,
             ).start()
 
 
-def by_ctx(links, ctx, got):
-    ctx_size, shard = links.ctx_size, got[0]
-    whole = jnp.zeros((ctx_size, *shard.shape), shard.dtype)
-    for step, piece in enumerate(got):
-        whole = lax.dynamic_update_index_in_dim(whole, piece, (ctx - step) % ctx_size, 0)
-    return whole
-
-
-def rows_of_plane(links, mine, a, b, low, high):
-    ctx_size = links.ctx_size
+def rows_layout(ctx_size):
     half = ctx_size // 2
-    early = links.core(jnp.stack([mine, a, b]))
-    late = links.core(jnp.concatenate([low, high]))
-    pieces = [mine, a, b, low, high, early, late]
     layout = []
-    for c in range(ctx_size):
-        layout += [(mask, (c,), c, mask, 0) for mask in range(3)]
-        layout.append((3, (c,), c, 3, 0) if c < half else (4, (c - half,), c, 3, 0))
-        layout += [(5, (mask, c), c, mask, 1) for mask in range(3)]
-        layout.append((6, (c,), c, 3, 1))
-    return Rows(ctx_size, links.fsdp_size // 2, pieces, layout)
+    for step in range(ctx_size):
+        layout += [(mask, (step,), step, mask, 0) for mask in range(3)]
+        layout.append((3, (step,), step, 3, 0) if step < half else (4, (step - half,), step, 3, 0))
+        layout.append((5, (step,), step, 0, 1))
+        layout += [(6, (i * ctx_size + step,), step, i + 1, 1) for i in range(3)]
+    return layout
 
 
 def wait_all(weight, semaphore):
     pltpu.make_async_copy(weight, weight, semaphore).wait()
 
 
-def call(body, place, arrays, weight, out_shapes, cost):
+def call(body, place, arrays, weight, out_shapes, cost, scratch=()):
     any_spec = pl.BlockSpec(memory_space=pl.ANY)
     vmem = pl.BlockSpec(memory_space=pltpu.VMEM)
     count, pieces = len(arrays), len(weight.pieces)
 
     def kernel(place, *refs):
         ins, parts, outs = refs[:count], refs[count : count + pieces], refs[count + pieces : -2]
-        scratch, semaphore = refs[-2:]
-        weight.start(place, parts, scratch, semaphore)
-        body(place, ins, outs, scratch, lambda: wait_all(scratch, semaphore))
+        whole, semaphore = refs[-2:]
+        weight.start(place, parts, whole, semaphore)
+        body(place, ins, outs, whole, lambda: wait_all(whole, semaphore))
 
     return pl.pallas_call(
         kernel,
         in_specs=[pl.BlockSpec(memory_space=pltpu.SMEM)] + [vmem] * count + [any_spec] * pieces,
         out_specs=[vmem] * len(out_shapes),
         out_shape=[jax.ShapeDtypeStruct(shape, dtype) for shape, dtype in out_shapes],
-        scratch_shapes=[pltpu.VMEM(weight.shape, BF16), pltpu.SemaphoreType.DMA],
+        scratch_shapes=[*scratch, pltpu.VMEM(weight.shape, BF16), pltpu.SemaphoreType.DMA],
         compiler_params=pltpu.CompilerParams(vmem_limit_bytes=56 * 2**20),
         cost_estimate=pl.CostEstimate(flops=cost, bytes_accessed=0, transcendentals=0),
     )(place, *arrays, *weight.pieces)
@@ -778,7 +823,7 @@
 def qkv_back_body(steps, place, ins, outs, weight, wait):
     terms, ins = ins[:steps], ins[steps:]
     tokens, small, cosine, sine, grad_query, grad_hidden, grad_hidden_low, gain_two = ins
-    stream_ref, share_ref = outs
+    stream_ref, *share_refs, share_ref = outs
     count, width = tokens.shape
     pairs = terms[0][...].astype(F32)
     for term in terms[1:]:
@@ -812,6 +857,77 @@
         share_ref[target, count:, q_columns:] = jnp.zeros(
             (16, share_ref.shape[2] - q_columns), BF16
         )
+    for step, ref in enumerate(share_refs):
+        ref[...] = share_ref[lax.rem(place[0] + step, targets)]
+
+
+def term_kernel(place, *refs):
+    *shares, normed_rows, mixed_rows, mine, other, share, terms, vectors = refs
+    ctx_size, width = len(shares), normed_rows.shape[1]
+    count = normed_rows.shape[0] // ctx_size
+    chips, height = mine.shape[0], mine.shape[1] - 16
+    devices = 2 * chips
+    q_columns, kv_columns = width // ctx_size, KV_WIDTH // ctx_size
+    kv_end = q_columns + 2 * kv_columns
+    gains = jnp.zeros((16, q_columns), F32)
+    for step, ref in enumerate(shares):
+        source = lax.rem(place[0] - step + ctx_size, ctx_size)
+        share[pl.ds(pl.multiple_of(source * count, count), count)] = ref[:count]
+        gains = gains + ref[count:, :q_columns].astype(F32)
+    terms[:, :kv_end] = tn(normed_rows[...], share[:, :kv_end])
+    terms[:, kv_end:] = tn(mixed_rows[...], share[:, kv_end:])
+    biases = jnp.sum(share[:, :kv_end].astype(F32), axis=0, keepdims=True)
+    vectors[...] = jnp.zeros_like(vectors)
+    parts = (gains[0:1], gains[1:2], biases[:, :q_columns])
+    parts += (biases[:, q_columns : q_columns + kv_columns], biases[:, q_columns + kv_columns :])
+    for f in range(devices):
+        start = 0
+        for part in parts:
+            size = part.shape[1] // devices
+            vectors[f : f + 1, start : start + size] = part[:, f * size : (f + 1) * size]
+            start += size
+    first = lax.broadcasted_iota(jnp.int32, (16, terms.shape[1]), 0) == 0
+    for ref, core in ((mine, place[2]), (other, 1 - place[2])):
+        for mask in range(chips):
+            f = (place[1] ^ mask) * 2 + core
+            start = pl.multiple_of(f * height, 64)
+            ref[mask, :height] = terms[pl.ds(start, height)].astype(BF16)
+            row = jnp.broadcast_to(vectors[pl.ds(f, 1)], first.shape)
+            ref[mask, height:] = jnp.where(first, row, 0.0).astype(BF16)
+
+
+def sum_cores_kernel(mine, got, keep, *sends):
+    keep[...] = mine[0].astype(F32) + got[0].astype(F32)
+    for mask, ref in enumerate(sends, 1):
+        ref[...] = (mine[mask].astype(F32) + got[mask].astype(F32)).astype(BF16)
+
+
+def sum_plane_kernel(keep, *refs):
+    got, outs = refs[:3], refs[3:]
+    total = keep[...] + got[0][...].astype(F32) + got[1][...].astype(F32) + got[2][...].astype(F32)
+    height = total.shape[0] - 16
+    start = 0
+    for ref in outs[:4]:
+        ref[...] = total[:height, start : start + ref.shape[1]]
+        start += ref.shape[1]
+    start = 0
+    for ref in outs[4:]:
+        ref[...] = total[height : height + 1, start : start + ref.shape[1]]
+        start += ref.shape[1]
+
+
+def small_call(body, arrays, out_shapes, scratch=(), place=None, cost=0):
+    vmem = pl.BlockSpec(memory_space=pltpu.VMEM)
+    smem = [] if place is None else [place]
+    return pl.pallas_call(
+        body,
+        in_specs=[pl.BlockSpec(memory_space=pltpu.SMEM)] * len(smem) + [vmem] * len(arrays),
+        out_specs=[vmem] * len(out_shapes),
+        out_shape=[jax.ShapeDtypeStruct(shape, dtype) for shape, dtype in out_shapes],
+        scratch_shapes=list(scratch),
+        compiler_params=pltpu.CompilerParams(vmem_limit_bytes=56 * 2**20),
+        cost_estimate=pl.CostEstimate(flops=cost, bytes_accessed=0, transcendentals=0),
+    )(*smem, *arrays)
 
 
 def per_device_plane_of_four(
@@ -853,58 +969,49 @@
         axis=1,
     )
     extra = jnp.pad(extra, ((0, 0), (0, 128 - extra.shape[1])))
-    packed = jnp.concatenate([q_weight, key_projection, value_projection, extra], axis=1)
-    links.label = "qkv_ctx"
-    qkv_got = [packed] + [links.turn(packed, step) for step in steps]
-    links.label = "o_ctx"
-    o_got = [o_weight] + [links.turn(o_weight, step) for step in steps]
+    packed = jnp.concatenate([q_weight, key_projection, value_projection, extra, o_weight], axis=1)
+    links.label = "qkvo_ctx"
+    packed_got = [links.turn(packed, step) for step in steps]
 
     mine, other = split_hidden(
         links, place, (gate_weight, up_weight, jnp.transpose(down_weight))
     )
     links.label = "ff_core"
-    qkv_got, o_got, (mine, got) = phase(qkv_got, o_got, (mine, links.core(other)))
+    got = links.core(other)
 
     def for_ctx(step):
         target = (ctx + step) % ctx_size
         a, b = pick(mine, target), pick(got, target)
         return jnp.stack([jnp.where(even, a, b), jnp.where(even, b, a)])
 
-    qkv_mine = by_ctx(links, ctx, qkv_got)
-    o_mine = by_ctx(links, ctx, o_got)
-    own_piece = for_ctx(0)
-    links.label = "qkv_plane1"
-    qkv_stage = plane_start(links, qkv_mine)
+    packed_got, (mine, got) = phase(packed_got, (mine, got))
+    packed_mine = jnp.stack([packed] + packed_got)
+    links.label = "qkvo_plane1"
+    packed_stage = plane_start(links, packed_mine)
+    links.label = "ff_ctx_a"
+    near_steps, far_steps = (1, ctx_size - 1), tuple(range(2, ctx_size - 1))
+    near = [links.turn(for_ctx(step), step) for step in near_steps]
+    far = [for_ctx(step) for step in far_steps]
+    links.label = "qkvo_core"
+    packed_stage, near, far, (own_piece, early) = phase(
+        packed_stage, near, far, (for_ctx(0), links.core(packed_mine))
+    )
+    links.label = "ff_ctx_b"
+    far = [links.turn(piece, step) for step, piece in zip(far_steps, far)]
+    links.label = "qkvo_plane2"
+    packed_parts = plane_end(links, packed_mine, *packed_stage)
     links.label = "ff_own1"
     own_stage = plane_start(links, own_piece)
-    links.label = "ff_ctx_a"
-    moved = {step: links.turn(for_ctx(step), step) for step in (1, ctx_size - 1)}
-    far = {step: for_ctx(step) for step in range(2, ctx_size - 1)}
-    qkv_stage, own_stage, near, far_list, (o_mine,) = phase(
-        qkv_stage, own_stage, moved.values(), far.values(), (o_mine,)
-    )
-    moved = dict(zip(moved, near))
-    links.label = "ff_ctx_b"
-    for step, piece in zip(far, far_list):
-        moved[step] = links.turn(piece, step)
-    links.label = "qkv_plane2"
-    qkv_parts = plane_end(links, qkv_mine, *qkv_stage)
-    links.label = "ff_own2"
-    own_parts = plane_end(links, own_piece, *own_stage)
-    links.label = "o_plane1"
-    o_stage = plane_start(links, o_mine)
-    moved_list, qkv_late, own_late, o_stage = phase(
-        [moved[step] for step in steps], qkv_parts[3:], own_parts[3:], o_stage
-    )
-    own_parts = (*own_parts[:3], *own_late)
-    links.label = "qkv_core"
-    weight_qkv = rows_of_plane(links, *qkv_parts[:3], *qkv_late)
-    links.label = "o_plane2"
-    o_parts = plane_end(links, o_mine, *o_stage)
-    links.label = "o_core"
-    weight_o = rows_of_plane(links, *o_parts)
+    near, far, late, own_stage = phase(near, far, packed_parts[3:], own_stage)
+    links.label = "qkvo_core"
+    pieces = [*packed_parts[:3], *late, early]
+    pieces.append(links.core(jnp.concatenate([*packed_parts[1:3], *late])))
+    sizes, qkv_columns = (ctx_size, fsdp_size // 2), packed.shape[1] - width
+    weight_qkv = Rows(sizes, pieces, rows_layout(ctx_size), 0, qkv_columns)
+    weight_o = Rows(sizes, pieces, rows_layout(ctx_size), qkv_columns, width)
     links.label = "ff_plane1"
-    moved_piece = jnp.concatenate(moved_list)
+    moved = dict(zip(near_steps + far_steps, near + far))
+    moved_piece = jnp.concatenate([moved[step] for step in steps])
     moved_stage = plane_start(links, moved_piece)
 
     low_tokens, out_low = tokens[0], cotangent[0]
@@ -936,34 +1043,46 @@
         0,
     )
 
-    out_row = lax.all_gather(after(out_low, *moved_list), "ctx", axis=0, tiled=True)
+    out_row = lax.all_gather(after(out_low, *far), "ctx", axis=0, tiled=True)
     normed_row = lax.all_gather(normed_two, "ctx", axis=0, tiled=True)
     links.label = "gy_core"
     out_other = links.core(out_row)
     links.label = "ff_plane2"
-    moved_parts = plane_end(links, moved_piece, *moved_stage)
-    layout = [
-        *laid_out([(0, 0), (0, 1)], *own_parts),
-        *laid_out([(step, core) for step in steps for core in range(2)], *moved_parts),
+    half = ctx_size - 1
+    last = [
+        links.plane(jnp.concatenate([moved_stage[1][:half], own_stage[1][:1]]), 2),
+        links.plane(jnp.concatenate([moved_stage[0][half:], own_stage[0][1:]]), 4),
+    ]
+    own_entries = [(0, 0), (0, 1)]
+    entries = [(step, core) for step in steps for core in range(2)]
+    layout = [(own_entries, mask, x) for mask, x in enumerate((own_piece, *own_stage))]
+    layout += [(entries, mask, x) for mask, x in enumerate((moved_piece, *moved_stage))]
+    layout += [
+        (entries[:half] + own_entries[:1], 3, last[0]),
+        (entries[half:] + own_entries[1:], 3, last[1]),
     ]
     links.label = "n2_core"
-    normed_other = links.core(after(normed_row, *moved_parts[3:]))
+    normed_other = links.core(after(normed_row, *last, out_other))
     act_a, gate_a, up_a, down_a, y_a = feed_forward(links, layout, place, normed_row, out_row)
+    normed_other = after(normed_other, act_a)
     act_b, gate_b, up_b, down_b, y_b = feed_forward(links, layout, place, normed_other, out_other)
     links.label = "gn2_core"
     down_got = links.core(down_b)
+    normed_rows = lax.all_gather(after(normed_one, normed_row), "ctx", axis=0, tiled=True)
     grad_normed_two = lax.psum_scatter(
-        added(down_a, down_got), "ctx", scatter_dimension=0, tiled=True
-    )
-
-    ff_terms = ff_grad_terms(
-        place,
-        (after(normed_row, down_got), normed_other, out_row, out_other),
-        (gate_a, gate_b, up_a, up_b, act_a, act_b),
-    )
+        after(added(down_a, down_got), normed_rows), "ctx", scatter_dimension=0, tiled=True
+    )
+
+    rights = (gate_a, gate_b, up_a, up_b, act_a, act_b)
+    lefts = (after(normed_row, down_got), normed_other, out_row, out_other)
+    send_terms = ff_grad_terms(place, lefts, rights, lambda j: 2 + j, lambda j: 1 + 2 * j, (1, 2))
     links.label = "ff_sum1"
-    ff_first = reduce_start(links, ff_terms)
-    grad_normed_two = after(grad_normed_two, ff_terms[0])
+    ff_first = reduce_start(links, send_terms)
+    lefts = (after(normed_row, *send_terms), *lefts[1:])
+    ff_terms = ff_grad_terms(place, lefts, rights, lambda j: j, lambda j: 2 * j, (3,))
+    links.label = "y_core"
+    y_got = links.core(after(y_b, down_got))
+    grad_normed_two = after(grad_normed_two, ff_terms[0], y_got, *ff_first[::2])
 
     def mix_back(*refs):
         mix_back_body(1, *refs)
@@ -977,15 +1096,9 @@
         BACK_COST,
     )
     links.label = "y_core"
-    both_rows = lax.all_gather(
-        after(jnp.concatenate([normed_one, mixed_low], axis=1), grad_normed_two),
-        "ctx",
-        axis=0,
-        tiled=True,
-    )
-    y_both = after(added(y_a, links.core(y_b)), both_rows)
-    y_sum = lax.psum_scatter(y_both, "ctx", scatter_dimension=0, tiled=True)
-    layer_out = hidden_one + y_sum.astype(F32)
+    mixed_rows = lax.all_gather(
+        after(mixed_low, grad_normed_two), "ctx", axis=0, tiled=True
+    )
     links.label = "gkv"
     pair_terms = [pair_terms[0]] + [links.shift(pair_terms[step], -step) for step in steps]
     def columns_over_ctx(parts):
@@ -1000,68 +1113,78 @@
         qkv_back_body(ctx_size, *refs)
 
     columns = (width + 2 * KV_WIDTH) // ctx_size
-    grad_stream, parts = call(
+    share_shape = (count + 16, columns + width // ctx_size)
+    grad_stream, *shares = call(
         qkv_back,
         place,
         (*pair_terms, low_tokens, small, cosine, sine, grad_query, grad_hidden, grad_hidden_low, gain_two),
         weight_qkv,
-        [(wide, F32), ((ctx_size, count + 16, columns + width // ctx_size), BF16)],
+        [(wide, F32)] + [(share_shape, BF16)] * ctx_size,
         0,
-    )
-
+        [pltpu.VMEM((ctx_size, *share_shape), BF16)],
+    )
 
     links.label = "gqkv_ctx"
-    share = after(columns_over_ctx(parts), *ff_first)
+    first_share = shares[0]
+    shares = [first_share] + [links.turn(shares[step], step) for step in steps]
+    shares[0] = after(shares[0], *ff_first)
+    y_both = after(added(y_a, y_got), *shares[1:])
+    y_sum = lax.psum_scatter(y_both, "ctx", scatter_dimension=0, tiled=True)
+    layer_out = hidden_one + y_sum.astype(F32)
     links.label = "ff_sum2"
-    ff_second = reduce_next(links, ff_terms, ff_first)
-    gain_sums = jnp.sum(share[:, count:].astype(F32), axis=0)[:2]
-    share = share[:, :count].reshape(ctx_size * count, -1)
-    share_o, share = share[:, columns:], share[:, :columns]
-    bias_sums = jnp.sum(share.astype(F32), axis=0)
+    ff_second = reduce_next(links, ff_terms, phase(ff_first, (first_share,))[0])
+    chips = fsdp_size // 2
+    term_shape = (chips, width // fsdp_size + 16, share_shape[1])
+    term_mine, term_other = small_call(
+        term_kernel,
+        (*shares, normed_rows, mixed_rows),
+        [(term_shape, BF16)] * 2,
+        [
+            pltpu.VMEM((ctx_size * count, share_shape[1]), BF16),
+            pltpu.VMEM((width, share_shape[1]), F32),
+            pltpu.VMEM((fsdp_size, share_shape[1]), F32),
+        ],
+        place,
+    )
+    links.label = "term_core"
+    ff_mine, ff_send = reduce_end(place, ff_terms, ff_first, ff_second)
+    term_mine = after(term_mine, ff_send)
+    keep, *sends = small_call(
+        sum_cores_kernel,
+        (term_mine, links.core(term_other)),
+        [(term_shape[1:], F32)] + [(term_shape[1:], BF16)] * (chips - 1),
+    )
+    links.label = "term_plane"
     q_columns, kv_columns = width // ctx_size, KV_WIDTH // ctx_size
-    bounds = (0, q_columns, q_columns + kv_columns, columns)
-    sums = [gain_sums[0, :q_columns], gain_sums[1, :q_columns]]
-    sums += [bias_sums[i:j] for i, j in zip(bounds, bounds[1:])]
-    sums = jnp.concatenate([x.reshape(fsdp_size, -1) for x in sums], axis=1)
-    sums = jnp.pad(sums, ((0, 0), (0, columns - sums.shape[1])))
-    sums = jnp.pad(sums[:, None], ((0, 0), (0, 15), (0, 0)))
-    term = tn(both_rows[:, :width], share).reshape(fsdp_size, -1, columns)
-    term = jnp.concatenate([term, sums], axis=1).astype(BF16)
-    term_o = tn(both_rows[:, width:], share_o).astype(BF16).reshape(fsdp_size, -1, q_columns)
-    term_o = jnp.pad(term_o, ((0, 0), (0, 16), (0, 0)))
-    term = jnp.concatenate([term, term_o], axis=2)
-    term = jnp.transpose(term.reshape(fsdp_size // 2, 2, *term.shape[1:]), (1, 0, 2, 3))
-    links.label = "term_core"
-    term = added(pick(term, core), links.core(pick(term, 1 - core)))
-    links.label = "term_plane"
-    total = pick(term, chip).astype(F32)
-    for mask in range(1, fsdp_size // 2):
-        total = total + links.plane(pick(term, chip ^ mask), 2 * mask).astype(F32)
-    grad_packed, grad_o, sums = total[:-16, :columns], total[:-16, columns:], total[-16]
-    vectors = []
-    start = 0
-    for size in (width, width, width, KV_WIDTH, KV_WIDTH):
-        part = size // (ctx_size * fsdp_size)
-        vectors.append(sums[start : start + part])
-        start += part
+    height, devices = width // fsdp_size, ctx_size * fsdp_size
+    plane_got = [links.plane(x, 2 * mask) for mask, x in enumerate(sends, 1)]
+    grad_q, grad_k, grad_v, grad_o, *vectors = small_call(
+        sum_plane_kernel,
+        (keep, *plane_got),
+        [((height, x), F32) for x in (q_columns, kv_columns, kv_columns, q_columns)]
+        + [((1, x // devices), F32) for x in (width, width, width, KV_WIDTH, KV_WIDTH)],
+    )
+    vectors = [x[0] for x in vectors]
 
     links.label = "final_core"
-    links.label = "final_core"
-    low, high = reduce_end(ff_terms, ff_first, ff_second)
-    mine = jnp.where(even, low, high)
-    got = links.core(jnp.where(even, high, low).astype(BF16)).astype(F32)
-    ff_grads = jnp.concatenate([jnp.where(even, mine, got), jnp.where(even, got, mine)], axis=2)
-    grad_gate, grad_up, grad_down = ff_grads[0], ff_grads[1], jnp.transpose(ff_grads[2])
+    hidden = 2 * ff_mine.shape[2]
+    grad_gate, grad_up, grad_down = small_call(
+        join_cores_kernel,
+        (ff_mine, after(links.core(ff_send), *sends)),
+        [((height, hidden), F32), ((height, hidden), F32), ((hidden, height), F32)],
+        place=place,
+        cost=2*10**9,
+    )
 
     return (
         layer_out[None],
         grad_stream[None],
         vectors[0],
-        grad_packed[:, :q_columns],
+        grad_q,
         vectors[2],
-        grad_packed[:, q_columns : q_columns + kv_columns],
+        grad_k,
         vectors[3],
-        grad_packed[:, q_columns + kv_columns :],
+        grad_v,
         vectors[4],
         grad_o,
         vectors[1],

time: 476 us -> 439 us (0.922)
  waiting for transfers between devices: 230 us -> 192 us
  Pallas kernels: 93.6 us -> 124 us
  other arithmetic: 35.9 us -> 16.1 us
    pallas_call x0 -> x6, Pallas kernels: none -> 28.5 us  [the longest x4 17.2 us: small_call(): pl.pallas_call(body, in_specs=[pl.BlockSpec(memory_space=pltpu.SMEM)] * l...]
    ppermute x52 -> x43, waiting for transfers between devices: 216 us -> 190 us  [send(): return lax.ppermute(x, BOTH, pairs)]
    unnamed x105 -> x101, local copies, waits for them, and re-layouts: 11.1 us -> 22.6 us
    convert_element_type x5 -> x2, other arithmetic: 13 us -> 4.48 us  [added(): return (a.astype(F32) + b.astype(F32)).astype(BF16)]
    reduce_scatter x1, waiting for transfers between devices: 5.59 us -> 0.01 us  [per_device_plane_of_four(): lax.psum_scatter(after(added(down_a, down_got), normed_rows), 'ctx', scat...]
    convert_element_type x1 -> x0, other arithmetic: 4.98 us -> none  [per_device_plane_of_four(): got = links.core(jnp.where(even, high, low).astype(BF16)).astype(F32)]
    reduce_scatter x1, waiting for transfers between devices: 5.92 us -> 0.98 us  [per_device_plane_of_four(): y_sum = lax.psum_scatter(y_both, 'ctx', scatter_dimension=0, tiled=True)]
    select_n x1 -> x0, other arithmetic: 4.88 us -> none  [per_device_plane_of_four(): jnp.where(even, got, mine)]
  transfers between devices with their start and end apart: 57 -> 49, of which waited for: 31 -> 21; matrix products, arithmetic and copies ran while one was open for 12% -> 5% of each run, Pallas kernels for 16% -> 28%
where the time goes in v3:
time: 439 us; the launch traced here: 430 us
  waiting for transfers between devices  192 us (44%)
  Pallas kernels  124 us (28%)
  starting transfers between devices  57.1 us (13%)
  local copies, waits for them, and re-layouts  26.9 us (6%)
  other arithmetic  16.1 us (4%)
  between operations  15.2 us (3%)
    ppermute x43, waiting for transfers between devices, send(): return lax.ppermute(x, BOTH, pairs)  190 us
    ppermute x43, starting transfers between devices, send(): return lax.ppermute(x, BOTH, pairs)  56.5 us
    pallas_call x2, Pallas kernels, feed_forward(): pl.pallas_call(body, grid_spec=pltpu.PrefetchScalarGridSpec(num_scalar_pr...  37.7 us
    pallas_call x4, Pallas kernels, call(): pl.pallas_call(kernel, in_specs=[pl.BlockSpec(memory_space=pltpu.SMEM)] +...  30.3 us
    pallas_call x2, Pallas kernels, ff_grad_terms(): pl.pallas_call(grad_kernel, grid_spec=pltpu.PrefetchScalarGridSpec(num_sc...  25.8 us
    unnamed x101, local copies, waits for them, and re-layouts  22.6 us
    pallas_call x4, Pallas kernels, small_call(): pl.pallas_call(body, in_specs=[pl.BlockSpec(memory_space=pltpu.SMEM)] * l...  17.2 us
  transfers between devices with their start and end apart: 49, of which 21 were waited for; matrix products, arithmetic and copies ran while one was open for 5% of the time, Pallas kernels for 28%

profile of v3, /device:TPU:0, one launch (start us, length us, event | category | flops | bytes accessed | tf_op | source)
XLA Modules:
  0.0 430.4 jit_solution(4643255252350145098)
XLA Ops:
  12.9 2.7 collective-permute-start
  15.6 2.6 collective-permute-start.1
  18.2 1.3 collective-permute-start.2
  19.5 7.4 %collective-permute-done = bf16[48,3712]{1,0:T(8,128)(2,1)S(1)} collective-permute-done((bf16[48,3712]{1,0:T(8,128)(2,1)S(1)}, bf16[48,3712]{1,0:T(8,128)(2,1)S(1)}, u32[]{:S(2)}, u32[]{:S(2)}) %collective-permute-start) | collective-permute-done | bytes 356384 | tf_op jit(solution)/shard_map/qkvo_ctx/ppermute | solution.py:73
  26.9 15.1 %collective-permute-done.1 = bf16[48,3712]{1,0:T(8,128)(2,1)} collective-permute-done((bf16[48,3712]{1,0:T(8,128)(2,1)S(1)}, bf16[48,3712]{1,0:T(8,128)(2,1)}, u32[]{:S(2)}, u32[]{:S(2)}) %collective-permute-start.1) | collective-permute-done | bytes 356384 | tf_op jit(solution)/shard_map/qkvo_ctx/ppermute | solution.py:73
  42.1 1.3 pad_maximum_fusion.1.refs_3_.refs_8_.refs_12_
  43.4 1.6 collective-permute-start.4
  44.9 1.5 collective-permute-start.5
  46.4 1.5 broadcast_select_fusion.1
  48.1 8.2 %collective-permute-start.6 = (bf16[2,3,48,1120]{3,2,1,0:T(8,128)(2,1)S(1)}, bf16[2,3,48,1120]{3,2,1,0:T(8,128)(2,1)S(1)}, u32[]{:S(2)}, u32[]{:S(2)}) collective-permute-start(bf16[2,3,48,1120]{3,2,1,0:T(8,128)(2,1)S(1)} %pad_maximum_fusion.4), channel_id=1, source_target_pairs={{0,8},{1,9},{2,10},{3,11},{4,12},{5,13},{6,14},{7,15},{8,16},{9,17... | collective-permute-start | bytes 1935368 | tf_op jit(solution)/shard_map/ff_ctx_a/ppermute | solution.py:73
  57.6 15.5 %collective-permute-done.6 = bf16[2,3,48,1120]{3,2,1,0:T(8,128)(2,1)S(1)} collective-permute-done((bf16[2,3,48,1120]{3,2,1,0:T(8,128)(2,1)S(1)}, bf16[2,3,48,1120]{3,2,1,0:T(8,128)(2,1)S(1)}, u32[]{:S(2)}, u32[]{:S(2)}) %collective-permute-start.6) | collective-permute-done | bytes 645152 | tf_op jit(solution)/shard_map/ff_ctx_a/ppermute | solution.py:73
  73.1 14.0 %collective-permute-done.7 = bf16[2,3,48,1120]{3,2,1,0:T(8,128)(2,1)S(1)} collective-permute-done((bf16[2,3,48,1120]{3,2,1,0:T(8,128)(2,1)S(1)}, bf16[2,3,48,1120]{3,2,1,0:T(8,128)(2,1)S(1)}, u32[]{:S(2)}, u32[]{:S(2)}) %collective-permute-start.7) | collective-permute-done | bytes 645152 | tf_op jit(solution)/shard_map/ff_ctx_a/ppermute | solution.py:73
  90.2 1.5 collective-permute-start.12
  91.7 1.5 collective-permute-start.13
  93.2 27.8 %collective-permute-done.9 = bf16[2,3,48,1120]{3,2,1,0:T(8,128)(2,1)S(1)} collective-permute-done((bf16[2,3,48,1120]{3,2,1,0:T(8,128)(2,1)S(1)}, bf16[2,3,48,1120]{3,2,1,0:T(8,128)(2,1)S(1)}, u32[]{:S(2)}, u32[]{:S(2)}) %collective-permute-start.9) | collective-permute-done | bytes 645152 | tf_op jit(solution)/shard_map/ff_ctx_b/ppermute | solution.py:73
  121.8 2.5 pad_maximum_fusion
  127.2 1.5 collective-permute-start.19
  128.7 1.5 collective-permute-start.18
  132.0 6.0 %shard_map.255 = (bf16[128,1536]{1,0:T(8,128)(2,1)}, bf16[128,1536]{1,0:T(8,128)(2,1)}, bf16[128,512]{1,0:T(8,128)(2,1)}, f32[8,1536]{1,0:T(8,128)}) custom-call(s32[3]{0:T(128)} %copy-done.3, bf16[128,1536]{1,0:T(8,128)(2,1)} %bitcast.29, f32[128,128]{1,0:T(8,128)} %get-tuple-element.247.refs_1_.refs_6_, f32[128,128]{1,0:T(8,128)} %get-tuple-element.248.refs_2_.refs_7_, ...), custom_call_target="tpu_custom_call" | custom-call | tf_op jit(solution)/shard_map/pallas_call | solution.py:680
  138.0 2.0 collective-permute-start.15
  140.0 4.8 %collective-permute-start.16 = (bf16[128,512]{1,0:T(8,128)(2,1)}, bf16[128,512]{1,0:T(8,128)(2,1)}, u32[]{:S(2)}, u32[]{:S(2)}) collective-permute-start(bf16[128,512]{1,0:T(8,128)(2,1)} %get-tuple-element.129.refs_4_.refs_8_), channel_id=1, source_target_pairs={{0,16},{1,17},{2,18},{3,19},{4,20},{5,21},{6,22},{7,23},{8,24},{9,... | collective-permute-start | bytes 393224 | tf_op jit(solution)/shard_map/kv/ppermute | solution.py:73
  144.8 1.9 collective-permute-start.17
  147.4 5.1 %collective-permute-done.16.refs_6_.refs_10_ = bf16[128,512]{1,0:T(8,128)(2,1)} collective-permute-done((bf16[128,512]{1,0:T(8,128)(2,1)}, bf16[128,512]{1,0:T(8,128)(2,1)}, u32[]{:S(2)}, u32[]{:S(2)}) %collective-permute-start.16) | collective-permute-done | bytes 131104 | tf_op jit(solution)/shard_map/kv/ppermute | solution.py:73
  152.5 5.3 %collective-permute-done.17.refs_7_.refs_11_ = bf16[128,512]{1,0:T(8,128)(2,1)} collective-permute-done((bf16[128,512]{1,0:T(8,128)(2,1)}, bf16[128,512]{1,0:T(8,128)(2,1)}, u32[]{:S(2)}, u32[]{:S(2)}) %collective-permute-start.17) | collective-permute-done | bytes 131104 | tf_op jit(solution)/shard_map/kv/ppermute | solution.py:73
  157.9 5.8 %shard_map.256 = (bf16[128,1536]{1,0:T(8,128)(2,1)}, f32[128,1536]{1,0:T(8,128)}, bf16[128,1536]{1,0:T(8,128)(2,1)}) custom-call(s32[3]{0:T(128)} %copy-done.3, bf16[128,1536]{1,0:T(8,128)(2,1)} %bitcast.30, f32[8,1536]{1,0:T(8,128)} %get-tuple-element.127.refs_1_.refs_2_.refs_5_, s32[128,1]{1,0:T(8,128)} %copy.40.refs_2_.refs_4_, ...), custom_call_target="tpu_custom_call" | custom-call | tf_op jit(solution)/shard_map/pallas_call | solution.py:680
  163.8 9.3 %collective-permute-done.19.refs_8_ = bf16[6,3,48,1120]{3,2,1,0:T(8,128)(2,1)S(1)} collective-permute-done((bf16[6,3,48,1120]{3,2,1,0:T(8,128)(2,1)}, bf16[6,3,48,1120]{3,2,1,0:T(8,128)(2,1)S(1)}, u32[]{:S(2)}, u32[]{:S(2)}) %collective-permute-start.19) | collective-permute-done | bytes 1935392 | tf_op jit(solution)/shard_map/ff_plane1/ppermute | solution.py:73
  173.2 1.4 pad_maximum_fusion.2
  174.9 1.5 collective-permute-start.20
  176.4 2.3 slice.25
  178.7 1.4 pad_maximum_fusion.3
  180.1 1.6 collective-permute-start.21
  181.7 24.3 %collective-permute-done.20.refs_9_ = bf16[4,3,48,1120]{3,2,1,0:T(8,128)(2,1)S(1)} collective-permute-done((bf16[4,3,48,1120]{3,2,1,0:T(8,128)(2,1)}, bf16[4,3,48,1120]{3,2,1,0:T(8,128)(2,1)S(1)}, u32[]{:S(2)}, u32[]{:S(2)}) %collective-permute-start.20) | collective-permute-done | bytes 1290272 | tf_op jit(solution)/shard_map/ff_plane2/ppermute | solution.py:73
  206.0 5.8 %collective-permute-done.21.refs_10_ = bf16[4,3,48,1120]{3,2,1,0:T(8,128)(2,1)} collective-permute-done((bf16[4,3,48,1120]{3,2,1,0:T(8,128)(2,1)S(1)}, bf16[4,3,48,1120]{3,2,1,0:T(8,128)(2,1)}, u32[]{:S(2)}, u32[]{:S(2)}) %collective-permute-start.21) | collective-permute-done | bytes 1290272 | tf_op jit(solution)/shard_map/ff_plane2/ppermute | solution.py:73
  212.2 18.7 %shard_map.257 = (bf16[512,1120]{1,0:T(8,128)(2,1)}, bf16[512,1120]{1,0:T(8,128)(2,1)}, bf16[512,1120]{1,0:T(8,128)(2,1)}, bf16[512,1536]{1,0:T(8,128)(2,1)}, bf16[512,1536]{1,0:T(8,128)(2,1)}) custom-call(s32[3]{0:T(128)} %copy-done.3, bf16[512,1536]{1,0:T(8,128)(2,1)} %all-gather.5.cloned.1.call-done.refs_1_.refs_0_.refs_2_, ...), custom_call_target="tpu_custom_call" | custom-call | tf_op jit(solution)/shard_map/pallas_call | solution.py:435
  232.1 18.9 %shard_map.258 = (bf16[512,1120]{1,0:T(8,128)(2,1)}, bf16[512,1120]{1,0:T(8,128)(2,1)}, bf16[512,1120]{1,0:T(8,128)(2,1)}, bf16[512,1536]{1,0:T(8,128)(2,1)}, bf16[512,1536]{1,0:T(8,128)(2,1)}) custom-call(s32[3]{0:T(128)} %copy-done.3, bf16[512,1536]{1,0:T(8,128)(2,1)} %copy-done.5, bf16[512,1536]{1,0:T(8,128)(2,1)} %copy-done.4, ...), custom_call_target="tpu_custom_call" | custom-call | tf_op jit(solution)/shard_map/pallas_call | solution.py:435
  251.5 3.2 collective-permute-done.24
  254.8 1.5 add_convert_fusion
  258.1 13.0 %shard_map.259 = (bf16[2,1,192,1120]{3,2,1,0:T(8,128)(2,1)}, bf16[2,2,192,1120]{3,2,1,0:T(8,128)(2,1)}, bf16[2,1,192,1120]{3,2,1,0:T(8,128)(2,1)}, bf16[2,2,192,1120]{3,2,1,0:T(8,128)(2,1)}) custom-call(s32[3]{0:T(128)} %copy-done.3, bf16[512,1536]{1,0:T(8,128)(2,1)} %all-gather.5.cloned.1.call-done.refs_1_.refs_0_.refs_2_, bf16[512,1536]{1,0:T(8,128)(2,1)} %copy-done.5, ...), custom_call_target="tpu_custom_call" | custom-call | tf_op jit(solution)/shard_map/pallas_call | solution.py:482
  271.1 1.6 collective-permute-start.26
  272.9 12.8 %shard_map.260 = (bf16[2,3,192,1120]{3,2,1,0:T(8,128)(2,1)}, bf16[2,3,192,1120]{3,2,1,0:T(8,128)(2,1)}) custom-call(s32[3]{0:T(128)} %copy-done.3, bf16[512,1536]{1,0:T(8,128)(2,1)} %all-gather.5.cloned.1.call-done.refs_1_.refs_0_.refs_2_, bf16[512,1536]{1,0:T(8,128)(2,1)} %copy-done.5, ...), custom_call_target="tpu_custom_call" | custom-call | tf_op jit(solution)/shard_map/pallas_call | solution.py:482
  285.8 7.4 %collective-permute-done.26.refs_1_ = bf16[2,1,192,1120]{3,2,1,0:T(8,128)(2,1)} collective-permute-done((bf16[2,1,192,1120]{3,2,1,0:T(8,128)(2,1)}, bf16[2,1,192,1120]{3,2,1,0:T(8,128)(2,1)}, u32[]{:S(2)}, u32[]{:S(2)}) %collective-permute-start.26) | collective-permute-done | bytes 860192 | tf_op jit(solution)/shard_map/ff_sum1/ppermute | solution.py:73
  295.4 10.0 %shard_map.261 = (f32[128,1536]{1,0:T(8,128)}, bf16[128,1536]{1,0:T(8,128)(2,1)}, bf16[128,1536]{1,0:T(8,128)(2,1)}, f32[1,1536]{1,0:T(1,128)}, bf16[128,512]{1,...) custom-call(s32[3]{0:T(128)} %copy-done.3, ...), custom_call_target="tpu_custom_call" | custom-call | flops 8000000000 | tf_op jit(solution)/shard_map/pallas_call | solution.py:680
  308.0 1.5 collective-permute-start.30
  309.6 8.9 %collective-permute-done.28.refs_1_ = bf16[128,512]{1,0:T(8,128)(2,1)S(1)} collective-permute-done((bf16[128,512]{1,0:T(8,128)(2,1)}, bf16[128,512]{1,0:T(8,128)(2,1)S(1)}, u32[]{:S(2)}, u32[]{:S(2)}) %collective-permute-start.28) | collective-permute-done | bytes 131104 | tf_op jit(solution)/shard_map/gkv/ppermute | solution.py:73
  318.5 16.4 %collective-permute-done.29.refs_2_ = bf16[128,512]{1,0:T(8,128)(2,1)S(1)} collective-permute-done((bf16[128,512]{1,0:T(8,128)(2,1)}, bf16[128,512]{1,0:T(8,128)(2,1)S(1)}, u32[]{:S(2)}, u32[]{:S(2)}) %collective-permute-start.29) | collective-permute-done | bytes 131104 | tf_op jit(solution)/shard_map/gkv/ppermute | solution.py:73
  335.6 8.5 %shard_map.262 = (f32[128,1536]{1,0:T(8,128)}, bf16[144,896]{1,0:T(8,128)(2,1)}, bf16[144,896]{1,0:T(8,128)(2,1)}, bf16[144,896]{1,0:T(8,128)(2,1)}, bf16[144,896]{1,0:T(8,128)(2,1)}) custom-call(s32[3]{0:T(128)} %copy-done.3, bf16[128,512]{1,0:T(8,128)(2,1)} %get-tuple-element.162.refs_0_, bf16[128,512]{1,0:T(8,128)(2,1)} %copy-done.31, ...), custom_call_target="tpu_custom_call" | custom-call | tf_op jit(solution)/shard_map/pallas_call | solution.py:680
  344.3 3.7 collective-permute-start.33
  349.8 4.5 %shard_map.264 = (bf16[3,192,1120]{2,1,0:T(8,128)(2,1)}, bf16[3,192,1120]{2,1,0:T(8,128)(2,1)}) custom-call(bf16[2,3,192,1120]{3,2,1,0:T(8,128)(2,1)} %get-tuple-element.160.refs_0_, bf16[2,1,192,1120]{3,2,1,0:T(8,128)(2,1)} %collective-permute-done.26.refs_1_, bf16[2,2,192,1120]{3,2,1,0:T(8,128)(2,1)} %copy-done.17, ...), custom_call_target="tpu_custom_call" | custom-call | tf_op jit(solution)/shard_map/pallas_call | solution.py:523
  354.3 1.5 collective-permute-start.36
  356.5 2.9 add_convert_fusion.1
  359.4 4.1 collective-permute-done.32.refs_2_
  363.6 6.0 %shard_map.263 = (bf16[4,208,896]{2,1,0:T(8,128)(2,1)}, bf16[4,208,896]{2,1,0:T(8,128)(2,1)}) custom-call(s32[3]{0:T(128)} %copy-done.3, bf16[144,896]{1,0:T(8,128)(2,1)} %get-tuple-element.176.refs_0_, bf16[144,896]{1,0:T(8,128)(2,1)} %collective-permute-done.31.refs_1_, bf16[144,896]{1,0:T(8,128)(2,1)} %collective-permute-done.32.refs_2_, ...), custom_call_target="tpu_custom_call" | custom-call | tf_op jit(solution)/shard_map/pallas_call | solution.py:922
  369.6 13.2 %collective-permute-done.36.refs_3_ = bf16[3,192,1120]{2,1,0:T(8,128)(2,1)S(1)} collective-permute-done((bf16[3,192,1120]{2,1,0:T(8,128)(2,1)}, bf16[3,192,1120]{2,1,0:T(8,128)(2,1)S(1)}, u32[]{:S(2)}, u32[]{:S(2)}) %collective-permute-start.36) | collective-permute-done | bytes 1290272 | tf_op jit(solution)/shard_map/ff_sum2/ppermute | solution.py:73
  385.0 6.9 %shard_map.265 = (f32[3,192,1120]{2,1,0:T(8,128)}, bf16[3,192,1120]{2,1,0:T(8,128)(2,1)}) custom-call(s32[3]{0:T(128)} %copy-done.3, bf16[2,3,192,1120]{3,2,1,0:T(8,128)(2,1)} %get-tuple-element.160.refs_0_, bf16[2,1,192,1120]{3,2,1,0:T(8,128)(2,1)} %collective-permute-done.26.refs_1_, bf16[2,2,192,1120]{3,2,1,0:T(8,128)(2,1)} %copy-done.17, ...), custom_call_target="tpu_custom_call" | custom-call | flops 12000000000 | tf_op jit(solution)/shard_map/pallas_call | solution.py:562
  393.0 3.2 shard_map.266
  396.2 1.4 collective-permute-start.39
  398.1 1.6 collective-permute-start.41
  400.7 2.0 add_bitcast_fusion
  403.7 5.6 %shard_map.268 = (f32[192,2240]{1,0:T(8,128)}, f32[192,2240]{1,0:T(8,128)}, f32[2240,192]{1,0:T(8,128)}) custom-call(s32[3]{0:T(128)} %copy-done.3, f32[3,192,1120]{2,1,0:T(8,128)} %get-tuple-element.203.mine, bf16[3,192,1120]{2,1,0:T(8,128)(2,1)} %copy-done.45), custom_call_target="tpu_custom_call" | custom-call | flops 2000000000 | tf_op jit(solution)/shard_map/pallas_call | solution.py:922
  409.3 2.9 copy.44
  412.2 4.4 %collective-permute-done.40.refs_1_ = bf16[208,896]{1,0:T(8,128)(2,1)S(1)} collective-permute-done((bf16[208,896]{1,0:T(8,128)(2,1)}, bf16[208,896]{1,0:T(8,128)(2,1)S(1)}, u32[]{:S(2)}, u32[]{:S(2)}) %collective-permute-start.40) | collective-permute-done | bytes 372768 | tf_op jit(solution)/shard_map/term_plane/ppermute | solution.py:73
  417.5 2.4 shard_map.267
  419.9 1.6 copy.42
  421.5 1.6 copy.43
  (187 shorter events, 35.6 us)
Async XLA Ops:
  7.2 5.6 %copy-start.34 = (bf16[48,256]{1,0:T(8,128)(2,1)S(1)}, bf16[48,256]{1,0:T(8,128)(2,1)}, u32[]{:S(2)}) copy-start(bf16[48,256]{1,0:T(8,128)(2,1)} %param.20) | copy-start | bytes 73732
  7.2 5.6 %copy-start.35 = (bf16[48,256]{1,0:T(8,128)(2,1)S(1)}, bf16[48,256]{1,0:T(8,128)(2,1)}, u32[]{:S(2)}) copy-start(bf16[48,256]{1,0:T(8,128)(2,1)} %param.22) | copy-start | bytes 73732
  7.3 171.4 %all-gather.7.cloned.1.call-start = ((), (), s32[]{:S(2)}) async-start(), calls=%async_computation.3 | async-start | bytes 1966080 | tf_op jit(solution)/shard_map/all_gather | solution.py:1046
  12.1 30.0 %collective-permute-start.3 = (bf16[4,3,48,1120]{3,2,1,0:T(8,128)(2,1)S(1)}, bf16[4,3,48,1120]{3,2,1,0:T(8,128)(2,1)}, u32[]{:S(2)}, u32[]{:S(2)}) collective-permute-start(bf16[4,3,48,1120]{3,2,1,0:T(8,128)(2,1)S(1)} %get-tuple-element.112), channel_id=1, source_target_pairs={{0,1},{1,0},{2,3},{3,2},{4,5},{5,4},{6,7},{7,6},{8,9},{9,8},{10,11... | collective-permute-start | bytes 3870728 | tf_op jit(solution)/shard_map/ff_core/ppermute | solution.py:73
  12.9 14.0 %collective-permute-start = (bf16[48,3712]{1,0:T(8,128)(2,1)S(1)}, bf16[48,3712]{1,0:T(8,128)(2,1)S(1)}, u32[]{:S(2)}, u32[]{:S(2)}) collective-permute-start(bf16[48,3712]{1,0:T(8,128)(2,1)S(1)} %constant_dynamic-update-slice_fusion), channel_id=1, source_target_pairs={{0,8},{1,9},{2,10},{3,11},{4,12},{5,13},{6,14},{7,15},{8,16},{9,17... | collective-permute-start | bytes 1069064 | tf_op jit(solution)/shard_map/qkvo_ctx/ppermute | solution.py:73
  15.6 26.5 %collective-permute-start.1 = (bf16[48,3712]{1,0:T(8,128)(2,1)S(1)}, bf16[48,3712]{1,0:T(8,128)(2,1)}, u32[]{:S(2)}, u32[]{:S(2)}) collective-permute-start(bf16[48,3712]{1,0:T(8,128)(2,1)S(1)} %constant_dynamic-update-slice_fusion), channel_id=1, source_target_pairs={{0,16},{1,17},{2,18},{3,19},{4,20},{5,21},{6,22},{7,23},{8,24},{9,... | collective-permute-start | bytes 1069064 | tf_op jit(solution)/shard_map/qkvo_ctx/ppermute | solution.py:73
  18.2 23.9 %collective-permute-start.2 = (bf16[48,3712]{1,0:T(8,128)(2,1)S(1)}, bf16[48,3712]{1,0:T(8,128)(2,1)}, u32[]{:S(2)}, u32[]{:S(2)}) collective-permute-start(bf16[48,3712]{1,0:T(8,128)(2,1)S(1)} %constant_dynamic-update-slice_fusion), channel_id=1, source_target_pairs={{0,24},{1,25},{2,26},{3,27},{4,28},{5,29},{6,30},{7,31},{8,0},{9,1... | collective-permute-start | bytes 1069064 | tf_op jit(solution)/shard_map/qkvo_ctx/ppermute | solution.py:73
  43.4 43.7 %collective-permute-start.4 = (bf16[4,48,3712]{2,1,0:T(8,128)(2,1)S(1)}, bf16[4,48,3712]{2,1,0:T(8,128)(2,1)S(1)}, u32[]{:S(2)}, u32[]{:S(2)}) collective-permute-start(bf16[4,48,3712]{2,1,0:T(8,128)(2,1)S(1)} %pad_maximum_fusion.1.refs_3_.refs_8_.refs_12_), channel_id=1, source_target_pairs={{0,2},{1,3},{2,0},{3,1},{4,6},{5,7},{6,4},{7,5},{8,10},{9,11},{10,... | collective-permute-start | bytes 4276232 | tf_op jit(solution)/shard_map/qkvo_plane1/ppermute | solution.py:73
  44.9 42.2 %collective-permute-start.5 = (bf16[4,48,3712]{2,1,0:T(8,128)(2,1)S(1)}, bf16[4,48,3712]{2,1,0:T(8,128)(2,1)S(1)}, u32[]{:S(2)}, u32[]{:S(2)}) collective-permute-start(bf16[4,48,3712]{2,1,0:T(8,128)(2,1)S(1)} %pad_maximum_fusion.1.refs_3_.refs_8_.refs_12_), channel_id=1, source_target_pairs={{0,4},{1,5},{2,6},{3,7},{4,0},{5,1},{6,2},{7,3},{8,12},{9,13},{10,... | collective-permute-start | bytes 4276232 | tf_op jit(solution)/shard_map/qkvo_plane1/ppermute | solution.py:73
  46.4 40.7 %collective-permute-start.8 = (bf16[4,48,3712]{2,1,0:T(8,128)(2,1)S(1)}, bf16[4,48,3712]{2,1,0:T(8,128)(2,1)S(1)}, u32[]{:S(2)}, u32[]{:S(2)}) collective-permute-start(bf16[4,48,3712]{2,1,0:T(8,128)(2,1)S(1)} %pad_maximum_fusion.1.refs_3_.refs_8_.refs_12_), channel_id=1, source_target_pairs={{0,1},{1,0},{2,3},{3,2},{4,5},{5,4},{6,7},{7,6},{8,9},{9,8},{10,11... | collective-permute-start | bytes 4276232 | tf_op jit(solution)/shard_map/qkvo_core/ppermute | solution.py:73
  48.1 25.0 %collective-permute-start.6 = (bf16[2,3,48,1120]{3,2,1,0:T(8,128)(2,1)S(1)}, bf16[2,3,48,1120]{3,2,1,0:T(8,128)(2,1)S(1)}, u32[]{:S(2)}, u32[]{:S(2)}) collective-permute-start(bf16[2,3,48,1120]{3,2,1,0:T(8,128)(2,1)S(1)} %pad_maximum_fusion.4), channel_id=1, source_target_pairs={{0,8},{1,9},{2,10},{3,11},{4,12},{5,13},{6,14},{7,15},{8,16},{9,17... | collective-permute-start | bytes 1935368 | tf_op jit(solution)/shard_map/ff_ctx_a/ppermute | solution.py:73
  56.4 30.7 %collective-permute-start.7 = (bf16[2,3,48,1120]{3,2,1,0:T(8,128)(2,1)S(1)}, bf16[2,3,48,1120]{3,2,1,0:T(8,128)(2,1)S(1)}, u32[]{:S(2)}, u32[]{:S(2)}) collective-permute-start(bf16[2,3,48,1120]{3,2,1,0:T(8,128)(2,1)S(1)} %pad_maximum_fusion.5), channel_id=1, source_target_pairs={{0,24},{1,25},{2,26},{3,27},{4,28},{5,29},{6,30},{7,31},{8,0},{9,1... | collective-permute-start | bytes 1935368 | tf_op jit(solution)/shard_map/ff_ctx_a/ppermute | solution.py:73
  57.6 63.3 %copy-start.13 = (bf16[2,3,48,1120]{3,2,1,0:T(8,128)(2,1)}, bf16[2,3,48,1120]{3,2,1,0:T(8,128)(2,1)S(1)}, u32[]{:S(2)}) copy-start(bf16[2,3,48,1120]{3,2,1,0:T(8,128)(2,1)S(1)} %pad_maximum_fusion.7.refs_3_) | copy-start | bytes 1935364
  87.1 37.1 %copy-start.6 = (bf16[4,48,3712]{2,1,0:T(8,128)(2,1)}, bf16[4,48,3712]{2,1,0:T(8,128)(2,1)S(1)}, u32[]{:S(2)}) copy-start(bf16[4,48,3712]{2,1,0:T(8,128)(2,1)S(1)} %collective-permute-done.4.refs_4_.refs_9_.refs_13_) | copy-start | bytes 4276228
  87.1 37.1 %copy-start.7 = (bf16[4,48,3712]{2,1,0:T(8,128)(2,1)}, bf16[4,48,3712]{2,1,0:T(8,128)(2,1)S(1)}, u32[]{:S(2)}) copy-start(bf16[4,48,3712]{2,1,0:T(8,128)(2,1)S(1)} %collective-permute-done.5.refs_5_.refs_10_.refs_14_) | copy-start | bytes 4276228
  88.3 32.6 %collective-permute-start.10 = (bf16[2,48,3712]{2,1,0:T(8,128)(2,1)S(1)}, bf16[2,48,3712]{2,1,0:T(8,128)(2,1)S(1)}, u32[]{:S(2)}, u32[]{:S(2)}) collective-permute-start(bf16[2,48,3712]{2,1,0:T(8,128)(2,1)S(1)} %slice.18), channel_id=1, source_target_pairs={{0,2},{1,3},{2,0},{3,1},{4,6},{5,7},{6,4},{7,5},{8,10},{9,11},{10,... | collective-permute-start | bytes 2138120 | tf_op jit(solution)/shard_map/qkvo_plane2/ppermute | solution.py:73
  89.0 32.8 %collective-permute-start.11 = (bf16[2,48,3712]{2,1,0:T(8,128)(2,1)S(1)}, bf16[2,48,3712]{2,1,0:T(8,128)(2,1)S(1)}, u32[]{:S(2)}, u32[]{:S(2)}) collective-permute-start(bf16[2,48,3712]{2,1,0:T(8,128)(2,1)S(1)} %slice.19), channel_id=1, source_target_pairs={{0,4},{1,5},{2,6},{3,7},{4,0},{5,1},{6,2},{7,3},{8,12},{9,13},{10,... | collective-permute-start | bytes 2138120 | tf_op jit(solution)/shard_map/qkvo_plane2/ppermute | solution.py:73
  89.6 31.4 %collective-permute-start.9 = (bf16[2,3,48,1120]{3,2,1,0:T(8,128)(2,1)S(1)}, bf16[2,3,48,1120]{3,2,1,0:T(8,128)(2,1)S(1)}, u32[]{:S(2)}, u32[]{:S(2)}) collective-permute-start(bf16[2,3,48,1120]{3,2,1,0:T(8,128)(2,1)S(1)} %pad_maximum_fusion.6), channel_id=1, source_target_pairs={{0,16},{1,17},{2,18},{3,19},{4,20},{5,21},{6,22},{7,23},{8,24},{9,... | collective-permute-start | bytes 1935368 | tf_op jit(solution)/shard_map/ff_ctx_b/ppermute | solution.py:73
  90.2 30.8 %collective-permute-start.12 = (bf16[2,3,48,1120]{3,2,1,0:T(8,128)(2,1)S(1)}, bf16[2,3,48,1120]{3,2,1,0:T(8,128)(2,1)S(1)}, u32[]{:S(2)}, u32[]{:S(2)}) collective-permute-start(bf16[2,3,48,1120]{3,2,1,0:T(8,128)(2,1)S(1)} %pad_maximum_fusion.7.refs_3_), channel_id=1, source_target_pairs={{0,2},{1,3},{2,0},{3,1},{4,6},{5,7},{6,4},{7,5},{8,10},{9,11},{10,... | collective-permute-start | bytes 1935368 | tf_op jit(solution)/shard_map/ff_own1/ppermute | solution.py:73
  91.7 29.3 %collective-permute-start.13 = (bf16[2,3,48,1120]{3,2,1,0:T(8,128)(2,1)S(1)}, bf16[2,3,48,1120]{3,2,1,0:T(8,128)(2,1)S(1)}, u32[]{:S(2)}, u32[]{:S(2)}) collective-permute-start(bf16[2,3,48,1120]{3,2,1,0:T(8,128)(2,1)S(1)} %pad_maximum_fusion.7.refs_3_), channel_id=1, source_target_pairs={{0,4},{1,5},{2,6},{3,7},{4,0},{5,1},{6,2},{7,3},{8,12},{9,13},{10,... | collective-permute-start | bytes 1935368 | tf_op jit(solution)/shard_map/ff_own1/ppermute | solution.py:73
  120.9 42.8 %copy-start.15 = (bf16[2,3,48,1120]{3,2,1,0:T(8,128)(2,1)}, bf16[2,3,48,1120]{3,2,1,0:T(8,128)(2,1)S(1)}, u32[]{:S(2)}) copy-start(bf16[2,3,48,1120]{3,2,1,0:T(8,128)(2,1)S(1)} %collective-permute-done.12.refs_4_) | copy-start | bytes 1935364
  120.9 42.8 %copy-start.16 = (bf16[2,3,48,1120]{3,2,1,0:T(8,128)(2,1)}, bf16[2,3,48,1120]{3,2,1,0:T(8,128)(2,1)S(1)}, u32[]{:S(2)}) copy-start(bf16[2,3,48,1120]{3,2,1,0:T(8,128)(2,1)S(1)} %collective-permute-done.13.refs_5_) | copy-start | bytes 1935364
  124.3 7.7 %collective-permute-start.14 = (bf16[12,48,3712]{2,1,0:T(8,128)(2,1)}, bf16[12,48,3712]{2,1,0:T(8,128)(2,1)}, u32[]{:S(2)}, u32[]{:S(2)}) collective-permute-start(bf16[12,48,3712]{2,1,0:T(8,128)(2,1)} %pad_maximum_fusion), channel_id=1, source_target_pairs={{0,1},{1,0},{2,3},{3,2},{4,5},{5,4},{6,7},{7,6},{8,9},{9,8},{10,11... | collective-permute-start | bytes 12828680 | tf_op jit(solution)/shard_map/qkvo_core/ppermute | solution.py:73
  124.4 87.5 %all-gather.5.cloned.1.call-start = ((), (), s32[]{:S(2)}) async-start(), calls=%async_computation.2 | async-start | bytes 1966080 | tf_op jit(solution)/shard_map/all_gather | solution.py:1047
  127.2 46.0 %collective-permute-start.19 = (bf16[6,3,48,1120]{3,2,1,0:T(8,128)(2,1)}, bf16[6,3,48,1120]{3,2,1,0:T(8,128)(2,1)S(1)}, u32[]{:S(2)}, u32[]{:S(2)}) collective-permute-start(bf16[6,3,48,1120]{3,2,1,0:T(8,128)(2,1)} %constant_dynamic-update-slice_fusion.5.refs_6_), channel_id=1, source_target_pairs={{0,4},{1,5},{2,6},{3,7},{4,0},{5,1},{6,2},{7,3},{8,12},{9,13},{10,... | collective-permute-start | bytes 5806088 | tf_op jit(solution)/shard_map/ff_plane1/ppermute | solution.py:73
  128.7 47.7 %collective-permute-start.18 = (bf16[6,3,48,1120]{3,2,1,0:T(8,128)(2,1)}, bf16[6,3,48,1120]{3,2,1,0:T(8,128)(2,1)}, u32[]{:S(2)}, u32[]{:S(2)}) collective-permute-start(bf16[6,3,48,1120]{3,2,1,0:T(8,128)(2,1)} %constant_dynamic-update-slice_fusion.5.refs_6_), channel_id=1, source_target_pairs={{0,2},{1,3},{2,0},{3,1},{4,6},{5,7},{6,4},{7,5},{8,10},{9,11},{10,... | collective-permute-start | bytes 5806088 | tf_op jit(solution)/shard_map/ff_plane1/ppermute | solution.py:73
  138.0 9.4 %collective-permute-start.15 = (bf16[128,512]{1,0:T(8,128)(2,1)}, bf16[128,512]{1,0:T(8,128)(2,1)S(1)}, u32[]{:S(2)}, u32[]{:S(2)}) collective-permute-start(bf16[128,512]{1,0:T(8,128)(2,1)} %get-tuple-element.129.refs_4_.refs_8_), channel_id=1, source_target_pairs={{0,8},{1,9},{2,10},{3,11},{4,12},{5,13},{6,14},{7,15},{8,16},{9,17... | collective-permute-start | bytes 393224 | tf_op jit(solution)/shard_map/kv/ppermute | solution.py:73
  140.0 12.6 %collective-permute-start.16 = (bf16[128,512]{1,0:T(8,128)(2,1)}, bf16[128,512]{1,0:T(8,128)(2,1)}, u32[]{:S(2)}, u32[]{:S(2)}) collective-permute-start(bf16[128,512]{1,0:T(8,128)(2,1)} %get-tuple-element.129.refs_4_.refs_8_), channel_id=1, source_target_pairs={{0,16},{1,17},{2,18},{3,19},{4,20},{5,21},{6,22},{7,23},{8,24},{9,... | collective-permute-start | bytes 393224 | tf_op jit(solution)/shard_map/kv/ppermute | solution.py:73
  144.8 13.1 %collective-permute-start.17 = (bf16[128,512]{1,0:T(8,128)(2,1)}, bf16[128,512]{1,0:T(8,128)(2,1)}, u32[]{:S(2)}, u32[]{:S(2)}) collective-permute-start(bf16[128,512]{1,0:T(8,128)(2,1)} %get-tuple-element.129.refs_4_.refs_8_), channel_id=1, source_target_pairs={{0,24},{1,25},{2,26},{3,27},{4,28},{5,29},{6,30},{7,31}} | collective-permute-start | bytes 393224 | tf_op jit(solution)/shard_map/kv/ppermute | solution.py:73
  147.4 10.5 %copy-start.30 = (bf16[128,512]{1,0:T(8,128)(2,1)}, bf16[128,512]{1,0:T(8,128)(2,1)S(1)}, u32[]{:S(2)}) copy-start(bf16[128,512]{1,0:T(8,128)(2,1)S(1)} %collective-permute-done.15.refs_5_.refs_9_) | copy-start | bytes 393220
  163.7 92.6 %all-gather.9.cloned.1.call-start = ((), (), s32[]{:S(2)}) async-start(), calls=%async_computation.4 | async-start | bytes 1966080 | tf_op jit(solution)/shard_map/all_gather | solution.py:1071
  163.8 9.4 %slice-start.1 = ((bf16[2,3,48,1120]{3,2,1,0:T(8,128)(2,1)}), bf16[1,3,48,1120]{3,2,1,0:T(8,128)(2,1)S(1)}, s32[]{:S(2)}) async-start(bf16[2,3,48,1120]{3,2,1,0:T(8,128)(2,1)} %copy-done.16), calls=%async_computation.9 | async-start | bytes 663552 | tf_op jit(solution)/shard_map/slice | solution.py:1053
  174.9 31.1 %collective-permute-start.20 = (bf16[4,3,48,1120]{3,2,1,0:T(8,128)(2,1)}, bf16[4,3,48,1120]{3,2,1,0:T(8,128)(2,1)S(1)}, u32[]{:S(2)}, u32[]{:S(2)}) collective-permute-start(bf16[4,3,48,1120]{3,2,1,0:T(8,128)(2,1)} %pad_maximum_fusion.2), channel_id=1, source_target_pairs={{0,2},{1,3},{2,0},{3,1},{4,6},{5,7},{6,4},{7,5},{8,10},{9,11},{10,... | collective-permute-start | bytes 3870728 | tf_op jit(solution)/shard_map/ff_plane2/ppermute | solution.py:73
  178.7 33.1 %collective-permute-start.22 = (bf16[512,1536]{1,0:T(8,128)(2,1)}, bf16[512,1536]{1,0:T(8,128)(2,1)S(1)}, u32[]{:S(2)}, u32[]{:S(2)}) collective-permute-start(bf16[512,1536]{1,0:T(8,128)(2,1)} %all-gather.7.cloned.1.call-done.refs_2_.refs_4_.refs_6_), channel_id=1, source_target_pairs={{0,1},{1,0},{2,3},{3,2},{4,5},{5,4},{6,7},{7,6},{8,9},{9,8},{10,11... | collective-permute-start | bytes 4718600 | tf_op jit(solution)/shard_map/gy_core/ppermute | solution.py:73
  180.1 31.7 %collective-permute-start.21 = (bf16[4,3,48,1120]{3,2,1,0:T(8,128)(2,1)S(1)}, bf16[4,3,48,1120]{3,2,1,0:T(8,128)(2,1)}, u32[]{:S(2)}, u32[]{:S(2)}) collective-permute-start(bf16[4,3,48,1120]{3,2,1,0:T(8,128)(2,1)S(1)} %pad_maximum_fusion.3), channel_id=1, source_target_pairs={{0,4},{1,5},{2,6},{3,7},{4,0},{5,1},{6,2},{7,3},{8,12},{9,13},{10,... | collective-permute-start | bytes 3870728 | tf_op jit(solution)/shard_map/ff_plane2/ppermute | solution.py:73
  206.0 5.8 %copy-start.14 = (bf16[4,3,48,1120]{3,2,1,0:T(8,128)(2,1)}, bf16[4,3,48,1120]{3,2,1,0:T(8,128)(2,1)S(1)}, u32[]{:S(2)}) copy-start(bf16[4,3,48,1120]{3,2,1,0:T(8,128)(2,1)S(1)} %collective-permute-done.20.refs_9_) | copy-start | bytes 3870724
  211.8 19.1 %copy-start.4 = (bf16[512,1536]{1,0:T(8,128)(2,1)}, bf16[512,1536]{1,0:T(8,128)(2,1)S(1)}, u32[]{:S(2)}) copy-start(bf16[512,1536]{1,0:T(8,128)(2,1)S(1)} %collective-permute-done.22.refs_2_.refs_5_.refs_7_) | copy-start | bytes 4718596
  211.9 19.1 %collective-permute-start.23 = (bf16[512,1536]{1,0:T(8,128)(2,1)}, bf16[512,1536]{1,0:T(8,128)(2,1)S(1)}, u32[]{:S(2)}, u32[]{:S(2)}) collective-permute-start(bf16[512,1536]{1,0:T(8,128)(2,1)} %all-gather.5.cloned.1.call-done.refs_1_.refs_0_.refs_2_), channel_id=1, source_target_pairs={{0,1},{1,0},{2,3},{3,2},{4,5},{5,4},{6,7},{7,6},{8,9},{9,8},{10,11... | collective-permute-start | bytes 4718600 | tf_op jit(solution)/shard_map/n2_core/ppermute | solution.py:73
  212.0 82.5 %reduce-scatter.3.cloned.1.call-start = ((), (), s32[]{:S(2)}) async-start(), calls=%async_computation.5 | async-start | bytes 1966080 | tf_op jit(solution)/shard_map/reduce_scatter | solution.py:1072
  232.1 22.7 %copy-start.20 = (bf16[512,1536]{1,0:T(8,128)(2,1)S(1)}, bf16[512,1536]{1,0:T(8,128)(2,1)}, u32[]{:S(2)}) copy-start(bf16[512,1536]{1,0:T(8,128)(2,1)} %get-tuple-element.145) | copy-start | bytes 4718596
  251.0 3.8 collective-permute-start.24
  256.4 107.2 %all-gather.11.cloned.1.call-start = ((), (), s32[]{:S(2)}) async-start(), calls=%async_computation.7 | async-start | bytes 1966080 | tf_op jit(solution)/shard_map/all_gather | solution.py:1099
  257.7 36.7 %collective-permute-start.25 = (bf16[512,1536]{1,0:T(8,128)(2,1)S(1)}, bf16[512,1536]{1,0:T(8,128)(2,1)}, u32[]{:S(2)}, u32[]{:S(2)}) collective-permute-start(bf16[512,1536]{1,0:T(8,128)(2,1)S(1)} %copy-done.42), channel_id=1, source_target_pairs={{0,1},{1,0},{2,3},{3,2},{4,5},{5,4},{6,7},{7,6},{8,9},{9,8},{10,11... | collective-permute-start | bytes 4718600 | tf_op jit(solution)/shard_map/y_core/ppermute | solution.py:73
  271.1 22.1 %collective-permute-start.26 = (bf16[2,1,192,1120]{3,2,1,0:T(8,128)(2,1)}, bf16[2,1,192,1120]{3,2,1,0:T(8,128)(2,1)}, u32[]{:S(2)}, u32[]{:S(2)}) collective-permute-start(bf16[2,1,192,1120]{3,2,1,0:T(8,128)(2,1)} %get-tuple-element.155), channel_id=1, source_target_pairs={{0,4},{1,5},{2,6},{3,7},{4,0},{5,1},{6,2},{7,3},{8,12},{9,13},{10,... | collective-permute-start | bytes 2580488 | tf_op jit(solution)/shard_map/ff_sum1/ppermute | solution.py:73
  272.7 21.7 %collective-permute-start.27 = (bf16[2,1,192,1120]{3,2,1,0:T(8,128)(2,1)}, bf16[2,1,192,1120]{3,2,1,0:T(8,128)(2,1)}, u32[]{:S(2)}, u32[]{:S(2)}) collective-permute-start(bf16[2,1,192,1120]{3,2,1,0:T(8,128)(2,1)} %get-tuple-element.157), channel_id=1, source_target_pairs={{0,2},{1,3},{2,0},{3,1},{4,6},{5,7},{6,4},{7,5},{8,10},{9,11},{10,... | collective-permute-start | bytes 2580488 | tf_op jit(solution)/shard_map/ff_sum1/ppermute | solution.py:73
  294.4 106.2 %reduce-scatter.5.cloned.1.call-start = ((), (), s32[]{:S(2)}) async-start(), calls=%async_computation.6 | async-start | bytes 1966080 | tf_op jit(solution)/shard_map/reduce_scatter | solution.py:1132
  294.5 53.5 %collective-permute-start.34 = (bf16[2,2,192,1120]{3,2,1,0:T(8,128)(2,1)}, bf16[2,2,192,1120]{3,2,1,0:T(8,128)(2,1)S(1)}, u32[]{:S(2)}, u32[]{:S(2)}) collective-permute-start(bf16[2,2,192,1120]{3,2,1,0:T(8,128)(2,1)} %get-tuple-element.156), channel_id=1, source_target_pairs={{0,4},{1,5},{2,6},{3,7},{4,0},{5,1},{6,2},{7,3},{8,12},{9,13},{10,... | collective-permute-start | bytes 5160968 | tf_op jit(solution)/shard_map/ff_sum1/ppermute | solution.py:73
  295.1 53.0 %collective-permute-start.35 = (bf16[2,2,192,1120]{3,2,1,0:T(8,128)(2,1)}, bf16[2,2,192,1120]{3,2,1,0:T(8,128)(2,1)S(1)}, u32[]{:S(2)}, u32[]{:S(2)}) collective-permute-start(bf16[2,2,192,1120]{3,2,1,0:T(8,128)(2,1)} %get-tuple-element.158), channel_id=1, source_target_pairs={{0,2},{1,3},{2,0},{3,1},{4,6},{5,7},{6,4},{7,5},{8,10},{9,11},{10,... | collective-permute-start | bytes 5160968 | tf_op jit(solution)/shard_map/ff_sum1/ppermute | solution.py:73
  305.4 13.1 %collective-permute-start.28 = (bf16[128,512]{1,0:T(8,128)(2,1)}, bf16[128,512]{1,0:T(8,128)(2,1)S(1)}, u32[]{:S(2)}, u32[]{:S(2)}) collective-permute-start(bf16[128,512]{1,0:T(8,128)(2,1)} %get-tuple-element.163), channel_id=1, source_target_pairs={{8,0},{9,1},{10,2},{11,3},{12,4},{13,5},{14,6},{15,7},{16,8},{17,9... | collective-permute-start | bytes 393224 | tf_op jit(solution)/shard_map/gkv/ppermute | solution.py:73
  306.7 28.2 %collective-permute-start.29 = (bf16[128,512]{1,0:T(8,128)(2,1)}, bf16[128,512]{1,0:T(8,128)(2,1)S(1)}, u32[]{:S(2)}, u32[]{:S(2)}) collective-permute-start(bf16[128,512]{1,0:T(8,128)(2,1)} %get-tuple-element.164), channel_id=1, source_target_pairs={{16,0},{17,1},{18,2},{19,3},{20,4},{21,5},{22,6},{23,7},{24,8},{25... | collective-permute-start | bytes 393224 | tf_op jit(solution)/shard_map/gkv/ppermute | solution.py:73
  308.0 26.9 %collective-permute-start.30 = (bf16[128,512]{1,0:T(8,128)(2,1)}, bf16[128,512]{1,0:T(8,128)(2,1)S(1)}, u32[]{:S(2)}, u32[]{:S(2)}) collective-permute-start(bf16[128,512]{1,0:T(8,128)(2,1)} %get-tuple-element.165), channel_id=1, source_target_pairs={{24,0},{25,1},{26,2},{27,3},{28,4},{29,5},{30,6},{31,7}} | collective-permute-start | bytes 393224 | tf_op jit(solution)/shard_map/gkv/ppermute | solution.py:73
  318.5 16.4 %copy-start.31 = (bf16[128,512]{1,0:T(8,128)(2,1)}, bf16[128,512]{1,0:T(8,128)(2,1)S(1)}, u32[]{:S(2)}) copy-start(bf16[128,512]{1,0:T(8,128)(2,1)S(1)} %collective-permute-done.28.refs_1_) | copy-start | bytes 393220
  344.1 15.3 %collective-permute-start.31 = (bf16[144,896]{1,0:T(8,128)(2,1)}, bf16[144,896]{1,0:T(8,128)(2,1)}, u32[]{:S(2)}, u32[]{:S(2)}) collective-permute-start(bf16[144,896]{1,0:T(8,128)(2,1)} %get-tuple-element.170), channel_id=1, source_target_pairs={{0,8},{1,9},{2,10},{3,11},{4,12},{5,13},{6,14},{7,15},{8,16},{9,17... | collective-permute-start | bytes 774152 | tf_op jit(solution)/shard_map/gqkv_ctx/ppermute | solution.py:73
  344.2 19.3 %collective-permute-start.32 = (bf16[144,896]{1,0:T(8,128)(2,1)}, bf16[144,896]{1,0:T(8,128)(2,1)}, u32[]{:S(2)}, u32[]{:S(2)}) collective-permute-start(bf16[144,896]{1,0:T(8,128)(2,1)} %get-tuple-element.171), channel_id=1, source_target_pairs={{0,16},{1,17},{2,18},{3,19},{4,20},{5,21},{6,22},{7,23},{8,24},{9,... | collective-permute-start | bytes 774152 | tf_op jit(solution)/shard_map/gqkv_ctx/ppermute | solution.py:73
  344.3 19.2 %collective-permute-start.33 = (bf16[144,896]{1,0:T(8,128)(2,1)}, bf16[144,896]{1,0:T(8,128)(2,1)}, u32[]{:S(2)}, u32[]{:S(2)}) collective-permute-start(bf16[144,896]{1,0:T(8,128)(2,1)} %get-tuple-element.172), channel_id=1, source_target_pairs={{0,24},{1,25},{2,26},{3,27},{4,28},{5,29},{6,30},{7,31},{8,0},{9,1... | collective-permute-start | bytes 774152 | tf_op jit(solution)/shard_map/gqkv_ctx/ppermute | solution.py:73
  349.8 6.7 %copy-start.19 = (bf16[512,1536]{1,0:T(8,128)(2,1)S(1)}, bf16[512,1536]{1,0:T(8,128)(2,1)}, u32[]{:S(2)}) copy-start(bf16[512,1536]{1,0:T(8,128)(2,1)} %get-tuple-element.138) | copy-start | bytes 4718596
  354.3 28.5 %collective-permute-start.36 = (bf16[3,192,1120]{2,1,0:T(8,128)(2,1)}, bf16[3,192,1120]{2,1,0:T(8,128)(2,1)S(1)}, u32[]{:S(2)}, u32[]{:S(2)}) collective-permute-start(bf16[3,192,1120]{2,1,0:T(8,128)(2,1)} %get-tuple-element.185), channel_id=1, source_target_pairs={{0,2},{1,3},{2,0},{3,1},{4,6},{5,7},{6,4},{7,5},{8,10},{9,11},{10,... | collective-permute-start | bytes 3870728 | tf_op jit(solution)/shard_map/ff_sum2/ppermute | solution.py:73
  355.7 28.1 %collective-permute-start.37 = (bf16[3,192,1120]{2,1,0:T(8,128)(2,1)}, bf16[3,192,1120]{2,1,0:T(8,128)(2,1)S(1)}, u32[]{:S(2)}, u32[]{:S(2)}) collective-permute-start(bf16[3,192,1120]{2,1,0:T(8,128)(2,1)} %get-tuple-element.186), channel_id=1, source_target_pairs={{0,4},{1,5},{2,6},{3,7},{4,0},{5,1},{6,2},{7,3},{8,12},{9,13},{10,... | collective-permute-start | bytes 3870728 | tf_op jit(solution)/shard_map/ff_sum2/ppermute | solution.py:73
  369.6 22.3 %collective-permute-start.38 = (bf16[4,208,896]{2,1,0:T(8,128)(2,1)}, bf16[4,208,896]{2,1,0:T(8,128)(2,1)S(1)}, u32[]{:S(2)}, u32[]{:S(2)}) collective-permute-start(bf16[4,208,896]{2,1,0:T(8,128)(2,1)} %get-tuple-element.189), channel_id=1, source_target_pairs={{0,1},{1,0},{2,3},{3,2},{4,5},{5,4},{6,7},{7,6},{8,9},{9,8},{10,11... | collective-permute-start | bytes 4472840 | tf_op jit(solution)/shard_map/term_core/ppermute | solution.py:73
  391.9 8.8 %copy-start.22 = (f32[128,1536]{1,0:T(8,128)S(1)}, f32[128,1536]{1,0:T(8,128)}, u32[]{:S(2)}) copy-start(f32[128,1536]{1,0:T(8,128)} %get-tuple-element.130.refs_1_) | copy-start | bytes 2359300
  391.9 10.8 %collective-permute-start.42 = (bf16[3,192,1120]{2,1,0:T(8,128)(2,1)}, bf16[3,192,1120]{2,1,0:T(8,128)(2,1)S(1)}, u32[]{:S(2)}, u32[]{:S(2)}) collective-permute-start(bf16[3,192,1120]{2,1,0:T(8,128)(2,1)} %get-tuple-element.187), channel_id=1, source_target_pairs={{0,1},{1,0},{2,3},{3,2},{4,5},{5,4},{6,7},{7,6},{8,9},{9,8},{10,11... | collective-permute-start | bytes 3870728 | tf_op jit(solution)/shard_map/final_core/ppermute | solution.py:73
  396.2 16.0 %collective-permute-start.39 = (bf16[208,896]{1,0:T(8,128)(2,1)}, bf16[208,896]{1,0:T(8,128)(2,1)S(1)}, u32[]{:S(2)}, u32[]{:S(2)}) collective-permute-start(bf16[208,896]{1,0:T(8,128)(2,1)} %get-tuple-element.191), channel_id=1, source_target_pairs={{0,2},{1,3},{2,0},{3,1},{4,6},{5,7},{6,4},{7,5},{8,10},{9,11},{10,... | collective-permute-start | bytes 1118216 | tf_op jit(solution)/shard_map/term_plane/ppermute | solution.py:73
  397.6 19.0 %collective-permute-start.40 = (bf16[208,896]{1,0:T(8,128)(2,1)}, bf16[208,896]{1,0:T(8,128)(2,1)S(1)}, u32[]{:S(2)}, u32[]{:S(2)}) collective-permute-start(bf16[208,896]{1,0:T(8,128)(2,1)} %get-tuple-element.192), channel_id=1, source_target_pairs={{0,4},{1,5},{2,6},{3,7},{4,0},{5,1},{6,2},{7,3},{8,12},{9,13},{10,... | collective-permute-start | bytes 1118216 | tf_op jit(solution)/shard_map/term_plane/ppermute | solution.py:73
  398.1 18.5 %collective-permute-start.41 = (bf16[208,896]{1,0:T(8,128)(2,1)}, bf16[208,896]{1,0:T(8,128)(2,1)S(1)}, u32[]{:S(2)}, u32[]{:S(2)}) collective-permute-start(bf16[208,896]{1,0:T(8,128)(2,1)} %get-tuple-element.193), channel_id=1, source_target_pairs={{0,6},{1,7},{2,4},{3,5},{4,2},{5,3},{6,0},{7,1},{8,14},{9,15},{10,... | collective-permute-start | bytes 1118216 | tf_op jit(solution)/shard_map/term_plane/ppermute | solution.py:73
  (33 other events, 78.9 us)
Sparse Core Ops, SparseCore 0:
  124.5 41.2 all-gather.6
  167.9 42.3 all-gather.4
  212.1 36.8 all-gather.8
  256.5 34.9 reduce-scatter.2
  294.6 47.0 all-gather.10
  363.7 36.9 reduce-scatter.4

commit v4 on v3

--- a/solution.py
+++ b/solution.py
@@ -374,31 +374,34 @@
     return shard, a, b, links.plane(b[:half], 2), links.plane(a[half:], 4)
 
 
+def load_pieces(layout, sizes, place, pieces, which, weight, semaphore):
+    ctx_size, chips, rows = sizes
+    for (entries, mask, _), piece in zip(layout, pieces):
+        for i, (step, core) in enumerate(entries):
+            source = lax.rem(place[0] - step + ctx_size, ctx_size)
+            start = ((source * chips + (place[1] ^ mask)) * 2 + core) * rows
+            pltpu.make_async_copy(
+                piece.at[i, which],
+                weight.at[pl.ds(pl.multiple_of(start, rows), rows)],
+                semaphore,
+            ).start()
+
+
 def ff_kernel(layout, sizes, place, normed, out_grad, *refs):
-    ctx_size, chips, rows = sizes
     pieces, refs = refs[: len(layout)], refs[len(layout) :]
-    act_ref, gate_ref, up_ref, down_ref, y_ref, weights, semaphores = refs
+    act_ref, gate_ref, up_ref, down_ref, weights, semaphores = refs
 
     @pl.when(pl.program_id(0) == 0)
     def _():
-        ctx, chip = place[0], place[1]
         for which in range(3):
-            for (entries, mask, _), piece in zip(layout, pieces):
-                for i, (step, core) in enumerate(entries):
-                    source = lax.rem(ctx - step + ctx_size, ctx_size)
-                    start = ((source * chips + (chip ^ mask)) * 2 + core) * rows
-                    pltpu.make_async_copy(
-                        piece.at[i, which],
-                        weights.at[which, pl.ds(pl.multiple_of(start, rows), rows)],
-                        semaphores.at[which],
-                    ).start()
+            load_pieces(
+                layout, sizes, place, pieces, which, weights.at[which], semaphores.at[which]
+            )
 
     def arrived(which):
         @pl.when(pl.program_id(0) == 0)
         def _():
-            pltpu.make_async_copy(
-                weights.at[which], weights.at[which], semaphores.at[which]
-            ).wait()
+            wait_all(weights.at[which], semaphores.at[which])
 
     x, gy = normed[...], out_grad[...]
     arrived(0)
@@ -409,45 +412,60 @@
     grad = nn(gy, weights[2])
     sigmoid = 1.0 / (1.0 + jnp.exp(-gate))
     silu = gate * sigmoid
-    act = (silu * up).astype(BF16)
     grad_gate = (grad * up * sigmoid * (1.0 + gate * (1.0 - sigmoid))).astype(BF16)
     grad_up = (grad * silu).astype(BF16)
-    act_ref[...] = act
+    act_ref[...] = (silu * up).astype(BF16)
     gate_ref[...] = grad_gate
     up_ref[...] = grad_up
     down_ref[...] = (nt(grad_gate, weights[0]) + nt(grad_up, weights[1])).astype(BF16)
-    y_ref[...] = nt(act, weights[2]).astype(BF16)
-
-
-def feed_forward(links, layout, place, normed, out_grad):
-    tokens, width = normed.shape
+
+
+def y_kernel(layout, sizes, place, act_a, act_b, *refs):
+    pieces, (y_a, y_b, weight, semaphore) = refs[: len(layout)], refs[len(layout) :]
+
+    @pl.when(pl.program_id(0) == 0)
+    def _():
+        load_pieces(layout, sizes, place, pieces, 2, weight, semaphore)
+        wait_all(weight, semaphore)
+
+    y_a[...] = nt(act_a[...], weight[...]).astype(BF16)
+    y_b[...] = nt(act_b[...], weight[...]).astype(BF16)
+
+
+def ff_call(links, kernel, layout, place, arrays, widths, matrices):
+    tokens = arrays[0].shape[0]
     rows, block = layout[0][2].shape[2:]
+    sizes = (links.ctx_size, links.fsdp_size // 2, rows)
+    depth = 2 * sizes[0] * sizes[1] * rows
     tile = 256
-    wide = pl.BlockSpec((tile, width), lambda i, place: (i, 0))
-    narrow = pl.BlockSpec((tile, block), lambda i, place: (i, 0))
-    small = jax.ShapeDtypeStruct((tokens, block), BF16)
-    large = jax.ShapeDtypeStruct((tokens, width), BF16)
-    sizes = (links.ctx_size, links.fsdp_size // 2, rows)
+
+    def spec(size):
+        return pl.BlockSpec((tile, size), lambda i, place: (i, 0))
 
     def body(*refs):
-        ff_kernel(layout, sizes, *refs)
-
+        kernel(layout, sizes, *refs)
+
+    if matrices == 1:
+        scratch = [pltpu.VMEM((depth, block), BF16), pltpu.SemaphoreType.DMA]
+    else:
+        scratch = [
+            pltpu.VMEM((matrices, depth, block), BF16),
+            pltpu.SemaphoreType.DMA((matrices,)),
+        ]
     return pl.pallas_call(
         body,
         grid_spec=pltpu.PrefetchScalarGridSpec(
             num_scalar_prefetch=1,
             grid=(tokens // tile,),
-            in_specs=[wide, wide] + [pl.BlockSpec(memory_space=pl.ANY)] * len(layout),
-            out_specs=[narrow, narrow, narrow, wide, wide],
-            scratch_shapes=[
-                pltpu.VMEM((3, width, block), BF16),
-                pltpu.SemaphoreType.DMA((3,)),
-            ],
+            in_specs=[spec(x.shape[1]) for x in arrays]
+            + [pl.BlockSpec(memory_space=pl.ANY)] * len(layout),
+            out_specs=[spec(x) for x in widths],
+            scratch_shapes=scratch,
         ),
-        out_shape=[small, small, small, large, large],
+        out_shape=[jax.ShapeDtypeStruct((tokens, x), BF16) for x in widths],
         compiler_params=pltpu.CompilerParams(vmem_limit_bytes=56 * 2**20),
         cost_estimate=pl.CostEstimate(flops=0, bytes_accessed=0, transcendentals=0),
-    )(place, normed, out_grad, *[piece for _, _, piece in layout])
+    )(place, *arrays, *[piece for _, _, piece in layout])
 
 
 def grad_kernel(place, *refs):
@@ -569,18 +587,14 @@
         ),
         out_shape=[jax.ShapeDtypeStruct(shape, F32), jax.ShapeDtypeStruct(shape, BF16)],
         compiler_params=pltpu.CompilerParams(vmem_limit_bytes=56 * 2**20),
-        cost_estimate=pl.CostEstimate(flops=12 * 10**9, bytes_accessed=0, transcendentals=0),
+        cost_estimate=pl.CostEstimate(flops=12*10**9, bytes_accessed=0, transcendentals=0),
     )(place, *low, second[0], *high, second[1])
 
 
 def join_cores_kernel(place, mine, got, gate, up, down):
-    block = mine.shape[2]
-
     def write(even, odd):
-        for which, ref in enumerate((gate, up)):
+        for which, ref in enumerate((gate, up, down)):
             ref[...] = jnp.concatenate([even(which), odd(which)], axis=1)
-        down[:block] = jnp.transpose(even(2))
-        down[block:] = jnp.transpose(odd(2))
 
     def own(which):
         return mine[which]
@@ -907,9 +921,11 @@
     total = keep[...] + got[0][...].astype(F32) + got[1][...].astype(F32) + got[2][...].astype(F32)
     height = total.shape[0] - 16
     start = 0
-    for ref in outs[:4]:
-        ref[...] = total[:height, start : start + ref.shape[1]]
-        start += ref.shape[1]
+    for ref, turned in zip(outs[:4], (False, True, True, False)):
+        size = ref.shape[0] if turned else ref.shape[1]
+        part = total[:height, start : start + size]
+        ref[...] = jnp.transpose(part) if turned else part
+        start += size
     start = 0
     for ref in outs[4:]:
         ref[...] = total[height : height + 1, start : start + ref.shape[1]]
@@ -1063,9 +1079,15 @@
     ]
     links.label = "n2_core"
     normed_other = links.core(after(normed_row, *last, out_other))
-    act_a, gate_a, up_a, down_a, y_a = feed_forward(links, layout, place, normed_row, out_row)
+    block = own_piece.shape[3]
+    ff_widths = (block, block, block, width)
+    act_a, gate_a, up_a, down_a = ff_call(
+        links, ff_kernel, layout, place, (normed_row, out_row), ff_widths, 3
+    )
     normed_other = after(normed_other, act_a)
-    act_b, gate_b, up_b, down_b, y_b = feed_forward(links, layout, place, normed_other, out_other)
+    act_b, gate_b, up_b, down_b = ff_call(
+        links, ff_kernel, layout, place, (normed_other, out_other), ff_widths, 3
+    )
     links.label = "gn2_core"
     down_got = links.core(down_b)
     normed_rows = lax.all_gather(after(normed_one, normed_row), "ctx", axis=0, tiled=True)
@@ -1078,11 +1100,12 @@
     send_terms = ff_grad_terms(place, lefts, rights, lambda j: 2 + j, lambda j: 1 + 2 * j, (1, 2))
     links.label = "ff_sum1"
     ff_first = reduce_start(links, send_terms)
-    lefts = (after(normed_row, *send_terms), *lefts[1:])
-    ff_terms = ff_grad_terms(place, lefts, rights, lambda j: j, lambda j: 2 * j, (3,))
     links.label = "y_core"
-    y_got = links.core(after(y_b, down_got))
-    grad_normed_two = after(grad_normed_two, ff_terms[0], y_got, *ff_first[::2])
+    y_a, y_b = ff_call(
+        links, y_kernel, layout, place, (after(act_a, *send_terms), act_b), (width, width), 1
+    )
+    y_got = links.core(y_b)
+    grad_normed_two = after(grad_normed_two, y_b, *ff_first[::2])
 
     def mix_back(*refs):
         mix_back_body(1, *refs)
@@ -1099,8 +1122,11 @@
     mixed_rows = lax.all_gather(
         after(mixed_low, grad_normed_two), "ctx", axis=0, tiled=True
     )
+    lefts = (after(normed_row, grad_hidden_low, y_got), *lefts[1:])
+    ff_terms = ff_grad_terms(place, lefts, rights, lambda j: j, lambda j: 2 * j, (3,))
     links.label = "gkv"
     pair_terms = [pair_terms[0]] + [links.shift(pair_terms[step], -step) for step in steps]
+    pair_terms[0] = after(pair_terms[0], ff_terms[0])
     def columns_over_ctx(parts):
         whole = jnp.zeros_like(parts)
         whole = lax.dynamic_update_index_in_dim(whole, pick(parts, ctx), ctx, 0)
@@ -1147,8 +1173,6 @@
         place,
     )
     links.label = "term_core"
-    ff_mine, ff_send = reduce_end(place, ff_terms, ff_first, ff_second)
-    term_mine = after(term_mine, ff_send)
     keep, *sends = small_call(
         sum_cores_kernel,
         (term_mine, links.core(term_other)),
@@ -1161,17 +1185,21 @@
     grad_q, grad_k, grad_v, grad_o, *vectors = small_call(
         sum_plane_kernel,
         (keep, *plane_got),
-        [((height, x), F32) for x in (q_columns, kv_columns, kv_columns, q_columns)]
+        [((height, q_columns), F32)]
+        + [((kv_columns, height), F32)] * 2
+        + [((height, q_columns), F32)]
         + [((1, x // devices), F32) for x in (width, width, width, KV_WIDTH, KV_WIDTH)],
+        cost=0,
     )
     vectors = [x[0] for x in vectors]
 
     links.label = "final_core"
+    ff_mine, ff_send = reduce_end(place, ff_terms, ff_first, phase(ff_second, sends)[0])
     hidden = 2 * ff_mine.shape[2]
     grad_gate, grad_up, grad_down = small_call(
         join_cores_kernel,
         (ff_mine, after(links.core(ff_send), *sends)),
-        [((height, hidden), F32), ((height, hidden), F32), ((hidden, height), F32)],
+        [((height, hidden), F32)] * 3,
         place=place,
         cost=2*10**9,
     )
@@ -1182,15 +1210,15 @@
         vectors[0],
         grad_q,
         vectors[2],
-        grad_k,
+        jnp.transpose(grad_k),
         vectors[3],
-        grad_v,
+        jnp.transpose(grad_v),
         vectors[4],
         grad_o,
         vectors[1],
         grad_gate,
         grad_up,
-        grad_down,
+        jnp.transpose(grad_down),
     )
 
 

time: 439 us -> 434 us (0.989)
  waiting for transfers between devices: 192 us -> 203 us
  local copies, waits for them, and re-layouts: 26.9 us -> 16.7 us
  starting transfers between devices: 57.1 us -> 47.9 us
    reduce_scatter x1, waiting for transfers between devices: 0.98 us -> 15.1 us  [per_device_plane_of_four(): y_sum = lax.psum_scatter(y_both, 'ctx', scatter_dimension=0, tiled=True)]
    unnamed x101 -> x90, local copies, waits for them, and re-layouts: 22.6 us -> 12.4 us
    ppermute x43, starting transfers between devices: 56.5 us -> 47.3 us  [send(): return lax.ppermute(x, BOTH, pairs)]
    pallas_call x2 -> x3, Pallas kernels: 37.7 us -> 42.8 us  [ff_call(): pl.pallas_call(body, grid_spec=pltpu.PrefetchScalarGridSpec(num_scalar_pr...]
  transfers between devices with their start and end apart: 49 -> 49, of which waited for: 21 -> 22; matrix products, arithmetic and copies ran while one was open for 5% -> 4% of each run, Pallas kernels for 28% -> 29%
where the time goes in v4:
time: 434 us; the launch traced here: 426 us
  waiting for transfers between devices  203 us (47%)
  Pallas kernels  128 us (29%)
  starting transfers between devices  47.9 us (11%)
  local copies, waits for them, and re-layouts  16.7 us (4%)
  between operations  15.3 us (4%)
  other arithmetic  14.9 us (3%)
    ppermute x43, waiting for transfers between devices, send(): return lax.ppermute(x, BOTH, pairs)  188 us
    ppermute x43, starting transfers between devices, send(): return lax.ppermute(x, BOTH, pairs)  47.3 us
    pallas_call x3, Pallas kernels, ff_call(): pl.pallas_call(body, grid_spec=pltpu.PrefetchScalarGridSpec(num_scalar_pr...  42.8 us
    pallas_call x4, Pallas kernels, call(): pl.pallas_call(kernel, in_specs=[pl.BlockSpec(memory_space=pltpu.SMEM)] +...  30.4 us
    pallas_call x2, Pallas kernels, ff_grad_terms(): pl.pallas_call(grad_kernel, grid_spec=pltpu.PrefetchScalarGridSpec(num_sc...  25.7 us
    pallas_call x4, Pallas kernels, small_call(): pl.pallas_call(body, in_specs=[pl.BlockSpec(memory_space=pltpu.SMEM)] * l...  16.7 us
    reduce_scatter x1, waiting for transfers between devices, per_device_plane_of_four(): y_sum = lax.psum_scatter(y_both, 'ctx', scatter_dimension=0, tiled=True)  15.1 us
    unnamed x90, local copies, waits for them, and re-layouts  12.4 us
  transfers between devices with their start and end apart: 49, of which 22 were waited for; matrix products, arithmetic and copies ran while one was open for 4% of the time, Pallas kernels for 29%

profile of v4, /device:TPU:0, one launch (start us, length us, event | category | flops | bytes accessed | tf_op | source)
XLA Modules:
  0.0 426.0 jit_solution(17336471350665755635)
XLA Ops:
  12.9 4.7 %collective-permute-start.2 = (bf16[48,3712]{1,0:T(8,128)(2,1)S(1)}, bf16[48,3712]{1,0:T(8,128)(2,1)S(1)}, u32[]{:S(2)}, u32[]{:S(2)}) collective-permute-start(bf16[48,3712]{1,0:T(8,128)(2,1)S(1)} %constant_dynamic-update-slice_fusion), channel_id=1, source_target_pairs={{0,24},{1,25},{2,26},{3,27},{4,28},{5,29},{6,30},{7,31},{8,0},{9,1... | collective-permute-start | bytes 1069064 | tf_op jit(solution)/shard_map/qkvo_ctx/ppermute | solution.py:73
  18.6 7.7 %collective-permute-done.2 = bf16[48,3712]{1,0:T(8,128)(2,1)S(1)} collective-permute-done((bf16[48,3712]{1,0:T(8,128)(2,1)S(1)}, bf16[48,3712]{1,0:T(8,128)(2,1)S(1)}, u32[]{:S(2)}, u32[]{:S(2)}) %collective-permute-start.2) | collective-permute-done | bytes 356384 | tf_op jit(solution)/shard_map/qkvo_ctx/ppermute | solution.py:73
  26.3 22.4 %collective-permute-done.1 = bf16[48,3712]{1,0:T(8,128)(2,1)} collective-permute-done((bf16[48,3712]{1,0:T(8,128)(2,1)S(1)}, bf16[48,3712]{1,0:T(8,128)(2,1)}, u32[]{:S(2)}, u32[]{:S(2)}) %collective-permute-start.1) | collective-permute-done | bytes 356384 | tf_op jit(solution)/shard_map/qkvo_ctx/ppermute | solution.py:73
  48.7 1.3 pad_maximum_fusion.1.refs_3_.refs_8_.refs_12_
  50.1 1.6 collective-permute-start.5
  51.7 1.5 collective-permute-start.4
  53.2 1.5 broadcast_select_fusion.1
  55.0 2.1 collective-permute-start.6
  57.2 14.3 %collective-permute-done.7 = bf16[2,3,48,1120]{3,2,1,0:T(8,128)(2,1)S(1)} collective-permute-done((bf16[2,3,48,1120]{3,2,1,0:T(8,128)(2,1)S(1)}, bf16[2,3,48,1120]{3,2,1,0:T(8,128)(2,1)S(1)}, u32[]{:S(2)}, u32[]{:S(2)}) %collective-permute-start.7) | collective-permute-done | bytes 645152 | tf_op jit(solution)/shard_map/ff_ctx_a/ppermute | solution.py:73
  71.6 16.5 %collective-permute-done.6 = bf16[2,3,48,1120]{3,2,1,0:T(8,128)(2,1)S(1)} collective-permute-done((bf16[2,3,48,1120]{3,2,1,0:T(8,128)(2,1)S(1)}, bf16[2,3,48,1120]{3,2,1,0:T(8,128)(2,1)S(1)}, u32[]{:S(2)}, u32[]{:S(2)}) %collective-permute-start.6) | collective-permute-done | bytes 645152 | tf_op jit(solution)/shard_map/ff_ctx_a/ppermute | solution.py:73
  90.4 1.5 collective-permute-start.13
  91.9 1.5 collective-permute-start.12
  93.4 25.6 %collective-permute-done.9 = bf16[2,3,48,1120]{3,2,1,0:T(8,128)(2,1)S(1)} collective-permute-done((bf16[2,3,48,1120]{3,2,1,0:T(8,128)(2,1)S(1)}, bf16[2,3,48,1120]{3,2,1,0:T(8,128)(2,1)S(1)}, u32[]{:S(2)}, u32[]{:S(2)}) %collective-permute-start.9) | collective-permute-done | bytes 645152 | tf_op jit(solution)/shard_map/ff_ctx_b/ppermute | solution.py:73
  119.0 1.7 collective-permute-done.13.refs_5_
  120.8 2.7 pad_maximum_fusion
  126.9 1.5 collective-permute-start.18
  129.5 1.7 collective-permute-done.14.refs_9_.refs_14_.refs_18_
  131.2 6.0 %shard_map.255 = (bf16[128,1536]{1,0:T(8,128)(2,1)}, bf16[128,1536]{1,0:T(8,128)(2,1)}, bf16[128,512]{1,0:T(8,128)(2,1)}, f32[8,1536]{1,0:T(8,128)}) custom-call(s32[3]{0:T(128)} %copy-done.3, bf16[128,1536]{1,0:T(8,128)(2,1)} %bitcast.32, f32[128,128]{1,0:T(8,128)} %get-tuple-element.223.refs_1_.refs_6_, f32[128,128]{1,0:T(8,128)} %get-tuple-element.224.refs_2_.refs_7_, ...), custom_call_target="tpu_custom_call" | custom-call | tf_op jit(solution)/shard_map/pallas_call | solution.py:694
  137.2 3.0 collective-permute-start.17
  140.2 2.0 collective-permute-start.16
  142.2 3.1 collective-permute-start.15
  147.1 5.6 %collective-permute-done.16.refs_6_.refs_10_ = bf16[128,512]{1,0:T(8,128)(2,1)} collective-permute-done((bf16[128,512]{1,0:T(8,128)(2,1)}, bf16[128,512]{1,0:T(8,128)(2,1)}, u32[]{:S(2)}, u32[]{:S(2)}) %collective-permute-start.16) | collective-permute-done | bytes 131104 | tf_op jit(solution)/shard_map/kv/ppermute | solution.py:73
  152.8 5.3 %collective-permute-done.15.refs_5_.refs_9_ = bf16[128,512]{1,0:T(8,128)(2,1)} collective-permute-done((bf16[128,512]{1,0:T(8,128)(2,1)}, bf16[128,512]{1,0:T(8,128)(2,1)}, u32[]{:S(2)}, u32[]{:S(2)}) %collective-permute-start.15) | collective-permute-done | bytes 131104 | tf_op jit(solution)/shard_map/kv/ppermute | solution.py:73
  158.1 5.8 %shard_map.256 = (bf16[128,1536]{1,0:T(8,128)(2,1)}, f32[128,1536]{1,0:T(8,128)}, bf16[128,1536]{1,0:T(8,128)(2,1)}) custom-call(s32[3]{0:T(128)} %copy-done.3, bf16[128,1536]{1,0:T(8,128)(2,1)} %bitcast.33, f32[8,1536]{1,0:T(8,128)} %get-tuple-element.129.refs_1_.refs_2_.refs_5_, s32[128,1]{1,0:T(8,128)} %copy.37.refs_2_.refs_4_, ...), custom_call_target="tpu_custom_call" | custom-call | tf_op jit(solution)/shard_map/pallas_call | solution.py:694
  164.0 8.3 %collective-permute-done.19.refs_8_ = bf16[6,3,48,1120]{3,2,1,0:T(8,128)(2,1)S(1)} collective-permute-done((bf16[6,3,48,1120]{3,2,1,0:T(8,128)(2,1)}, bf16[6,3,48,1120]{3,2,1,0:T(8,128)(2,1)S(1)}, u32[]{:S(2)}, u32[]{:S(2)}) %collective-permute-start.19) | collective-permute-done | bytes 1935392 | tf_op jit(solution)/shard_map/ff_plane1/ppermute | solution.py:73
  172.4 1.4 pad_maximum_fusion.2
  174.1 1.5 collective-permute-start.20
  175.6 2.3 slice.25
  177.8 1.4 pad_maximum_fusion.3
  179.8 25.3 %collective-permute-done.20.refs_9_ = bf16[4,3,48,1120]{3,2,1,0:T(8,128)(2,1)S(1)} collective-permute-done((bf16[4,3,48,1120]{3,2,1,0:T(8,128)(2,1)}, bf16[4,3,48,1120]{3,2,1,0:T(8,128)(2,1)S(1)}, u32[]{:S(2)}, u32[]{:S(2)}) %collective-permute-start.20) | collective-permute-done | bytes 1290272 | tf_op jit(solution)/shard_map/ff_plane2/ppermute | solution.py:73
  205.1 5.8 %collective-permute-done.21.refs_10_ = bf16[4,3,48,1120]{3,2,1,0:T(8,128)(2,1)} collective-permute-done((bf16[4,3,48,1120]{3,2,1,0:T(8,128)(2,1)S(1)}, bf16[4,3,48,1120]{3,2,1,0:T(8,128)(2,1)}, u32[]{:S(2)}, u32[]{:S(2)}) %collective-permute-start.21) | collective-permute-done | bytes 1290272 | tf_op jit(solution)/shard_map/ff_plane2/ppermute | solution.py:73
  211.3 16.7 %shard_map.257 = (bf16[512,1120]{1,0:T(8,128)(2,1)}, bf16[512,1120]{1,0:T(8,128)(2,1)}, bf16[512,1120]{1,0:T(8,128)(2,1)}, bf16[512,1536]{1,0:T(8,128)(2,1)}) custom-call(s32[3]{0:T(128)} %copy-done.3, bf16[512,1536]{1,0:T(8,128)(2,1)} %all-gather.5.cloned.1.call-done.refs_1_.refs_0_.refs_2_, ...), custom_call_target="tpu_custom_call" | custom-call | tf_op jit(solution)/shard_map/pallas_call | solution.py:455
  229.2 16.8 %shard_map.258 = (bf16[512,1120]{1,0:T(8,128)(2,1)}, bf16[512,1120]{1,0:T(8,128)(2,1)}, bf16[512,1120]{1,0:T(8,128)(2,1)}, bf16[512,1536]{1,0:T(8,128)(2,1)}) custom-call(s32[3]{0:T(128)} %copy-done.3, bf16[512,1536]{1,0:T(8,128)(2,1)} %copy-done.5, bf16[512,1536]{1,0:T(8,128)(2,1)} %copy-done.4, bf16[2,3,48,1120]{3,2,1,0:T(8,128)(2,1)} %copy-done.14, ...), custom_call_target="tpu_custom_call" | custom-call | tf_op jit(solution)/shard_map/pallas_call | solution.py:455
  246.5 3.2 collective-permute-done.24
  249.8 1.6 add_convert_fusion
  251.7 12.7 %shard_map.259 = (bf16[2,1,192,1120]{3,2,1,0:T(8,128)(2,1)}, bf16[2,2,192,1120]{3,2,1,0:T(8,128)(2,1)}, bf16[2,1,192,1120]{3,2,1,0:T(8,128)(2,1)}, bf16[2,2,192,1120]{3,2,1,0:T(8,128)(2,1)}) custom-call(s32[3]{0:T(128)} %copy-done.3, bf16[512,1536]{1,0:T(8,128)(2,1)} %all-gather.5.cloned.1.call-done.refs_1_.refs_0_.refs_2_, bf16[512,1536]{1,0:T(8,128)(2,1)} %copy-done.5, ...), custom_call_target="tpu_custom_call" | custom-call | tf_op jit(solution)/shard_map/pallas_call | solution.py:500
  265.9 9.3 %shard_map.260 = (bf16[512,1536]{1,0:T(8,128)(2,1)}, bf16[512,1536]{1,0:T(8,128)(2,1)}) custom-call(s32[3]{0:T(128)} %copy-done.3, bf16[512,1120]{1,0:T(8,128)(2,1)} %get-tuple-element.154.refs_12_.refs_1_, bf16[512,1120]{1,0:T(8,128)(2,1)} %get-tuple-element.149.refs_13_.refs_2_, bf16[2,3,48,1120]{3,2,1,0:T(8,128)(2,1)} %copy-done.14, ...), custom_call_target="tpu_custom_call" | custom-call | tf_op jit(solution)/shard_map/pallas_call | solution.py:455
  275.2 11.5 %collective-permute-done.26.refs_1_ = bf16[2,1,192,1120]{3,2,1,0:T(8,128)(2,1)} collective-permute-done((bf16[2,1,192,1120]{3,2,1,0:T(8,128)(2,1)}, bf16[2,1,192,1120]{3,2,1,0:T(8,128)(2,1)}, u32[]{:S(2)}, u32[]{:S(2)}) %collective-permute-start.26) | collective-permute-done | bytes 860192 | tf_op jit(solution)/shard_map/ff_sum1/ppermute | solution.py:73
  287.1 1.6 collective-permute-start.34
  289.8 10.1 %shard_map.261 = (f32[128,1536]{1,0:T(8,128)}, bf16[128,1536]{1,0:T(8,128)(2,1)}, bf16[128,1536]{1,0:T(8,128)(2,1)}, f32[1,1536]{1,0:T(1,128)}, bf16[128,512]{1,...) custom-call(s32[3]{0:T(128)} %copy-done.3, ...), custom_call_target="tpu_custom_call" | custom-call | flops 8000000000 | tf_op jit(solution)/shard_map/pallas_call | solution.py:694
  299.9 1.3 collective-permute-start.28
  301.2 1.3 collective-permute-start.29
  302.5 1.5 collective-permute-start.30
  304.1 12.9 %shard_map.262 = (bf16[2,3,192,1120]{3,2,1,0:T(8,128)(2,1)}, bf16[2,3,192,1120]{3,2,1,0:T(8,128)(2,1)}) custom-call(s32[3]{0:T(128)} %copy-done.3, bf16[512,1536]{1,0:T(8,128)(2,1)} %all-gather.5.cloned.1.call-done.refs_1_.refs_0_.refs_2_, bf16[512,1536]{1,0:T(8,128)(2,1)} %copy-done.5, ...), custom_call_target="tpu_custom_call" | custom-call | tf_op jit(solution)/shard_map/pallas_call | solution.py:500
  317.1 13.6 %collective-permute-done.29.refs_2_ = bf16[128,512]{1,0:T(8,128)(2,1)S(1)} collective-permute-done((bf16[128,512]{1,0:T(8,128)(2,1)}, bf16[128,512]{1,0:T(8,128)(2,1)S(1)}, u32[]{:S(2)}, u32[]{:S(2)}) %collective-permute-start.29) | collective-permute-done | bytes 131104 | tf_op jit(solution)/shard_map/gkv/ppermute | solution.py:73
  331.4 8.5 %shard_map.263 = (f32[128,1536]{1,0:T(8,128)}, bf16[144,896]{1,0:T(8,128)(2,1)}, bf16[144,896]{1,0:T(8,128)(2,1)}, bf16[144,896]{1,0:T(8,128)(2,1)}, bf16[144,896]{1,0:T(8,128)(2,1)}) custom-call(s32[3]{0:T(128)} %copy-done.3, bf16[128,512]{1,0:T(8,128)(2,1)} %get-tuple-element.166.refs_0_, bf16[128,512]{1,0:T(8,128)(2,1)} %copy-done.30, ...), custom_call_target="tpu_custom_call" | custom-call | tf_op jit(solution)/shard_map/pallas_call | solution.py:694
  340.1 3.7 collective-permute-start.33
  345.6 4.3 %shard_map.267 = (bf16[3,192,1120]{2,1,0:T(8,128)(2,1)}, bf16[3,192,1120]{2,1,0:T(8,128)(2,1)}) custom-call(bf16[2,3,192,1120]{3,2,1,0:T(8,128)(2,1)} %get-tuple-element.165.refs_0_, bf16[2,1,192,1120]{3,2,1,0:T(8,128)(2,1)} %collective-permute-done.26.refs_1_, bf16[2,2,192,1120]{3,2,1,0:T(8,128)(2,1)} %copy-done.17, ...), custom_call_target="tpu_custom_call" | custom-call | tf_op jit(solution)/shard_map/pallas_call | solution.py:541
  349.9 1.6 collective-permute-start.40
  351.5 1.5 collective-permute-start.41
  353.0 8.1 %collective-permute-done.32.refs_2_ = bf16[144,896]{1,0:T(8,128)(2,1)} collective-permute-done((bf16[144,896]{1,0:T(8,128)(2,1)}, bf16[144,896]{1,0:T(8,128)(2,1)}, u32[]{:S(2)}, u32[]{:S(2)}) %collective-permute-start.32) | collective-permute-done | bytes 258080 | tf_op jit(solution)/shard_map/gqkv_ctx/ppermute | solution.py:73
  361.1 6.0 %shard_map.264 = (bf16[4,208,896]{2,1,0:T(8,128)(2,1)}, bf16[4,208,896]{2,1,0:T(8,128)(2,1)}) custom-call(s32[3]{0:T(128)} %copy-done.3, bf16[144,896]{1,0:T(8,128)(2,1)} %get-tuple-element.179.refs_0_, bf16[144,896]{1,0:T(8,128)(2,1)} %collective-permute-done.31.refs_1_, bf16[144,896]{1,0:T(8,128)(2,1)} %collective-permute-done.32.refs_2_, ...), custom_call_target="tpu_custom_call" | custom-call | tf_op jit(solution)/shard_map/pallas_call | solution.py:938
  367.1 1.5 add_convert_fusion.1
  368.6 2.1 collective-permute-done.36.got
  370.7 3.2 shard_map.265
  373.9 6.4 %collective-permute-done.40.refs_3_ = bf16[3,192,1120]{2,1,0:T(8,128)(2,1)} collective-permute-done((bf16[3,192,1120]{2,1,0:T(8,128)(2,1)}, bf16[3,192,1120]{2,1,0:T(8,128)(2,1)}, u32[]{:S(2)}, u32[]{:S(2)}) %collective-permute-start.40) | collective-permute-done | bytes 1290272 | tf_op jit(solution)/shard_map/ff_sum2/ppermute | solution.py:73
  380.3 1.3 collective-permute-done.41.refs_7_
  381.6 7.0 %shard_map.268 = (f32[3,192,1120]{2,1,0:T(8,128)}, bf16[3,192,1120]{2,1,0:T(8,128)(2,1)}) custom-call(s32[3]{0:T(128)} %copy-done.3, bf16[2,3,192,1120]{3,2,1,0:T(8,128)(2,1)} %get-tuple-element.165.refs_0_, bf16[2,1,192,1120]{3,2,1,0:T(8,128)(2,1)} %collective-permute-done.26.refs_1_, bf16[2,2,192,1120]{3,2,1,0:T(8,128)(2,1)} %copy-done.17, ...), custom_call_target="tpu_custom_call" | custom-call | flops 12000000000 | tf_op jit(solution)/shard_map/pallas_call | solution.py:580
  389.0 1.6 collective-permute-start.38
  390.6 1.5 collective-permute-start.39
  392.1 15.1 %reduce-scatter.5.cloned.1.call-done = bf16[128,1536]{1,0:T(8,128)(2,1)} async-done(((bf16[512,1536]{1,0:T(8,128)(2,1)}), bf16[128,1536]{1,0:T(8,128)(2,1)}) %reduce-scatter.5.cloned.1.call-update) | async-done | bytes 393232 | tf_op jit(solution)/shard_map/reduce_scatter | solution.py:1158
  407.2 2.0 add_bitcast_fusion
  410.1 2.5 shard_map.266
  413.7 5.0 %shard_map.269 = (f32[192,2240]{1,0:T(8,128)}, f32[192,2240]{1,0:T(8,128)}, f32[192,2240]{1,0:T(8,128)}) custom-call(s32[3]{0:T(128)} %copy-done.3, f32[3,192,1120]{2,1,0:T(8,128)} %get-tuple-element.206.mine, bf16[3,192,1120]{2,1,0:T(8,128)(2,1)} %copy-done.41), custom_call_target="tpu_custom_call" | custom-call | flops 2000000000 | tf_op jit(solution)/shard_map/pallas_call | solution.py:938
  (177 shorter events, 27.0 us)
Async XLA Ops:
  7.3 170.6 %all-gather.7.cloned.1.call-start = ((), (), s32[]{:S(2)}) async-start(), calls=%async_computation.3 | async-start | bytes 1966080 | tf_op jit(solution)/shard_map/all_gather | solution.py:1062
  12.1 36.6 %collective-permute-start.3 = (bf16[4,3,48,1120]{3,2,1,0:T(8,128)(2,1)S(1)}, bf16[4,3,48,1120]{3,2,1,0:T(8,128)(2,1)}, u32[]{:S(2)}, u32[]{:S(2)}) collective-permute-start(bf16[4,3,48,1120]{3,2,1,0:T(8,128)(2,1)S(1)} %get-tuple-element.114), channel_id=1, source_target_pairs={{0,1},{1,0},{2,3},{3,2},{4,5},{5,4},{6,7},{7,6},{8,9},{9,8},{10,11... | collective-permute-start | bytes 3870728 | tf_op jit(solution)/shard_map/ff_core/ppermute | solution.py:73
  12.9 13.4 %collective-permute-start.2 = (bf16[48,3712]{1,0:T(8,128)(2,1)S(1)}, bf16[48,3712]{1,0:T(8,128)(2,1)S(1)}, u32[]{:S(2)}, u32[]{:S(2)}) collective-permute-start(bf16[48,3712]{1,0:T(8,128)(2,1)S(1)} %constant_dynamic-update-slice_fusion), channel_id=1, source_target_pairs={{0,24},{1,25},{2,26},{3,27},{4,28},{5,29},{6,30},{7,31},{8,0},{9,1... | collective-permute-start | bytes 1069064 | tf_op jit(solution)/shard_map/qkvo_ctx/ppermute | solution.py:73
  17.6 31.1 %collective-permute-start.1 = (bf16[48,3712]{1,0:T(8,128)(2,1)S(1)}, bf16[48,3712]{1,0:T(8,128)(2,1)}, u32[]{:S(2)}, u32[]{:S(2)}) collective-permute-start(bf16[48,3712]{1,0:T(8,128)(2,1)S(1)} %constant_dynamic-update-slice_fusion), channel_id=1, source_target_pairs={{0,16},{1,17},{2,18},{3,19},{4,20},{5,21},{6,22},{7,23},{8,24},{9,... | collective-permute-start | bytes 1069064 | tf_op jit(solution)/shard_map/qkvo_ctx/ppermute | solution.py:73
  17.6 31.1 %collective-permute-start = (bf16[48,3712]{1,0:T(8,128)(2,1)S(1)}, bf16[48,3712]{1,0:T(8,128)(2,1)}, u32[]{:S(2)}, u32[]{:S(2)}) collective-permute-start(bf16[48,3712]{1,0:T(8,128)(2,1)S(1)} %constant_dynamic-update-slice_fusion), channel_id=1, source_target_pairs={{0,8},{1,9},{2,10},{3,11},{4,12},{5,13},{6,14},{7,15},{8,16},{9,17... | collective-permute-start | bytes 1069064 | tf_op jit(solution)/shard_map/qkvo_ctx/ppermute | solution.py:73
  50.0 38.0 %collective-permute-start.8 = (bf16[4,48,3712]{2,1,0:T(8,128)(2,1)S(1)}, bf16[4,48,3712]{2,1,0:T(8,128)(2,1)S(1)}, u32[]{:S(2)}, u32[]{:S(2)}) collective-permute-start(bf16[4,48,3712]{2,1,0:T(8,128)(2,1)S(1)} %pad_maximum_fusion.1.refs_3_.refs_8_.refs_12_), channel_id=1, source_target_pairs={{0,1},{1,0},{2,3},{3,2},{4,5},{5,4},{6,7},{7,6},{8,9},{9,8},{10,11... | collective-permute-start | bytes 4276232 | tf_op jit(solution)/shard_map/qkvo_core/ppermute | solution.py:73
  50.1 37.9 %collective-permute-start.5 = (bf16[4,48,3712]{2,1,0:T(8,128)(2,1)S(1)}, bf16[4,48,3712]{2,1,0:T(8,128)(2,1)S(1)}, u32[]{:S(2)}, u32[]{:S(2)}) collective-permute-start(bf16[4,48,3712]{2,1,0:T(8,128)(2,1)S(1)} %pad_maximum_fusion.1.refs_3_.refs_8_.refs_12_), channel_id=1, source_target_pairs={{0,4},{1,5},{2,6},{3,7},{4,0},{5,1},{6,2},{7,3},{8,12},{9,13},{10,... | collective-permute-start | bytes 4276232 | tf_op jit(solution)/shard_map/qkvo_plane1/ppermute | solution.py:73
  51.7 36.4 %collective-permute-start.4 = (bf16[4,48,3712]{2,1,0:T(8,128)(2,1)S(1)}, bf16[4,48,3712]{2,1,0:T(8,128)(2,1)S(1)}, u32[]{:S(2)}, u32[]{:S(2)}) collective-permute-start(bf16[4,48,3712]{2,1,0:T(8,128)(2,1)S(1)} %pad_maximum_fusion.1.refs_3_.refs_8_.refs_12_), channel_id=1, source_target_pairs={{0,2},{1,3},{2,0},{3,1},{4,6},{5,7},{6,4},{7,5},{8,10},{9,11},{10,... | collective-permute-start | bytes 4276232 | tf_op jit(solution)/shard_map/qkvo_plane1/ppermute | solution.py:73
  54.8 16.8 %collective-permute-start.7 = (bf16[2,3,48,1120]{3,2,1,0:T(8,128)(2,1)S(1)}, bf16[2,3,48,1120]{3,2,1,0:T(8,128)(2,1)S(1)}, u32[]{:S(2)}, u32[]{:S(2)}) collective-permute-start(bf16[2,3,48,1120]{3,2,1,0:T(8,128)(2,1)S(1)} %pad_maximum_fusion.5), channel_id=1, source_target_pairs={{0,24},{1,25},{2,26},{3,27},{4,28},{5,29},{6,30},{7,31},{8,0},{9,1... | collective-permute-start | bytes 1935368 | tf_op jit(solution)/shard_map/ff_ctx_a/ppermute | solution.py:73
  55.0 33.1 %collective-permute-start.6 = (bf16[2,3,48,1120]{3,2,1,0:T(8,128)(2,1)S(1)}, bf16[2,3,48,1120]{3,2,1,0:T(8,128)(2,1)S(1)}, u32[]{:S(2)}, u32[]{:S(2)}) collective-permute-start(bf16[2,3,48,1120]{3,2,1,0:T(8,128)(2,1)S(1)} %pad_maximum_fusion.4), channel_id=1, source_target_pairs={{0,8},{1,9},{2,10},{3,11},{4,12},{5,13},{6,14},{7,15},{8,16},{9,17... | collective-permute-start | bytes 1935368 | tf_op jit(solution)/shard_map/ff_ctx_a/ppermute | solution.py:73
  57.1 34.8 %copy-start.14 = (bf16[2,3,48,1120]{3,2,1,0:T(8,128)(2,1)}, bf16[2,3,48,1120]{3,2,1,0:T(8,128)(2,1)S(1)}, u32[]{:S(2)}) copy-start(bf16[2,3,48,1120]{3,2,1,0:T(8,128)(2,1)S(1)} %pad_maximum_fusion.7.refs_3_) | copy-start | bytes 1935364
  88.1 35.4 %copy-start.6 = (bf16[4,48,3712]{2,1,0:T(8,128)(2,1)}, bf16[4,48,3712]{2,1,0:T(8,128)(2,1)S(1)}, u32[]{:S(2)}) copy-start(bf16[4,48,3712]{2,1,0:T(8,128)(2,1)S(1)} %collective-permute-done.5.refs_5_.refs_10_.refs_14_) | copy-start | bytes 4276228
  89.2 34.3 %copy-start.7 = (bf16[4,48,3712]{2,1,0:T(8,128)(2,1)}, bf16[4,48,3712]{2,1,0:T(8,128)(2,1)S(1)}, u32[]{:S(2)}) copy-start(bf16[4,48,3712]{2,1,0:T(8,128)(2,1)S(1)} %collective-permute-done.4.refs_4_.refs_9_.refs_13_) | copy-start | bytes 4276228
  89.3 31.4 %collective-permute-start.10 = (bf16[2,48,3712]{2,1,0:T(8,128)(2,1)S(1)}, bf16[2,48,3712]{2,1,0:T(8,128)(2,1)S(1)}, u32[]{:S(2)}, u32[]{:S(2)}) collective-permute-start(bf16[2,48,3712]{2,1,0:T(8,128)(2,1)S(1)} %slice.18), channel_id=1, source_target_pairs={{0,2},{1,3},{2,0},{3,1},{4,6},{5,7},{6,4},{7,5},{8,10},{9,11},{10,... | collective-permute-start | bytes 2138120 | tf_op jit(solution)/shard_map/qkvo_plane2/ppermute | solution.py:73
  89.9 30.9 %collective-permute-start.11 = (bf16[2,48,3712]{2,1,0:T(8,128)(2,1)S(1)}, bf16[2,48,3712]{2,1,0:T(8,128)(2,1)S(1)}, u32[]{:S(2)}, u32[]{:S(2)}) collective-permute-start(bf16[2,48,3712]{2,1,0:T(8,128)(2,1)S(1)} %slice.19), channel_id=1, source_target_pairs={{0,4},{1,5},{2,6},{3,7},{4,0},{5,1},{6,2},{7,3},{8,12},{9,13},{10,... | collective-permute-start | bytes 2138120 | tf_op jit(solution)/shard_map/qkvo_plane2/ppermute | solution.py:73
  90.4 28.6 %collective-permute-start.9 = (bf16[2,3,48,1120]{3,2,1,0:T(8,128)(2,1)S(1)}, bf16[2,3,48,1120]{3,2,1,0:T(8,128)(2,1)S(1)}, u32[]{:S(2)}, u32[]{:S(2)}) collective-permute-start(bf16[2,3,48,1120]{3,2,1,0:T(8,128)(2,1)S(1)} %pad_maximum_fusion.6), channel_id=1, source_target_pairs={{0,16},{1,17},{2,18},{3,19},{4,20},{5,21},{6,22},{7,23},{8,24},{9,... | collective-permute-start | bytes 1935368 | tf_op jit(solution)/shard_map/ff_ctx_b/ppermute | solution.py:73
  90.4 30.3 %collective-permute-start.13 = (bf16[2,3,48,1120]{3,2,1,0:T(8,128)(2,1)S(1)}, bf16[2,3,48,1120]{3,2,1,0:T(8,128)(2,1)S(1)}, u32[]{:S(2)}, u32[]{:S(2)}) collective-permute-start(bf16[2,3,48,1120]{3,2,1,0:T(8,128)(2,1)S(1)} %pad_maximum_fusion.7.refs_3_), channel_id=1, source_target_pairs={{0,4},{1,5},{2,6},{3,7},{4,0},{5,1},{6,2},{7,3},{8,12},{9,13},{10,... | collective-permute-start | bytes 1935368 | tf_op jit(solution)/shard_map/ff_own1/ppermute | solution.py:73
  91.9 28.8 %collective-permute-start.12 = (bf16[2,3,48,1120]{3,2,1,0:T(8,128)(2,1)S(1)}, bf16[2,3,48,1120]{3,2,1,0:T(8,128)(2,1)S(1)}, u32[]{:S(2)}, u32[]{:S(2)}) collective-permute-start(bf16[2,3,48,1120]{3,2,1,0:T(8,128)(2,1)S(1)} %pad_maximum_fusion.7.refs_3_), channel_id=1, source_target_pairs={{0,2},{1,3},{2,0},{3,1},{4,6},{5,7},{6,4},{7,5},{8,10},{9,11},{10,... | collective-permute-start | bytes 1935368 | tf_op jit(solution)/shard_map/ff_own1/ppermute | solution.py:73
  120.7 43.3 %copy-start.15 = (bf16[2,3,48,1120]{3,2,1,0:T(8,128)(2,1)}, bf16[2,3,48,1120]{3,2,1,0:T(8,128)(2,1)S(1)}, u32[]{:S(2)}) copy-start(bf16[2,3,48,1120]{3,2,1,0:T(8,128)(2,1)S(1)} %collective-permute-done.13.refs_5_) | copy-start | bytes 1935364
  120.7 43.2 %copy-start.16 = (bf16[2,3,48,1120]{3,2,1,0:T(8,128)(2,1)}, bf16[2,3,48,1120]{3,2,1,0:T(8,128)(2,1)S(1)}, u32[]{:S(2)}) copy-start(bf16[2,3,48,1120]{3,2,1,0:T(8,128)(2,1)S(1)} %collective-permute-done.12.refs_4_) | copy-start | bytes 1935364
  123.5 7.7 %collective-permute-start.14 = (bf16[12,48,3712]{2,1,0:T(8,128)(2,1)}, bf16[12,48,3712]{2,1,0:T(8,128)(2,1)}, u32[]{:S(2)}, u32[]{:S(2)}) collective-permute-start(bf16[12,48,3712]{2,1,0:T(8,128)(2,1)} %pad_maximum_fusion), channel_id=1, source_target_pairs={{0,1},{1,0},{2,3},{3,2},{4,5},{5,4},{6,7},{7,6},{8,9},{9,8},{10,11... | collective-permute-start | bytes 12828680 | tf_op jit(solution)/shard_map/qkvo_core/ppermute | solution.py:73
  123.6 87.4 %all-gather.5.cloned.1.call-start = ((), (), s32[]{:S(2)}) async-start(), calls=%async_computation.2 | async-start | bytes 1966080 | tf_op jit(solution)/shard_map/all_gather | solution.py:1063
  126.4 46.0 %collective-permute-start.19 = (bf16[6,3,48,1120]{3,2,1,0:T(8,128)(2,1)}, bf16[6,3,48,1120]{3,2,1,0:T(8,128)(2,1)S(1)}, u32[]{:S(2)}, u32[]{:S(2)}) collective-permute-start(bf16[6,3,48,1120]{3,2,1,0:T(8,128)(2,1)} %constant_dynamic-update-slice_fusion.5.refs_6_), channel_id=1, source_target_pairs={{0,4},{1,5},{2,6},{3,7},{4,0},{5,1},{6,2},{7,3},{8,12},{9,13},{10,... | collective-permute-start | bytes 5806088 | tf_op jit(solution)/shard_map/ff_plane1/ppermute | solution.py:73
  126.9 48.7 %collective-permute-start.18 = (bf16[6,3,48,1120]{3,2,1,0:T(8,128)(2,1)}, bf16[6,3,48,1120]{3,2,1,0:T(8,128)(2,1)}, u32[]{:S(2)}, u32[]{:S(2)}) collective-permute-start(bf16[6,3,48,1120]{3,2,1,0:T(8,128)(2,1)} %constant_dynamic-update-slice_fusion.5.refs_6_), channel_id=1, source_target_pairs={{0,2},{1,3},{2,0},{3,1},{4,6},{5,7},{6,4},{7,5},{8,10},{9,11},{10,... | collective-permute-start | bytes 5806088 | tf_op jit(solution)/shard_map/ff_plane1/ppermute | solution.py:73
  137.2 10.0 %collective-permute-start.17 = (bf16[128,512]{1,0:T(8,128)(2,1)}, bf16[128,512]{1,0:T(8,128)(2,1)S(1)}, u32[]{:S(2)}, u32[]{:S(2)}) collective-permute-start(bf16[128,512]{1,0:T(8,128)(2,1)} %get-tuple-element.131.refs_4_.refs_8_), channel_id=1, source_target_pairs={{0,24},{1,25},{2,26},{3,27},{4,28},{5,29},{6,30},{7,31}} | collective-permute-start | bytes 393224 | tf_op jit(solution)/shard_map/kv/ppermute | solution.py:73
  140.2 12.6 %collective-permute-start.16 = (bf16[128,512]{1,0:T(8,128)(2,1)}, bf16[128,512]{1,0:T(8,128)(2,1)}, u32[]{:S(2)}, u32[]{:S(2)}) collective-permute-start(bf16[128,512]{1,0:T(8,128)(2,1)} %get-tuple-element.131.refs_4_.refs_8_), channel_id=1, source_target_pairs={{0,16},{1,17},{2,18},{3,19},{4,20},{5,21},{6,22},{7,23},{8,24},{9,... | collective-permute-start | bytes 393224 | tf_op jit(solution)/shard_map/kv/ppermute | solution.py:73
  142.2 16.0 %collective-permute-start.15 = (bf16[128,512]{1,0:T(8,128)(2,1)}, bf16[128,512]{1,0:T(8,128)(2,1)}, u32[]{:S(2)}, u32[]{:S(2)}) collective-permute-start(bf16[128,512]{1,0:T(8,128)(2,1)} %get-tuple-element.131.refs_4_.refs_8_), channel_id=1, source_target_pairs={{0,8},{1,9},{2,10},{3,11},{4,12},{5,13},{6,14},{7,15},{8,16},{9,17... | collective-permute-start | bytes 393224 | tf_op jit(solution)/shard_map/kv/ppermute | solution.py:73
  147.1 11.0 %copy-start.29 = (bf16[128,512]{1,0:T(8,128)(2,1)}, bf16[128,512]{1,0:T(8,128)(2,1)S(1)}, u32[]{:S(2)}) copy-start(bf16[128,512]{1,0:T(8,128)(2,1)S(1)} %collective-permute-done.17.refs_7_.refs_11_) | copy-start | bytes 393220
  163.9 87.5 %all-gather.9.cloned.1.call-start = ((), (), s32[]{:S(2)}) async-start(), calls=%async_computation.4 | async-start | bytes 1966080 | tf_op jit(solution)/shard_map/all_gather | solution.py:1093
  164.0 8.4 %slice-start = ((bf16[2,3,48,1120]{3,2,1,0:T(8,128)(2,1)}), bf16[1,3,48,1120]{3,2,1,0:T(8,128)(2,1)S(1)}, s32[]{:S(2)}) async-start(bf16[2,3,48,1120]{3,2,1,0:T(8,128)(2,1)} %copy-done.15), calls=%async_computation.8 | async-start | bytes 663552 | tf_op jit(solution)/shard_map/slice | solution.py:1069
  174.1 31.1 %collective-permute-start.20 = (bf16[4,3,48,1120]{3,2,1,0:T(8,128)(2,1)}, bf16[4,3,48,1120]{3,2,1,0:T(8,128)(2,1)S(1)}, u32[]{:S(2)}, u32[]{:S(2)}) collective-permute-start(bf16[4,3,48,1120]{3,2,1,0:T(8,128)(2,1)} %pad_maximum_fusion.2), channel_id=1, source_target_pairs={{0,2},{1,3},{2,0},{3,1},{4,6},{5,7},{6,4},{7,5},{8,10},{9,11},{10,... | collective-permute-start | bytes 3870728 | tf_op jit(solution)/shard_map/ff_plane2/ppermute | solution.py:73
  177.8 33.1 %collective-permute-start.22 = (bf16[512,1536]{1,0:T(8,128)(2,1)}, bf16[512,1536]{1,0:T(8,128)(2,1)S(1)}, u32[]{:S(2)}, u32[]{:S(2)}) collective-permute-start(bf16[512,1536]{1,0:T(8,128)(2,1)} %all-gather.7.cloned.1.call-done.refs_2_.refs_4_.refs_6_), channel_id=1, source_target_pairs={{0,1},{1,0},{2,3},{3,2},{4,5},{5,4},{6,7},{7,6},{8,9},{9,8},{10,11... | collective-permute-start | bytes 4718600 | tf_op jit(solution)/shard_map/gy_core/ppermute | solution.py:73
  179.3 31.7 %collective-permute-start.21 = (bf16[4,3,48,1120]{3,2,1,0:T(8,128)(2,1)S(1)}, bf16[4,3,48,1120]{3,2,1,0:T(8,128)(2,1)}, u32[]{:S(2)}, u32[]{:S(2)}) collective-permute-start(bf16[4,3,48,1120]{3,2,1,0:T(8,128)(2,1)S(1)} %pad_maximum_fusion.3), channel_id=1, source_target_pairs={{0,4},{1,5},{2,6},{3,7},{4,0},{5,1},{6,2},{7,3},{8,12},{9,13},{10,... | collective-permute-start | bytes 3870728 | tf_op jit(solution)/shard_map/ff_plane2/ppermute | solution.py:73
  205.1 5.8 %copy-start.11 = (bf16[4,3,48,1120]{3,2,1,0:T(8,128)(2,1)}, bf16[4,3,48,1120]{3,2,1,0:T(8,128)(2,1)S(1)}, u32[]{:S(2)}) copy-start(bf16[4,3,48,1120]{3,2,1,0:T(8,128)(2,1)S(1)} %collective-permute-done.20.refs_9_) | copy-start | bytes 3870724
  211.0 17.0 %copy-start.4 = (bf16[512,1536]{1,0:T(8,128)(2,1)}, bf16[512,1536]{1,0:T(8,128)(2,1)S(1)}, u32[]{:S(2)}) copy-start(bf16[512,1536]{1,0:T(8,128)(2,1)S(1)} %collective-permute-done.22.refs_2_.refs_5_.refs_7_) | copy-start | bytes 4718596
  211.0 17.0 %collective-permute-start.23 = (bf16[512,1536]{1,0:T(8,128)(2,1)}, bf16[512,1536]{1,0:T(8,128)(2,1)S(1)}, u32[]{:S(2)}, u32[]{:S(2)}) collective-permute-start(bf16[512,1536]{1,0:T(8,128)(2,1)} %all-gather.5.cloned.1.call-done.refs_1_.refs_0_.refs_2_), channel_id=1, source_target_pairs={{0,1},{1,0},{2,3},{3,2},{4,5},{5,4},{6,7},{7,6},{8,9},{9,8},{10,11... | collective-permute-start | bytes 4718600 | tf_op jit(solution)/shard_map/n2_core/ppermute | solution.py:73
  211.1 75.8 %reduce-scatter.3.cloned.1.call-start = ((), (), s32[]{:S(2)}) async-start(), calls=%async_computation.5 | async-start | bytes 1966080 | tf_op jit(solution)/shard_map/reduce_scatter | solution.py:1094
  229.2 20.6 %copy-start.22 = (bf16[512,1536]{1,0:T(8,128)(2,1)S(1)}, bf16[512,1536]{1,0:T(8,128)(2,1)}, u32[]{:S(2)}) copy-start(bf16[512,1536]{1,0:T(8,128)(2,1)} %get-tuple-element.157) | copy-start | bytes 4718596
  246.0 3.8 collective-permute-start.24
  251.4 109.6 %all-gather.11.cloned.1.call-start = ((), (), s32[]{:S(2)}) async-start(), calls=%async_computation.7 | async-start | bytes 1966080 | tf_op jit(solution)/shard_map/all_gather | solution.py:1122
  264.4 22.3 %collective-permute-start.26 = (bf16[2,1,192,1120]{3,2,1,0:T(8,128)(2,1)}, bf16[2,1,192,1120]{3,2,1,0:T(8,128)(2,1)}, u32[]{:S(2)}, u32[]{:S(2)}) collective-permute-start(bf16[2,1,192,1120]{3,2,1,0:T(8,128)(2,1)} %get-tuple-element.150), channel_id=1, source_target_pairs={{0,4},{1,5},{2,6},{3,7},{4,0},{5,1},{6,2},{7,3},{8,12},{9,13},{10,... | collective-permute-start | bytes 2580488 | tf_op jit(solution)/shard_map/ff_sum1/ppermute | solution.py:73
  265.0 21.9 %collective-permute-start.27 = (bf16[2,1,192,1120]{3,2,1,0:T(8,128)(2,1)}, bf16[2,1,192,1120]{3,2,1,0:T(8,128)(2,1)}, u32[]{:S(2)}, u32[]{:S(2)}) collective-permute-start(bf16[2,1,192,1120]{3,2,1,0:T(8,128)(2,1)} %get-tuple-element.152), channel_id=1, source_target_pairs={{0,2},{1,3},{2,0},{3,1},{4,6},{5,7},{6,4},{7,5},{8,10},{9,11},{10,... | collective-permute-start | bytes 2580488 | tf_op jit(solution)/shard_map/ff_sum1/ppermute | solution.py:73
  286.9 120.2 %reduce-scatter.5.cloned.1.call-start = ((), (), s32[]{:S(2)}) async-start(), calls=%async_computation.6 | async-start | bytes 1966080 | tf_op jit(solution)/shard_map/reduce_scatter | solution.py:1158
  287.0 15.5 %collective-permute-start.25 = (bf16[512,1536]{1,0:T(8,128)(2,1)}, bf16[512,1536]{1,0:T(8,128)(2,1)S(1)}, u32[]{:S(2)}, u32[]{:S(2)}) collective-permute-start(bf16[512,1536]{1,0:T(8,128)(2,1)} %get-tuple-element.156), channel_id=1, source_target_pairs={{0,1},{1,0},{2,3},{3,2},{4,5},{5,4},{6,7},{7,6},{8,9},{9,8},{10,11... | collective-permute-start | bytes 4718600 | tf_op jit(solution)/shard_map/y_core/ppermute | solution.py:73
  287.1 56.7 %collective-permute-start.34 = (bf16[2,2,192,1120]{3,2,1,0:T(8,128)(2,1)}, bf16[2,2,192,1120]{3,2,1,0:T(8,128)(2,1)S(1)}, u32[]{:S(2)}, u32[]{:S(2)}) collective-permute-start(bf16[2,2,192,1120]{3,2,1,0:T(8,128)(2,1)} %get-tuple-element.151), channel_id=1, source_target_pairs={{0,4},{1,5},{2,6},{3,7},{4,0},{5,1},{6,2},{7,3},{8,12},{9,13},{10,... | collective-permute-start | bytes 5160968 | tf_op jit(solution)/shard_map/ff_sum1/ppermute | solution.py:73
  288.7 55.1 %collective-permute-start.35 = (bf16[2,2,192,1120]{3,2,1,0:T(8,128)(2,1)}, bf16[2,2,192,1120]{3,2,1,0:T(8,128)(2,1)S(1)}, u32[]{:S(2)}, u32[]{:S(2)}) collective-permute-start(bf16[2,2,192,1120]{3,2,1,0:T(8,128)(2,1)} %get-tuple-element.153), channel_id=1, source_target_pairs={{0,2},{1,3},{2,0},{3,1},{4,6},{5,7},{6,4},{7,5},{8,10},{9,11},{10,... | collective-permute-start | bytes 5160968 | tf_op jit(solution)/shard_map/ff_sum1/ppermute | solution.py:73
  299.9 17.1 %collective-permute-start.28 = (bf16[128,512]{1,0:T(8,128)(2,1)}, bf16[128,512]{1,0:T(8,128)(2,1)S(1)}, u32[]{:S(2)}, u32[]{:S(2)}) collective-permute-start(bf16[128,512]{1,0:T(8,128)(2,1)} %get-tuple-element.167), channel_id=1, source_target_pairs={{8,0},{9,1},{10,2},{11,3},{12,4},{13,5},{14,6},{15,7},{16,8},{17,9... | collective-permute-start | bytes 393224 | tf_op jit(solution)/shard_map/gkv/ppermute | solution.py:73
  301.2 29.5 %collective-permute-start.29 = (bf16[128,512]{1,0:T(8,128)(2,1)}, bf16[128,512]{1,0:T(8,128)(2,1)S(1)}, u32[]{:S(2)}, u32[]{:S(2)}) collective-permute-start(bf16[128,512]{1,0:T(8,128)(2,1)} %get-tuple-element.168), channel_id=1, source_target_pairs={{16,0},{17,1},{18,2},{19,3},{20,4},{21,5},{22,6},{23,7},{24,8},{25... | collective-permute-start | bytes 393224 | tf_op jit(solution)/shard_map/gkv/ppermute | solution.py:73
  302.5 14.5 %copy-start.20 = (bf16[512,1536]{1,0:T(8,128)(2,1)}, bf16[512,1536]{1,0:T(8,128)(2,1)S(1)}, u32[]{:S(2)}) copy-start(bf16[512,1536]{1,0:T(8,128)(2,1)S(1)} %collective-permute-done.25) | copy-start | bytes 4718596
  302.5 28.2 %collective-permute-start.30 = (bf16[128,512]{1,0:T(8,128)(2,1)}, bf16[128,512]{1,0:T(8,128)(2,1)S(1)}, u32[]{:S(2)}, u32[]{:S(2)}) collective-permute-start(bf16[128,512]{1,0:T(8,128)(2,1)} %get-tuple-element.169), channel_id=1, source_target_pairs={{24,0},{25,1},{26,2},{27,3},{28,4},{29,5},{30,6},{31,7}} | collective-permute-start | bytes 393224 | tf_op jit(solution)/shard_map/gkv/ppermute | solution.py:73
  317.1 13.6 %copy-start.30 = (bf16[128,512]{1,0:T(8,128)(2,1)}, bf16[128,512]{1,0:T(8,128)(2,1)S(1)}, u32[]{:S(2)}) copy-start(bf16[128,512]{1,0:T(8,128)(2,1)S(1)} %collective-permute-done.28.refs_1_) | copy-start | bytes 393220
  339.9 13.1 %collective-permute-start.31 = (bf16[144,896]{1,0:T(8,128)(2,1)}, bf16[144,896]{1,0:T(8,128)(2,1)}, u32[]{:S(2)}, u32[]{:S(2)}) collective-permute-start(bf16[144,896]{1,0:T(8,128)(2,1)} %get-tuple-element.173), channel_id=1, source_target_pairs={{0,8},{1,9},{2,10},{3,11},{4,12},{5,13},{6,14},{7,15},{8,16},{9,17... | collective-permute-start | bytes 774152 | tf_op jit(solution)/shard_map/gqkv_ctx/ppermute | solution.py:73
  340.0 21.1 %collective-permute-start.32 = (bf16[144,896]{1,0:T(8,128)(2,1)}, bf16[144,896]{1,0:T(8,128)(2,1)}, u32[]{:S(2)}, u32[]{:S(2)}) collective-permute-start(bf16[144,896]{1,0:T(8,128)(2,1)} %get-tuple-element.174), channel_id=1, source_target_pairs={{0,16},{1,17},{2,18},{3,19},{4,20},{5,21},{6,22},{7,23},{8,24},{9,... | collective-permute-start | bytes 774152 | tf_op jit(solution)/shard_map/gqkv_ctx/ppermute | solution.py:73
  340.1 21.0 %collective-permute-start.33 = (bf16[144,896]{1,0:T(8,128)(2,1)}, bf16[144,896]{1,0:T(8,128)(2,1)}, u32[]{:S(2)}, u32[]{:S(2)}) collective-permute-start(bf16[144,896]{1,0:T(8,128)(2,1)} %get-tuple-element.175), channel_id=1, source_target_pairs={{0,24},{1,25},{2,26},{3,27},{4,28},{5,29},{6,30},{7,31},{8,0},{9,1... | collective-permute-start | bytes 774152 | tf_op jit(solution)/shard_map/gqkv_ctx/ppermute | solution.py:73
  349.9 30.4 %collective-permute-start.40 = (bf16[3,192,1120]{2,1,0:T(8,128)(2,1)}, bf16[3,192,1120]{2,1,0:T(8,128)(2,1)}, u32[]{:S(2)}, u32[]{:S(2)}) collective-permute-start(bf16[3,192,1120]{2,1,0:T(8,128)(2,1)} %get-tuple-element.202), channel_id=1, source_target_pairs={{0,2},{1,3},{2,0},{3,1},{4,6},{5,7},{6,4},{7,5},{8,10},{9,11},{10,... | collective-permute-start | bytes 3870728 | tf_op jit(solution)/shard_map/ff_sum2/ppermute | solution.py:73
  351.5 15.6 %copy-start.19 = (bf16[512,1536]{1,0:T(8,128)(2,1)S(1)}, bf16[512,1536]{1,0:T(8,128)(2,1)}, u32[]{:S(2)}) copy-start(bf16[512,1536]{1,0:T(8,128)(2,1)} %get-tuple-element.155) | copy-start | bytes 4718596
  351.5 15.6 %copy-start.21 = (bf16[512,1536]{1,0:T(8,128)(2,1)S(1)}, bf16[512,1536]{1,0:T(8,128)(2,1)}, u32[]{:S(2)}) copy-start(bf16[512,1536]{1,0:T(8,128)(2,1)} %copy-done.20) | copy-start | bytes 4718596
  351.5 30.1 %collective-permute-start.41 = (bf16[3,192,1120]{2,1,0:T(8,128)(2,1)}, bf16[3,192,1120]{2,1,0:T(8,128)(2,1)}, u32[]{:S(2)}, u32[]{:S(2)}) collective-permute-start(bf16[3,192,1120]{2,1,0:T(8,128)(2,1)} %get-tuple-element.203), channel_id=1, source_target_pairs={{0,4},{1,5},{2,6},{3,7},{4,0},{5,1},{6,2},{7,3},{8,12},{9,13},{10,... | collective-permute-start | bytes 3870728 | tf_op jit(solution)/shard_map/ff_sum2/ppermute | solution.py:73
  367.1 3.6 collective-permute-start.36
  381.6 25.6 %copy-start.23 = (f32[128,1536]{1,0:T(8,128)S(1)}, f32[128,1536]{1,0:T(8,128)}, u32[]{:S(2)}) copy-start(f32[128,1536]{1,0:T(8,128)} %get-tuple-element.132.refs_1_) | copy-start | bytes 2359300
  388.6 24.0 %collective-permute-start.42 = (bf16[3,192,1120]{2,1,0:T(8,128)(2,1)}, bf16[3,192,1120]{2,1,0:T(8,128)(2,1)S(1)}, u32[]{:S(2)}, u32[]{:S(2)}) collective-permute-start(bf16[3,192,1120]{2,1,0:T(8,128)(2,1)} %get-tuple-element.207), channel_id=1, source_target_pairs={{0,1},{1,0},{2,3},{3,2},{4,5},{5,4},{6,7},{7,6},{8,9},{9,8},{10,11... | collective-permute-start | bytes 3870728 | tf_op jit(solution)/shard_map/final_core/ppermute | solution.py:73
  388.6 20.6 %collective-permute-start.37 = (bf16[208,896]{1,0:T(8,128)(2,1)}, bf16[208,896]{1,0:T(8,128)(2,1)S(1)}, u32[]{:S(2)}, u32[]{:S(2)}) collective-permute-start(bf16[208,896]{1,0:T(8,128)(2,1)} %get-tuple-element.185), channel_id=1, source_target_pairs={{0,2},{1,3},{2,0},{3,1},{4,6},{5,7},{6,4},{7,5},{8,10},{9,11},{10,... | collective-permute-start | bytes 1118216 | tf_op jit(solution)/shard_map/term_plane/ppermute | solution.py:73
  389.0 20.1 %collective-permute-start.38 = (bf16[208,896]{1,0:T(8,128)(2,1)}, bf16[208,896]{1,0:T(8,128)(2,1)S(1)}, u32[]{:S(2)}, u32[]{:S(2)}) collective-permute-start(bf16[208,896]{1,0:T(8,128)(2,1)} %get-tuple-element.186), channel_id=1, source_target_pairs={{0,4},{1,5},{2,6},{3,7},{4,0},{5,1},{6,2},{7,3},{8,12},{9,13},{10,... | collective-permute-start | bytes 1118216 | tf_op jit(solution)/shard_map/term_plane/ppermute | solution.py:73
  390.6 18.6 %collective-permute-start.39 = (bf16[208,896]{1,0:T(8,128)(2,1)}, bf16[208,896]{1,0:T(8,128)(2,1)S(1)}, u32[]{:S(2)}, u32[]{:S(2)}) collective-permute-start(bf16[208,896]{1,0:T(8,128)(2,1)} %get-tuple-element.187), channel_id=1, source_target_pairs={{0,6},{1,7},{2,4},{3,5},{4,2},{5,3},{6,0},{7,1},{8,14},{9,15},{10,... | collective-permute-start | bytes 1118216 | tf_op jit(solution)/shard_map/term_plane/ppermute | solution.py:73
  (29 other events, 79.3 us)
Sparse Core Ops, SparseCore 0:
  123.7 40.7 all-gather.6
  166.6 42.9 all-gather.4
  211.2 36.9 all-gather.8
  251.6 35.0 reduce-scatter.2
  288.0 47.3 all-gather.10
  368.8 38.3 reduce-scatter.4

commit v5 on v4

--- a/solution.py
+++ b/solution.py
@@ -1154,9 +1154,8 @@
     first_share = shares[0]
     shares = [first_share] + [links.turn(shares[step], step) for step in steps]
     shares[0] = after(shares[0], *ff_first)
-    y_both = after(added(y_a, y_got), *shares[1:])
+    y_both = after(added(y_a, y_got), shares[1])
     y_sum = lax.psum_scatter(y_both, "ctx", scatter_dimension=0, tiled=True)
-    layer_out = hidden_one + y_sum.astype(F32)
     links.label = "ff_sum2"
     ff_second = reduce_next(links, ff_terms, phase(ff_first, (first_share,))[0])
     chips = fsdp_size // 2
@@ -1203,6 +1202,8 @@
         place=place,
         cost=2*10**9,
     )
+
+    layer_out = hidden_one + after(y_sum, grad_q).astype(F32)
 
     return (
         layer_out[None],

time: 434 us -> 436 us (level)
    ppermute x43, waiting for transfers between devices: 188 us -> 204 us  [send(): return lax.ppermute(x, BOTH, pairs)]
    reduce_scatter x1, waiting for transfers between devices: 15.1 us -> 0.02 us  [per_device_plane_of_four(): y_sum = lax.psum_scatter(y_both, 'ctx', scatter_dimension=0, tiled=True)]
    unnamed x90 -> x96, local copies, waits for them, and re-layouts: 12.4 us -> 12.3 us
  transfers between devices with their start and end apart: 49 -> 49, of which waited for: 22 -> 24; matrix products, arithmetic and copies ran while one was open for 4% -> 4% of each run, Pallas kernels for 29% -> 29%
where the time goes in v5:
time: 436 us; the launch traced here: 427 us
  waiting for transfers between devices  205 us (47%)
  Pallas kernels  128 us (29%)
  starting transfers between devices  48.1 us (11%)
  local copies, waits for them, and re-layouts  16.5 us (4%)
  between operations  15.3 us (4%)
  other arithmetic  15 us (3%)
    ppermute x43, waiting for transfers between devices, send(): return lax.ppermute(x, BOTH, pairs)  204 us
    ppermute x43, starting transfers between devices, send(): return lax.ppermute(x, BOTH, pairs)  47.4 us
    pallas_call x3, Pallas kernels, ff_call(): pl.pallas_call(body, grid_spec=pltpu.PrefetchScalarGridSpec(num_scalar_pr...  42.8 us
    pallas_call x4, Pallas kernels, call(): pl.pallas_call(kernel, in_specs=[pl.BlockSpec(memory_space=pltpu.SMEM)] +...  30.5 us
    pallas_call x2, Pallas kernels, ff_grad_terms(): pl.pallas_call(grad_kernel, grid_spec=pltpu.PrefetchScalarGridSpec(num_sc...  25.6 us
    pallas_call x4, Pallas kernels, small_call(): pl.pallas_call(body, in_specs=[pl.BlockSpec(memory_space=pltpu.SMEM)] * l...  16.7 us
    unnamed x96, local copies, waits for them, and re-layouts  12.3 us
  transfers between devices with their start and end apart: 49, of which 24 were waited for; matrix products, arithmetic and copies ran while one was open for 4% of the time, Pallas kernels for 29%

profile of v5, /device:TPU:0, one launch (start us, length us, event | category | flops | bytes accessed | tf_op | source)
XLA Modules:
  0.0 427.4 jit_solution(14488604864363717421)
XLA Ops:
  12.9 4.7 %collective-permute-start.2 = (bf16[48,3712]{1,0:T(8,128)(2,1)S(1)}, bf16[48,3712]{1,0:T(8,128)(2,1)S(1)}, u32[]{:S(2)}, u32[]{:S(2)}) collective-permute-start(bf16[48,3712]{1,0:T(8,128)(2,1)S(1)} %constant_dynamic-update-slice_fusion), channel_id=1, source_target_pairs={{0,24},{1,25},{2,26},{3,27},{4,28},{5,29},{6,30},{7,31},{8,0},{9,1... | collective-permute-start | bytes 1069064 | tf_op jit(solution)/shard_map/qkvo_ctx/ppermute | solution.py:73
  18.6 7.7 %collective-permute-done.2 = bf16[48,3712]{1,0:T(8,128)(2,1)S(1)} collective-permute-done((bf16[48,3712]{1,0:T(8,128)(2,1)S(1)}, bf16[48,3712]{1,0:T(8,128)(2,1)S(1)}, u32[]{:S(2)}, u32[]{:S(2)}) %collective-permute-start.2) | collective-permute-done | bytes 356384 | tf_op jit(solution)/shard_map/qkvo_ctx/ppermute | solution.py:73
  26.3 22.4 %collective-permute-done.1 = bf16[48,3712]{1,0:T(8,128)(2,1)} collective-permute-done((bf16[48,3712]{1,0:T(8,128)(2,1)S(1)}, bf16[48,3712]{1,0:T(8,128)(2,1)}, u32[]{:S(2)}, u32[]{:S(2)}) %collective-permute-start.1) | collective-permute-done | bytes 356384 | tf_op jit(solution)/shard_map/qkvo_ctx/ppermute | solution.py:73
  48.7 1.3 pad_maximum_fusion.1.refs_3_.refs_8_.refs_12_
  50.1 1.6 collective-permute-start.5
  51.7 1.5 collective-permute-start.4
  53.2 1.5 broadcast_select_fusion.1
  55.0 2.1 collective-permute-start.6
  57.2 14.3 %collective-permute-done.7 = bf16[2,3,48,1120]{3,2,1,0:T(8,128)(2,1)S(1)} collective-permute-done((bf16[2,3,48,1120]{3,2,1,0:T(8,128)(2,1)S(1)}, bf16[2,3,48,1120]{3,2,1,0:T(8,128)(2,1)S(1)}, u32[]{:S(2)}, u32[]{:S(2)}) %collective-permute-start.7) | collective-permute-done | bytes 645152 | tf_op jit(solution)/shard_map/ff_ctx_a/ppermute | solution.py:73
  71.6 16.5 %collective-permute-done.6 = bf16[2,3,48,1120]{3,2,1,0:T(8,128)(2,1)S(1)} collective-permute-done((bf16[2,3,48,1120]{3,2,1,0:T(8,128)(2,1)S(1)}, bf16[2,3,48,1120]{3,2,1,0:T(8,128)(2,1)S(1)}, u32[]{:S(2)}, u32[]{:S(2)}) %collective-permute-start.6) | collective-permute-done | bytes 645152 | tf_op jit(solution)/shard_map/ff_ctx_a/ppermute | solution.py:73
  90.4 1.5 collective-permute-start.13
  91.9 1.5 collective-permute-start.12
  93.4 25.6 %collective-permute-done.9 = bf16[2,3,48,1120]{3,2,1,0:T(8,128)(2,1)S(1)} collective-permute-done((bf16[2,3,48,1120]{3,2,1,0:T(8,128)(2,1)S(1)}, bf16[2,3,48,1120]{3,2,1,0:T(8,128)(2,1)S(1)}, u32[]{:S(2)}, u32[]{:S(2)}) %collective-permute-start.9) | collective-permute-done | bytes 645152 | tf_op jit(solution)/shard_map/ff_ctx_b/ppermute | solution.py:73
  119.0 1.7 collective-permute-done.13.refs_5_
  120.8 2.7 pad_maximum_fusion
  126.9 1.5 collective-permute-start.18
  129.5 1.7 collective-permute-done.14.refs_9_.refs_14_.refs_18_
  131.2 6.0 %shard_map.255 = (bf16[128,1536]{1,0:T(8,128)(2,1)}, bf16[128,1536]{1,0:T(8,128)(2,1)}, bf16[128,512]{1,0:T(8,128)(2,1)}, f32[8,1536]{1,0:T(8,128)}) custom-call(s32[3]{0:T(128)} %copy-done.3, bf16[128,1536]{1,0:T(8,128)(2,1)} %bitcast.32, f32[128,128]{1,0:T(8,128)} %get-tuple-element.225.refs_1_.refs_6_, f32[128,128]{1,0:T(8,128)} %get-tuple-element.226.refs_2_.refs_7_, ...), custom_call_target="tpu_custom_call" | custom-call | tf_op jit(solution)/shard_map/pallas_call | solution.py:694
  137.2 3.0 collective-permute-start.17
  140.2 1.9 collective-permute-start.16
  142.1 3.1 collective-permute-start.15
  147.1 5.6 %collective-permute-done.16.refs_6_.refs_10_ = bf16[128,512]{1,0:T(8,128)(2,1)} collective-permute-done((bf16[128,512]{1,0:T(8,128)(2,1)}, bf16[128,512]{1,0:T(8,128)(2,1)}, u32[]{:S(2)}, u32[]{:S(2)}) %collective-permute-start.16) | collective-permute-done | bytes 131104 | tf_op jit(solution)/shard_map/kv/ppermute | solution.py:73
  152.7 5.3 %collective-permute-done.15.refs_5_.refs_9_ = bf16[128,512]{1,0:T(8,128)(2,1)} collective-permute-done((bf16[128,512]{1,0:T(8,128)(2,1)}, bf16[128,512]{1,0:T(8,128)(2,1)}, u32[]{:S(2)}, u32[]{:S(2)}) %collective-permute-start.15) | collective-permute-done | bytes 131104 | tf_op jit(solution)/shard_map/kv/ppermute | solution.py:73
  158.1 5.8 %shard_map.256 = (bf16[128,1536]{1,0:T(8,128)(2,1)}, f32[128,1536]{1,0:T(8,128)}, bf16[128,1536]{1,0:T(8,128)(2,1)}) custom-call(s32[3]{0:T(128)} %copy-done.3, bf16[128,1536]{1,0:T(8,128)(2,1)} %bitcast.33, f32[8,1536]{1,0:T(8,128)} %get-tuple-element.130.refs_1_.refs_2_.refs_5_, s32[128,1]{1,0:T(8,128)} %copy.37.refs_2_.refs_4_, ...), custom_call_target="tpu_custom_call" | custom-call | tf_op jit(solution)/shard_map/pallas_call | solution.py:694
  164.0 8.3 %collective-permute-done.19.refs_8_ = bf16[6,3,48,1120]{3,2,1,0:T(8,128)(2,1)S(1)} collective-permute-done((bf16[6,3,48,1120]{3,2,1,0:T(8,128)(2,1)}, bf16[6,3,48,1120]{3,2,1,0:T(8,128)(2,1)S(1)}, u32[]{:S(2)}, u32[]{:S(2)}) %collective-permute-start.19) | collective-permute-done | bytes 1935392 | tf_op jit(solution)/shard_map/ff_plane1/ppermute | solution.py:73
  172.4 1.4 pad_maximum_fusion.2
  174.0 1.5 collective-permute-start.20
  175.5 2.3 slice.25
  177.8 1.4 pad_maximum_fusion.3
  179.8 25.3 %collective-permute-done.20.refs_9_ = bf16[4,3,48,1120]{3,2,1,0:T(8,128)(2,1)S(1)} collective-permute-done((bf16[4,3,48,1120]{3,2,1,0:T(8,128)(2,1)}, bf16[4,3,48,1120]{3,2,1,0:T(8,128)(2,1)S(1)}, u32[]{:S(2)}, u32[]{:S(2)}) %collective-permute-start.20) | collective-permute-done | bytes 1290272 | tf_op jit(solution)/shard_map/ff_plane2/ppermute | solution.py:73
  205.1 5.8 %collective-permute-done.21.refs_10_ = bf16[4,3,48,1120]{3,2,1,0:T(8,128)(2,1)} collective-permute-done((bf16[4,3,48,1120]{3,2,1,0:T(8,128)(2,1)S(1)}, bf16[4,3,48,1120]{3,2,1,0:T(8,128)(2,1)}, u32[]{:S(2)}, u32[]{:S(2)}) %collective-permute-start.21) | collective-permute-done | bytes 1290272 | tf_op jit(solution)/shard_map/ff_plane2/ppermute | solution.py:73
  211.3 16.7 %shard_map.257 = (bf16[512,1120]{1,0:T(8,128)(2,1)}, bf16[512,1120]{1,0:T(8,128)(2,1)}, bf16[512,1120]{1,0:T(8,128)(2,1)}, bf16[512,1536]{1,0:T(8,128)(2,1)}) custom-call(s32[3]{0:T(128)} %copy-done.3, bf16[512,1536]{1,0:T(8,128)(2,1)} %all-gather.5.cloned.1.call-done.refs_1_.refs_0_.refs_2_, ...), custom_call_target="tpu_custom_call" | custom-call | tf_op jit(solution)/shard_map/pallas_call | solution.py:455
  229.1 16.8 %shard_map.258 = (bf16[512,1120]{1,0:T(8,128)(2,1)}, bf16[512,1120]{1,0:T(8,128)(2,1)}, bf16[512,1120]{1,0:T(8,128)(2,1)}, bf16[512,1536]{1,0:T(8,128)(2,1)}) custom-call(s32[3]{0:T(128)} %copy-done.3, bf16[512,1536]{1,0:T(8,128)(2,1)} %copy-done.5, bf16[512,1536]{1,0:T(8,128)(2,1)} %copy-done.4, bf16[2,3,48,1120]{3,2,1,0:T(8,128)(2,1)} %copy-done.14, ...), custom_call_target="tpu_custom_call" | custom-call | tf_op jit(solution)/shard_map/pallas_call | solution.py:455
  246.5 3.2 collective-permute-done.24
  249.7 1.6 add_convert_fusion
  251.7 12.7 %shard_map.259 = (bf16[2,1,192,1120]{3,2,1,0:T(8,128)(2,1)}, bf16[2,2,192,1120]{3,2,1,0:T(8,128)(2,1)}, bf16[2,1,192,1120]{3,2,1,0:T(8,128)(2,1)}, bf16[2,2,192,1120]{3,2,1,0:T(8,128)(2,1)}) custom-call(s32[3]{0:T(128)} %copy-done.3, bf16[512,1536]{1,0:T(8,128)(2,1)} %all-gather.5.cloned.1.call-done.refs_1_.refs_0_.refs_2_, bf16[512,1536]{1,0:T(8,128)(2,1)} %copy-done.5, ...), custom_call_target="tpu_custom_call" | custom-call | tf_op jit(solution)/shard_map/pallas_call | solution.py:500
  265.9 9.3 %shard_map.260 = (bf16[512,1536]{1,0:T(8,128)(2,1)}, bf16[512,1536]{1,0:T(8,128)(2,1)}) custom-call(s32[3]{0:T(128)} %copy-done.3, bf16[512,1120]{1,0:T(8,128)(2,1)} %get-tuple-element.155.refs_12_.refs_1_, bf16[512,1120]{1,0:T(8,128)(2,1)} %get-tuple-element.150.refs_13_.refs_2_, bf16[2,3,48,1120]{3,2,1,0:T(8,128)(2,1)} %copy-done.14, ...), custom_call_target="tpu_custom_call" | custom-call | tf_op jit(solution)/shard_map/pallas_call | solution.py:455
  275.3 11.4 %collective-permute-done.26.refs_1_ = bf16[2,1,192,1120]{3,2,1,0:T(8,128)(2,1)} collective-permute-done((bf16[2,1,192,1120]{3,2,1,0:T(8,128)(2,1)}, bf16[2,1,192,1120]{3,2,1,0:T(8,128)(2,1)}, u32[]{:S(2)}, u32[]{:S(2)}) %collective-permute-start.26) | collective-permute-done | bytes 860192 | tf_op jit(solution)/shard_map/ff_sum1/ppermute | solution.py:73
  287.1 1.6 collective-permute-start.32
  289.8 10.1 %shard_map.261 = (f32[128,1536]{1,0:T(8,128)}, bf16[128,1536]{1,0:T(8,128)(2,1)}, bf16[128,1536]{1,0:T(8,128)(2,1)}, f32[1,1536]{1,0:T(1,128)}, bf16[128,512]{1,...) custom-call(s32[3]{0:T(128)} %copy-done.3, ...), custom_call_target="tpu_custom_call" | custom-call | flops 8000000000 | tf_op jit(solution)/shard_map/pallas_call | solution.py:694
  302.6 1.5 collective-permute-start.30
  304.2 12.9 %shard_map.262 = (bf16[2,3,192,1120]{3,2,1,0:T(8,128)(2,1)}, bf16[2,3,192,1120]{3,2,1,0:T(8,128)(2,1)}) custom-call(s32[3]{0:T(128)} %copy-done.3, bf16[512,1536]{1,0:T(8,128)(2,1)} %all-gather.5.cloned.1.call-done.refs_1_.refs_0_.refs_2_, bf16[512,1536]{1,0:T(8,128)(2,1)} %copy-done.5, ...), custom_call_target="tpu_custom_call" | custom-call | tf_op jit(solution)/shard_map/pallas_call | solution.py:500
  317.1 13.6 %collective-permute-done.29.refs_2_ = bf16[128,512]{1,0:T(8,128)(2,1)S(1)} collective-permute-done((bf16[128,512]{1,0:T(8,128)(2,1)}, bf16[128,512]{1,0:T(8,128)(2,1)S(1)}, u32[]{:S(2)}, u32[]{:S(2)}) %collective-permute-start.29) | collective-permute-done | bytes 131104 | tf_op jit(solution)/shard_map/gkv/ppermute | solution.py:73
  331.4 8.5 %shard_map.263 = (f32[128,1536]{1,0:T(8,128)}, bf16[144,896]{1,0:T(8,128)(2,1)}, bf16[144,896]{1,0:T(8,128)(2,1)}, bf16[144,896]{1,0:T(8,128)(2,1)}, bf16[144,896]{1,0:T(8,128)(2,1)}) custom-call(s32[3]{0:T(128)} %copy-done.3, bf16[128,512]{1,0:T(8,128)(2,1)} %get-tuple-element.167.refs_0_, bf16[128,512]{1,0:T(8,128)(2,1)} %copy-done.30, ...), custom_call_target="tpu_custom_call" | custom-call | tf_op jit(solution)/shard_map/pallas_call | solution.py:694
  340.1 3.7 collective-permute-start.35
  345.6 4.3 %shard_map.267 = (bf16[3,192,1120]{2,1,0:T(8,128)(2,1)}, bf16[3,192,1120]{2,1,0:T(8,128)(2,1)}) custom-call(bf16[2,3,192,1120]{3,2,1,0:T(8,128)(2,1)} %get-tuple-element.166.refs_0_, bf16[2,1,192,1120]{3,2,1,0:T(8,128)(2,1)} %collective-permute-done.26.refs_1_, bf16[2,2,192,1120]{3,2,1,0:T(8,128)(2,1)} %copy-done.17, ...), custom_call_target="tpu_custom_call" | custom-call | tf_op jit(solution)/shard_map/pallas_call | solution.py:541
  349.9 1.6 collective-permute-start.40
  351.5 1.5 collective-permute-start.41
  353.1 8.0 %collective-permute-done.34.refs_2_ = bf16[144,896]{1,0:T(8,128)(2,1)} collective-permute-done((bf16[144,896]{1,0:T(8,128)(2,1)}, bf16[144,896]{1,0:T(8,128)(2,1)}, u32[]{:S(2)}, u32[]{:S(2)}) %collective-permute-start.34) | collective-permute-done | bytes 258080 | tf_op jit(solution)/shard_map/gqkv_ctx/ppermute | solution.py:73
  361.1 6.0 %shard_map.264 = (bf16[4,208,896]{2,1,0:T(8,128)(2,1)}, bf16[4,208,896]{2,1,0:T(8,128)(2,1)}) custom-call(s32[3]{0:T(128)} %copy-done.3, bf16[144,896]{1,0:T(8,128)(2,1)} %get-tuple-element.177.refs_0_, bf16[144,896]{1,0:T(8,128)(2,1)} %collective-permute-done.31.refs_1_, bf16[144,896]{1,0:T(8,128)(2,1)} %collective-permute-done.34.refs_2_, ...), custom_call_target="tpu_custom_call" | custom-call | tf_op jit(solution)/shard_map/pallas_call | solution.py:938
  367.1 1.5 add_convert_fusion.1
  368.7 2.1 collective-permute-done.36.got
  370.7 3.2 shard_map.265
  374.0 6.4 %collective-permute-done.40.refs_3_ = bf16[3,192,1120]{2,1,0:T(8,128)(2,1)} collective-permute-done((bf16[3,192,1120]{2,1,0:T(8,128)(2,1)}, bf16[3,192,1120]{2,1,0:T(8,128)(2,1)}, u32[]{:S(2)}, u32[]{:S(2)}) %collective-permute-start.40) | collective-permute-done | bytes 1290272 | tf_op jit(solution)/shard_map/ff_sum2/ppermute | solution.py:73
  380.3 1.3 collective-permute-done.41.refs_7_
  381.6 7.0 %shard_map.268 = (f32[3,192,1120]{2,1,0:T(8,128)}, bf16[3,192,1120]{2,1,0:T(8,128)(2,1)}) custom-call(s32[3]{0:T(128)} %copy-done.3, bf16[2,3,192,1120]{3,2,1,0:T(8,128)(2,1)} %get-tuple-element.166.refs_0_, bf16[2,1,192,1120]{3,2,1,0:T(8,128)(2,1)} %collective-permute-done.26.refs_1_, bf16[2,2,192,1120]{3,2,1,0:T(8,128)(2,1)} %copy-done.17, ...), custom_call_target="tpu_custom_call" | custom-call | flops 12000000000 | tf_op jit(solution)/shard_map/pallas_call | solution.py:580
  389.1 1.7 collective-permute-start.38
  390.8 1.4 collective-permute-start.39
  392.2 8.0 %collective-permute-done.37.refs_0_ = bf16[208,896]{1,0:T(8,128)(2,1)S(1)} collective-permute-done((bf16[208,896]{1,0:T(8,128)(2,1)S(1)}, bf16[208,896]{1,0:T(8,128)(2,1)S(1)}, u32[]{:S(2)}, u32[]{:S(2)}) %collective-permute-start.37) | collective-permute-done | bytes 372768 | tf_op jit(solution)/shard_map/term_plane/ppermute | solution.py:73
  400.2 6.9 %collective-permute-done.38.refs_1_ = bf16[208,896]{1,0:T(8,128)(2,1)S(1)} collective-permute-done((bf16[208,896]{1,0:T(8,128)(2,1)S(1)}, bf16[208,896]{1,0:T(8,128)(2,1)S(1)}, u32[]{:S(2)}, u32[]{:S(2)}) %collective-permute-start.38) | collective-permute-done | bytes 372768 | tf_op jit(solution)/shard_map/term_plane/ppermute | solution.py:73
  407.1 1.7 collective-permute-done.39.refs_2_
  409.5 2.5 shard_map.266
  412.0 2.0 add_bitcast_fusion
  415.1 5.0 %shard_map.269 = (f32[192,2240]{1,0:T(8,128)}, f32[192,2240]{1,0:T(8,128)}, f32[192,2240]{1,0:T(8,128)}) custom-call(s32[3]{0:T(128)} %copy-done.3, f32[3,192,1120]{2,1,0:T(8,128)} %get-tuple-element.208.mine, bf16[3,192,1120]{2,1,0:T(8,128)(2,1)} %copy-done.41), custom_call_target="tpu_custom_call" | custom-call | flops 2000000000 | tf_op jit(solution)/shard_map/pallas_call | solution.py:938
  (183 shorter events, 29.6 us)
Async XLA Ops:
  7.3 170.6 %all-gather.7.cloned.1.call-start = ((), (), s32[]{:S(2)}) async-start(), calls=%async_computation.3 | async-start | bytes 1966080 | tf_op jit(solution)/shard_map/all_gather | solution.py:1062
  12.1 36.6 %collective-permute-start.3 = (bf16[4,3,48,1120]{3,2,1,0:T(8,128)(2,1)S(1)}, bf16[4,3,48,1120]{3,2,1,0:T(8,128)(2,1)}, u32[]{:S(2)}, u32[]{:S(2)}) collective-permute-start(bf16[4,3,48,1120]{3,2,1,0:T(8,128)(2,1)S(1)} %get-tuple-element.115), channel_id=1, source_target_pairs={{0,1},{1,0},{2,3},{3,2},{4,5},{5,4},{6,7},{7,6},{8,9},{9,8},{10,11... | collective-permute-start | bytes 3870728 | tf_op jit(solution)/shard_map/ff_core/ppermute | solution.py:73
  12.9 13.4 %collective-permute-start.2 = (bf16[48,3712]{1,0:T(8,128)(2,1)S(1)}, bf16[48,3712]{1,0:T(8,128)(2,1)S(1)}, u32[]{:S(2)}, u32[]{:S(2)}) collective-permute-start(bf16[48,3712]{1,0:T(8,128)(2,1)S(1)} %constant_dynamic-update-slice_fusion), channel_id=1, source_target_pairs={{0,24},{1,25},{2,26},{3,27},{4,28},{5,29},{6,30},{7,31},{8,0},{9,1... | collective-permute-start | bytes 1069064 | tf_op jit(solution)/shard_map/qkvo_ctx/ppermute | solution.py:73
  17.6 31.1 %collective-permute-start.1 = (bf16[48,3712]{1,0:T(8,128)(2,1)S(1)}, bf16[48,3712]{1,0:T(8,128)(2,1)}, u32[]{:S(2)}, u32[]{:S(2)}) collective-permute-start(bf16[48,3712]{1,0:T(8,128)(2,1)S(1)} %constant_dynamic-update-slice_fusion), channel_id=1, source_target_pairs={{0,16},{1,17},{2,18},{3,19},{4,20},{5,21},{6,22},{7,23},{8,24},{9,... | collective-permute-start | bytes 1069064 | tf_op jit(solution)/shard_map/qkvo_ctx/ppermute | solution.py:73
  17.6 31.1 %collective-permute-start = (bf16[48,3712]{1,0:T(8,128)(2,1)S(1)}, bf16[48,3712]{1,0:T(8,128)(2,1)}, u32[]{:S(2)}, u32[]{:S(2)}) collective-permute-start(bf16[48,3712]{1,0:T(8,128)(2,1)S(1)} %constant_dynamic-update-slice_fusion), channel_id=1, source_target_pairs={{0,8},{1,9},{2,10},{3,11},{4,12},{5,13},{6,14},{7,15},{8,16},{9,17... | collective-permute-start | bytes 1069064 | tf_op jit(solution)/shard_map/qkvo_ctx/ppermute | solution.py:73
  50.0 38.0 %collective-permute-start.8 = (bf16[4,48,3712]{2,1,0:T(8,128)(2,1)S(1)}, bf16[4,48,3712]{2,1,0:T(8,128)(2,1)S(1)}, u32[]{:S(2)}, u32[]{:S(2)}) collective-permute-start(bf16[4,48,3712]{2,1,0:T(8,128)(2,1)S(1)} %pad_maximum_fusion.1.refs_3_.refs_8_.refs_12_), channel_id=1, source_target_pairs={{0,1},{1,0},{2,3},{3,2},{4,5},{5,4},{6,7},{7,6},{8,9},{9,8},{10,11... | collective-permute-start | bytes 4276232 | tf_op jit(solution)/shard_map/qkvo_core/ppermute | solution.py:73
  50.1 37.9 %collective-permute-start.5 = (bf16[4,48,3712]{2,1,0:T(8,128)(2,1)S(1)}, bf16[4,48,3712]{2,1,0:T(8,128)(2,1)S(1)}, u32[]{:S(2)}, u32[]{:S(2)}) collective-permute-start(bf16[4,48,3712]{2,1,0:T(8,128)(2,1)S(1)} %pad_maximum_fusion.1.refs_3_.refs_8_.refs_12_), channel_id=1, source_target_pairs={{0,4},{1,5},{2,6},{3,7},{4,0},{5,1},{6,2},{7,3},{8,12},{9,13},{10,... | collective-permute-start | bytes 4276232 | tf_op jit(solution)/shard_map/qkvo_plane1/ppermute | solution.py:73
  51.7 36.4 %collective-permute-start.4 = (bf16[4,48,3712]{2,1,0:T(8,128)(2,1)S(1)}, bf16[4,48,3712]{2,1,0:T(8,128)(2,1)S(1)}, u32[]{:S(2)}, u32[]{:S(2)}) collective-permute-start(bf16[4,48,3712]{2,1,0:T(8,128)(2,1)S(1)} %pad_maximum_fusion.1.refs_3_.refs_8_.refs_12_), channel_id=1, source_target_pairs={{0,2},{1,3},{2,0},{3,1},{4,6},{5,7},{6,4},{7,5},{8,10},{9,11},{10,... | collective-permute-start | bytes 4276232 | tf_op jit(solution)/shard_map/qkvo_plane1/ppermute | solution.py:73
  54.8 16.8 %collective-permute-start.7 = (bf16[2,3,48,1120]{3,2,1,0:T(8,128)(2,1)S(1)}, bf16[2,3,48,1120]{3,2,1,0:T(8,128)(2,1)S(1)}, u32[]{:S(2)}, u32[]{:S(2)}) collective-permute-start(bf16[2,3,48,1120]{3,2,1,0:T(8,128)(2,1)S(1)} %pad_maximum_fusion.5), channel_id=1, source_target_pairs={{0,24},{1,25},{2,26},{3,27},{4,28},{5,29},{6,30},{7,31},{8,0},{9,1... | collective-permute-start | bytes 1935368 | tf_op jit(solution)/shard_map/ff_ctx_a/ppermute | solution.py:73
  55.0 33.1 %collective-permute-start.6 = (bf16[2,3,48,1120]{3,2,1,0:T(8,128)(2,1)S(1)}, bf16[2,3,48,1120]{3,2,1,0:T(8,128)(2,1)S(1)}, u32[]{:S(2)}, u32[]{:S(2)}) collective-permute-start(bf16[2,3,48,1120]{3,2,1,0:T(8,128)(2,1)S(1)} %pad_maximum_fusion.4), channel_id=1, source_target_pairs={{0,8},{1,9},{2,10},{3,11},{4,12},{5,13},{6,14},{7,15},{8,16},{9,17... | collective-permute-start | bytes 1935368 | tf_op jit(solution)/shard_map/ff_ctx_a/ppermute | solution.py:73
  57.1 34.8 %copy-start.14 = (bf16[2,3,48,1120]{3,2,1,0:T(8,128)(2,1)}, bf16[2,3,48,1120]{3,2,1,0:T(8,128)(2,1)S(1)}, u32[]{:S(2)}) copy-start(bf16[2,3,48,1120]{3,2,1,0:T(8,128)(2,1)S(1)} %pad_maximum_fusion.7.refs_3_) | copy-start | bytes 1935364
  88.1 35.4 %copy-start.6 = (bf16[4,48,3712]{2,1,0:T(8,128)(2,1)}, bf16[4,48,3712]{2,1,0:T(8,128)(2,1)S(1)}, u32[]{:S(2)}) copy-start(bf16[4,48,3712]{2,1,0:T(8,128)(2,1)S(1)} %collective-permute-done.5.refs_5_.refs_10_.refs_14_) | copy-start | bytes 4276228
  89.2 34.3 %copy-start.7 = (bf16[4,48,3712]{2,1,0:T(8,128)(2,1)}, bf16[4,48,3712]{2,1,0:T(8,128)(2,1)S(1)}, u32[]{:S(2)}) copy-start(bf16[4,48,3712]{2,1,0:T(8,128)(2,1)S(1)} %collective-permute-done.4.refs_4_.refs_9_.refs_13_) | copy-start | bytes 4276228
  89.3 31.4 %collective-permute-start.10 = (bf16[2,48,3712]{2,1,0:T(8,128)(2,1)S(1)}, bf16[2,48,3712]{2,1,0:T(8,128)(2,1)S(1)}, u32[]{:S(2)}, u32[]{:S(2)}) collective-permute-start(bf16[2,48,3712]{2,1,0:T(8,128)(2,1)S(1)} %slice.18), channel_id=1, source_target_pairs={{0,2},{1,3},{2,0},{3,1},{4,6},{5,7},{6,4},{7,5},{8,10},{9,11},{10,... | collective-permute-start | bytes 2138120 | tf_op jit(solution)/shard_map/qkvo_plane2/ppermute | solution.py:73
  89.9 30.9 %collective-permute-start.11 = (bf16[2,48,3712]{2,1,0:T(8,128)(2,1)S(1)}, bf16[2,48,3712]{2,1,0:T(8,128)(2,1)S(1)}, u32[]{:S(2)}, u32[]{:S(2)}) collective-permute-start(bf16[2,48,3712]{2,1,0:T(8,128)(2,1)S(1)} %slice.19), channel_id=1, source_target_pairs={{0,4},{1,5},{2,6},{3,7},{4,0},{5,1},{6,2},{7,3},{8,12},{9,13},{10,... | collective-permute-start | bytes 2138120 | tf_op jit(solution)/shard_map/qkvo_plane2/ppermute | solution.py:73
  90.4 28.6 %collective-permute-start.9 = (bf16[2,3,48,1120]{3,2,1,0:T(8,128)(2,1)S(1)}, bf16[2,3,48,1120]{3,2,1,0:T(8,128)(2,1)S(1)}, u32[]{:S(2)}, u32[]{:S(2)}) collective-permute-start(bf16[2,3,48,1120]{3,2,1,0:T(8,128)(2,1)S(1)} %pad_maximum_fusion.6), channel_id=1, source_target_pairs={{0,16},{1,17},{2,18},{3,19},{4,20},{5,21},{6,22},{7,23},{8,24},{9,... | collective-permute-start | bytes 1935368 | tf_op jit(solution)/shard_map/ff_ctx_b/ppermute | solution.py:73
  90.4 30.3 %collective-permute-start.13 = (bf16[2,3,48,1120]{3,2,1,0:T(8,128)(2,1)S(1)}, bf16[2,3,48,1120]{3,2,1,0:T(8,128)(2,1)S(1)}, u32[]{:S(2)}, u32[]{:S(2)}) collective-permute-start(bf16[2,3,48,1120]{3,2,1,0:T(8,128)(2,1)S(1)} %pad_maximum_fusion.7.refs_3_), channel_id=1, source_target_pairs={{0,4},{1,5},{2,6},{3,7},{4,0},{5,1},{6,2},{7,3},{8,12},{9,13},{10,... | collective-permute-start | bytes 1935368 | tf_op jit(solution)/shard_map/ff_own1/ppermute | solution.py:73
  91.9 28.8 %collective-permute-start.12 = (bf16[2,3,48,1120]{3,2,1,0:T(8,128)(2,1)S(1)}, bf16[2,3,48,1120]{3,2,1,0:T(8,128)(2,1)S(1)}, u32[]{:S(2)}, u32[]{:S(2)}) collective-permute-start(bf16[2,3,48,1120]{3,2,1,0:T(8,128)(2,1)S(1)} %pad_maximum_fusion.7.refs_3_), channel_id=1, source_target_pairs={{0,2},{1,3},{2,0},{3,1},{4,6},{5,7},{6,4},{7,5},{8,10},{9,11},{10,... | collective-permute-start | bytes 1935368 | tf_op jit(solution)/shard_map/ff_own1/ppermute | solution.py:73
  120.7 43.3 %copy-start.15 = (bf16[2,3,48,1120]{3,2,1,0:T(8,128)(2,1)}, bf16[2,3,48,1120]{3,2,1,0:T(8,128)(2,1)S(1)}, u32[]{:S(2)}) copy-start(bf16[2,3,48,1120]{3,2,1,0:T(8,128)(2,1)S(1)} %collective-permute-done.13.refs_5_) | copy-start | bytes 1935364
  120.7 43.2 %copy-start.16 = (bf16[2,3,48,1120]{3,2,1,0:T(8,128)(2,1)}, bf16[2,3,48,1120]{3,2,1,0:T(8,128)(2,1)S(1)}, u32[]{:S(2)}) copy-start(bf16[2,3,48,1120]{3,2,1,0:T(8,128)(2,1)S(1)} %collective-permute-done.12.refs_4_) | copy-start | bytes 1935364
  123.5 7.7 %collective-permute-start.14 = (bf16[12,48,3712]{2,1,0:T(8,128)(2,1)}, bf16[12,48,3712]{2,1,0:T(8,128)(2,1)}, u32[]{:S(2)}, u32[]{:S(2)}) collective-permute-start(bf16[12,48,3712]{2,1,0:T(8,128)(2,1)} %pad_maximum_fusion), channel_id=1, source_target_pairs={{0,1},{1,0},{2,3},{3,2},{4,5},{5,4},{6,7},{7,6},{8,9},{9,8},{10,11... | collective-permute-start | bytes 12828680 | tf_op jit(solution)/shard_map/qkvo_core/ppermute | solution.py:73
  123.6 87.4 %all-gather.5.cloned.1.call-start = ((), (), s32[]{:S(2)}) async-start(), calls=%async_computation.2 | async-start | bytes 1966080 | tf_op jit(solution)/shard_map/all_gather | solution.py:1063
  126.4 46.0 %collective-permute-start.19 = (bf16[6,3,48,1120]{3,2,1,0:T(8,128)(2,1)}, bf16[6,3,48,1120]{3,2,1,0:T(8,128)(2,1)S(1)}, u32[]{:S(2)}, u32[]{:S(2)}) collective-permute-start(bf16[6,3,48,1120]{3,2,1,0:T(8,128)(2,1)} %constant_dynamic-update-slice_fusion.5.refs_6_), channel_id=1, source_target_pairs={{0,4},{1,5},{2,6},{3,7},{4,0},{5,1},{6,2},{7,3},{8,12},{9,13},{10,... | collective-permute-start | bytes 5806088 | tf_op jit(solution)/shard_map/ff_plane1/ppermute | solution.py:73
  126.9 48.7 %collective-permute-start.18 = (bf16[6,3,48,1120]{3,2,1,0:T(8,128)(2,1)}, bf16[6,3,48,1120]{3,2,1,0:T(8,128)(2,1)}, u32[]{:S(2)}, u32[]{:S(2)}) collective-permute-start(bf16[6,3,48,1120]{3,2,1,0:T(8,128)(2,1)} %constant_dynamic-update-slice_fusion.5.refs_6_), channel_id=1, source_target_pairs={{0,2},{1,3},{2,0},{3,1},{4,6},{5,7},{6,4},{7,5},{8,10},{9,11},{10,... | collective-permute-start | bytes 5806088 | tf_op jit(solution)/shard_map/ff_plane1/ppermute | solution.py:73
  137.2 10.0 %collective-permute-start.17 = (bf16[128,512]{1,0:T(8,128)(2,1)}, bf16[128,512]{1,0:T(8,128)(2,1)S(1)}, u32[]{:S(2)}, u32[]{:S(2)}) collective-permute-start(bf16[128,512]{1,0:T(8,128)(2,1)} %get-tuple-element.132.refs_4_.refs_8_), channel_id=1, source_target_pairs={{0,24},{1,25},{2,26},{3,27},{4,28},{5,29},{6,30},{7,31}} | collective-permute-start | bytes 393224 | tf_op jit(solution)/shard_map/kv/ppermute | solution.py:73
  140.2 12.6 %collective-permute-start.16 = (bf16[128,512]{1,0:T(8,128)(2,1)}, bf16[128,512]{1,0:T(8,128)(2,1)}, u32[]{:S(2)}, u32[]{:S(2)}) collective-permute-start(bf16[128,512]{1,0:T(8,128)(2,1)} %get-tuple-element.132.refs_4_.refs_8_), channel_id=1, source_target_pairs={{0,16},{1,17},{2,18},{3,19},{4,20},{5,21},{6,22},{7,23},{8,24},{9,... | collective-permute-start | bytes 393224 | tf_op jit(solution)/shard_map/kv/ppermute | solution.py:73
  142.1 16.0 %collective-permute-start.15 = (bf16[128,512]{1,0:T(8,128)(2,1)}, bf16[128,512]{1,0:T(8,128)(2,1)}, u32[]{:S(2)}, u32[]{:S(2)}) collective-permute-start(bf16[128,512]{1,0:T(8,128)(2,1)} %get-tuple-element.132.refs_4_.refs_8_), channel_id=1, source_target_pairs={{0,8},{1,9},{2,10},{3,11},{4,12},{5,13},{6,14},{7,15},{8,16},{9,17... | collective-permute-start | bytes 393224 | tf_op jit(solution)/shard_map/kv/ppermute | solution.py:73
  147.1 11.0 %copy-start.29 = (bf16[128,512]{1,0:T(8,128)(2,1)}, bf16[128,512]{1,0:T(8,128)(2,1)S(1)}, u32[]{:S(2)}) copy-start(bf16[128,512]{1,0:T(8,128)(2,1)S(1)} %collective-permute-done.17.refs_7_.refs_11_) | copy-start | bytes 393220
  163.9 87.5 %all-gather.9.cloned.1.call-start = ((), (), s32[]{:S(2)}) async-start(), calls=%async_computation.4 | async-start | bytes 1966080 | tf_op jit(solution)/shard_map/all_gather | solution.py:1093
  174.0 31.1 %collective-permute-start.20 = (bf16[4,3,48,1120]{3,2,1,0:T(8,128)(2,1)}, bf16[4,3,48,1120]{3,2,1,0:T(8,128)(2,1)S(1)}, u32[]{:S(2)}, u32[]{:S(2)}) collective-permute-start(bf16[4,3,48,1120]{3,2,1,0:T(8,128)(2,1)} %pad_maximum_fusion.2), channel_id=1, source_target_pairs={{0,2},{1,3},{2,0},{3,1},{4,6},{5,7},{6,4},{7,5},{8,10},{9,11},{10,... | collective-permute-start | bytes 3870728 | tf_op jit(solution)/shard_map/ff_plane2/ppermute | solution.py:73
  177.8 33.1 %collective-permute-start.22 = (bf16[512,1536]{1,0:T(8,128)(2,1)}, bf16[512,1536]{1,0:T(8,128)(2,1)S(1)}, u32[]{:S(2)}, u32[]{:S(2)}) collective-permute-start(bf16[512,1536]{1,0:T(8,128)(2,1)} %all-gather.7.cloned.1.call-done.refs_2_.refs_4_.refs_6_), channel_id=1, source_target_pairs={{0,1},{1,0},{2,3},{3,2},{4,5},{5,4},{6,7},{7,6},{8,9},{9,8},{10,11... | collective-permute-start | bytes 4718600 | tf_op jit(solution)/shard_map/gy_core/ppermute | solution.py:73
  179.2 31.7 %collective-permute-start.21 = (bf16[4,3,48,1120]{3,2,1,0:T(8,128)(2,1)S(1)}, bf16[4,3,48,1120]{3,2,1,0:T(8,128)(2,1)}, u32[]{:S(2)}, u32[]{:S(2)}) collective-permute-start(bf16[4,3,48,1120]{3,2,1,0:T(8,128)(2,1)S(1)} %pad_maximum_fusion.3), channel_id=1, source_target_pairs={{0,4},{1,5},{2,6},{3,7},{4,0},{5,1},{6,2},{7,3},{8,12},{9,13},{10,... | collective-permute-start | bytes 3870728 | tf_op jit(solution)/shard_map/ff_plane2/ppermute | solution.py:73
  210.9 17.0 %copy-start.4 = (bf16[512,1536]{1,0:T(8,128)(2,1)}, bf16[512,1536]{1,0:T(8,128)(2,1)S(1)}, u32[]{:S(2)}) copy-start(bf16[512,1536]{1,0:T(8,128)(2,1)S(1)} %collective-permute-done.22.refs_2_.refs_5_.refs_7_) | copy-start | bytes 4718596
  211.0 17.0 %collective-permute-start.23 = (bf16[512,1536]{1,0:T(8,128)(2,1)}, bf16[512,1536]{1,0:T(8,128)(2,1)S(1)}, u32[]{:S(2)}, u32[]{:S(2)}) collective-permute-start(bf16[512,1536]{1,0:T(8,128)(2,1)} %all-gather.5.cloned.1.call-done.refs_1_.refs_0_.refs_2_), channel_id=1, source_target_pairs={{0,1},{1,0},{2,3},{3,2},{4,5},{5,4},{6,7},{7,6},{8,9},{9,8},{10,11... | collective-permute-start | bytes 4718600 | tf_op jit(solution)/shard_map/n2_core/ppermute | solution.py:73
  211.1 75.8 %reduce-scatter.3.cloned.1.call-start = ((), (), s32[]{:S(2)}) async-start(), calls=%async_computation.5 | async-start | bytes 1966080 | tf_op jit(solution)/shard_map/reduce_scatter | solution.py:1094
  229.1 20.6 %copy-start.22 = (bf16[512,1536]{1,0:T(8,128)(2,1)S(1)}, bf16[512,1536]{1,0:T(8,128)(2,1)}, u32[]{:S(2)}) copy-start(bf16[512,1536]{1,0:T(8,128)(2,1)} %get-tuple-element.158) | copy-start | bytes 4718596
  246.0 3.8 collective-permute-start.24
  251.4 109.7 %all-gather.11.cloned.1.call-start = ((), (), s32[]{:S(2)}) async-start(), calls=%async_computation.7 | async-start | bytes 1966080 | tf_op jit(solution)/shard_map/all_gather | solution.py:1122
  264.4 22.3 %collective-permute-start.26 = (bf16[2,1,192,1120]{3,2,1,0:T(8,128)(2,1)}, bf16[2,1,192,1120]{3,2,1,0:T(8,128)(2,1)}, u32[]{:S(2)}, u32[]{:S(2)}) collective-permute-start(bf16[2,1,192,1120]{3,2,1,0:T(8,128)(2,1)} %get-tuple-element.151), channel_id=1, source_target_pairs={{0,4},{1,5},{2,6},{3,7},{4,0},{5,1},{6,2},{7,3},{8,12},{9,13},{10,... | collective-permute-start | bytes 2580488 | tf_op jit(solution)/shard_map/ff_sum1/ppermute | solution.py:73
  265.0 21.9 %collective-permute-start.27 = (bf16[2,1,192,1120]{3,2,1,0:T(8,128)(2,1)}, bf16[2,1,192,1120]{3,2,1,0:T(8,128)(2,1)}, u32[]{:S(2)}, u32[]{:S(2)}) collective-permute-start(bf16[2,1,192,1120]{3,2,1,0:T(8,128)(2,1)} %get-tuple-element.153), channel_id=1, source_target_pairs={{0,2},{1,3},{2,0},{3,1},{4,6},{5,7},{6,4},{7,5},{8,10},{9,11},{10,... | collective-permute-start | bytes 2580488 | tf_op jit(solution)/shard_map/ff_sum1/ppermute | solution.py:73
  286.9 125.1 %reduce-scatter.5.cloned.1.call-start = ((), (), s32[]{:S(2)}) async-start(), calls=%async_computation.6 | async-start | bytes 1966080 | tf_op jit(solution)/shard_map/reduce_scatter | solution.py:1158
  287.0 15.6 %collective-permute-start.25 = (bf16[512,1536]{1,0:T(8,128)(2,1)}, bf16[512,1536]{1,0:T(8,128)(2,1)S(1)}, u32[]{:S(2)}, u32[]{:S(2)}) collective-permute-start(bf16[512,1536]{1,0:T(8,128)(2,1)} %get-tuple-element.157), channel_id=1, source_target_pairs={{0,1},{1,0},{2,3},{3,2},{4,5},{5,4},{6,7},{7,6},{8,9},{9,8},{10,11... | collective-permute-start | bytes 4718600 | tf_op jit(solution)/shard_map/y_core/ppermute | solution.py:73
  287.1 56.8 %collective-permute-start.32 = (bf16[2,2,192,1120]{3,2,1,0:T(8,128)(2,1)}, bf16[2,2,192,1120]{3,2,1,0:T(8,128)(2,1)S(1)}, u32[]{:S(2)}, u32[]{:S(2)}) collective-permute-start(bf16[2,2,192,1120]{3,2,1,0:T(8,128)(2,1)} %get-tuple-element.152), channel_id=1, source_target_pairs={{0,4},{1,5},{2,6},{3,7},{4,0},{5,1},{6,2},{7,3},{8,12},{9,13},{10,... | collective-permute-start | bytes 5160968 | tf_op jit(solution)/shard_map/ff_sum1/ppermute | solution.py:73
  288.6 55.2 %collective-permute-start.33 = (bf16[2,2,192,1120]{3,2,1,0:T(8,128)(2,1)}, bf16[2,2,192,1120]{3,2,1,0:T(8,128)(2,1)S(1)}, u32[]{:S(2)}, u32[]{:S(2)}) collective-permute-start(bf16[2,2,192,1120]{3,2,1,0:T(8,128)(2,1)} %get-tuple-element.154), channel_id=1, source_target_pairs={{0,2},{1,3},{2,0},{3,1},{4,6},{5,7},{6,4},{7,5},{8,10},{9,11},{10,... | collective-permute-start | bytes 5160968 | tf_op jit(solution)/shard_map/ff_sum1/ppermute | solution.py:73
  300.0 17.1 %collective-permute-start.28 = (bf16[128,512]{1,0:T(8,128)(2,1)}, bf16[128,512]{1,0:T(8,128)(2,1)S(1)}, u32[]{:S(2)}, u32[]{:S(2)}) collective-permute-start(bf16[128,512]{1,0:T(8,128)(2,1)} %get-tuple-element.168), channel_id=1, source_target_pairs={{8,0},{9,1},{10,2},{11,3},{12,4},{13,5},{14,6},{15,7},{16,8},{17,9... | collective-permute-start | bytes 393224 | tf_op jit(solution)/shard_map/gkv/ppermute | solution.py:73
  301.3 29.4 %collective-permute-start.29 = (bf16[128,512]{1,0:T(8,128)(2,1)}, bf16[128,512]{1,0:T(8,128)(2,1)S(1)}, u32[]{:S(2)}, u32[]{:S(2)}) collective-permute-start(bf16[128,512]{1,0:T(8,128)(2,1)} %get-tuple-element.169), channel_id=1, source_target_pairs={{16,0},{17,1},{18,2},{19,3},{20,4},{21,5},{22,6},{23,7},{24,8},{25... | collective-permute-start | bytes 393224 | tf_op jit(solution)/shard_map/gkv/ppermute | solution.py:73
  302.6 14.5 %copy-start.20 = (bf16[512,1536]{1,0:T(8,128)(2,1)}, bf16[512,1536]{1,0:T(8,128)(2,1)S(1)}, u32[]{:S(2)}) copy-start(bf16[512,1536]{1,0:T(8,128)(2,1)S(1)} %collective-permute-done.25) | copy-start | bytes 4718596
  302.6 28.1 %collective-permute-start.30 = (bf16[128,512]{1,0:T(8,128)(2,1)}, bf16[128,512]{1,0:T(8,128)(2,1)S(1)}, u32[]{:S(2)}, u32[]{:S(2)}) collective-permute-start(bf16[128,512]{1,0:T(8,128)(2,1)} %get-tuple-element.170), channel_id=1, source_target_pairs={{24,0},{25,1},{26,2},{27,3},{28,4},{29,5},{30,6},{31,7}} | collective-permute-start | bytes 393224 | tf_op jit(solution)/shard_map/gkv/ppermute | solution.py:73
  317.1 13.6 %copy-start.30 = (bf16[128,512]{1,0:T(8,128)(2,1)}, bf16[128,512]{1,0:T(8,128)(2,1)S(1)}, u32[]{:S(2)}) copy-start(bf16[128,512]{1,0:T(8,128)(2,1)S(1)} %collective-permute-done.28.refs_1_) | copy-start | bytes 393220
  340.0 13.1 %collective-permute-start.31 = (bf16[144,896]{1,0:T(8,128)(2,1)}, bf16[144,896]{1,0:T(8,128)(2,1)}, u32[]{:S(2)}, u32[]{:S(2)}) collective-permute-start(bf16[144,896]{1,0:T(8,128)(2,1)} %get-tuple-element.174), channel_id=1, source_target_pairs={{0,8},{1,9},{2,10},{3,11},{4,12},{5,13},{6,14},{7,15},{8,16},{9,17... | collective-permute-start | bytes 774152 | tf_op jit(solution)/shard_map/gqkv_ctx/ppermute | solution.py:73
  340.0 21.1 %collective-permute-start.34 = (bf16[144,896]{1,0:T(8,128)(2,1)}, bf16[144,896]{1,0:T(8,128)(2,1)}, u32[]{:S(2)}, u32[]{:S(2)}) collective-permute-start(bf16[144,896]{1,0:T(8,128)(2,1)} %get-tuple-element.178), channel_id=1, source_target_pairs={{0,16},{1,17},{2,18},{3,19},{4,20},{5,21},{6,22},{7,23},{8,24},{9,... | collective-permute-start | bytes 774152 | tf_op jit(solution)/shard_map/gqkv_ctx/ppermute | solution.py:73
  340.1 21.0 %collective-permute-start.35 = (bf16[144,896]{1,0:T(8,128)(2,1)}, bf16[144,896]{1,0:T(8,128)(2,1)}, u32[]{:S(2)}, u32[]{:S(2)}) collective-permute-start(bf16[144,896]{1,0:T(8,128)(2,1)} %get-tuple-element.179), channel_id=1, source_target_pairs={{0,24},{1,25},{2,26},{3,27},{4,28},{5,29},{6,30},{7,31},{8,0},{9,1... | collective-permute-start | bytes 774152 | tf_op jit(solution)/shard_map/gqkv_ctx/ppermute | solution.py:73
  349.9 30.4 %collective-permute-start.40 = (bf16[3,192,1120]{2,1,0:T(8,128)(2,1)}, bf16[3,192,1120]{2,1,0:T(8,128)(2,1)}, u32[]{:S(2)}, u32[]{:S(2)}) collective-permute-start(bf16[3,192,1120]{2,1,0:T(8,128)(2,1)} %get-tuple-element.204), channel_id=1, source_target_pairs={{0,2},{1,3},{2,0},{3,1},{4,6},{5,7},{6,4},{7,5},{8,10},{9,11},{10,... | collective-permute-start | bytes 3870728 | tf_op jit(solution)/shard_map/ff_sum2/ppermute | solution.py:73
  351.5 15.6 %copy-start.19 = (bf16[512,1536]{1,0:T(8,128)(2,1)S(1)}, bf16[512,1536]{1,0:T(8,128)(2,1)}, u32[]{:S(2)}) copy-start(bf16[512,1536]{1,0:T(8,128)(2,1)} %get-tuple-element.156) | copy-start | bytes 4718596
  351.5 15.6 %copy-start.21 = (bf16[512,1536]{1,0:T(8,128)(2,1)S(1)}, bf16[512,1536]{1,0:T(8,128)(2,1)}, u32[]{:S(2)}) copy-start(bf16[512,1536]{1,0:T(8,128)(2,1)} %copy-done.20) | copy-start | bytes 4718596
  351.5 30.1 %collective-permute-start.41 = (bf16[3,192,1120]{2,1,0:T(8,128)(2,1)}, bf16[3,192,1120]{2,1,0:T(8,128)(2,1)}, u32[]{:S(2)}, u32[]{:S(2)}) collective-permute-start(bf16[3,192,1120]{2,1,0:T(8,128)(2,1)} %get-tuple-element.205), channel_id=1, source_target_pairs={{0,4},{1,5},{2,6},{3,7},{4,0},{5,1},{6,2},{7,3},{8,12},{9,13},{10,... | collective-permute-start | bytes 3870728 | tf_op jit(solution)/shard_map/ff_sum2/ppermute | solution.py:73
  367.1 3.6 collective-permute-start.36
  381.6 9.2 %copy-start.42 = (bf16[208,896]{1,0:T(8,128)(2,1)S(1)}, bf16[208,896]{1,0:T(8,128)(2,1)}, u32[]{:S(2)}) copy-start(bf16[208,896]{1,0:T(8,128)(2,1)} %get-tuple-element.187) | copy-start | bytes 1118212
  388.6 23.4 %copy-start.23 = (f32[128,1536]{1,0:T(8,128)S(1)}, f32[128,1536]{1,0:T(8,128)}, u32[]{:S(2)}) copy-start(f32[128,1536]{1,0:T(8,128)} %get-tuple-element.133.refs_1_) | copy-start | bytes 2359300
  388.7 25.3 %collective-permute-start.42 = (bf16[3,192,1120]{2,1,0:T(8,128)(2,1)}, bf16[3,192,1120]{2,1,0:T(8,128)(2,1)S(1)}, u32[]{:S(2)}, u32[]{:S(2)}) collective-permute-start(bf16[3,192,1120]{2,1,0:T(8,128)(2,1)} %get-tuple-element.209), channel_id=1, source_target_pairs={{0,1},{1,0},{2,3},{3,2},{4,5},{5,4},{6,7},{7,6},{8,9},{9,8},{10,11... | collective-permute-start | bytes 3870728 | tf_op jit(solution)/shard_map/final_core/ppermute | solution.py:73
  388.7 11.5 %collective-permute-start.37 = (bf16[208,896]{1,0:T(8,128)(2,1)S(1)}, bf16[208,896]{1,0:T(8,128)(2,1)S(1)}, u32[]{:S(2)}, u32[]{:S(2)}) collective-permute-start(bf16[208,896]{1,0:T(8,128)(2,1)S(1)} %copy-done.44), channel_id=1, source_target_pairs={{0,2},{1,3},{2,0},{3,1},{4,6},{5,7},{6,4},{7,5},{8,10},{9,11},{10,... | collective-permute-start | bytes 1118216 | tf_op jit(solution)/shard_map/term_plane/ppermute | solution.py:73
  389.1 18.0 %collective-permute-start.38 = (bf16[208,896]{1,0:T(8,128)(2,1)S(1)}, bf16[208,896]{1,0:T(8,128)(2,1)S(1)}, u32[]{:S(2)}, u32[]{:S(2)}) collective-permute-start(bf16[208,896]{1,0:T(8,128)(2,1)S(1)} %copy-done.43), channel_id=1, source_target_pairs={{0,4},{1,5},{2,6},{3,7},{4,0},{5,1},{6,2},{7,3},{8,12},{9,13},{10,... | collective-permute-start | bytes 1118216 | tf_op jit(solution)/shard_map/term_plane/ppermute | solution.py:73
  390.8 18.0 %collective-permute-start.39 = (bf16[208,896]{1,0:T(8,128)(2,1)S(1)}, bf16[208,896]{1,0:T(8,128)(2,1)S(1)}, u32[]{:S(2)}, u32[]{:S(2)}) collective-permute-start(bf16[208,896]{1,0:T(8,128)(2,1)S(1)} %copy-done.42), channel_id=1, source_target_pairs={{0,6},{1,7},{2,4},{3,5},{4,2},{5,3},{6,0},{7,1},{8,14},{9,15},{10,... | collective-permute-start | bytes 1118216 | tf_op jit(solution)/shard_map/term_plane/ppermute | solution.py:73
  400.2 8.6 %copy-start.24 = (bf16[208,896]{1,0:T(8,128)(2,1)}, bf16[208,896]{1,0:T(8,128)(2,1)S(1)}, u32[]{:S(2)}) copy-start(bf16[208,896]{1,0:T(8,128)(2,1)S(1)} %collective-permute-done.37.refs_0_) | copy-start | bytes 1118212
  (32 other events, 108.0 us)
Sparse Core Ops, SparseCore 0:
  123.7 40.7 all-gather.6
  166.6 42.9 all-gather.4
  211.2 36.9 all-gather.8
  251.5 35.0 reduce-scatter.2
  288.1 47.3 all-gather.10
  368.8 38.3 reduce-scatter.4

commit v6 on v4

--- a/solution.py
+++ b/solution.py
@@ -550,8 +550,8 @@
     return links.plane(low, 2), links.plane(high, 4)
 
 
-def reduce_end_kernel(place, *refs):
-    low, high, (mine, send) = refs[:4], refs[4:8], refs[8:]
+def reduce_end_kernel(turned, place, *refs):
+    low, high, (out,) = refs[:4], refs[4:8], refs[8:]
 
     def write(ref, parts):
         keep, one, rest, last = parts
@@ -560,34 +560,35 @@
         total = keep[0, 1:].astype(F32) + rest[0].astype(F32) + last[1:].astype(F32)
         ref[1:] = total.astype(ref.dtype)
 
-    @pl.when(place[2] == 0)
+    @pl.when(place[2] == turned)
     def _():
-        write(mine, low)
-        write(send, high)
-
-    @pl.when(place[2] != 0)
+        write(out, low)
+
+    @pl.when(place[2] != turned)
     def _():
-        write(mine, high)
-        write(send, low)
-
-
-def reduce_end(place, terms, first, second):
+        write(out, high)
+
+
+def reduce_end(place, terms, first, second, turned, dtype, cost):
     shape = terms[0].shape[1:]
     spec = first_specs(0)
     whole = pl.BlockSpec(shape, lambda i, place: (0, 0, 0))
     low = (terms[0], first[0], first[1])
     high = (terms[1], first[2], first[3])
+    def body(*refs):
+        reduce_end_kernel(turned, *refs)
+
     return pl.pallas_call(
-        reduce_end_kernel,
+        body,
         grid_spec=pltpu.PrefetchScalarGridSpec(
             num_scalar_prefetch=1,
             grid=(1,),
             in_specs=[*map(spec, low), whole, *map(spec, high), whole],
-            out_specs=[whole] * 2,
+            out_specs=whole,
         ),
-        out_shape=[jax.ShapeDtypeStruct(shape, F32), jax.ShapeDtypeStruct(shape, BF16)],
+        out_shape=jax.ShapeDtypeStruct(shape, dtype),
         compiler_params=pltpu.CompilerParams(vmem_limit_bytes=56 * 2**20),
-        cost_estimate=pl.CostEstimate(flops=12*10**9, bytes_accessed=0, transcendentals=0),
+        cost_estimate=pl.CostEstimate(flops=cost, bytes_accessed=0, transcendentals=0),
     )(place, *low, second[0], *high, second[1])
 
 
@@ -1173,6 +1174,8 @@
         place,
     )
     links.label = "term_core"
+    ff_send = reduce_end(place, ff_terms, ff_first, ff_second, 1, BF16, 12 * 10**9)
+    term_mine = after(term_mine, ff_send)
     keep, *sends = small_call(
         sum_cores_kernel,
         (term_mine, links.core(term_other)),
@@ -1194,7 +1197,8 @@
     vectors = [x[0] for x in vectors]
 
     links.label = "final_core"
-    ff_mine, ff_send = reduce_end(place, ff_terms, ff_first, phase(ff_second, sends)[0])
+    ff_second = phase(ff_second, sends)[0]
+    ff_mine = reduce_end(place, ff_terms, ff_first, ff_second, 0, F32, 0)
     hidden = 2 * ff_mine.shape[2]
     grad_gate, grad_up, grad_down = small_call(
         join_cores_kernel,

time: 434 us -> 433 us (level)
  waiting for transfers between devices: 203 us -> 196 us
  Pallas kernels: 128 us -> 133 us
    reduce_scatter x1, waiting for transfers between devices: 15.1 us -> 3.45 us  [per_device_plane_of_four(): y_sum = lax.psum_scatter(y_both, 'ctx', scatter_dimension=0, tiled=True)]
    pallas_call x1 -> x2, Pallas kernels: 6.99 us -> 11.4 us  [reduce_end(): pl.pallas_call(body, grid_spec=pltpu.PrefetchScalarGridSpec(num_scalar_pr...]
    unnamed x90 -> x92, local copies, waits for them, and re-layouts: 12.4 us -> 13.4 us
  transfers between devices with their start and end apart: 49 -> 49, of which waited for: 22 -> 22; matrix products, arithmetic and copies ran while one was open for 4% -> 4% of each run, Pallas kernels for 29% -> 30%
where the time goes in v6:
time: 433 us; the launch traced here: 424 us
  waiting for transfers between devices  196 us (45%)
  Pallas kernels  133 us (31%)
  starting transfers between devices  47.9 us (11%)
  local copies, waits for them, and re-layouts  17.6 us (4%)
  between operations  15.2 us (4%)
  other arithmetic  14.8 us (3%)
    ppermute x43, waiting for transfers between devices, send(): return lax.ppermute(x, BOTH, pairs)  192 us
    ppermute x43, starting transfers between devices, send(): return lax.ppermute(x, BOTH, pairs)  47.3 us
    pallas_call x3, Pallas kernels, ff_call(): pl.pallas_call(body, grid_spec=pltpu.PrefetchScalarGridSpec(num_scalar_pr...  42.8 us
    pallas_call x4, Pallas kernels, call(): pl.pallas_call(kernel, in_specs=[pl.BlockSpec(memory_space=pltpu.SMEM)] +...  30.4 us
    pallas_call x2, Pallas kernels, ff_grad_terms(): pl.pallas_call(grad_kernel, grid_spec=pltpu.PrefetchScalarGridSpec(num_sc...  25.8 us
    pallas_call x4, Pallas kernels, small_call(): pl.pallas_call(body, in_specs=[pl.BlockSpec(memory_space=pltpu.SMEM)] * l...  16.7 us
    unnamed x92, local copies, waits for them, and re-layouts  13.4 us
    pallas_call x2, Pallas kernels, reduce_end(): pl.pallas_call(body, grid_spec=pltpu.PrefetchScalarGridSpec(num_scalar_pr...  11.4 us
  transfers between devices with their start and end apart: 49, of which 22 were waited for; matrix products, arithmetic and copies ran while one was open for 4% of the time, Pallas kernels for 30%

profile of v6, /device:TPU:0, one launch (start us, length us, event | category | flops | bytes accessed | tf_op | source)
XLA Modules:
  0.0 424.1 jit_solution(12072030279056078325)
XLA Ops:
  12.9 4.7 %collective-permute-start.2 = (bf16[48,3712]{1,0:T(8,128)(2,1)S(1)}, bf16[48,3712]{1,0:T(8,128)(2,1)S(1)}, u32[]{:S(2)}, u32[]{:S(2)}) collective-permute-start(bf16[48,3712]{1,0:T(8,128)(2,1)S(1)} %constant_dynamic-update-slice_fusion), channel_id=1, source_target_pairs={{0,24},{1,25},{2,26},{3,27},{4,28},{5,29},{6,30},{7,31},{8,0},{9,1... | collective-permute-start | bytes 1069064 | tf_op jit(solution)/shard_map/qkvo_ctx/ppermute | solution.py:73
  18.6 7.7 %collective-permute-done.2 = bf16[48,3712]{1,0:T(8,128)(2,1)S(1)} collective-permute-done((bf16[48,3712]{1,0:T(8,128)(2,1)S(1)}, bf16[48,3712]{1,0:T(8,128)(2,1)S(1)}, u32[]{:S(2)}, u32[]{:S(2)}) %collective-permute-start.2) | collective-permute-done | bytes 356384 | tf_op jit(solution)/shard_map/qkvo_ctx/ppermute | solution.py:73
  26.3 22.4 %collective-permute-done.1 = bf16[48,3712]{1,0:T(8,128)(2,1)} collective-permute-done((bf16[48,3712]{1,0:T(8,128)(2,1)S(1)}, bf16[48,3712]{1,0:T(8,128)(2,1)}, u32[]{:S(2)}, u32[]{:S(2)}) %collective-permute-start.1) | collective-permute-done | bytes 356384 | tf_op jit(solution)/shard_map/qkvo_ctx/ppermute | solution.py:73
  48.7 1.3 pad_maximum_fusion.1.refs_3_.refs_8_.refs_12_
  50.1 1.6 collective-permute-start.5
  51.7 1.5 collective-permute-start.4
  53.2 1.5 broadcast_select_fusion.1
  55.0 2.1 collective-permute-start.6
  57.2 14.3 %collective-permute-done.7 = bf16[2,3,48,1120]{3,2,1,0:T(8,128)(2,1)S(1)} collective-permute-done((bf16[2,3,48,1120]{3,2,1,0:T(8,128)(2,1)S(1)}, bf16[2,3,48,1120]{3,2,1,0:T(8,128)(2,1)S(1)}, u32[]{:S(2)}, u32[]{:S(2)}) %collective-permute-start.7) | collective-permute-done | bytes 645152 | tf_op jit(solution)/shard_map/ff_ctx_a/ppermute | solution.py:73
  71.6 16.5 %collective-permute-done.6 = bf16[2,3,48,1120]{3,2,1,0:T(8,128)(2,1)S(1)} collective-permute-done((bf16[2,3,48,1120]{3,2,1,0:T(8,128)(2,1)S(1)}, bf16[2,3,48,1120]{3,2,1,0:T(8,128)(2,1)S(1)}, u32[]{:S(2)}, u32[]{:S(2)}) %collective-permute-start.6) | collective-permute-done | bytes 645152 | tf_op jit(solution)/shard_map/ff_ctx_a/ppermute | solution.py:73
  90.4 1.5 collective-permute-start.13
  91.9 1.5 collective-permute-start.12
  93.4 25.6 %collective-permute-done.9 = bf16[2,3,48,1120]{3,2,1,0:T(8,128)(2,1)S(1)} collective-permute-done((bf16[2,3,48,1120]{3,2,1,0:T(8,128)(2,1)S(1)}, bf16[2,3,48,1120]{3,2,1,0:T(8,128)(2,1)S(1)}, u32[]{:S(2)}, u32[]{:S(2)}) %collective-permute-start.9) | collective-permute-done | bytes 645152 | tf_op jit(solution)/shard_map/ff_ctx_b/ppermute | solution.py:73
  119.0 1.7 collective-permute-done.13.refs_5_
  120.8 2.7 pad_maximum_fusion
  126.9 1.5 collective-permute-start.18
  129.5 1.7 collective-permute-done.14.refs_9_.refs_14_.refs_18_
  131.2 6.0 %shard_map.255 = (bf16[128,1536]{1,0:T(8,128)(2,1)}, bf16[128,1536]{1,0:T(8,128)(2,1)}, bf16[128,512]{1,0:T(8,128)(2,1)}, f32[8,1536]{1,0:T(8,128)}) custom-call(s32[3]{0:T(128)} %copy-done.3, bf16[128,1536]{1,0:T(8,128)(2,1)} %bitcast.32, f32[128,128]{1,0:T(8,128)} %get-tuple-element.221.refs_1_.refs_6_, f32[128,128]{1,0:T(8,128)} %get-tuple-element.222.refs_2_.refs_7_, ...), custom_call_target="tpu_custom_call" | custom-call | tf_op jit(solution)/shard_map/pallas_call | solution.py:695
  137.2 3.0 collective-permute-start.17
  140.2 2.0 collective-permute-start.16
  142.2 3.1 collective-permute-start.15
  147.1 5.6 %collective-permute-done.16.refs_6_.refs_10_ = bf16[128,512]{1,0:T(8,128)(2,1)} collective-permute-done((bf16[128,512]{1,0:T(8,128)(2,1)}, bf16[128,512]{1,0:T(8,128)(2,1)}, u32[]{:S(2)}, u32[]{:S(2)}) %collective-permute-start.16) | collective-permute-done | bytes 131104 | tf_op jit(solution)/shard_map/kv/ppermute | solution.py:73
  152.8 5.3 %collective-permute-done.15.refs_5_.refs_9_ = bf16[128,512]{1,0:T(8,128)(2,1)} collective-permute-done((bf16[128,512]{1,0:T(8,128)(2,1)}, bf16[128,512]{1,0:T(8,128)(2,1)}, u32[]{:S(2)}, u32[]{:S(2)}) %collective-permute-start.15) | collective-permute-done | bytes 131104 | tf_op jit(solution)/shard_map/kv/ppermute | solution.py:73
  158.1 5.8 %shard_map.256 = (bf16[128,1536]{1,0:T(8,128)(2,1)}, f32[128,1536]{1,0:T(8,128)}, bf16[128,1536]{1,0:T(8,128)(2,1)}) custom-call(s32[3]{0:T(128)} %copy-done.3, bf16[128,1536]{1,0:T(8,128)(2,1)} %bitcast.33, f32[8,1536]{1,0:T(8,128)} %get-tuple-element.128.refs_1_.refs_2_.refs_5_, s32[128,1]{1,0:T(8,128)} %copy.37.refs_2_.refs_4_, ...), custom_call_target="tpu_custom_call" | custom-call | tf_op jit(solution)/shard_map/pallas_call | solution.py:695
  164.0 8.3 %collective-permute-done.19.refs_8_ = bf16[6,3,48,1120]{3,2,1,0:T(8,128)(2,1)S(1)} collective-permute-done((bf16[6,3,48,1120]{3,2,1,0:T(8,128)(2,1)}, bf16[6,3,48,1120]{3,2,1,0:T(8,128)(2,1)S(1)}, u32[]{:S(2)}, u32[]{:S(2)}) %collective-permute-start.19) | collective-permute-done | bytes 1935392 | tf_op jit(solution)/shard_map/ff_plane1/ppermute | solution.py:73
  172.4 1.4 pad_maximum_fusion.2
  174.1 1.5 collective-permute-start.20
  175.6 2.3 slice.25
  177.8 1.4 pad_maximum_fusion.3
  179.8 25.3 %collective-permute-done.20.refs_9_ = bf16[4,3,48,1120]{3,2,1,0:T(8,128)(2,1)S(1)} collective-permute-done((bf16[4,3,48,1120]{3,2,1,0:T(8,128)(2,1)}, bf16[4,3,48,1120]{3,2,1,0:T(8,128)(2,1)S(1)}, u32[]{:S(2)}, u32[]{:S(2)}) %collective-permute-start.20) | collective-permute-done | bytes 1290272 | tf_op jit(solution)/shard_map/ff_plane2/ppermute | solution.py:73
  205.1 5.8 %collective-permute-done.21.refs_10_ = bf16[4,3,48,1120]{3,2,1,0:T(8,128)(2,1)} collective-permute-done((bf16[4,3,48,1120]{3,2,1,0:T(8,128)(2,1)S(1)}, bf16[4,3,48,1120]{3,2,1,0:T(8,128)(2,1)}, u32[]{:S(2)}, u32[]{:S(2)}) %collective-permute-start.21) | collective-permute-done | bytes 1290272 | tf_op jit(solution)/shard_map/ff_plane2/ppermute | solution.py:73
  211.3 16.7 %shard_map.257 = (bf16[512,1120]{1,0:T(8,128)(2,1)}, bf16[512,1120]{1,0:T(8,128)(2,1)}, bf16[512,1120]{1,0:T(8,128)(2,1)}, bf16[512,1536]{1,0:T(8,128)(2,1)}) custom-call(s32[3]{0:T(128)} %copy-done.3, bf16[512,1536]{1,0:T(8,128)(2,1)} %all-gather.5.cloned.1.call-done.refs_1_.refs_0_.refs_2_, ...), custom_call_target="tpu_custom_call" | custom-call | tf_op jit(solution)/shard_map/pallas_call | solution.py:455
  229.2 16.8 %shard_map.258 = (bf16[512,1120]{1,0:T(8,128)(2,1)}, bf16[512,1120]{1,0:T(8,128)(2,1)}, bf16[512,1120]{1,0:T(8,128)(2,1)}, bf16[512,1536]{1,0:T(8,128)(2,1)}) custom-call(s32[3]{0:T(128)} %copy-done.3, bf16[512,1536]{1,0:T(8,128)(2,1)} %copy-done.5, bf16[512,1536]{1,0:T(8,128)(2,1)} %copy-done.4, bf16[2,3,48,1120]{3,2,1,0:T(8,128)(2,1)} %copy-done.14, ...), custom_call_target="tpu_custom_call" | custom-call | tf_op jit(solution)/shard_map/pallas_call | solution.py:455
  246.5 3.2 collective-permute-done.24
  249.8 1.5 add_convert_fusion
  251.6 12.7 %shard_map.259 = (bf16[2,1,192,1120]{3,2,1,0:T(8,128)(2,1)}, bf16[2,2,192,1120]{3,2,1,0:T(8,128)(2,1)}, bf16[2,1,192,1120]{3,2,1,0:T(8,128)(2,1)}, bf16[2,2,192,1120]{3,2,1,0:T(8,128)(2,1)}) custom-call(s32[3]{0:T(128)} %copy-done.3, bf16[512,1536]{1,0:T(8,128)(2,1)} %all-gather.5.cloned.1.call-done.refs_1_.refs_0_.refs_2_, bf16[512,1536]{1,0:T(8,128)(2,1)} %copy-done.5, ...), custom_call_target="tpu_custom_call" | custom-call | tf_op jit(solution)/shard_map/pallas_call | solution.py:500
  265.9 9.4 %shard_map.260 = (bf16[512,1536]{1,0:T(8,128)(2,1)}, bf16[512,1536]{1,0:T(8,128)(2,1)}) custom-call(s32[3]{0:T(128)} %copy-done.3, bf16[512,1120]{1,0:T(8,128)(2,1)} %get-tuple-element.153.refs_12_.refs_1_, bf16[512,1120]{1,0:T(8,128)(2,1)} %get-tuple-element.148.refs_13_.refs_2_, bf16[2,3,48,1120]{3,2,1,0:T(8,128)(2,1)} %copy-done.14, ...), custom_call_target="tpu_custom_call" | custom-call | tf_op jit(solution)/shard_map/pallas_call | solution.py:455
  275.2 11.4 %collective-permute-done.26.refs_1_.refs_2_ = bf16[2,1,192,1120]{3,2,1,0:T(8,128)(2,1)} collective-permute-done((bf16[2,1,192,1120]{3,2,1,0:T(8,128)(2,1)}, bf16[2,1,192,1120]{3,2,1,0:T(8,128)(2,1)}, u32[]{:S(2)}, u32[]{:S(2)}) %collective-permute-start.26) | collective-permute-done | bytes 860192 | tf_op jit(solution)/shard_map/ff_sum1/ppermute | solution.py:73
  286.9 1.6 collective-permute-start.34
  289.7 10.1 %shard_map.261 = (f32[128,1536]{1,0:T(8,128)}, bf16[128,1536]{1,0:T(8,128)(2,1)}, bf16[128,1536]{1,0:T(8,128)(2,1)}, f32[1,1536]{1,0:T(1,128)}, bf16[128,512]{1,...) custom-call(s32[3]{0:T(128)} %copy-done.3, ...), custom_call_target="tpu_custom_call" | custom-call | flops 8000000000 | tf_op jit(solution)/shard_map/pallas_call | solution.py:695
  299.8 1.3 collective-permute-start.28
  301.1 1.3 collective-permute-start.29
  302.4 1.5 collective-permute-start.30
  303.9 13.1 %shard_map.262 = (bf16[2,3,192,1120]{3,2,1,0:T(8,128)(2,1)}, bf16[2,3,192,1120]{3,2,1,0:T(8,128)(2,1)}) custom-call(s32[3]{0:T(128)} %copy-done.3, bf16[512,1536]{1,0:T(8,128)(2,1)} %all-gather.5.cloned.1.call-done.refs_1_.refs_0_.refs_2_, bf16[512,1536]{1,0:T(8,128)(2,1)} %copy-done.5, ...), custom_call_target="tpu_custom_call" | custom-call | tf_op jit(solution)/shard_map/pallas_call | solution.py:500
  317.1 13.7 %collective-permute-done.29.refs_2_ = bf16[128,512]{1,0:T(8,128)(2,1)S(1)} collective-permute-done((bf16[128,512]{1,0:T(8,128)(2,1)}, bf16[128,512]{1,0:T(8,128)(2,1)S(1)}, u32[]{:S(2)}, u32[]{:S(2)}) %collective-permute-start.29) | collective-permute-done | bytes 131104 | tf_op jit(solution)/shard_map/gkv/ppermute | solution.py:73
  331.5 8.5 %shard_map.263 = (f32[128,1536]{1,0:T(8,128)}, bf16[144,896]{1,0:T(8,128)(2,1)}, bf16[144,896]{1,0:T(8,128)(2,1)}, bf16[144,896]{1,0:T(8,128)(2,1)}, bf16[144,896]{1,0:T(8,128)(2,1)}) custom-call(s32[3]{0:T(128)} %copy-done.3, bf16[128,512]{1,0:T(8,128)(2,1)} %get-tuple-element.165.refs_0_, bf16[128,512]{1,0:T(8,128)(2,1)} %copy-done.31, ...), custom_call_target="tpu_custom_call" | custom-call | tf_op jit(solution)/shard_map/pallas_call | solution.py:695
  340.2 3.7 collective-permute-start.33
  345.7 4.4 %shard_map.265 = (bf16[3,192,1120]{2,1,0:T(8,128)(2,1)}, bf16[3,192,1120]{2,1,0:T(8,128)(2,1)}) custom-call(bf16[2,3,192,1120]{3,2,1,0:T(8,128)(2,1)} %get-tuple-element.164.refs_0_.refs_1_, bf16[2,1,192,1120]{3,2,1,0:T(8,128)(2,1)} %collective-permute-done.26.refs_1_.refs_2_, bf16[2,2,192,1120]{3,2,1,0:T(8,128)(2,1)} %copy-done.17, ...), custom_call_target="tpu_custom_call" | custom-call | tf_op jit(solution)/shard_map/pallas_call | solution.py:541
  350.1 1.6 collective-permute-start.36
  351.8 1.5 collective-permute-start.37
  353.3 1.5 add_convert_fusion.1
  354.8 6.7 %collective-permute-done.32.refs_2_ = bf16[144,896]{1,0:T(8,128)(2,1)} collective-permute-done((bf16[144,896]{1,0:T(8,128)(2,1)}, bf16[144,896]{1,0:T(8,128)(2,1)}, u32[]{:S(2)}, u32[]{:S(2)}) %collective-permute-start.32) | collective-permute-done | bytes 258080 | tf_op jit(solution)/shard_map/gqkv_ctx/ppermute | solution.py:73
  361.6 6.0 %shard_map.264 = (bf16[4,208,896]{2,1,0:T(8,128)(2,1)}, bf16[4,208,896]{2,1,0:T(8,128)(2,1)}) custom-call(s32[3]{0:T(128)} %copy-done.3, bf16[144,896]{1,0:T(8,128)(2,1)} %get-tuple-element.178.refs_0_, bf16[144,896]{1,0:T(8,128)(2,1)} %collective-permute-done.31.refs_1_, bf16[144,896]{1,0:T(8,128)(2,1)} %collective-permute-done.32.refs_2_, ...), custom_call_target="tpu_custom_call" | custom-call | tf_op jit(solution)/shard_map/pallas_call | solution.py:939
  367.6 13.3 %collective-permute-done.36.refs_4_ = bf16[3,192,1120]{2,1,0:T(8,128)(2,1)S(1)} collective-permute-done((bf16[3,192,1120]{2,1,0:T(8,128)(2,1)}, bf16[3,192,1120]{2,1,0:T(8,128)(2,1)S(1)}, u32[]{:S(2)}, u32[]{:S(2)}) %collective-permute-start.36) | collective-permute-done | bytes 1290272 | tf_op jit(solution)/shard_map/ff_sum2/ppermute | solution.py:73
  380.9 1.3 collective-permute-done.37.refs_8_
  383.3 5.6 %shard_map.266 = bf16[3,192,1120]{2,1,0:T(8,128)(2,1)} custom-call(s32[3]{0:T(128)} %copy-done.3, bf16[2,3,192,1120]{3,2,1,0:T(8,128)(2,1)} %get-tuple-element.164.refs_0_.refs_1_, bf16[2,1,192,1120]{3,2,1,0:T(8,128)(2,1)} %collective-permute-done.26.refs_1_.refs_2_, bf16[2,2,192,1120]{3,2,1,0:T(8,128)(2,1)} %copy-done.17, bf16[3,192,1120]{2,1,0:T(8,128)(2,1)} %copy-done.22, ...), custom_call_target="tpu_custom_call" | custom-call | flops 12000000000 | tf_op jit(solution)/shard_map/pallas_call | solution.py:581
  390.0 3.2 shard_map.267
  393.2 1.4 collective-permute-start.39
  394.6 1.6 collective-permute-start.40
  396.7 3.4 reduce-scatter.5.cloned.1.call-done
  400.1 2.0 add_bitcast_fusion
  402.1 5.9 %shard_map.269.mine = f32[3,192,1120]{2,1,0:T(8,128)} custom-call(s32[3]{0:T(128)} %copy-done.3, bf16[2,3,192,1120]{3,2,1,0:T(8,128)(2,1)} %get-tuple-element.164.refs_0_.refs_1_, bf16[2,1,192,1120]{3,2,1,0:T(8,128)(2,1)} %collective-permute-done.26.refs_1_.refs_2_, bf16[2,2,192,1120]{3,2,1,0:T(8,128)(2,1)} %copy-done.17, bf16[3,192,1120]{2,1,0:T(8,128)(2,1)} %copy-done.22, ...), custom_call_target="tpu_custom_call" | custom-call | tf_op jit(solution)/shard_map/pallas_call | solution.py:581
  408.0 5.0 %shard_map.270 = (f32[192,2240]{1,0:T(8,128)}, f32[192,2240]{1,0:T(8,128)}, f32[192,2240]{1,0:T(8,128)}) custom-call(s32[3]{0:T(128)} %copy-done.3, f32[3,192,1120]{2,1,0:T(8,128)} %shard_map.269.mine, bf16[3,192,1120]{2,1,0:T(8,128)(2,1)} %copy-done.42), custom_call_target="tpu_custom_call" | custom-call | flops 2000000000 | tf_op jit(solution)/shard_map/pallas_call | solution.py:939
  414.3 2.5 shard_map.268
  (180 shorter events, 28.5 us)
Async XLA Ops:
  7.2 5.6 %copy-start.35 = (bf16[48,256]{1,0:T(8,128)(2,1)S(1)}, bf16[48,256]{1,0:T(8,128)(2,1)}, u32[]{:S(2)}) copy-start(bf16[48,256]{1,0:T(8,128)(2,1)} %param.22) | copy-start | bytes 73732
  7.3 170.6 %all-gather.7.cloned.1.call-start = ((), (), s32[]{:S(2)}) async-start(), calls=%async_computation.3 | async-start | bytes 1966080 | tf_op jit(solution)/shard_map/all_gather | solution.py:1063
  12.1 36.6 %collective-permute-start.3 = (bf16[4,3,48,1120]{3,2,1,0:T(8,128)(2,1)S(1)}, bf16[4,3,48,1120]{3,2,1,0:T(8,128)(2,1)}, u32[]{:S(2)}, u32[]{:S(2)}) collective-permute-start(bf16[4,3,48,1120]{3,2,1,0:T(8,128)(2,1)S(1)} %get-tuple-element.113), channel_id=1, source_target_pairs={{0,1},{1,0},{2,3},{3,2},{4,5},{5,4},{6,7},{7,6},{8,9},{9,8},{10,11... | collective-permute-start | bytes 3870728 | tf_op jit(solution)/shard_map/ff_core/ppermute | solution.py:73
  12.9 13.4 %collective-permute-start.2 = (bf16[48,3712]{1,0:T(8,128)(2,1)S(1)}, bf16[48,3712]{1,0:T(8,128)(2,1)S(1)}, u32[]{:S(2)}, u32[]{:S(2)}) collective-permute-start(bf16[48,3712]{1,0:T(8,128)(2,1)S(1)} %constant_dynamic-update-slice_fusion), channel_id=1, source_target_pairs={{0,24},{1,25},{2,26},{3,27},{4,28},{5,29},{6,30},{7,31},{8,0},{9,1... | collective-permute-start | bytes 1069064 | tf_op jit(solution)/shard_map/qkvo_ctx/ppermute | solution.py:73
  17.6 31.1 %collective-permute-start.1 = (bf16[48,3712]{1,0:T(8,128)(2,1)S(1)}, bf16[48,3712]{1,0:T(8,128)(2,1)}, u32[]{:S(2)}, u32[]{:S(2)}) collective-permute-start(bf16[48,3712]{1,0:T(8,128)(2,1)S(1)} %constant_dynamic-update-slice_fusion), channel_id=1, source_target_pairs={{0,16},{1,17},{2,18},{3,19},{4,20},{5,21},{6,22},{7,23},{8,24},{9,... | collective-permute-start | bytes 1069064 | tf_op jit(solution)/shard_map/qkvo_ctx/ppermute | solution.py:73
  17.6 31.1 %collective-permute-start = (bf16[48,3712]{1,0:T(8,128)(2,1)S(1)}, bf16[48,3712]{1,0:T(8,128)(2,1)}, u32[]{:S(2)}, u32[]{:S(2)}) collective-permute-start(bf16[48,3712]{1,0:T(8,128)(2,1)S(1)} %constant_dynamic-update-slice_fusion), channel_id=1, source_target_pairs={{0,8},{1,9},{2,10},{3,11},{4,12},{5,13},{6,14},{7,15},{8,16},{9,17... | collective-permute-start | bytes 1069064 | tf_op jit(solution)/shard_map/qkvo_ctx/ppermute | solution.py:73
  50.0 38.0 %collective-permute-start.8 = (bf16[4,48,3712]{2,1,0:T(8,128)(2,1)S(1)}, bf16[4,48,3712]{2,1,0:T(8,128)(2,1)S(1)}, u32[]{:S(2)}, u32[]{:S(2)}) collective-permute-start(bf16[4,48,3712]{2,1,0:T(8,128)(2,1)S(1)} %pad_maximum_fusion.1.refs_3_.refs_8_.refs_12_), channel_id=1, source_target_pairs={{0,1},{1,0},{2,3},{3,2},{4,5},{5,4},{6,7},{7,6},{8,9},{9,8},{10,11... | collective-permute-start | bytes 4276232 | tf_op jit(solution)/shard_map/qkvo_core/ppermute | solution.py:73
  50.1 37.9 %collective-permute-start.5 = (bf16[4,48,3712]{2,1,0:T(8,128)(2,1)S(1)}, bf16[4,48,3712]{2,1,0:T(8,128)(2,1)S(1)}, u32[]{:S(2)}, u32[]{:S(2)}) collective-permute-start(bf16[4,48,3712]{2,1,0:T(8,128)(2,1)S(1)} %pad_maximum_fusion.1.refs_3_.refs_8_.refs_12_), channel_id=1, source_target_pairs={{0,4},{1,5},{2,6},{3,7},{4,0},{5,1},{6,2},{7,3},{8,12},{9,13},{10,... | collective-permute-start | bytes 4276232 | tf_op jit(solution)/shard_map/qkvo_plane1/ppermute | solution.py:73
  51.7 36.4 %collective-permute-start.4 = (bf16[4,48,3712]{2,1,0:T(8,128)(2,1)S(1)}, bf16[4,48,3712]{2,1,0:T(8,128)(2,1)S(1)}, u32[]{:S(2)}, u32[]{:S(2)}) collective-permute-start(bf16[4,48,3712]{2,1,0:T(8,128)(2,1)S(1)} %pad_maximum_fusion.1.refs_3_.refs_8_.refs_12_), channel_id=1, source_target_pairs={{0,2},{1,3},{2,0},{3,1},{4,6},{5,7},{6,4},{7,5},{8,10},{9,11},{10,... | collective-permute-start | bytes 4276232 | tf_op jit(solution)/shard_map/qkvo_plane1/ppermute | solution.py:73
  54.8 16.8 %collective-permute-start.7 = (bf16[2,3,48,1120]{3,2,1,0:T(8,128)(2,1)S(1)}, bf16[2,3,48,1120]{3,2,1,0:T(8,128)(2,1)S(1)}, u32[]{:S(2)}, u32[]{:S(2)}) collective-permute-start(bf16[2,3,48,1120]{3,2,1,0:T(8,128)(2,1)S(1)} %pad_maximum_fusion.5), channel_id=1, source_target_pairs={{0,24},{1,25},{2,26},{3,27},{4,28},{5,29},{6,30},{7,31},{8,0},{9,1... | collective-permute-start | bytes 1935368 | tf_op jit(solution)/shard_map/ff_ctx_a/ppermute | solution.py:73
  55.0 33.1 %collective-permute-start.6 = (bf16[2,3,48,1120]{3,2,1,0:T(8,128)(2,1)S(1)}, bf16[2,3,48,1120]{3,2,1,0:T(8,128)(2,1)S(1)}, u32[]{:S(2)}, u32[]{:S(2)}) collective-permute-start(bf16[2,3,48,1120]{3,2,1,0:T(8,128)(2,1)S(1)} %pad_maximum_fusion.4), channel_id=1, source_target_pairs={{0,8},{1,9},{2,10},{3,11},{4,12},{5,13},{6,14},{7,15},{8,16},{9,17... | collective-permute-start | bytes 1935368 | tf_op jit(solution)/shard_map/ff_ctx_a/ppermute | solution.py:73
  57.1 34.8 %copy-start.14 = (bf16[2,3,48,1120]{3,2,1,0:T(8,128)(2,1)}, bf16[2,3,48,1120]{3,2,1,0:T(8,128)(2,1)S(1)}, u32[]{:S(2)}) copy-start(bf16[2,3,48,1120]{3,2,1,0:T(8,128)(2,1)S(1)} %pad_maximum_fusion.7.refs_3_) | copy-start | bytes 1935364
  88.1 35.4 %copy-start.6 = (bf16[4,48,3712]{2,1,0:T(8,128)(2,1)}, bf16[4,48,3712]{2,1,0:T(8,128)(2,1)S(1)}, u32[]{:S(2)}) copy-start(bf16[4,48,3712]{2,1,0:T(8,128)(2,1)S(1)} %collective-permute-done.5.refs_5_.refs_10_.refs_14_) | copy-start | bytes 4276228
  89.2 34.3 %copy-start.7 = (bf16[4,48,3712]{2,1,0:T(8,128)(2,1)}, bf16[4,48,3712]{2,1,0:T(8,128)(2,1)S(1)}, u32[]{:S(2)}) copy-start(bf16[4,48,3712]{2,1,0:T(8,128)(2,1)S(1)} %collective-permute-done.4.refs_4_.refs_9_.refs_13_) | copy-start | bytes 4276228
  89.3 31.4 %collective-permute-start.10 = (bf16[2,48,3712]{2,1,0:T(8,128)(2,1)S(1)}, bf16[2,48,3712]{2,1,0:T(8,128)(2,1)S(1)}, u32[]{:S(2)}, u32[]{:S(2)}) collective-permute-start(bf16[2,48,3712]{2,1,0:T(8,128)(2,1)S(1)} %slice.18), channel_id=1, source_target_pairs={{0,2},{1,3},{2,0},{3,1},{4,6},{5,7},{6,4},{7,5},{8,10},{9,11},{10,... | collective-permute-start | bytes 2138120 | tf_op jit(solution)/shard_map/qkvo_plane2/ppermute | solution.py:73
  89.9 30.9 %collective-permute-start.11 = (bf16[2,48,3712]{2,1,0:T(8,128)(2,1)S(1)}, bf16[2,48,3712]{2,1,0:T(8,128)(2,1)S(1)}, u32[]{:S(2)}, u32[]{:S(2)}) collective-permute-start(bf16[2,48,3712]{2,1,0:T(8,128)(2,1)S(1)} %slice.19), channel_id=1, source_target_pairs={{0,4},{1,5},{2,6},{3,7},{4,0},{5,1},{6,2},{7,3},{8,12},{9,13},{10,... | collective-permute-start | bytes 2138120 | tf_op jit(solution)/shard_map/qkvo_plane2/ppermute | solution.py:73
  90.4 28.6 %collective-permute-start.9 = (bf16[2,3,48,1120]{3,2,1,0:T(8,128)(2,1)S(1)}, bf16[2,3,48,1120]{3,2,1,0:T(8,128)(2,1)S(1)}, u32[]{:S(2)}, u32[]{:S(2)}) collective-permute-start(bf16[2,3,48,1120]{3,2,1,0:T(8,128)(2,1)S(1)} %pad_maximum_fusion.6), channel_id=1, source_target_pairs={{0,16},{1,17},{2,18},{3,19},{4,20},{5,21},{6,22},{7,23},{8,24},{9,... | collective-permute-start | bytes 1935368 | tf_op jit(solution)/shard_map/ff_ctx_b/ppermute | solution.py:73
  90.4 30.3 %collective-permute-start.13 = (bf16[2,3,48,1120]{3,2,1,0:T(8,128)(2,1)S(1)}, bf16[2,3,48,1120]{3,2,1,0:T(8,128)(2,1)S(1)}, u32[]{:S(2)}, u32[]{:S(2)}) collective-permute-start(bf16[2,3,48,1120]{3,2,1,0:T(8,128)(2,1)S(1)} %pad_maximum_fusion.7.refs_3_), channel_id=1, source_target_pairs={{0,4},{1,5},{2,6},{3,7},{4,0},{5,1},{6,2},{7,3},{8,12},{9,13},{10,... | collective-permute-start | bytes 1935368 | tf_op jit(solution)/shard_map/ff_own1/ppermute | solution.py:73
  91.9 28.8 %collective-permute-start.12 = (bf16[2,3,48,1120]{3,2,1,0:T(8,128)(2,1)S(1)}, bf16[2,3,48,1120]{3,2,1,0:T(8,128)(2,1)S(1)}, u32[]{:S(2)}, u32[]{:S(2)}) collective-permute-start(bf16[2,3,48,1120]{3,2,1,0:T(8,128)(2,1)S(1)} %pad_maximum_fusion.7.refs_3_), channel_id=1, source_target_pairs={{0,2},{1,3},{2,0},{3,1},{4,6},{5,7},{6,4},{7,5},{8,10},{9,11},{10,... | collective-permute-start | bytes 1935368 | tf_op jit(solution)/shard_map/ff_own1/ppermute | solution.py:73
  120.7 43.3 %copy-start.15 = (bf16[2,3,48,1120]{3,2,1,0:T(8,128)(2,1)}, bf16[2,3,48,1120]{3,2,1,0:T(8,128)(2,1)S(1)}, u32[]{:S(2)}) copy-start(bf16[2,3,48,1120]{3,2,1,0:T(8,128)(2,1)S(1)} %collective-permute-done.13.refs_5_) | copy-start | bytes 1935364
  120.7 43.2 %copy-start.16 = (bf16[2,3,48,1120]{3,2,1,0:T(8,128)(2,1)}, bf16[2,3,48,1120]{3,2,1,0:T(8,128)(2,1)S(1)}, u32[]{:S(2)}) copy-start(bf16[2,3,48,1120]{3,2,1,0:T(8,128)(2,1)S(1)} %collective-permute-done.12.refs_4_) | copy-start | bytes 1935364
  123.5 7.7 %collective-permute-start.14 = (bf16[12,48,3712]{2,1,0:T(8,128)(2,1)}, bf16[12,48,3712]{2,1,0:T(8,128)(2,1)}, u32[]{:S(2)}, u32[]{:S(2)}) collective-permute-start(bf16[12,48,3712]{2,1,0:T(8,128)(2,1)} %pad_maximum_fusion), channel_id=1, source_target_pairs={{0,1},{1,0},{2,3},{3,2},{4,5},{5,4},{6,7},{7,6},{8,9},{9,8},{10,11... | collective-permute-start | bytes 12828680 | tf_op jit(solution)/shard_map/qkvo_core/ppermute | solution.py:73
  123.6 87.4 %all-gather.5.cloned.1.call-start = ((), (), s32[]{:S(2)}) async-start(), calls=%async_computation.2 | async-start | bytes 1966080 | tf_op jit(solution)/shard_map/all_gather | solution.py:1064
  126.4 46.0 %collective-permute-start.19 = (bf16[6,3,48,1120]{3,2,1,0:T(8,128)(2,1)}, bf16[6,3,48,1120]{3,2,1,0:T(8,128)(2,1)S(1)}, u32[]{:S(2)}, u32[]{:S(2)}) collective-permute-start(bf16[6,3,48,1120]{3,2,1,0:T(8,128)(2,1)} %constant_dynamic-update-slice_fusion.5.refs_6_), channel_id=1, source_target_pairs={{0,4},{1,5},{2,6},{3,7},{4,0},{5,1},{6,2},{7,3},{8,12},{9,13},{10,... | collective-permute-start | bytes 5806088 | tf_op jit(solution)/shard_map/ff_plane1/ppermute | solution.py:73
  126.9 48.7 %collective-permute-start.18 = (bf16[6,3,48,1120]{3,2,1,0:T(8,128)(2,1)}, bf16[6,3,48,1120]{3,2,1,0:T(8,128)(2,1)}, u32[]{:S(2)}, u32[]{:S(2)}) collective-permute-start(bf16[6,3,48,1120]{3,2,1,0:T(8,128)(2,1)} %constant_dynamic-update-slice_fusion.5.refs_6_), channel_id=1, source_target_pairs={{0,2},{1,3},{2,0},{3,1},{4,6},{5,7},{6,4},{7,5},{8,10},{9,11},{10,... | collective-permute-start | bytes 5806088 | tf_op jit(solution)/shard_map/ff_plane1/ppermute | solution.py:73
  137.2 10.0 %collective-permute-start.17 = (bf16[128,512]{1,0:T(8,128)(2,1)}, bf16[128,512]{1,0:T(8,128)(2,1)S(1)}, u32[]{:S(2)}, u32[]{:S(2)}) collective-permute-start(bf16[128,512]{1,0:T(8,128)(2,1)} %get-tuple-element.130.refs_4_.refs_8_), channel_id=1, source_target_pairs={{0,24},{1,25},{2,26},{3,27},{4,28},{5,29},{6,30},{7,31}} | collective-permute-start | bytes 393224 | tf_op jit(solution)/shard_map/kv/ppermute | solution.py:73
  140.2 12.6 %collective-permute-start.16 = (bf16[128,512]{1,0:T(8,128)(2,1)}, bf16[128,512]{1,0:T(8,128)(2,1)}, u32[]{:S(2)}, u32[]{:S(2)}) collective-permute-start(bf16[128,512]{1,0:T(8,128)(2,1)} %get-tuple-element.130.refs_4_.refs_8_), channel_id=1, source_target_pairs={{0,16},{1,17},{2,18},{3,19},{4,20},{5,21},{6,22},{7,23},{8,24},{9,... | collective-permute-start | bytes 393224 | tf_op jit(solution)/shard_map/kv/ppermute | solution.py:73
  142.2 16.0 %collective-permute-start.15 = (bf16[128,512]{1,0:T(8,128)(2,1)}, bf16[128,512]{1,0:T(8,128)(2,1)}, u32[]{:S(2)}, u32[]{:S(2)}) collective-permute-start(bf16[128,512]{1,0:T(8,128)(2,1)} %get-tuple-element.130.refs_4_.refs_8_), channel_id=1, source_target_pairs={{0,8},{1,9},{2,10},{3,11},{4,12},{5,13},{6,14},{7,15},{8,16},{9,17... | collective-permute-start | bytes 393224 | tf_op jit(solution)/shard_map/kv/ppermute | solution.py:73
  147.1 11.0 %copy-start.30 = (bf16[128,512]{1,0:T(8,128)(2,1)}, bf16[128,512]{1,0:T(8,128)(2,1)S(1)}, u32[]{:S(2)}) copy-start(bf16[128,512]{1,0:T(8,128)(2,1)S(1)} %collective-permute-done.17.refs_7_.refs_11_) | copy-start | bytes 393220
  163.9 87.4 %all-gather.9.cloned.1.call-start = ((), (), s32[]{:S(2)}) async-start(), calls=%async_computation.4 | async-start | bytes 1966080 | tf_op jit(solution)/shard_map/all_gather | solution.py:1094
  164.0 8.4 %slice-start = ((bf16[2,3,48,1120]{3,2,1,0:T(8,128)(2,1)}), bf16[1,3,48,1120]{3,2,1,0:T(8,128)(2,1)S(1)}, s32[]{:S(2)}) async-start(bf16[2,3,48,1120]{3,2,1,0:T(8,128)(2,1)} %copy-done.15), calls=%async_computation.8 | async-start | bytes 663552 | tf_op jit(solution)/shard_map/slice | solution.py:1070
  174.1 31.1 %collective-permute-start.20 = (bf16[4,3,48,1120]{3,2,1,0:T(8,128)(2,1)}, bf16[4,3,48,1120]{3,2,1,0:T(8,128)(2,1)S(1)}, u32[]{:S(2)}, u32[]{:S(2)}) collective-permute-start(bf16[4,3,48,1120]{3,2,1,0:T(8,128)(2,1)} %pad_maximum_fusion.2), channel_id=1, source_target_pairs={{0,2},{1,3},{2,0},{3,1},{4,6},{5,7},{6,4},{7,5},{8,10},{9,11},{10,... | collective-permute-start | bytes 3870728 | tf_op jit(solution)/shard_map/ff_plane2/ppermute | solution.py:73
  177.8 33.1 %collective-permute-start.22 = (bf16[512,1536]{1,0:T(8,128)(2,1)}, bf16[512,1536]{1,0:T(8,128)(2,1)S(1)}, u32[]{:S(2)}, u32[]{:S(2)}) collective-permute-start(bf16[512,1536]{1,0:T(8,128)(2,1)} %all-gather.7.cloned.1.call-done.refs_2_.refs_4_.refs_6_), channel_id=1, source_target_pairs={{0,1},{1,0},{2,3},{3,2},{4,5},{5,4},{6,7},{7,6},{8,9},{9,8},{10,11... | collective-permute-start | bytes 4718600 | tf_op jit(solution)/shard_map/gy_core/ppermute | solution.py:73
  179.3 31.7 %collective-permute-start.21 = (bf16[4,3,48,1120]{3,2,1,0:T(8,128)(2,1)S(1)}, bf16[4,3,48,1120]{3,2,1,0:T(8,128)(2,1)}, u32[]{:S(2)}, u32[]{:S(2)}) collective-permute-start(bf16[4,3,48,1120]{3,2,1,0:T(8,128)(2,1)S(1)} %pad_maximum_fusion.3), channel_id=1, source_target_pairs={{0,4},{1,5},{2,6},{3,7},{4,0},{5,1},{6,2},{7,3},{8,12},{9,13},{10,... | collective-permute-start | bytes 3870728 | tf_op jit(solution)/shard_map/ff_plane2/ppermute | solution.py:73
  205.1 5.8 %copy-start.11 = (bf16[4,3,48,1120]{3,2,1,0:T(8,128)(2,1)}, bf16[4,3,48,1120]{3,2,1,0:T(8,128)(2,1)S(1)}, u32[]{:S(2)}) copy-start(bf16[4,3,48,1120]{3,2,1,0:T(8,128)(2,1)S(1)} %collective-permute-done.20.refs_9_) | copy-start | bytes 3870724
  211.0 17.0 %copy-start.4 = (bf16[512,1536]{1,0:T(8,128)(2,1)}, bf16[512,1536]{1,0:T(8,128)(2,1)S(1)}, u32[]{:S(2)}) copy-start(bf16[512,1536]{1,0:T(8,128)(2,1)S(1)} %collective-permute-done.22.refs_2_.refs_5_.refs_7_) | copy-start | bytes 4718596
  211.0 17.0 %collective-permute-start.23 = (bf16[512,1536]{1,0:T(8,128)(2,1)}, bf16[512,1536]{1,0:T(8,128)(2,1)S(1)}, u32[]{:S(2)}, u32[]{:S(2)}) collective-permute-start(bf16[512,1536]{1,0:T(8,128)(2,1)} %all-gather.5.cloned.1.call-done.refs_1_.refs_0_.refs_2_), channel_id=1, source_target_pairs={{0,1},{1,0},{2,3},{3,2},{4,5},{5,4},{6,7},{7,6},{8,9},{9,8},{10,11... | collective-permute-start | bytes 4718600 | tf_op jit(solution)/shard_map/n2_core/ppermute | solution.py:73
  211.1 75.7 %reduce-scatter.3.cloned.1.call-start = ((), (), s32[]{:S(2)}) async-start(), calls=%async_computation.5 | async-start | bytes 1966080 | tf_op jit(solution)/shard_map/reduce_scatter | solution.py:1095
  229.2 20.6 %copy-start.20 = (bf16[512,1536]{1,0:T(8,128)(2,1)S(1)}, bf16[512,1536]{1,0:T(8,128)(2,1)}, u32[]{:S(2)}) copy-start(bf16[512,1536]{1,0:T(8,128)(2,1)} %get-tuple-element.156) | copy-start | bytes 4718596
  246.0 3.8 collective-permute-start.24
  251.4 110.2 %all-gather.11.cloned.1.call-start = ((), (), s32[]{:S(2)}) async-start(), calls=%async_computation.7 | async-start | bytes 1966080 | tf_op jit(solution)/shard_map/all_gather | solution.py:1123
  264.3 22.3 %collective-permute-start.26 = (bf16[2,1,192,1120]{3,2,1,0:T(8,128)(2,1)}, bf16[2,1,192,1120]{3,2,1,0:T(8,128)(2,1)}, u32[]{:S(2)}, u32[]{:S(2)}) collective-permute-start(bf16[2,1,192,1120]{3,2,1,0:T(8,128)(2,1)} %get-tuple-element.149), channel_id=1, source_target_pairs={{0,4},{1,5},{2,6},{3,7},{4,0},{5,1},{6,2},{7,3},{8,12},{9,13},{10,... | collective-permute-start | bytes 2580488 | tf_op jit(solution)/shard_map/ff_sum1/ppermute | solution.py:73
  264.9 22.0 %collective-permute-start.27 = (bf16[2,1,192,1120]{3,2,1,0:T(8,128)(2,1)}, bf16[2,1,192,1120]{3,2,1,0:T(8,128)(2,1)}, u32[]{:S(2)}, u32[]{:S(2)}) collective-permute-start(bf16[2,1,192,1120]{3,2,1,0:T(8,128)(2,1)} %get-tuple-element.151), channel_id=1, source_target_pairs={{0,2},{1,3},{2,0},{3,1},{4,6},{5,7},{6,4},{7,5},{8,10},{9,11},{10,... | collective-permute-start | bytes 2580488 | tf_op jit(solution)/shard_map/ff_sum1/ppermute | solution.py:73
  286.9 113.2 %reduce-scatter.5.cloned.1.call-start = ((), (), s32[]{:S(2)}) async-start(), calls=%async_computation.6 | async-start | bytes 1966080 | tf_op jit(solution)/shard_map/reduce_scatter | solution.py:1159
  286.9 57.0 %collective-permute-start.34 = (bf16[2,2,192,1120]{3,2,1,0:T(8,128)(2,1)}, bf16[2,2,192,1120]{3,2,1,0:T(8,128)(2,1)S(1)}, u32[]{:S(2)}, u32[]{:S(2)}) collective-permute-start(bf16[2,2,192,1120]{3,2,1,0:T(8,128)(2,1)} %get-tuple-element.150), channel_id=1, source_target_pairs={{0,4},{1,5},{2,6},{3,7},{4,0},{5,1},{6,2},{7,3},{8,12},{9,13},{10,... | collective-permute-start | bytes 5160968 | tf_op jit(solution)/shard_map/ff_sum1/ppermute | solution.py:73
  288.5 55.4 %collective-permute-start.35 = (bf16[2,2,192,1120]{3,2,1,0:T(8,128)(2,1)}, bf16[2,2,192,1120]{3,2,1,0:T(8,128)(2,1)S(1)}, u32[]{:S(2)}, u32[]{:S(2)}) collective-permute-start(bf16[2,2,192,1120]{3,2,1,0:T(8,128)(2,1)} %get-tuple-element.152), channel_id=1, source_target_pairs={{0,2},{1,3},{2,0},{3,1},{4,6},{5,7},{6,4},{7,5},{8,10},{9,11},{10,... | collective-permute-start | bytes 5160968 | tf_op jit(solution)/shard_map/ff_sum1/ppermute | solution.py:73
  289.7 12.7 %collective-permute-start.25 = (bf16[512,1536]{1,0:T(8,128)(2,1)}, bf16[512,1536]{1,0:T(8,128)(2,1)S(1)}, u32[]{:S(2)}, u32[]{:S(2)}) collective-permute-start(bf16[512,1536]{1,0:T(8,128)(2,1)} %get-tuple-element.155), channel_id=1, source_target_pairs={{0,1},{1,0},{2,3},{3,2},{4,5},{5,4},{6,7},{7,6},{8,9},{9,8},{10,11... | collective-permute-start | bytes 4718600 | tf_op jit(solution)/shard_map/y_core/ppermute | solution.py:73
  299.8 17.3 %collective-permute-start.28 = (bf16[128,512]{1,0:T(8,128)(2,1)}, bf16[128,512]{1,0:T(8,128)(2,1)S(1)}, u32[]{:S(2)}, u32[]{:S(2)}) collective-permute-start(bf16[128,512]{1,0:T(8,128)(2,1)} %get-tuple-element.166), channel_id=1, source_target_pairs={{8,0},{9,1},{10,2},{11,3},{12,4},{13,5},{14,6},{15,7},{16,8},{17,9... | collective-permute-start | bytes 393224 | tf_op jit(solution)/shard_map/gkv/ppermute | solution.py:73
  301.1 29.7 %collective-permute-start.29 = (bf16[128,512]{1,0:T(8,128)(2,1)}, bf16[128,512]{1,0:T(8,128)(2,1)S(1)}, u32[]{:S(2)}, u32[]{:S(2)}) collective-permute-start(bf16[128,512]{1,0:T(8,128)(2,1)} %get-tuple-element.167), channel_id=1, source_target_pairs={{16,0},{17,1},{18,2},{19,3},{20,4},{21,5},{22,6},{23,7},{24,8},{25... | collective-permute-start | bytes 393224 | tf_op jit(solution)/shard_map/gkv/ppermute | solution.py:73
  302.4 28.4 %collective-permute-start.30 = (bf16[128,512]{1,0:T(8,128)(2,1)}, bf16[128,512]{1,0:T(8,128)(2,1)S(1)}, u32[]{:S(2)}, u32[]{:S(2)}) collective-permute-start(bf16[128,512]{1,0:T(8,128)(2,1)} %get-tuple-element.168), channel_id=1, source_target_pairs={{24,0},{25,1},{26,2},{27,3},{28,4},{29,5},{30,6},{31,7}} | collective-permute-start | bytes 393224 | tf_op jit(solution)/shard_map/gkv/ppermute | solution.py:73
  317.1 13.7 %copy-start.31 = (bf16[128,512]{1,0:T(8,128)(2,1)}, bf16[128,512]{1,0:T(8,128)(2,1)S(1)}, u32[]{:S(2)}) copy-start(bf16[128,512]{1,0:T(8,128)(2,1)S(1)} %collective-permute-done.28.refs_1_) | copy-start | bytes 393220
  340.0 14.8 %collective-permute-start.31 = (bf16[144,896]{1,0:T(8,128)(2,1)}, bf16[144,896]{1,0:T(8,128)(2,1)}, u32[]{:S(2)}, u32[]{:S(2)}) collective-permute-start(bf16[144,896]{1,0:T(8,128)(2,1)} %get-tuple-element.172), channel_id=1, source_target_pairs={{0,8},{1,9},{2,10},{3,11},{4,12},{5,13},{6,14},{7,15},{8,16},{9,17... | collective-permute-start | bytes 774152 | tf_op jit(solution)/shard_map/gqkv_ctx/ppermute | solution.py:73
  340.1 21.4 %collective-permute-start.32 = (bf16[144,896]{1,0:T(8,128)(2,1)}, bf16[144,896]{1,0:T(8,128)(2,1)}, u32[]{:S(2)}, u32[]{:S(2)}) collective-permute-start(bf16[144,896]{1,0:T(8,128)(2,1)} %get-tuple-element.173), channel_id=1, source_target_pairs={{0,16},{1,17},{2,18},{3,19},{4,20},{5,21},{6,22},{7,23},{8,24},{9,... | collective-permute-start | bytes 774152 | tf_op jit(solution)/shard_map/gqkv_ctx/ppermute | solution.py:73
  340.2 21.4 %collective-permute-start.33 = (bf16[144,896]{1,0:T(8,128)(2,1)}, bf16[144,896]{1,0:T(8,128)(2,1)}, u32[]{:S(2)}, u32[]{:S(2)}) collective-permute-start(bf16[144,896]{1,0:T(8,128)(2,1)} %get-tuple-element.174), channel_id=1, source_target_pairs={{0,24},{1,25},{2,26},{3,27},{4,28},{5,29},{6,30},{7,31},{8,0},{9,1... | collective-permute-start | bytes 774152 | tf_op jit(solution)/shard_map/gqkv_ctx/ppermute | solution.py:73
  345.7 7.6 %copy-start.19 = (bf16[512,1536]{1,0:T(8,128)(2,1)S(1)}, bf16[512,1536]{1,0:T(8,128)(2,1)}, u32[]{:S(2)}) copy-start(bf16[512,1536]{1,0:T(8,128)(2,1)} %get-tuple-element.154) | copy-start | bytes 4718596
  350.1 30.8 %collective-permute-start.36 = (bf16[3,192,1120]{2,1,0:T(8,128)(2,1)}, bf16[3,192,1120]{2,1,0:T(8,128)(2,1)S(1)}, u32[]{:S(2)}, u32[]{:S(2)}) collective-permute-start(bf16[3,192,1120]{2,1,0:T(8,128)(2,1)} %get-tuple-element.187), channel_id=1, source_target_pairs={{0,2},{1,3},{2,0},{3,1},{4,6},{5,7},{6,4},{7,5},{8,10},{9,11},{10,... | collective-permute-start | bytes 3870728 | tf_op jit(solution)/shard_map/ff_sum2/ppermute | solution.py:73
  351.8 30.4 %collective-permute-start.37 = (bf16[3,192,1120]{2,1,0:T(8,128)(2,1)}, bf16[3,192,1120]{2,1,0:T(8,128)(2,1)S(1)}, u32[]{:S(2)}, u32[]{:S(2)}) collective-permute-start(bf16[3,192,1120]{2,1,0:T(8,128)(2,1)} %get-tuple-element.188), channel_id=1, source_target_pairs={{0,4},{1,5},{2,6},{3,7},{4,0},{5,1},{6,2},{7,3},{8,12},{9,13},{10,... | collective-permute-start | bytes 3870728 | tf_op jit(solution)/shard_map/ff_sum2/ppermute | solution.py:73
  367.6 21.3 %collective-permute-start.38 = (bf16[4,208,896]{2,1,0:T(8,128)(2,1)}, bf16[4,208,896]{2,1,0:T(8,128)(2,1)S(1)}, u32[]{:S(2)}, u32[]{:S(2)}) collective-permute-start(bf16[4,208,896]{2,1,0:T(8,128)(2,1)} %get-tuple-element.190), channel_id=1, source_target_pairs={{0,1},{1,0},{2,3},{3,2},{4,5},{5,4},{6,7},{7,6},{8,9},{9,8},{10,11... | collective-permute-start | bytes 4472840 | tf_op jit(solution)/shard_map/term_core/ppermute | solution.py:73
  388.9 11.2 %copy-start.24 = (f32[128,1536]{1,0:T(8,128)S(1)}, f32[128,1536]{1,0:T(8,128)}, u32[]{:S(2)}) copy-start(f32[128,1536]{1,0:T(8,128)} %get-tuple-element.131.refs_1_) | copy-start | bytes 2359300
  388.9 13.2 %collective-permute-start.42 = (bf16[3,192,1120]{2,1,0:T(8,128)(2,1)}, bf16[3,192,1120]{2,1,0:T(8,128)(2,1)S(1)}, u32[]{:S(2)}, u32[]{:S(2)}) collective-permute-start(bf16[3,192,1120]{2,1,0:T(8,128)(2,1)} %shard_map.266), channel_id=1, source_target_pairs={{0,1},{1,0},{2,3},{3,2},{4,5},{5,4},{6,7},{7,6},{8,9},{9,8},{10,11... | collective-permute-start | bytes 3870728 | tf_op jit(solution)/shard_map/final_core/ppermute | solution.py:73
  393.2 19.8 %collective-permute-start.39 = (bf16[208,896]{1,0:T(8,128)(2,1)}, bf16[208,896]{1,0:T(8,128)(2,1)S(1)}, u32[]{:S(2)}, u32[]{:S(2)}) collective-permute-start(bf16[208,896]{1,0:T(8,128)(2,1)} %get-tuple-element.192), channel_id=1, source_target_pairs={{0,2},{1,3},{2,0},{3,1},{4,6},{5,7},{6,4},{7,5},{8,10},{9,11},{10,... | collective-permute-start | bytes 1118216 | tf_op jit(solution)/shard_map/term_plane/ppermute | solution.py:73
  394.6 18.4 %collective-permute-start.40 = (bf16[208,896]{1,0:T(8,128)(2,1)}, bf16[208,896]{1,0:T(8,128)(2,1)S(1)}, u32[]{:S(2)}, u32[]{:S(2)}) collective-permute-start(bf16[208,896]{1,0:T(8,128)(2,1)} %get-tuple-element.193), channel_id=1, source_target_pairs={{0,4},{1,5},{2,6},{3,7},{4,0},{5,1},{6,2},{7,3},{8,12},{9,13},{10,... | collective-permute-start | bytes 1118216 | tf_op jit(solution)/shard_map/term_plane/ppermute | solution.py:73
  396.2 17.4 %collective-permute-start.41 = (bf16[208,896]{1,0:T(8,128)(2,1)}, bf16[208,896]{1,0:T(8,128)(2,1)S(1)}, u32[]{:S(2)}, u32[]{:S(2)}) collective-permute-start(bf16[208,896]{1,0:T(8,128)(2,1)} %get-tuple-element.194), channel_id=1, source_target_pairs={{0,6},{1,7},{2,4},{3,5},{4,2},{5,3},{6,0},{7,1},{8,14},{9,15},{10,... | collective-permute-start | bytes 1118216 | tf_op jit(solution)/shard_map/term_plane/ppermute | solution.py:73
  402.1 5.9 %copy-start.42 = (bf16[3,192,1120]{2,1,0:T(8,128)(2,1)}, bf16[3,192,1120]{2,1,0:T(8,128)(2,1)S(1)}, u32[]{:S(2)}) copy-start(bf16[3,192,1120]{2,1,0:T(8,128)(2,1)S(1)} %collective-permute-done.42.got) | copy-start | bytes 3870724
  (30 other events, 76.0 us)
Sparse Core Ops, SparseCore 0:
  123.7 40.7 all-gather.6
  166.6 42.9 all-gather.4
  211.2 36.9 all-gather.8
  251.5 35.0 reduce-scatter.2
  288.0 47.2 all-gather.10
  361.7 38.3 reduce-scatter.4

commit v7 on v6

--- a/solution.py
+++ b/solution.py
@@ -1157,7 +1157,6 @@
     shares[0] = after(shares[0], *ff_first)
     y_both = after(added(y_a, y_got), *shares[1:])
     y_sum = lax.psum_scatter(y_both, "ctx", scatter_dimension=0, tiled=True)
-    layer_out = hidden_one + y_sum.astype(F32)
     links.label = "ff_sum2"
     ff_second = reduce_next(links, ff_terms, phase(ff_first, (first_share,))[0])
     chips = fsdp_size // 2
@@ -1207,6 +1206,8 @@
         place=place,
         cost=2*10**9,
     )
+
+    layer_out = hidden_one + after(y_sum, grad_gate).astype(F32)
 
     return (
         layer_out[None],

time: 433 us -> 426 us (0.984)
  the two profiles are of different devices: /device:TPU:0 before, /device:TPU:8 now
where the time goes in v7:
time: 426 us; the launch traced here: 417 us
  waiting for transfers between devices  170 us (40%)
  Pallas kernels  133 us (31%)
  starting transfers between devices  63.2 us (15%)
  local copies, waits for them, and re-layouts  20.2 us (5%)
  other arithmetic  16.2 us (4%)
  between operations  15.3 us (4%)
    ppermute x43, waiting for transfers between devices, send(): return lax.ppermute(x, BOTH, pairs)  169 us
    ppermute x43, starting transfers between devices, send(): return lax.ppermute(x, BOTH, pairs)  62.6 us
    pallas_call x3, Pallas kernels, ff_call(): pl.pallas_call(body, grid_spec=pltpu.PrefetchScalarGridSpec(num_scalar_pr...  42.9 us
    pallas_call x4, Pallas kernels, call(): pl.pallas_call(kernel, in_specs=[pl.BlockSpec(memory_space=pltpu.SMEM)] +...  30.7 us
    pallas_call x2, Pallas kernels, ff_grad_terms(): pl.pallas_call(grad_kernel, grid_spec=pltpu.PrefetchScalarGridSpec(num_sc...  25.6 us
    pallas_call x4, Pallas kernels, small_call(): pl.pallas_call(body, in_specs=[pl.BlockSpec(memory_space=pltpu.SMEM)] * l...  16.8 us
    unnamed x98, local copies, waits for them, and re-layouts  14.9 us
    pallas_call x2, Pallas kernels, reduce_end(): pl.pallas_call(body, grid_spec=pltpu.PrefetchScalarGridSpec(num_scalar_pr...  11.4 us
  transfers between devices with their start and end apart: 49, of which 21 were waited for; matrix products, arithmetic and copies ran while one was open for 4% of the time, Pallas kernels for 31%

profile of v7, /device:TPU:8, one launch (start us, length us, event | category | flops | bytes accessed | tf_op | source)
XLA Modules:
  0.0 417.4 jit_solution(15417397871212355248)
XLA Ops:
  12.6 3.0 collective-permute-start.1
  15.6 2.5 collective-permute-start
  18.1 5.6 %collective-permute-done.2 = bf16[48,3712]{1,0:T(8,128)(2,1)S(1)} collective-permute-done((bf16[48,3712]{1,0:T(8,128)(2,1)S(1)}, bf16[48,3712]{1,0:T(8,128)(2,1)S(1)}, u32[]{:S(2)}, u32[]{:S(2)}) %collective-permute-start.2) | collective-permute-done | bytes 356384 | tf_op jit(solution)/shard_map/qkvo_ctx/ppermute | solution.py:73
  23.7 15.9 %collective-permute-done.1 = bf16[48,3712]{1,0:T(8,128)(2,1)} collective-permute-done((bf16[48,3712]{1,0:T(8,128)(2,1)S(1)}, bf16[48,3712]{1,0:T(8,128)(2,1)}, u32[]{:S(2)}, u32[]{:S(2)}) %collective-permute-start.1) | collective-permute-done | bytes 356384 | tf_op jit(solution)/shard_map/qkvo_ctx/ppermute | solution.py:73
  39.6 6.9 %collective-permute-done = bf16[48,3712]{1,0:T(8,128)(2,1)} collective-permute-done((bf16[48,3712]{1,0:T(8,128)(2,1)S(1)}, bf16[48,3712]{1,0:T(8,128)(2,1)}, u32[]{:S(2)}, u32[]{:S(2)}) %collective-permute-start) | collective-permute-done | bytes 356384 | tf_op jit(solution)/shard_map/qkvo_ctx/ppermute | solution.py:73
  46.5 1.3 pad_maximum_fusion.1.refs_3_.refs_8_.refs_12_
  47.9 1.6 collective-permute-start.5
  49.5 1.5 collective-permute-start.4
  50.9 1.6 broadcast_select_fusion.1
  52.6 1.3 collective-permute-start.7
  54.0 1.4 collective-permute-start.6
  55.6 14.6 %collective-permute-done.7 = bf16[2,3,48,1120]{3,2,1,0:T(8,128)(2,1)S(1)} collective-permute-done((bf16[2,3,48,1120]{3,2,1,0:T(8,128)(2,1)S(1)}, bf16[2,3,48,1120]{3,2,1,0:T(8,128)(2,1)S(1)}, u32[]{:S(2)}, u32[]{:S(2)}) %collective-permute-start.7) | collective-permute-done | bytes 645152 | tf_op jit(solution)/shard_map/ff_ctx_a/ppermute | solution.py:73
  70.2 12.9 %collective-permute-done.6 = bf16[2,3,48,1120]{3,2,1,0:T(8,128)(2,1)S(1)} collective-permute-done((bf16[2,3,48,1120]{3,2,1,0:T(8,128)(2,1)S(1)}, bf16[2,3,48,1120]{3,2,1,0:T(8,128)(2,1)S(1)}, u32[]{:S(2)}, u32[]{:S(2)}) %collective-permute-start.6) | collective-permute-done | bytes 645152 | tf_op jit(solution)/shard_map/ff_ctx_a/ppermute | solution.py:73
  85.5 2.3 collective-permute-start.9
  87.8 1.5 collective-permute-start.13
  89.3 1.5 collective-permute-start.12
  90.8 25.0 %collective-permute-done.9 = bf16[2,3,48,1120]{3,2,1,0:T(8,128)(2,1)S(1)} collective-permute-done((bf16[2,3,48,1120]{3,2,1,0:T(8,128)(2,1)S(1)}, bf16[2,3,48,1120]{3,2,1,0:T(8,128)(2,1)S(1)}, u32[]{:S(2)}, u32[]{:S(2)}) %collective-permute-start.9) | collective-permute-done | bytes 645152 | tf_op jit(solution)/shard_map/ff_ctx_b/ppermute | solution.py:73
  116.1 2.7 pad_maximum_fusion
  121.7 1.2 collective-permute-start.19
  123.0 1.5 collective-permute-start.18
  126.5 6.3 %shard_map.255 = (bf16[128,1536]{1,0:T(8,128)(2,1)}, bf16[128,1536]{1,0:T(8,128)(2,1)}, bf16[128,512]{1,0:T(8,128)(2,1)}, f32[8,1536]{1,0:T(8,128)}) custom-call(s32[3]{0:T(128)} %copy-done.3, bf16[128,1536]{1,0:T(8,128)(2,1)} %bitcast.32, f32[128,128]{1,0:T(8,128)} %get-tuple-element.223.refs_1_.refs_6_, f32[128,128]{1,0:T(8,128)} %get-tuple-element.224.refs_2_.refs_7_, ...), custom_call_target="tpu_custom_call" | custom-call | tf_op jit(solution)/shard_map/pallas_call | solution.py:695
  133.5 6.2 %collective-permute-start.16 = (bf16[128,512]{1,0:T(8,128)(2,1)}, bf16[128,512]{1,0:T(8,128)(2,1)}, u32[]{:S(2)}, u32[]{:S(2)}) collective-permute-start(bf16[128,512]{1,0:T(8,128)(2,1)} %get-tuple-element.131.refs_4_.refs_8_), channel_id=1, source_target_pairs={{0,16},{1,17},{2,18},{3,19},{4,20},{5,21},{6,22},{7,23},{8,24},{9,... | collective-permute-start | bytes 393224 | tf_op jit(solution)/shard_map/kv/ppermute | solution.py:73
  139.7 1.9 collective-permute-start.15
  142.4 12.4 %collective-permute-done.16.refs_6_.refs_10_ = bf16[128,512]{1,0:T(8,128)(2,1)} collective-permute-done((bf16[128,512]{1,0:T(8,128)(2,1)}, bf16[128,512]{1,0:T(8,128)(2,1)}, u32[]{:S(2)}, u32[]{:S(2)}) %collective-permute-start.16) | collective-permute-done | bytes 131104 | tf_op jit(solution)/shard_map/kv/ppermute | solution.py:73
  154.8 9.0 %collective-permute-done.15.refs_5_.refs_9_ = bf16[128,512]{1,0:T(8,128)(2,1)} collective-permute-done((bf16[128,512]{1,0:T(8,128)(2,1)}, bf16[128,512]{1,0:T(8,128)(2,1)}, u32[]{:S(2)}, u32[]{:S(2)}) %collective-permute-start.15) | collective-permute-done | bytes 131104 | tf_op jit(solution)/shard_map/kv/ppermute | solution.py:73
  163.8 5.8 %shard_map.256 = (bf16[128,1536]{1,0:T(8,128)(2,1)}, f32[128,1536]{1,0:T(8,128)}, bf16[128,1536]{1,0:T(8,128)(2,1)}) custom-call(s32[3]{0:T(128)} %copy-done.3, bf16[128,1536]{1,0:T(8,128)(2,1)} %bitcast.33, f32[8,1536]{1,0:T(8,128)} %get-tuple-element.129.refs_1_.refs_2_.refs_5_, s32[128,1]{1,0:T(8,128)} %copy.37.refs_2_.refs_4_, ...), custom_call_target="tpu_custom_call" | custom-call | tf_op jit(solution)/shard_map/pallas_call | solution.py:695
  170.8 1.2 pad_maximum_fusion.2
  172.0 1.5 collective-permute-start.20
  173.6 2.3 slice.25
  175.9 1.4 pad_maximum_fusion.3
  177.3 1.6 collective-permute-start.21
  178.9 24.4 %collective-permute-done.20.refs_9_ = bf16[4,3,48,1120]{3,2,1,0:T(8,128)(2,1)S(1)} collective-permute-done((bf16[4,3,48,1120]{3,2,1,0:T(8,128)(2,1)}, bf16[4,3,48,1120]{3,2,1,0:T(8,128)(2,1)S(1)}, u32[]{:S(2)}, u32[]{:S(2)}) %collective-permute-start.20) | collective-permute-done | bytes 1290272 | tf_op jit(solution)/shard_map/ff_plane2/ppermute | solution.py:73
  203.2 5.7 %collective-permute-done.21.refs_10_ = bf16[4,3,48,1120]{3,2,1,0:T(8,128)(2,1)} collective-permute-done((bf16[4,3,48,1120]{3,2,1,0:T(8,128)(2,1)S(1)}, bf16[4,3,48,1120]{3,2,1,0:T(8,128)(2,1)}, u32[]{:S(2)}, u32[]{:S(2)}) %collective-permute-start.21) | collective-permute-done | bytes 1290272 | tf_op jit(solution)/shard_map/ff_plane2/ppermute | solution.py:73
  209.3 16.7 %shard_map.257 = (bf16[512,1120]{1,0:T(8,128)(2,1)}, bf16[512,1120]{1,0:T(8,128)(2,1)}, bf16[512,1120]{1,0:T(8,128)(2,1)}, bf16[512,1536]{1,0:T(8,128)(2,1)}) custom-call(s32[3]{0:T(128)} %copy-done.3, bf16[512,1536]{1,0:T(8,128)(2,1)} %all-gather.5.cloned.1.call-done.refs_1_.refs_0_.refs_2_, ...), custom_call_target="tpu_custom_call" | custom-call | tf_op jit(solution)/shard_map/pallas_call | solution.py:455
  227.2 16.8 %shard_map.258 = (bf16[512,1120]{1,0:T(8,128)(2,1)}, bf16[512,1120]{1,0:T(8,128)(2,1)}, bf16[512,1120]{1,0:T(8,128)(2,1)}, bf16[512,1536]{1,0:T(8,128)(2,1)}) custom-call(s32[3]{0:T(128)} %copy-done.3, bf16[512,1536]{1,0:T(8,128)(2,1)} %copy-done.5, bf16[512,1536]{1,0:T(8,128)(2,1)} %copy-done.4, bf16[2,3,48,1120]{3,2,1,0:T(8,128)(2,1)} %copy-done.14, ...), custom_call_target="tpu_custom_call" | custom-call | tf_op jit(solution)/shard_map/pallas_call | solution.py:455
  244.6 3.2 collective-permute-done.24
  247.8 1.6 add_convert_fusion
  249.7 12.7 %shard_map.259 = (bf16[2,1,192,1120]{3,2,1,0:T(8,128)(2,1)}, bf16[2,2,192,1120]{3,2,1,0:T(8,128)(2,1)}, bf16[2,1,192,1120]{3,2,1,0:T(8,128)(2,1)}, bf16[2,2,192,1120]{3,2,1,0:T(8,128)(2,1)}) custom-call(s32[3]{0:T(128)} %copy-done.3, bf16[512,1536]{1,0:T(8,128)(2,1)} %all-gather.5.cloned.1.call-done.refs_1_.refs_0_.refs_2_, bf16[512,1536]{1,0:T(8,128)(2,1)} %copy-done.5, ...), custom_call_target="tpu_custom_call" | custom-call | tf_op jit(solution)/shard_map/pallas_call | solution.py:500
  262.4 1.6 collective-permute-start.26
  265.0 1.6 collective-permute-start.35
  266.6 9.4 %shard_map.260 = (bf16[512,1536]{1,0:T(8,128)(2,1)}, bf16[512,1536]{1,0:T(8,128)(2,1)}) custom-call(s32[3]{0:T(128)} %copy-done.3, bf16[512,1120]{1,0:T(8,128)(2,1)} %get-tuple-element.154.refs_12_.refs_1_, bf16[512,1120]{1,0:T(8,128)(2,1)} %get-tuple-element.149.refs_13_.refs_2_, bf16[2,3,48,1120]{3,2,1,0:T(8,128)(2,1)} %copy-done.14, ...), custom_call_target="tpu_custom_call" | custom-call | tf_op jit(solution)/shard_map/pallas_call | solution.py:455
  276.1 9.2 %collective-permute-done.26.refs_1_.refs_2_ = bf16[2,1,192,1120]{3,2,1,0:T(8,128)(2,1)} collective-permute-done((bf16[2,1,192,1120]{3,2,1,0:T(8,128)(2,1)}, bf16[2,1,192,1120]{3,2,1,0:T(8,128)(2,1)}, u32[]{:S(2)}, u32[]{:S(2)}) %collective-permute-start.26) | collective-permute-done | bytes 860192 | tf_op jit(solution)/shard_map/ff_sum1/ppermute | solution.py:73
  285.3 1.6 collective-permute-done.27.refs_4_.refs_6_
  287.0 10.1 %shard_map.261 = (f32[128,1536]{1,0:T(8,128)}, bf16[128,1536]{1,0:T(8,128)(2,1)}, bf16[128,1536]{1,0:T(8,128)(2,1)}, f32[1,1536]{1,0:T(1,128)}, bf16[128,512]{1,...) custom-call(s32[3]{0:T(128)} %copy-done.3, ...), custom_call_target="tpu_custom_call" | custom-call | flops 8000000000 | tf_op jit(solution)/shard_map/pallas_call | solution.py:695
  297.0 1.9 collective-permute-start.28
  299.0 1.3 collective-permute-start.29
  301.2 12.9 %shard_map.262 = (bf16[2,3,192,1120]{3,2,1,0:T(8,128)(2,1)}, bf16[2,3,192,1120]{3,2,1,0:T(8,128)(2,1)}) custom-call(s32[3]{0:T(128)} %copy-done.3, bf16[512,1536]{1,0:T(8,128)(2,1)} %all-gather.5.cloned.1.call-done.refs_1_.refs_0_.refs_2_, bf16[512,1536]{1,0:T(8,128)(2,1)} %copy-done.5, ...), custom_call_target="tpu_custom_call" | custom-call | tf_op jit(solution)/shard_map/pallas_call | solution.py:500
  316.5 8.5 %shard_map.263 = (f32[128,1536]{1,0:T(8,128)}, bf16[144,896]{1,0:T(8,128)(2,1)}, bf16[144,896]{1,0:T(8,128)(2,1)}, bf16[144,896]{1,0:T(8,128)(2,1)}, bf16[144,896]{1,0:T(8,128)(2,1)}) custom-call(s32[3]{0:T(128)} %copy-done.3, bf16[128,512]{1,0:T(8,128)(2,1)} %get-tuple-element.166.refs_0_, bf16[128,512]{1,0:T(8,128)(2,1)} %copy-done.34, ...), custom_call_target="tpu_custom_call" | custom-call | tf_op jit(solution)/shard_map/pallas_call | solution.py:695
  326.8 4.4 %shard_map.264 = (bf16[3,192,1120]{2,1,0:T(8,128)(2,1)}, bf16[3,192,1120]{2,1,0:T(8,128)(2,1)}) custom-call(bf16[2,3,192,1120]{3,2,1,0:T(8,128)(2,1)} %get-tuple-element.165.refs_0_.refs_1_, bf16[2,1,192,1120]{3,2,1,0:T(8,128)(2,1)} %collective-permute-done.26.refs_1_.refs_2_, bf16[2,2,192,1120]{3,2,1,0:T(8,128)(2,1)} %copy-done.17, ...), custom_call_target="tpu_custom_call" | custom-call | tf_op jit(solution)/shard_map/pallas_call | solution.py:541
  332.2 10.8 %collective-permute-start.31 = (bf16[144,896]{1,0:T(8,128)(2,1)}, bf16[144,896]{1,0:T(8,128)(2,1)S(1)}, u32[]{:S(2)}, u32[]{:S(2)}) collective-permute-start(bf16[144,896]{1,0:T(8,128)(2,1)} %get-tuple-element.173), channel_id=1, source_target_pairs={{0,8},{1,9},{2,10},{3,11},{4,12},{5,13},{6,14},{7,15},{8,16},{9,17... | collective-permute-start | bytes 774152 | tf_op jit(solution)/shard_map/gqkv_ctx/ppermute | solution.py:73
  343.1 5.1 %collective-permute-start.32 = (bf16[144,896]{1,0:T(8,128)(2,1)}, bf16[144,896]{1,0:T(8,128)(2,1)S(1)}, u32[]{:S(2)}, u32[]{:S(2)}) collective-permute-start(bf16[144,896]{1,0:T(8,128)(2,1)} %get-tuple-element.174), channel_id=1, source_target_pairs={{0,16},{1,17},{2,18},{3,19},{4,20},{5,21},{6,22},{7,23},{8,24},{9,... | collective-permute-start | bytes 774152 | tf_op jit(solution)/shard_map/gqkv_ctx/ppermute | solution.py:73
  348.2 3.0 add_convert_fusion.1
  351.2 8.9 %collective-permute-done.31.refs_1_ = bf16[144,896]{1,0:T(8,128)(2,1)S(1)} collective-permute-done((bf16[144,896]{1,0:T(8,128)(2,1)}, bf16[144,896]{1,0:T(8,128)(2,1)S(1)}, u32[]{:S(2)}, u32[]{:S(2)}) %collective-permute-start.31) | collective-permute-done | bytes 258080 | tf_op jit(solution)/shard_map/gqkv_ctx/ppermute | solution.py:73
  360.0 3.8 collective-permute-done.32.refs_2_
  363.8 3.5 collective-permute-done.33.refs_3_
  368.0 6.0 %shard_map.265 = (bf16[4,208,896]{2,1,0:T(8,128)(2,1)}, bf16[4,208,896]{2,1,0:T(8,128)(2,1)}) custom-call(s32[3]{0:T(128)} %copy-done.3, bf16[144,896]{1,0:T(8,128)(2,1)} %get-tuple-element.185.refs_0_, bf16[144,896]{1,0:T(8,128)(2,1)} %copy-done.28, bf16[144,896]{1,0:T(8,128)(2,1)} %copy-done.29, bf16[144,896]{1,0:T(8,128)(2,1)} %copy-done.30, ...), custom_call_target="tpu_custom_call" | custom-call | tf_op jit(solution)/shard_map/pallas_call | solution.py:939
  376.2 5.6 %shard_map.266 = bf16[3,192,1120]{2,1,0:T(8,128)(2,1)} custom-call(s32[3]{0:T(128)} %copy-done.3, bf16[2,3,192,1120]{3,2,1,0:T(8,128)(2,1)} %get-tuple-element.165.refs_0_.refs_1_, bf16[2,1,192,1120]{3,2,1,0:T(8,128)(2,1)} %collective-permute-done.26.refs_1_.refs_2_, bf16[2,2,192,1120]{3,2,1,0:T(8,128)(2,1)} %copy-done.17, bf16[3,192,1120]{2,1,0:T(8,128)(2,1)} %copy-done.22, ...), custom_call_target="tpu_custom_call" | custom-call | flops 12000000000 | tf_op jit(solution)/shard_map/pallas_call | solution.py:581
  383.3 3.2 shard_map.267
  386.5 1.7 collective-permute-start.40
  390.0 5.9 %shard_map.268.mine = f32[3,192,1120]{2,1,0:T(8,128)} custom-call(s32[3]{0:T(128)} %copy-done.3, bf16[2,3,192,1120]{3,2,1,0:T(8,128)(2,1)} %get-tuple-element.165.refs_0_.refs_1_, bf16[2,1,192,1120]{3,2,1,0:T(8,128)(2,1)} %collective-permute-done.26.refs_1_.refs_2_, bf16[2,2,192,1120]{3,2,1,0:T(8,128)(2,1)} %copy-done.17, bf16[3,192,1120]{2,1,0:T(8,128)(2,1)} %copy-done.22, ...), custom_call_target="tpu_custom_call" | custom-call | tf_op jit(solution)/shard_map/pallas_call | solution.py:581
  395.9 5.1 %shard_map.269 = (f32[192,2240]{1,0:T(8,128)}, f32[192,2240]{1,0:T(8,128)}, f32[192,2240]{1,0:T(8,128)}) custom-call(s32[3]{0:T(128)} %copy-done.3, f32[3,192,1120]{2,1,0:T(8,128)} %shard_map.268.mine, bf16[3,192,1120]{2,1,0:T(8,128)(2,1)} %copy-done.45), custom_call_target="tpu_custom_call" | custom-call | flops 2000000000 | tf_op jit(solution)/shard_map/pallas_call | solution.py:939
  401.1 2.0 add_bitcast_fusion
  403.0 3.7 collective-permute-done.41.refs_1_
  407.6 2.5 shard_map.270
  (186 shorter events, 32.3 us)
Async XLA Ops:
  7.2 5.2 %copy-start.37 = (bf16[48,256]{1,0:T(8,128)(2,1)S(1)}, bf16[48,256]{1,0:T(8,128)(2,1)}, u32[]{:S(2)}) copy-start(bf16[48,256]{1,0:T(8,128)(2,1)} %param.20) | copy-start | bytes 73732
  7.2 5.2 %copy-start.38 = (bf16[48,256]{1,0:T(8,128)(2,1)S(1)}, bf16[48,256]{1,0:T(8,128)(2,1)}, u32[]{:S(2)}) copy-start(bf16[48,256]{1,0:T(8,128)(2,1)} %param.22) | copy-start | bytes 73732
  7.3 168.6 %all-gather.7.cloned.1.call-start = ((), (), s32[]{:S(2)}) async-start(), calls=%async_computation.3 | async-start | bytes 1966080 | tf_op jit(solution)/shard_map/all_gather | solution.py:1063
  12.1 34.4 %collective-permute-start.3 = (bf16[4,3,48,1120]{3,2,1,0:T(8,128)(2,1)S(1)}, bf16[4,3,48,1120]{3,2,1,0:T(8,128)(2,1)}, u32[]{:S(2)}, u32[]{:S(2)}) collective-permute-start(bf16[4,3,48,1120]{3,2,1,0:T(8,128)(2,1)S(1)} %get-tuple-element.114), channel_id=1, source_target_pairs={{0,1},{1,0},{2,3},{3,2},{4,5},{5,4},{6,7},{7,6},{8,9},{9,8},{10,11... | collective-permute-start | bytes 3870728 | tf_op jit(solution)/shard_map/ff_core/ppermute | solution.py:73
  12.5 11.2 %collective-permute-start.2 = (bf16[48,3712]{1,0:T(8,128)(2,1)S(1)}, bf16[48,3712]{1,0:T(8,128)(2,1)S(1)}, u32[]{:S(2)}, u32[]{:S(2)}) collective-permute-start(bf16[48,3712]{1,0:T(8,128)(2,1)S(1)} %constant_dynamic-update-slice_fusion), channel_id=1, source_target_pairs={{0,24},{1,25},{2,26},{3,27},{4,28},{5,29},{6,30},{7,31},{8,0},{9,1... | collective-permute-start | bytes 1069064 | tf_op jit(solution)/shard_map/qkvo_ctx/ppermute | solution.py:73
  12.6 27.0 %collective-permute-start.1 = (bf16[48,3712]{1,0:T(8,128)(2,1)S(1)}, bf16[48,3712]{1,0:T(8,128)(2,1)}, u32[]{:S(2)}, u32[]{:S(2)}) collective-permute-start(bf16[48,3712]{1,0:T(8,128)(2,1)S(1)} %constant_dynamic-update-slice_fusion), channel_id=1, source_target_pairs={{0,16},{1,17},{2,18},{3,19},{4,20},{5,21},{6,22},{7,23},{8,24},{9,... | collective-permute-start | bytes 1069064 | tf_op jit(solution)/shard_map/qkvo_ctx/ppermute | solution.py:73
  15.6 30.9 %collective-permute-start = (bf16[48,3712]{1,0:T(8,128)(2,1)S(1)}, bf16[48,3712]{1,0:T(8,128)(2,1)}, u32[]{:S(2)}, u32[]{:S(2)}) collective-permute-start(bf16[48,3712]{1,0:T(8,128)(2,1)S(1)} %constant_dynamic-update-slice_fusion), channel_id=1, source_target_pairs={{0,8},{1,9},{2,10},{3,11},{4,12},{5,13},{6,14},{7,15},{8,16},{9,17... | collective-permute-start | bytes 1069064 | tf_op jit(solution)/shard_map/qkvo_ctx/ppermute | solution.py:73
  47.8 35.3 %collective-permute-start.8 = (bf16[4,48,3712]{2,1,0:T(8,128)(2,1)S(1)}, bf16[4,48,3712]{2,1,0:T(8,128)(2,1)S(1)}, u32[]{:S(2)}, u32[]{:S(2)}) collective-permute-start(bf16[4,48,3712]{2,1,0:T(8,128)(2,1)S(1)} %pad_maximum_fusion.1.refs_3_.refs_8_.refs_12_), channel_id=1, source_target_pairs={{0,1},{1,0},{2,3},{3,2},{4,5},{5,4},{6,7},{7,6},{8,9},{9,8},{10,11... | collective-permute-start | bytes 4276232 | tf_op jit(solution)/shard_map/qkvo_core/ppermute | solution.py:73
  47.9 35.3 %collective-permute-start.5 = (bf16[4,48,3712]{2,1,0:T(8,128)(2,1)S(1)}, bf16[4,48,3712]{2,1,0:T(8,128)(2,1)S(1)}, u32[]{:S(2)}, u32[]{:S(2)}) collective-permute-start(bf16[4,48,3712]{2,1,0:T(8,128)(2,1)S(1)} %pad_maximum_fusion.1.refs_3_.refs_8_.refs_12_), channel_id=1, source_target_pairs={{0,4},{1,5},{2,6},{3,7},{4,0},{5,1},{6,2},{7,3},{8,12},{9,13},{10,... | collective-permute-start | bytes 4276232 | tf_op jit(solution)/shard_map/qkvo_plane1/ppermute | solution.py:73
  49.5 33.7 %collective-permute-start.4 = (bf16[4,48,3712]{2,1,0:T(8,128)(2,1)S(1)}, bf16[4,48,3712]{2,1,0:T(8,128)(2,1)S(1)}, u32[]{:S(2)}, u32[]{:S(2)}) collective-permute-start(bf16[4,48,3712]{2,1,0:T(8,128)(2,1)S(1)} %pad_maximum_fusion.1.refs_3_.refs_8_.refs_12_), channel_id=1, source_target_pairs={{0,2},{1,3},{2,0},{3,1},{4,6},{5,7},{6,4},{7,5},{8,10},{9,11},{10,... | collective-permute-start | bytes 4276232 | tf_op jit(solution)/shard_map/qkvo_plane1/ppermute | solution.py:73
  52.6 17.6 %collective-permute-start.7 = (bf16[2,3,48,1120]{3,2,1,0:T(8,128)(2,1)S(1)}, bf16[2,3,48,1120]{3,2,1,0:T(8,128)(2,1)S(1)}, u32[]{:S(2)}, u32[]{:S(2)}) collective-permute-start(bf16[2,3,48,1120]{3,2,1,0:T(8,128)(2,1)S(1)} %pad_maximum_fusion.5), channel_id=1, source_target_pairs={{0,24},{1,25},{2,26},{3,27},{4,28},{5,29},{6,30},{7,31},{8,0},{9,1... | collective-permute-start | bytes 1935368 | tf_op jit(solution)/shard_map/ff_ctx_a/ppermute | solution.py:73
  54.0 29.1 %collective-permute-start.6 = (bf16[2,3,48,1120]{3,2,1,0:T(8,128)(2,1)S(1)}, bf16[2,3,48,1120]{3,2,1,0:T(8,128)(2,1)S(1)}, u32[]{:S(2)}, u32[]{:S(2)}) collective-permute-start(bf16[2,3,48,1120]{3,2,1,0:T(8,128)(2,1)S(1)} %pad_maximum_fusion.4), channel_id=1, source_target_pairs={{0,8},{1,9},{2,10},{3,11},{4,12},{5,13},{6,14},{7,15},{8,16},{9,17... | collective-permute-start | bytes 1935368 | tf_op jit(solution)/shard_map/ff_ctx_a/ppermute | solution.py:73
  55.5 33.8 %copy-start.14 = (bf16[2,3,48,1120]{3,2,1,0:T(8,128)(2,1)}, bf16[2,3,48,1120]{3,2,1,0:T(8,128)(2,1)S(1)}, u32[]{:S(2)}) copy-start(bf16[2,3,48,1120]{3,2,1,0:T(8,128)(2,1)S(1)} %pad_maximum_fusion.7.refs_3_) | copy-start | bytes 1935364
  83.1 35.7 %copy-start.6 = (bf16[4,48,3712]{2,1,0:T(8,128)(2,1)}, bf16[4,48,3712]{2,1,0:T(8,128)(2,1)S(1)}, u32[]{:S(2)}) copy-start(bf16[4,48,3712]{2,1,0:T(8,128)(2,1)S(1)} %collective-permute-done.5.refs_5_.refs_10_.refs_14_) | copy-start | bytes 4276228
  84.2 34.6 %copy-start.7 = (bf16[4,48,3712]{2,1,0:T(8,128)(2,1)}, bf16[4,48,3712]{2,1,0:T(8,128)(2,1)S(1)}, u32[]{:S(2)}) copy-start(bf16[4,48,3712]{2,1,0:T(8,128)(2,1)S(1)} %collective-permute-done.4.refs_4_.refs_9_.refs_13_) | copy-start | bytes 4276228
  84.4 31.8 %collective-permute-start.10 = (bf16[2,48,3712]{2,1,0:T(8,128)(2,1)S(1)}, bf16[2,48,3712]{2,1,0:T(8,128)(2,1)S(1)}, u32[]{:S(2)}, u32[]{:S(2)}) collective-permute-start(bf16[2,48,3712]{2,1,0:T(8,128)(2,1)S(1)} %slice.18), channel_id=1, source_target_pairs={{0,2},{1,3},{2,0},{3,1},{4,6},{5,7},{6,4},{7,5},{8,10},{9,11},{10,... | collective-permute-start | bytes 2138120 | tf_op jit(solution)/shard_map/qkvo_plane2/ppermute | solution.py:73
  85.0 31.2 %collective-permute-start.11 = (bf16[2,48,3712]{2,1,0:T(8,128)(2,1)S(1)}, bf16[2,48,3712]{2,1,0:T(8,128)(2,1)S(1)}, u32[]{:S(2)}, u32[]{:S(2)}) collective-permute-start(bf16[2,48,3712]{2,1,0:T(8,128)(2,1)S(1)} %slice.19), channel_id=1, source_target_pairs={{0,4},{1,5},{2,6},{3,7},{4,0},{5,1},{6,2},{7,3},{8,12},{9,13},{10,... | collective-permute-start | bytes 2138120 | tf_op jit(solution)/shard_map/qkvo_plane2/ppermute | solution.py:73
  85.5 30.3 %collective-permute-start.9 = (bf16[2,3,48,1120]{3,2,1,0:T(8,128)(2,1)S(1)}, bf16[2,3,48,1120]{3,2,1,0:T(8,128)(2,1)S(1)}, u32[]{:S(2)}, u32[]{:S(2)}) collective-permute-start(bf16[2,3,48,1120]{3,2,1,0:T(8,128)(2,1)S(1)} %pad_maximum_fusion.6), channel_id=1, source_target_pairs={{0,16},{1,17},{2,18},{3,19},{4,20},{5,21},{6,22},{7,23},{8,24},{9,... | collective-permute-start | bytes 1935368 | tf_op jit(solution)/shard_map/ff_ctx_b/ppermute | solution.py:73
  87.8 28.3 %collective-permute-start.13 = (bf16[2,3,48,1120]{3,2,1,0:T(8,128)(2,1)S(1)}, bf16[2,3,48,1120]{3,2,1,0:T(8,128)(2,1)S(1)}, u32[]{:S(2)}, u32[]{:S(2)}) collective-permute-start(bf16[2,3,48,1120]{3,2,1,0:T(8,128)(2,1)S(1)} %pad_maximum_fusion.7.refs_3_), channel_id=1, source_target_pairs={{0,4},{1,5},{2,6},{3,7},{4,0},{5,1},{6,2},{7,3},{8,12},{9,13},{10,... | collective-permute-start | bytes 1935368 | tf_op jit(solution)/shard_map/ff_own1/ppermute | solution.py:73
  89.3 26.8 %collective-permute-start.12 = (bf16[2,3,48,1120]{3,2,1,0:T(8,128)(2,1)S(1)}, bf16[2,3,48,1120]{3,2,1,0:T(8,128)(2,1)S(1)}, u32[]{:S(2)}, u32[]{:S(2)}) collective-permute-start(bf16[2,3,48,1120]{3,2,1,0:T(8,128)(2,1)S(1)} %pad_maximum_fusion.7.refs_3_), channel_id=1, source_target_pairs={{0,2},{1,3},{2,0},{3,1},{4,6},{5,7},{6,4},{7,5},{8,10},{9,11},{10,... | collective-permute-start | bytes 1935368 | tf_op jit(solution)/shard_map/ff_own1/ppermute | solution.py:73
  116.1 53.6 %copy-start.15 = (bf16[2,3,48,1120]{3,2,1,0:T(8,128)(2,1)}, bf16[2,3,48,1120]{3,2,1,0:T(8,128)(2,1)S(1)}, u32[]{:S(2)}) copy-start(bf16[2,3,48,1120]{3,2,1,0:T(8,128)(2,1)S(1)} %collective-permute-done.13.refs_5_) | copy-start | bytes 1935364
  116.1 53.6 %copy-start.16 = (bf16[2,3,48,1120]{3,2,1,0:T(8,128)(2,1)}, bf16[2,3,48,1120]{3,2,1,0:T(8,128)(2,1)S(1)}, u32[]{:S(2)}) copy-start(bf16[2,3,48,1120]{3,2,1,0:T(8,128)(2,1)S(1)} %collective-permute-done.12.refs_4_) | copy-start | bytes 1935364
  118.8 7.7 %collective-permute-start.14 = (bf16[12,48,3712]{2,1,0:T(8,128)(2,1)}, bf16[12,48,3712]{2,1,0:T(8,128)(2,1)}, u32[]{:S(2)}, u32[]{:S(2)}) collective-permute-start(bf16[12,48,3712]{2,1,0:T(8,128)(2,1)} %pad_maximum_fusion), channel_id=1, source_target_pairs={{0,1},{1,0},{2,3},{3,2},{4,5},{5,4},{6,7},{7,6},{8,9},{9,8},{10,11... | collective-permute-start | bytes 12828680 | tf_op jit(solution)/shard_map/qkvo_core/ppermute | solution.py:73
  119.0 90.0 %all-gather.5.cloned.1.call-start = ((), (), s32[]{:S(2)}) async-start(), calls=%async_computation.2 | async-start | bytes 1966080 | tf_op jit(solution)/shard_map/all_gather | solution.py:1064
  121.7 48.0 %collective-permute-start.19 = (bf16[6,3,48,1120]{3,2,1,0:T(8,128)(2,1)}, bf16[6,3,48,1120]{3,2,1,0:T(8,128)(2,1)S(1)}, u32[]{:S(2)}, u32[]{:S(2)}) collective-permute-start(bf16[6,3,48,1120]{3,2,1,0:T(8,128)(2,1)} %constant_dynamic-update-slice_fusion.5.refs_6_), channel_id=1, source_target_pairs={{0,4},{1,5},{2,6},{3,7},{4,0},{5,1},{6,2},{7,3},{8,12},{9,13},{10,... | collective-permute-start | bytes 5806088 | tf_op jit(solution)/shard_map/ff_plane1/ppermute | solution.py:73
  123.0 50.6 %collective-permute-start.18 = (bf16[6,3,48,1120]{3,2,1,0:T(8,128)(2,1)}, bf16[6,3,48,1120]{3,2,1,0:T(8,128)(2,1)}, u32[]{:S(2)}, u32[]{:S(2)}) collective-permute-start(bf16[6,3,48,1120]{3,2,1,0:T(8,128)(2,1)} %constant_dynamic-update-slice_fusion.5.refs_6_), channel_id=1, source_target_pairs={{0,2},{1,3},{2,0},{3,1},{4,6},{5,7},{6,4},{7,5},{8,10},{9,11},{10,... | collective-permute-start | bytes 5806088 | tf_op jit(solution)/shard_map/ff_plane1/ppermute | solution.py:73
  132.8 9.5 %collective-permute-start.17 = (bf16[128,512]{1,0:T(8,128)(2,1)}, bf16[128,512]{1,0:T(8,128)(2,1)S(1)}, u32[]{:S(2)}, u32[]{:S(2)}) collective-permute-start(bf16[128,512]{1,0:T(8,128)(2,1)} %get-tuple-element.131.refs_4_.refs_8_), channel_id=1, source_target_pairs={{0,24},{1,25},{2,26},{3,27},{4,28},{5,29},{6,30},{7,31}} | collective-permute-start | bytes 393224 | tf_op jit(solution)/shard_map/kv/ppermute | solution.py:73
  133.5 21.2 %collective-permute-start.16 = (bf16[128,512]{1,0:T(8,128)(2,1)}, bf16[128,512]{1,0:T(8,128)(2,1)}, u32[]{:S(2)}, u32[]{:S(2)}) collective-permute-start(bf16[128,512]{1,0:T(8,128)(2,1)} %get-tuple-element.131.refs_4_.refs_8_), channel_id=1, source_target_pairs={{0,16},{1,17},{2,18},{3,19},{4,20},{5,21},{6,22},{7,23},{8,24},{9,... | collective-permute-start | bytes 393224 | tf_op jit(solution)/shard_map/kv/ppermute | solution.py:73
  139.7 24.1 %collective-permute-start.15 = (bf16[128,512]{1,0:T(8,128)(2,1)}, bf16[128,512]{1,0:T(8,128)(2,1)}, u32[]{:S(2)}, u32[]{:S(2)}) collective-permute-start(bf16[128,512]{1,0:T(8,128)(2,1)} %get-tuple-element.131.refs_4_.refs_8_), channel_id=1, source_target_pairs={{0,8},{1,9},{2,10},{3,11},{4,12},{5,13},{6,14},{7,15},{8,16},{9,17... | collective-permute-start | bytes 393224 | tf_op jit(solution)/shard_map/kv/ppermute | solution.py:73
  142.3 21.5 %copy-start.33 = (bf16[128,512]{1,0:T(8,128)(2,1)}, bf16[128,512]{1,0:T(8,128)(2,1)S(1)}, u32[]{:S(2)}) copy-start(bf16[128,512]{1,0:T(8,128)(2,1)S(1)} %collective-permute-done.17.refs_7_.refs_11_) | copy-start | bytes 393220
  169.6 79.8 %all-gather.9.cloned.1.call-start = ((), (), s32[]{:S(2)}) async-start(), calls=%async_computation.4 | async-start | bytes 1966080 | tf_op jit(solution)/shard_map/all_gather | solution.py:1094
  172.0 31.2 %collective-permute-start.20 = (bf16[4,3,48,1120]{3,2,1,0:T(8,128)(2,1)}, bf16[4,3,48,1120]{3,2,1,0:T(8,128)(2,1)S(1)}, u32[]{:S(2)}, u32[]{:S(2)}) collective-permute-start(bf16[4,3,48,1120]{3,2,1,0:T(8,128)(2,1)} %pad_maximum_fusion.2), channel_id=1, source_target_pairs={{0,2},{1,3},{2,0},{3,1},{4,6},{5,7},{6,4},{7,5},{8,10},{9,11},{10,... | collective-permute-start | bytes 3870728 | tf_op jit(solution)/shard_map/ff_plane2/ppermute | solution.py:73
  175.9 33.1 %collective-permute-start.22 = (bf16[512,1536]{1,0:T(8,128)(2,1)}, bf16[512,1536]{1,0:T(8,128)(2,1)S(1)}, u32[]{:S(2)}, u32[]{:S(2)}) collective-permute-start(bf16[512,1536]{1,0:T(8,128)(2,1)} %all-gather.7.cloned.1.call-done.refs_2_.refs_4_.refs_6_), channel_id=1, source_target_pairs={{0,1},{1,0},{2,3},{3,2},{4,5},{5,4},{6,7},{7,6},{8,9},{9,8},{10,11... | collective-permute-start | bytes 4718600 | tf_op jit(solution)/shard_map/gy_core/ppermute | solution.py:73
  177.3 31.7 %collective-permute-start.21 = (bf16[4,3,48,1120]{3,2,1,0:T(8,128)(2,1)S(1)}, bf16[4,3,48,1120]{3,2,1,0:T(8,128)(2,1)}, u32[]{:S(2)}, u32[]{:S(2)}) collective-permute-start(bf16[4,3,48,1120]{3,2,1,0:T(8,128)(2,1)S(1)} %pad_maximum_fusion.3), channel_id=1, source_target_pairs={{0,4},{1,5},{2,6},{3,7},{4,0},{5,1},{6,2},{7,3},{8,12},{9,13},{10,... | collective-permute-start | bytes 3870728 | tf_op jit(solution)/shard_map/ff_plane2/ppermute | solution.py:73
  203.2 5.7 %copy-start.11 = (bf16[4,3,48,1120]{3,2,1,0:T(8,128)(2,1)}, bf16[4,3,48,1120]{3,2,1,0:T(8,128)(2,1)S(1)}, u32[]{:S(2)}) copy-start(bf16[4,3,48,1120]{3,2,1,0:T(8,128)(2,1)S(1)} %collective-permute-done.20.refs_9_) | copy-start | bytes 3870724
  209.0 17.0 %copy-start.4 = (bf16[512,1536]{1,0:T(8,128)(2,1)}, bf16[512,1536]{1,0:T(8,128)(2,1)S(1)}, u32[]{:S(2)}) copy-start(bf16[512,1536]{1,0:T(8,128)(2,1)S(1)} %collective-permute-done.22.refs_2_.refs_5_.refs_7_) | copy-start | bytes 4718596
  209.0 17.0 %collective-permute-start.23 = (bf16[512,1536]{1,0:T(8,128)(2,1)}, bf16[512,1536]{1,0:T(8,128)(2,1)S(1)}, u32[]{:S(2)}, u32[]{:S(2)}) collective-permute-start(bf16[512,1536]{1,0:T(8,128)(2,1)} %all-gather.5.cloned.1.call-done.refs_1_.refs_0_.refs_2_), channel_id=1, source_target_pairs={{0,1},{1,0},{2,3},{3,2},{4,5},{5,4},{6,7},{7,6},{8,9},{9,8},{10,11... | collective-permute-start | bytes 4718600 | tf_op jit(solution)/shard_map/n2_core/ppermute | solution.py:73
  209.1 77.8 %reduce-scatter.3.cloned.1.call-start = ((), (), s32[]{:S(2)}) async-start(), calls=%async_computation.5 | async-start | bytes 1966080 | tf_op jit(solution)/shard_map/reduce_scatter | solution.py:1095
  227.2 20.7 %copy-start.20 = (bf16[512,1536]{1,0:T(8,128)(2,1)S(1)}, bf16[512,1536]{1,0:T(8,128)(2,1)}, u32[]{:S(2)}) copy-start(bf16[512,1536]{1,0:T(8,128)(2,1)} %get-tuple-element.157) | copy-start | bytes 4718596
  244.0 3.9 collective-permute-start.24
  249.5 117.9 %all-gather.11.cloned.1.call-start = ((), (), s32[]{:S(2)}) async-start(), calls=%async_computation.7 | async-start | bytes 1966080 | tf_op jit(solution)/shard_map/all_gather | solution.py:1123
  262.4 22.9 %collective-permute-start.26 = (bf16[2,1,192,1120]{3,2,1,0:T(8,128)(2,1)}, bf16[2,1,192,1120]{3,2,1,0:T(8,128)(2,1)}, u32[]{:S(2)}, u32[]{:S(2)}) collective-permute-start(bf16[2,1,192,1120]{3,2,1,0:T(8,128)(2,1)} %get-tuple-element.150), channel_id=1, source_target_pairs={{0,4},{1,5},{2,6},{3,7},{4,0},{5,1},{6,2},{7,3},{8,12},{9,13},{10,... | collective-permute-start | bytes 2580488 | tf_op jit(solution)/shard_map/ff_sum1/ppermute | solution.py:73
  264.1 22.8 %collective-permute-start.27 = (bf16[2,1,192,1120]{3,2,1,0:T(8,128)(2,1)}, bf16[2,1,192,1120]{3,2,1,0:T(8,128)(2,1)}, u32[]{:S(2)}, u32[]{:S(2)}) collective-permute-start(bf16[2,1,192,1120]{3,2,1,0:T(8,128)(2,1)} %get-tuple-element.152), channel_id=1, source_target_pairs={{0,2},{1,3},{2,0},{3,1},{4,6},{5,7},{6,4},{7,5},{8,10},{9,11},{10,... | collective-permute-start | bytes 2580488 | tf_op jit(solution)/shard_map/ff_sum1/ppermute | solution.py:73
  264.5 60.5 %collective-permute-start.34 = (bf16[2,2,192,1120]{3,2,1,0:T(8,128)(2,1)}, bf16[2,2,192,1120]{3,2,1,0:T(8,128)(2,1)S(1)}, u32[]{:S(2)}, u32[]{:S(2)}) collective-permute-start(bf16[2,2,192,1120]{3,2,1,0:T(8,128)(2,1)} %get-tuple-element.151), channel_id=1, source_target_pairs={{0,4},{1,5},{2,6},{3,7},{4,0},{5,1},{6,2},{7,3},{8,12},{9,13},{10,... | collective-permute-start | bytes 5160968 | tf_op jit(solution)/shard_map/ff_sum1/ppermute | solution.py:73
  265.0 60.1 %collective-permute-start.35 = (bf16[2,2,192,1120]{3,2,1,0:T(8,128)(2,1)}, bf16[2,2,192,1120]{3,2,1,0:T(8,128)(2,1)S(1)}, u32[]{:S(2)}, u32[]{:S(2)}) collective-permute-start(bf16[2,2,192,1120]{3,2,1,0:T(8,128)(2,1)} %get-tuple-element.153), channel_id=1, source_target_pairs={{0,2},{1,3},{2,0},{3,1},{4,6},{5,7},{6,4},{7,5},{8,10},{9,11},{10,... | collective-permute-start | bytes 5160968 | tf_op jit(solution)/shard_map/ff_sum1/ppermute | solution.py:73
  276.0 24.3 %collective-permute-start.25 = (bf16[512,1536]{1,0:T(8,128)(2,1)}, bf16[512,1536]{1,0:T(8,128)(2,1)}, u32[]{:S(2)}, u32[]{:S(2)}) collective-permute-start(bf16[512,1536]{1,0:T(8,128)(2,1)} %get-tuple-element.156), channel_id=1, source_target_pairs={{0,1},{1,0},{2,3},{3,2},{4,5},{5,4},{6,7},{7,6},{8,9},{9,8},{10,11... | collective-permute-start | bytes 4718600 | tf_op jit(solution)/shard_map/y_core/ppermute | solution.py:73
  286.9 114.1 %reduce-scatter.5.cloned.1.call-start = ((), (), s32[]{:S(2)}) async-start(), calls=%async_computation.6 | async-start | bytes 1966080 | tf_op jit(solution)/shard_map/reduce_scatter | solution.py:1159
  297.0 18.0 %collective-permute-start.28 = (bf16[128,512]{1,0:T(8,128)(2,1)}, bf16[128,512]{1,0:T(8,128)(2,1)S(1)}, u32[]{:S(2)}, u32[]{:S(2)}) collective-permute-start(bf16[128,512]{1,0:T(8,128)(2,1)} %get-tuple-element.167), channel_id=1, source_target_pairs={{8,0},{9,1},{10,2},{11,3},{12,4},{13,5},{14,6},{15,7},{16,8},{17,9... | collective-permute-start | bytes 393224 | tf_op jit(solution)/shard_map/gkv/ppermute | solution.py:73
  299.0 16.8 %collective-permute-start.29 = (bf16[128,512]{1,0:T(8,128)(2,1)}, bf16[128,512]{1,0:T(8,128)(2,1)S(1)}, u32[]{:S(2)}, u32[]{:S(2)}) collective-permute-start(bf16[128,512]{1,0:T(8,128)(2,1)} %get-tuple-element.168), channel_id=1, source_target_pairs={{16,0},{17,1},{18,2},{19,3},{20,4},{21,5},{22,6},{23,7},{24,8},{25... | collective-permute-start | bytes 393224 | tf_op jit(solution)/shard_map/gkv/ppermute | solution.py:73
  300.3 15.5 %collective-permute-start.30 = (bf16[128,512]{1,0:T(8,128)(2,1)}, bf16[128,512]{1,0:T(8,128)(2,1)S(1)}, u32[]{:S(2)}, u32[]{:S(2)}) collective-permute-start(bf16[128,512]{1,0:T(8,128)(2,1)} %get-tuple-element.169), channel_id=1, source_target_pairs={{24,0},{25,1},{26,2},{27,3},{28,4},{29,5},{30,6},{31,7}} | collective-permute-start | bytes 393224 | tf_op jit(solution)/shard_map/gkv/ppermute | solution.py:73
  326.8 21.4 %copy-start.19 = (bf16[512,1536]{1,0:T(8,128)(2,1)S(1)}, bf16[512,1536]{1,0:T(8,128)(2,1)}, u32[]{:S(2)}) copy-start(bf16[512,1536]{1,0:T(8,128)(2,1)} %get-tuple-element.155) | copy-start | bytes 4718596
  331.3 42.7 %collective-permute-start.36 = (bf16[3,192,1120]{2,1,0:T(8,128)(2,1)}, bf16[3,192,1120]{2,1,0:T(8,128)(2,1)S(1)}, u32[]{:S(2)}, u32[]{:S(2)}) collective-permute-start(bf16[3,192,1120]{2,1,0:T(8,128)(2,1)} %get-tuple-element.183), channel_id=1, source_target_pairs={{0,2},{1,3},{2,0},{3,1},{4,6},{5,7},{6,4},{7,5},{8,10},{9,11},{10,... | collective-permute-start | bytes 3870728 | tf_op jit(solution)/shard_map/ff_sum2/ppermute | solution.py:73
  331.8 42.2 %collective-permute-start.37 = (bf16[3,192,1120]{2,1,0:T(8,128)(2,1)}, bf16[3,192,1120]{2,1,0:T(8,128)(2,1)S(1)}, u32[]{:S(2)}, u32[]{:S(2)}) collective-permute-start(bf16[3,192,1120]{2,1,0:T(8,128)(2,1)} %get-tuple-element.184), channel_id=1, source_target_pairs={{0,4},{1,5},{2,6},{3,7},{4,0},{5,1},{6,2},{7,3},{8,12},{9,13},{10,... | collective-permute-start | bytes 3870728 | tf_op jit(solution)/shard_map/ff_sum2/ppermute | solution.py:73
  332.2 27.8 %collective-permute-start.31 = (bf16[144,896]{1,0:T(8,128)(2,1)}, bf16[144,896]{1,0:T(8,128)(2,1)S(1)}, u32[]{:S(2)}, u32[]{:S(2)}) collective-permute-start(bf16[144,896]{1,0:T(8,128)(2,1)} %get-tuple-element.173), channel_id=1, source_target_pairs={{0,8},{1,9},{2,10},{3,11},{4,12},{5,13},{6,14},{7,15},{8,16},{9,17... | collective-permute-start | bytes 774152 | tf_op jit(solution)/shard_map/gqkv_ctx/ppermute | solution.py:73
  343.1 20.8 %collective-permute-start.32 = (bf16[144,896]{1,0:T(8,128)(2,1)}, bf16[144,896]{1,0:T(8,128)(2,1)S(1)}, u32[]{:S(2)}, u32[]{:S(2)}) collective-permute-start(bf16[144,896]{1,0:T(8,128)(2,1)} %get-tuple-element.174), channel_id=1, source_target_pairs={{0,16},{1,17},{2,18},{3,19},{4,20},{5,21},{6,22},{7,23},{8,24},{9,... | collective-permute-start | bytes 774152 | tf_op jit(solution)/shard_map/gqkv_ctx/ppermute | solution.py:73
  348.2 19.1 %collective-permute-start.33 = (bf16[144,896]{1,0:T(8,128)(2,1)}, bf16[144,896]{1,0:T(8,128)(2,1)S(1)}, u32[]{:S(2)}, u32[]{:S(2)}) collective-permute-start(bf16[144,896]{1,0:T(8,128)(2,1)} %get-tuple-element.175), channel_id=1, source_target_pairs={{0,24},{1,25},{2,26},{3,27},{4,28},{5,29},{6,30},{7,31},{8,0},{9,1... | collective-permute-start | bytes 774152 | tf_op jit(solution)/shard_map/gqkv_ctx/ppermute | solution.py:73
  360.0 7.3 %copy-start.28 = (bf16[144,896]{1,0:T(8,128)(2,1)}, bf16[144,896]{1,0:T(8,128)(2,1)S(1)}, u32[]{:S(2)}) copy-start(bf16[144,896]{1,0:T(8,128)(2,1)S(1)} %collective-permute-done.31.refs_1_) | copy-start | bytes 774148
  374.0 8.2 %collective-permute-start.38 = (bf16[4,208,896]{2,1,0:T(8,128)(2,1)}, bf16[4,208,896]{2,1,0:T(8,128)(2,1)S(1)}, u32[]{:S(2)}, u32[]{:S(2)}) collective-permute-start(bf16[4,208,896]{2,1,0:T(8,128)(2,1)} %get-tuple-element.190), channel_id=1, source_target_pairs={{0,1},{1,0},{2,3},{3,2},{4,5},{5,4},{6,7},{7,6},{8,9},{9,8},{10,11... | collective-permute-start | bytes 4472840 | tf_op jit(solution)/shard_map/term_core/ppermute | solution.py:73
  381.7 8.3 %collective-permute-start.39 = (bf16[3,192,1120]{2,1,0:T(8,128)(2,1)}, bf16[3,192,1120]{2,1,0:T(8,128)(2,1)S(1)}, u32[]{:S(2)}, u32[]{:S(2)}) collective-permute-start(bf16[3,192,1120]{2,1,0:T(8,128)(2,1)} %shard_map.266), channel_id=1, source_target_pairs={{0,1},{1,0},{2,3},{3,2},{4,5},{5,4},{6,7},{7,6},{8,9},{9,8},{10,11... | collective-permute-start | bytes 3870728 | tf_op jit(solution)/shard_map/final_core/ppermute | solution.py:73
  386.5 16.5 %collective-permute-start.40 = (bf16[208,896]{1,0:T(8,128)(2,1)}, bf16[208,896]{1,0:T(8,128)(2,1)S(1)}, u32[]{:S(2)}, u32[]{:S(2)}) collective-permute-start(bf16[208,896]{1,0:T(8,128)(2,1)} %get-tuple-element.191), channel_id=1, source_target_pairs={{0,2},{1,3},{2,0},{3,1},{4,6},{5,7},{6,4},{7,5},{8,10},{9,11},{10,... | collective-permute-start | bytes 1118216 | tf_op jit(solution)/shard_map/term_plane/ppermute | solution.py:73
  388.3 18.5 %collective-permute-start.41 = (bf16[208,896]{1,0:T(8,128)(2,1)}, bf16[208,896]{1,0:T(8,128)(2,1)S(1)}, u32[]{:S(2)}, u32[]{:S(2)}) collective-permute-start(bf16[208,896]{1,0:T(8,128)(2,1)} %get-tuple-element.192), channel_id=1, source_target_pairs={{0,4},{1,5},{2,6},{3,7},{4,0},{5,1},{6,2},{7,3},{8,12},{9,13},{10,... | collective-permute-start | bytes 1118216 | tf_op jit(solution)/shard_map/term_plane/ppermute | solution.py:73
  389.2 17.5 %collective-permute-start.42 = (bf16[208,896]{1,0:T(8,128)(2,1)}, bf16[208,896]{1,0:T(8,128)(2,1)S(1)}, u32[]{:S(2)}, u32[]{:S(2)}) collective-permute-start(bf16[208,896]{1,0:T(8,128)(2,1)} %get-tuple-element.193), channel_id=1, source_target_pairs={{0,6},{1,7},{2,4},{3,5},{4,2},{5,3},{6,0},{7,1},{8,14},{9,15},{10,... | collective-permute-start | bytes 1118216 | tf_op jit(solution)/shard_map/term_plane/ppermute | solution.py:73
  390.0 5.9 %copy-start.45 = (bf16[3,192,1120]{2,1,0:T(8,128)(2,1)}, bf16[3,192,1120]{2,1,0:T(8,128)(2,1)S(1)}, u32[]{:S(2)}) copy-start(bf16[3,192,1120]{2,1,0:T(8,128)(2,1)S(1)} %collective-permute-done.39.got) | copy-start | bytes 3870724
  395.9 5.1 %copy-start.24 = (f32[128,1536]{1,0:T(8,128)S(1)}, f32[128,1536]{1,0:T(8,128)}, u32[]{:S(2)}) copy-start(f32[128,1536]{1,0:T(8,128)} %get-tuple-element.132.refs_1_) | copy-start | bytes 2359300
  (33 other events, 77.2 us)
Sparse Core Ops, SparseCore 0:
  119.1 46.5 all-gather.6
  169.7 37.2 all-gather.4
  209.2 36.4 all-gather.8
  249.6 34.3 reduce-scatter.2
  287.0 45.2 all-gather.10
  367.4 33.0 reduce-scatter.4
